TPU v7x, 32 devices: a whole 2x2x4 slice. The times are simulated.
32 devices in a mesh: cgrp: 4 (over z), dev: 8 (over y, x, core).
Axes of the slice: x: 2, y: 2, z: 4, core: 2. Of those that a mesh axis runs over, the one named last changes fastest.
Arguments:
- docs: bfloat16 [16384, 1024], P('dev'), may hold values from -140 to 140
- centroids: float32 [1024, 1024], P(('cgrp', 'dev')), may hold values from -6 to 6
Outputs:
- centroids_next: float32 [1024, 1024], P(('cgrp', 'dev'))
- mass: float32 [1024], P(('cgrp', 'dev'))
- doc_lse: float32 [16384], P('dev')
All inputs are finite; a program needn't handle non-finite values.
Results may differ from a plain program's by a relative error of at most 0.012.
The roundings to bfloat16 on the way count: a program that leaves them out, or rounds other values in their place, can miss the bound.
Values may be sent and summed in bfloat16 or wider, within the bound.
No kernel may reach another device: no remote copies, remote signals or barrier semaphores. Data moves between devices by JAX's collectives and lax.ppermute only.
A program may use at most 64 MiB of HBM per device.

v0:
```python
import math

import jax
import jax.numpy as jnp
from jax import lax
from jax.sharding import PartitionSpec as P


def body(docs, centroids):
    width = docs.shape[1]
    scale = 4.0 / math.sqrt(width)
    rounded = centroids.astype(jnp.bfloat16)
    gathered = lax.all_gather(rounded, "dev", axis=0, tiled=True)
    gathered_wide = gathered.astype(jnp.float32)
    gathered_norms = jnp.sum(gathered_wide * gathered_wide, axis=1)
    dots = lax.dot_general(
        docs, gathered, (((1,), (1,)), ((), ())), preferred_element_type=jnp.float32
    )
    scores = (dots - 0.5 * gathered_norms[None, :]) * scale
    local_max = jnp.max(scores, axis=1)
    local_sum = jnp.sum(jnp.exp(scores - local_max[:, None]), axis=1)
    group_top = lax.pmax(local_max, "cgrp")
    group_sum = lax.psum(local_sum * jnp.exp(local_max - group_top), "cgrp")
    doc_lse = group_top + jnp.log(group_sum)
    resp = jnp.exp(scores - doc_lse[:, None])
    docs_wide = docs.astype(jnp.float32)
    local_mass = jnp.sum(resp, axis=0)
    term = lax.dot_general(
        resp,
        docs_wide,
        (((0,), (0,)), ((), ())),
        preferred_element_type=jnp.float32,
        precision=lax.Precision.HIGHEST,
    )
    weighted, mass = (
        lax.psum_scatter(term, "dev", scatter_dimension=0, tiled=True),
        lax.psum_scatter(local_mass, "dev", scatter_dimension=0, tiled=True),
    )
    centroids_next = (weighted + centroids) / (mass[:, None] + 1.0)
    return (centroids_next, mass, doc_lse)


def solution(mesh):
    in_specs = (P("dev", None), P(("cgrp", "dev"), None))
    out_specs = (P(("cgrp", "dev"), None), P(("cgrp", "dev")), P("dev"))
    return jax.shard_map(body, mesh=mesh, in_specs=in_specs, out_specs=out_specs, check_vma=False)
```

profile of v0, /device:TPU:0, one launch (start us, length us, event | category | flops | bytes accessed | tf_op | source)
XLA Modules:
  0.0 94.3 jit_solution(1609492005715149731)
XLA Ops:
  7.2 0.0 reduce-scatter.2.cloned.1.call-start
  7.2 0.9 convert_element_type.7
  8.1 11.3 %all_gather.3 = bf16[256,1024]{1,0:T(8,128)(2,1)S(1)} all-gather(bf16[32,1024]{1,0:T(8,128)(2,1)S(1)} %convert_element_type.7), channel_id=1, replica_groups=mesh['cgrp'=4,'dev'=8] {'dev'}, dimensions={0}, use_global_device_ids=true | all-gather | bytes 589824 | tf_op jit(solution)/shard_map/all_gather | solution.py:13
  19.4 0.2 multiply_reduce_fusion
  19.6 3.5 %fusion.4 = (f32[2048]{0:T(1024)S(1)}, f32[2048,256]{0,1:T(8,128)S(1)}) fusion(f32[256]{0:T(256)S(1)} %broadcast_multiply_fusion, bf16[2048,1024]{1,0:T(8,128)(2,1)} %param.2, bf16[256,1024]{1,0:T(8,128)(2,1)S(1)} %all_gather.3), kind=kOutput, calls=%fused_computation.13 | convolution fusion | flops 1075312640 | bytes 6824960 | tf_op jit(solution)/shard_map/dot_general | solution.py:16
  23.1 12.1 %pmax.7 = f32[2048]{0:T(1024)S(1)} all-reduce(f32[2048]{0:T(1024)S(1)} %get-tuple-element.5), channel_id=1, replica_groups=mesh['cgrp'=4,'dev'=8] {'cgrp'}, use_global_device_ids=true, to_apply=%region_2.0 | all-reduce | flops 2048 | bytes 16384 | tf_op jit(solution)/shard_map/pmax | solution.py:22
  35.2 0.3 exponential_reduce_fusion
  35.6 8.5 %psum.7 = f32[2048]{0:T(1024)S(1)} all-reduce(f32[2048]{0:T(1024)S(1)} %exponential_multiply_fusion), channel_id=1, replica_groups=mesh['cgrp'=4,'dev'=8] {'cgrp'}, use_global_device_ids=true, to_apply=%region_4.0 | all-reduce | flops 2048 | bytes 16384 | tf_op jit(solution)/shard_map/psum | solution.py:23
  44.1 0.0 copy-start.1
  44.1 0.0 copy-start.2
  44.1 6.7 %fusion.2 = f32[256,1024]{1,0:T(8,128)} fusion(bf16[2048,1024]{1,0:T(8,128)(2,1)} %param.2, f32[2048,256]{0,1:T(8,128)S(1)} %get-tuple-element.6, f32[2048]{0:T(1024)S(1)} %log_add_fusion), kind=kOutput, calls=%fused_computation.5 | convolution fusion | flops 6442975232 | bytes 7348224 | tf_op jit(solution)/shard_map/dot_general | solution.py:28
  50.9 0.0 copy-start
  50.9 0.0 reduce-scatter.2.cloned.1.call-update
  50.9 0.0 copy-done.2
  50.9 0.6 dynamic-slice
  52.2 0.0 copy-done.1
  52.2 0.4 fusion.1
  52.5 11.8 %all-reduce = f32[256]{0:T(256)S(1)} all-reduce(f32[256]{0:T(256)S(1)} %fusion.1), channel_id=3, replica_groups=mesh['cgrp'=4,'dev'=8] {'dev'}, use_global_device_ids=true, to_apply=%region_7.0.clone | all-reduce | flops 256 | bytes 2048
  64.4 0.6 broadcast_add_fusion
  65.0 20.9 %reduce-scatter.2.cloned.1.call-done = f32[32,1024]{1,0:T(8,128)} async-done(((f32[256,1024]{1,0:T(8,128)}), f32[32,1024]{1,0:T(8,128)}) %reduce-scatter.2.cloned.1.call-update) | async-done | bytes 131088 | tf_op jit(solution)/shard_map/reduce_scatter | solution.py:36
  85.8 0.0 copy-done
  85.8 1.6 %add_divide_fusion = f32[32,1024]{1,0:T(8,128)} fusion(f32[32,1024]{1,0:T(8,128)} %reduce-scatter.2.cloned.1.call-done, f32[32,1024]{1,0:T(8,128)S(1)} %copy-done, f32[32]{0:T(128)S(1)} %get-tuple-element.3), kind=kLoop, calls=%fused_computation.8 | loop fusion | flops 65536 | bytes 393344 | tf_op jit(solution)/shard_map/div | solution.py:39
  (3 shorter events, 0.0 us)
Async XLA Ops:
  7.2 78.6 %reduce-scatter.2.cloned.1.call-start = ((), (), s32[]{:S(2)}) async-start(), calls=%async_computation.1 | async-start | bytes 1179648 | tf_op jit(solution)/shard_map/reduce_scatter | solution.py:36
  44.1 8.0 %copy-start.1 = (f32[2048]{0:T(1024)}, f32[2048]{0:T(1024)S(1)}, u32[]{:S(2)}) copy-start(f32[2048]{0:T(1024)S(1)} %log_add_fusion) | copy-start | bytes 24580
  44.1 6.8 %copy-start.2 = (u32[32]{0:T(128)S(1)}, u32[32]{0:T(128)}, u32[]{:S(2)}) copy-start(u32[32]{0:T(128)} %constant.12) | copy-start | bytes 388
  50.9 34.9 %copy-start = (f32[32,1024]{1,0:T(8,128)S(1)}, f32[32,1024]{1,0:T(8,128)}, u32[]{:S(2)}) copy-start(f32[32,1024]{1,0:T(8,128)} %param.3) | copy-start | bytes 393220
Sparse Core Ops, SparseCore 0:
  51.0 34.7 reduce-scatter.1
where the time goes:
time: 94.6 us; the launch traced here: 94.3 us
  blocking collectives  43.8 us (46%)
  waiting for transfers between devices  20.9 us (22%)
  between operations  14.8 us (16%)
  matrix products  10.2 us (11%)
  other arithmetic  4.02 us (4%)
    reduce_scatter x1, waiting for transfers between devices, body(): lax.psum_scatter(term, 'dev', scatter_dimension=0, tiled=True)  20.9 us
    pmax x1, blocking collectives, body(): group_top = lax.pmax(local_max, 'cgrp')  12.1 us
    unnamed x1, blocking collectives  11.8 us
    all_gather x1, blocking collectives, body(): gathered = lax.all_gather(rounded, 'dev', axis=0, tiled=True)  11.3 us
    psum x1, blocking collectives, body(): group_sum = lax.psum(local_sum * jnp.exp(local_max - group_top), 'cgrp')  8.52 us
    dot_general x1, matrix products, body(): lax.dot_general(resp, docs_wide, (((0,), (0,)), ((), ())), preferred_elem...  6.74 us
    dot_general x1, matrix products, body(): lax.dot_general(docs, gathered, (((1,), (1,)), ((), ())), preferred_eleme...  3.49 us
  transfers between devices with their start and end apart: 1, of which 1 were waited for; matrix products, arithmetic and copies ran while one was open for 2% of the time, Pallas kernels for 0%

commit v1 on v0

v1 whole, which is shorter than its diff:
```python
import math

import jax
import jax.numpy as jnp
from jax import lax
from jax.sharding import PartitionSpec as P


def swap(x, axis, size, mask):
    return lax.ppermute(x, axis, [(i, i ^ mask) for i in range(size)])


def tree(parts, op):
    while len(parts) > 1:
        parts = [op(parts[i], parts[i + 1]) for i in range(0, len(parts), 2)]
    return parts[0]


def make_body(n, g):
    def body(docs, centroids):
        rows, width = centroids.shape
        scale = 4.0 / math.sqrt(width)
        rounded = centroids.astype(jnp.bfloat16)
        mine = jnp.concatenate(
            [rounded] + [swap(rounded, "dev", n, m) for m in range(2, n, 2)], axis=0
        )
        theirs = swap(mine, "dev", n, 1)
        table = jnp.concatenate([mine, theirs], axis=0)
        wide = table.astype(jnp.float32)
        norms = jnp.sum(wide * wide, axis=1)
        dots = lax.dot_general(
            docs, table, (((1,), (1,)), ((), ())), preferred_element_type=jnp.float32
        )
        scores = (dots - 0.5 * norms[None, :]) * scale
        top = jnp.max(scores, axis=1)
        group_lse = top + jnp.log(jnp.sum(jnp.exp(scores - top[:, None]), axis=1))
        all_lse = [group_lse] + [swap(group_lse, "cgrp", g, m) for m in range(1, g)]
        best = tree(all_lse, jnp.maximum)
        doc_lse = best + jnp.log(tree([jnp.exp(x - best) for x in all_lse], jnp.add))
        resp = jnp.exp(scores - doc_lse[:, None])
        mass = jnp.sum(resp, axis=0)
        term = lax.dot_general(
            resp.astype(jnp.bfloat16), docs, (((0,), (0,)), ((), ())),
            preferred_element_type=jnp.float32,
        )
        lane = lax.broadcasted_iota(jnp.int32, (1, 128), 1)

        def pack(term, mass):
            high = mass.astype(jnp.bfloat16)
            low = (mass - high.astype(jnp.float32)).astype(jnp.bfloat16)
            extra = jnp.where(
                lane == 0, high[:, None], jnp.where(lane == 1, low[:, None], 0)
            ).astype(jnp.bfloat16)
            return jnp.concatenate([term.astype(jnp.bfloat16), extra], axis=1)

        def unpack(x):
            wide = x.astype(jnp.float32)
            return wide[:, :width], wide[:, width] + wide[:, width + 1]

        half = table.shape[0] // 2
        got = swap(pack(term[half:], mass[half:]), "dev", n, 1)
        got_term, got_mass = unpack(got)
        term = term[:half] + got_term
        mass = mass[:half] + got_mass
        packed = pack(term[rows:], mass[rows:])
        arrived = [
            unpack(swap(packed[(j - 1) * rows : j * rows], "dev", n, 2 * j))
            for j in range(1, n // 2)
        ]
        weighted = tree([term[:rows]] + [a for a, _ in arrived], jnp.add)
        mass = tree([mass[:rows]] + [b for _, b in arrived], jnp.add)
        return ((weighted + centroids) / (mass[:, None] + 1.0), mass, doc_lse)

    return body


def solution(mesh):
    in_specs = (P("dev", None), P(("cgrp", "dev"), None))
    out_specs = (P(("cgrp", "dev"), None), P(("cgrp", "dev")), P("dev"))
    return jax.shard_map(
        make_body(mesh.shape["dev"], mesh.shape["cgrp"]),
        mesh=mesh, in_specs=in_specs, out_specs=out_specs, check_vma=False,
    )
```

time: 94.6 us -> 38.1 us (0.40)
  blocking collectives: 43.8 us -> 0 us
  between operations: 14.8 us -> 0.84 us
  starting transfers between devices: 0.04 us -> 12.7 us
  waiting for transfers between devices: 20.9 us -> 15.2 us
  matrix products: 10.2 us -> 4.84 us
    reduce_scatter x1 -> x0, waiting for transfers between devices: 20.9 us -> none  [body(): lax.psum_scatter(term, 'dev', scatter_dimension=0, tiled=True)]
    ppermute x0 -> x11, waiting for transfers between devices: none -> 15.2 us  [swap(): return lax.ppermute(x, axis, [(i, i ^ mask) for i in range(size)])]
    ppermute x0 -> x11, starting transfers between devices: none -> 12.7 us  [swap(): return lax.ppermute(x, axis, [(i, i ^ mask) for i in range(size)])]
    pmax x1 -> x0, blocking collectives: 12.1 us -> none  [body(): group_top = lax.pmax(local_max, 'cgrp')]
    unnamed x1 -> x0, blocking collectives: 11.8 us -> none
    all_gather x1 -> x0, blocking collectives: 11.3 us -> none  [body(): gathered = lax.all_gather(rounded, 'dev', axis=0, tiled=True)]
    psum x1 -> x0, blocking collectives: 8.52 us -> none  [body(): group_sum = lax.psum(local_sum * jnp.exp(local_max - group_top), 'cgrp')]
    dot_general x2, matrix products: 10.2 us -> 4.84 us  [the longest x1 3.54 us: body(): lax.dot_general(docs, table, (((1,), (1,)), ((), ())), preferred_element_...]
  transfers between devices with their start and end apart: 1 -> 11, of which waited for: 1 -> 10; matrix products, arithmetic and copies ran while one was open for 2% -> 1% of each run, Pallas kernels for 0% -> 0%
where the time goes in v1:
time: 38.1 us; the launch traced here: 37.9 us
  waiting for transfers between devices  15.2 us (40%)
  starting transfers between devices  12.7 us (33%)
  matrix products  4.84 us (13%)
  other arithmetic  4.11 us (11%)
  between operations  0.84 us (2%)
    ppermute x11, waiting for transfers between devices, swap(): return lax.ppermute(x, axis, [(i, i ^ mask) for i in range(size)])  15.2 us
    ppermute x11, starting transfers between devices, swap(): return lax.ppermute(x, axis, [(i, i ^ mask) for i in range(size)])  12.7 us
    dot_general x1, matrix products, body(): lax.dot_general(docs, table, (((1,), (1,)), ((), ())), preferred_element_...  3.54 us
    dot_general x1, matrix products, body(): lax.dot_general(resp.astype(jnp.bfloat16), docs, (((0,), (0,)), ((), ()))...  1.3 us
    unnamed x1, other arithmetic  0.92 us
  transfers between devices with their start and end apart: 11, of which 10 were waited for; matrix products, arithmetic and copies ran while one was open for 1% of the time, Pallas kernels for 0%

profile of v1, /device:TPU:0, one launch (start us, length us, event | category | flops | bytes accessed | tf_op | source)
XLA Modules:
  0.0 37.9 jit_solution(7375288742244491671)
XLA Ops:
  0.6 0.9 %constant_dynamic-update-slice_fusion.4 = (bf16[256,1024]{1,0:T(8,128)(2,1)S(1)}, bf16[32,1024]{1,0:T(8,128)(2,1)S(1)}) fusion(f32[32,1024]{1,0:T(8,128)} %param.3), kind=kLoop, calls=%fused_computation.40 | loop fusion | flops 32767 | bytes 262144
  1.6 4.0 %collective-permute-start.2 = (bf16[32,1024]{1,0:T(8,128)(2,1)S(1)}, bf16[32,1024]{1,0:T(8,128)(2,1)S(1)}, u32[]{:S(2)}, u32[]{:S(2)}) collective-permute-start(bf16[32,1024]{1,0:T(8,128)(2,1)S(1)} %get-tuple-element.6), channel_id=1, source_target_pairs={{0,6},{1,7},{2,4},{3,5},{4,2},{5,3},{6,0},{7,1},{8,14},{9,15},{10,... | collective-permute-start | bytes 196616 | tf_op jit(solution)/shard_map/ppermute | solution.py:10
  5.5 0.5 %collective-permute-start.1 = (bf16[32,1024]{1,0:T(8,128)(2,1)S(1)}, bf16[32,1024]{1,0:T(8,128)(2,1)S(1)}, u32[]{:S(2)}, u32[]{:S(2)}) collective-permute-start(bf16[32,1024]{1,0:T(8,128)(2,1)S(1)} %get-tuple-element.6), channel_id=1, source_target_pairs={{0,4},{1,5},{2,6},{3,7},{4,0},{5,1},{6,2},{7,3},{8,12},{9,13},{10,... | collective-permute-start | bytes 196616 | tf_op jit(solution)/shard_map/ppermute | solution.py:10
  6.0 0.1 collective-permute-start
  6.2 1.6 %collective-permute-done.2 = bf16[32,1024]{1,0:T(8,128)(2,1)S(1)} collective-permute-done((bf16[32,1024]{1,0:T(8,128)(2,1)S(1)}, bf16[32,1024]{1,0:T(8,128)(2,1)S(1)}, u32[]{:S(2)}, u32[]{:S(2)}) %collective-permute-start.2) | collective-permute-done | bytes 65568 | tf_op jit(solution)/shard_map/ppermute | solution.py:10
  7.8 2.0 %collective-permute-done.1 = bf16[32,1024]{1,0:T(8,128)(2,1)S(1)} collective-permute-done((bf16[32,1024]{1,0:T(8,128)(2,1)S(1)}, bf16[32,1024]{1,0:T(8,128)(2,1)S(1)}, u32[]{:S(2)}, u32[]{:S(2)}) %collective-permute-start.1) | collective-permute-done | bytes 65568 | tf_op jit(solution)/shard_map/ppermute | solution.py:10
  9.8 0.5 %collective-permute-done = bf16[32,1024]{1,0:T(8,128)(2,1)S(1)} collective-permute-done((bf16[32,1024]{1,0:T(8,128)(2,1)S(1)}, bf16[32,1024]{1,0:T(8,128)(2,1)S(1)}, u32[]{:S(2)}, u32[]{:S(2)}) %collective-permute-start) | collective-permute-done | bytes 65568 | tf_op jit(solution)/shard_map/ppermute | solution.py:10
  10.3 0.1 collective-permute-start.3
  10.4 1.5 %collective-permute-done.3 = bf16[128,1024]{1,0:T(8,128)(2,1)S(1)} collective-permute-done((bf16[128,1024]{1,0:T(8,128)(2,1)S(1)}, bf16[128,1024]{1,0:T(8,128)(2,1)S(1)}, u32[]{:S(2)}, u32[]{:S(2)}) %collective-permute-start.3) | collective-permute-done | bytes 262176 | tf_op jit(solution)/shard_map/ppermute | solution.py:10
  11.9 0.2 multiply_reduce_fusion
  12.1 3.5 %fusion.18 = (f32[2048]{0:T(1024)S(1)}, f32[256,2048]{1,0:T(8,128)S(1)}) fusion(f32[256]{0:T(256)S(1)} %broadcast_multiply_fusion, bf16[256,1024]{1,0:T(8,128)(2,1)S(1)} %constant_dynamic-update-slice_fusion, bf16[2048,1024]{1,0:T(8,128)(2,1)} %param.2), kind=kOutput, calls=%fused_computation.58 | convolution fusion | flops 1075312640 | bytes 6824960 | tf_op jit(solution)/shard_map/dot_general | solution.py:31
  15.7 0.0 copy-start.2
  15.7 0.3 exponential_reduce_fusion
  16.0 3.7 %collective-permute-start.6 = (f32[2048]{0:T(1024)S(1)}, f32[2048]{0:T(1024)S(1)}, u32[]{:S(2)}, u32[]{:S(2)}) collective-permute-start(f32[2048]{0:T(1024)S(1)} %log_add_fusion.1), channel_id=1, source_target_pairs={{0,24},{8,16},{16,8},{24,0},{1,25},{9,17},{17,9},{25,1},{2,26},{10... | collective-permute-start | bytes 24584 | tf_op jit(solution)/shard_map/ppermute | solution.py:10
  19.7 0.0 collective-permute-start.5
  19.7 0.8 %collective-permute-start.4 = (f32[2048]{0:T(1024)S(1)}, f32[2048]{0:T(1024)S(1)}, u32[]{:S(2)}, u32[]{:S(2)}) collective-permute-start(f32[2048]{0:T(1024)S(1)} %log_add_fusion.1), channel_id=1, source_target_pairs={{0,8},{8,0},{16,24},{24,16},{1,9},{9,1},{17,25},{25,17},{2,10},{10... | collective-permute-start | bytes 24584 | tf_op jit(solution)/shard_map/ppermute | solution.py:10
  20.5 1.1 %collective-permute-done.6 = f32[2048]{0:T(1024)S(1)} collective-permute-done((f32[2048]{0:T(1024)S(1)}, f32[2048]{0:T(1024)S(1)}, u32[]{:S(2)}, u32[]{:S(2)}) %collective-permute-start.6) | collective-permute-done | bytes 8224 | tf_op jit(solution)/shard_map/ppermute | solution.py:10
  21.5 2.7 %collective-permute-done.5 = f32[2048]{0:T(1024)S(1)} collective-permute-done((f32[2048]{0:T(1024)S(1)}, f32[2048]{0:T(1024)S(1)}, u32[]{:S(2)}, u32[]{:S(2)}) %collective-permute-start.5) | collective-permute-done | bytes 8224 | tf_op jit(solution)/shard_map/ppermute | solution.py:10
  24.2 0.0 collective-permute-done.4
  24.3 0.0 copy-start.1
  24.3 0.4 fusion.1
  24.6 0.0 copy-done.2
  24.6 1.3 %fusion.3 = f32[256,1024]{1,0:T(8,128)S(1)} fusion(bf16[2048,1024]{1,0:T(8,128)(2,1)S(1)} %copy-done.2, f32[256,2048]{1,0:T(8,128)S(1)} %get-tuple-element.11, f32[2048]{0:T(1024)S(1)} %log_add_fusion), kind=kOutput, calls=%fused_computation.6 | convolution fusion | flops 1074790400 | bytes 7348224 | tf_op jit(solution)/shard_map/dot_general | solution.py:42
  25.9 0.0 copy-done.1
  26.0 0.1 select_select_fusion
  26.2 0.0 copy-start
  26.2 0.1 collective-permute-start.7
  26.2 1.6 %collective-permute-done.7 = bf16[128,1152]{1,0:T(8,128)(2,1)S(1)} collective-permute-done((bf16[128,1152]{1,0:T(8,128)(2,1)S(1)}, bf16[128,1152]{1,0:T(8,128)(2,1)S(1)}, u32[]{:S(2)}, u32[]{:S(2)}) %collective-permute-start.7) | collective-permute-done | bytes 294944 | tf_op jit(solution)/shard_map/ppermute | solution.py:10
  27.9 0.1 slice_add_fusion
  27.9 0.2 fusion.11
  28.1 0.1 subtract_convert_fusion
  28.2 0.1 slice.172
  28.3 0.1 select_select_fusion.1
  28.4 0.6 %collective-permute-start.8 = (bf16[32,1152]{1,0:T(8,128)(2,1)S(1)}, bf16[32,1152]{1,0:T(8,128)(2,1)S(1)}, u32[]{:S(2)}, u32[]{:S(2)}) collective-permute-start(bf16[32,1152]{1,0:T(8,128)(2,1)S(1)} %get-tuple-element.7), channel_id=1, source_target_pairs={{0,2},{1,3},{2,0},{3,1},{4,6},{5,7},{6,4},{7,5},{8,10},{9,11},{10,... | collective-permute-start | bytes 221192 | tf_op jit(solution)/shard_map/ppermute | solution.py:10
  29.0 2.4 %collective-permute-start.10 = (bf16[32,1152]{1,0:T(8,128)(2,1)S(1)}, bf16[32,1152]{1,0:T(8,128)(2,1)S(1)}, u32[]{:S(2)}, u32[]{:S(2)}) collective-permute-start(bf16[32,1152]{1,0:T(8,128)(2,1)S(1)} %get-tuple-element.8), channel_id=1, source_target_pairs={{0,6},{1,7},{2,4},{3,5},{4,2},{5,3},{6,0},{7,1},{8,14},{9,15},{10,... | collective-permute-start | bytes 221192 | tf_op jit(solution)/shard_map/ppermute | solution.py:10
  31.5 0.5 %collective-permute-start.9 = (bf16[32,1152]{1,0:T(8,128)(2,1)S(1)}, bf16[32,1152]{1,0:T(8,128)(2,1)S(1)}, u32[]{:S(2)}, u32[]{:S(2)}) collective-permute-start(bf16[32,1152]{1,0:T(8,128)(2,1)S(1)} %get-tuple-element.9), channel_id=1, source_target_pairs={{0,4},{1,5},{2,6},{3,7},{4,0},{5,1},{6,2},{7,3},{8,12},{9,13},{10,... | collective-permute-start | bytes 221192 | tf_op jit(solution)/shard_map/ppermute | solution.py:10
  32.0 1.4 %collective-permute-done.8 = bf16[32,1152]{1,0:T(8,128)(2,1)S(1)} collective-permute-done((bf16[32,1152]{1,0:T(8,128)(2,1)S(1)}, bf16[32,1152]{1,0:T(8,128)(2,1)S(1)}, u32[]{:S(2)}, u32[]{:S(2)}) %collective-permute-start.8) | collective-permute-done | bytes 73760 | tf_op jit(solution)/shard_map/ppermute | solution.py:10
  33.4 2.1 %collective-permute-done.10 = bf16[32,1152]{1,0:T(8,128)(2,1)S(1)} collective-permute-done((bf16[32,1152]{1,0:T(8,128)(2,1)S(1)}, bf16[32,1152]{1,0:T(8,128)(2,1)S(1)}, u32[]{:S(2)}, u32[]{:S(2)}) %collective-permute-start.10) | collective-permute-done | bytes 73760 | tf_op jit(solution)/shard_map/ppermute | solution.py:10
  35.5 0.2 fusion.14
  35.7 0.8 %collective-permute-done.9 = bf16[32,1152]{1,0:T(8,128)(2,1)S(1)} collective-permute-done((bf16[32,1152]{1,0:T(8,128)(2,1)S(1)}, bf16[32,1152]{1,0:T(8,128)(2,1)S(1)}, u32[]{:S(2)}, u32[]{:S(2)}) %collective-permute-start.9) | collective-permute-done | bytes 73760 | tf_op jit(solution)/shard_map/ppermute | solution.py:10
  36.5 0.2 fusion.13
  36.7 0.5 %broadcast_add_fusion = (f32[32]{0:T(128)S(1)}, f32[32]{0:T(128)}) fusion(f32[32]{0:T(128)S(1)} %fusion.13, f32[32]{0:T(128)S(1)} %fusion.14, f32[128]{0:T(128)S(1)} %slice_add_fusion.7), kind=kLoop, calls=%fused_computation.57 | loop fusion | flops 96 | bytes 640 | tf_op jit(solution)/shard_map/add | solution.py:72
  37.2 0.0 copy-done
  37.2 0.7 %fusion.8 = f32[32,1024]{1,0:T(8,128)} fusion(f32[32,1024]{1,0:T(8,128)S(1)} %copy-done, f32[32,1152]{1,0:T(8,128)S(1)} %convert_element_type.54, f32[32,1152]{1,0:T(8,128)S(1)} %convert_element_type.53, f32[32,1152]{1,0:T(8,128)S(1)} %convert_element_type.52, f32[128,1024]{1,0:T(8,128)S(1)} %slice_add_fusion, f32[32]{0:T(128)S(1)} %get-tuple-element.3), kind=kLoop, calls=%fused_computation.21 | loop fusion | flops 163840 | bytes 786560 | tf_op jit(solution)/shard_map/div | solution.py:72
  (20 shorter events, 0.3 us)
Async XLA Ops:
  1.6 6.2 %collective-permute-start.2 = (bf16[32,1024]{1,0:T(8,128)(2,1)S(1)}, bf16[32,1024]{1,0:T(8,128)(2,1)S(1)}, u32[]{:S(2)}, u32[]{:S(2)}) collective-permute-start(bf16[32,1024]{1,0:T(8,128)(2,1)S(1)} %get-tuple-element.6), channel_id=1, source_target_pairs={{0,6},{1,7},{2,4},{3,5},{4,2},{5,3},{6,0},{7,1},{8,14},{9,15},{10,... | collective-permute-start | bytes 196616 | tf_op jit(solution)/shard_map/ppermute | solution.py:10
  5.5 4.3 %collective-permute-start.1 = (bf16[32,1024]{1,0:T(8,128)(2,1)S(1)}, bf16[32,1024]{1,0:T(8,128)(2,1)S(1)}, u32[]{:S(2)}, u32[]{:S(2)}) collective-permute-start(bf16[32,1024]{1,0:T(8,128)(2,1)S(1)} %get-tuple-element.6), channel_id=1, source_target_pairs={{0,4},{1,5},{2,6},{3,7},{4,0},{5,1},{6,2},{7,3},{8,12},{9,13},{10,... | collective-permute-start | bytes 196616 | tf_op jit(solution)/shard_map/ppermute | solution.py:10
  6.0 4.3 %collective-permute-start = (bf16[32,1024]{1,0:T(8,128)(2,1)S(1)}, bf16[32,1024]{1,0:T(8,128)(2,1)S(1)}, u32[]{:S(2)}, u32[]{:S(2)}) collective-permute-start(bf16[32,1024]{1,0:T(8,128)(2,1)S(1)} %get-tuple-element.6), channel_id=1, source_target_pairs={{0,2},{1,3},{2,0},{3,1},{4,6},{5,7},{6,4},{7,5},{8,10},{9,11},{10,... | collective-permute-start | bytes 196616 | tf_op jit(solution)/shard_map/ppermute | solution.py:10
  10.3 1.6 %collective-permute-start.3 = (bf16[128,1024]{1,0:T(8,128)(2,1)S(1)}, bf16[128,1024]{1,0:T(8,128)(2,1)S(1)}, u32[]{:S(2)}, u32[]{:S(2)}) collective-permute-start(bf16[128,1024]{1,0:T(8,128)(2,1)S(1)} %pad_maximum_fusion.1), channel_id=1, source_target_pairs={{0,1},{1,0},{2,3},{3,2},{4,5},{5,4},{6,7},{7,6},{8,9},{9,8},{10,11... | collective-permute-start | bytes 786440 | tf_op jit(solution)/shard_map/ppermute | solution.py:10
  15.7 9.0 %copy-start.2 = (bf16[2048,1024]{1,0:T(8,128)(2,1)S(1)}, bf16[2048,1024]{1,0:T(8,128)(2,1)}, u32[]{:S(2)}) copy-start(bf16[2048,1024]{1,0:T(8,128)(2,1)} %param.2) | copy-start | bytes 12582916
  16.0 5.5 %collective-permute-start.6 = (f32[2048]{0:T(1024)S(1)}, f32[2048]{0:T(1024)S(1)}, u32[]{:S(2)}, u32[]{:S(2)}) collective-permute-start(f32[2048]{0:T(1024)S(1)} %log_add_fusion.1), channel_id=1, source_target_pairs={{0,24},{8,16},{16,8},{24,0},{1,25},{9,17},{17,9},{25,1},{2,26},{10... | collective-permute-start | bytes 24584 | tf_op jit(solution)/shard_map/ppermute | solution.py:10
  19.7 4.5 %collective-permute-start.5 = (f32[2048]{0:T(1024)S(1)}, f32[2048]{0:T(1024)S(1)}, u32[]{:S(2)}, u32[]{:S(2)}) collective-permute-start(f32[2048]{0:T(1024)S(1)} %log_add_fusion.1), channel_id=1, source_target_pairs={{0,16},{8,24},{16,0},{24,8},{1,17},{9,25},{17,1},{25,9},{2,18},{10... | collective-permute-start | bytes 24584 | tf_op jit(solution)/shard_map/ppermute | solution.py:10
  19.7 4.5 %collective-permute-start.4 = (f32[2048]{0:T(1024)S(1)}, f32[2048]{0:T(1024)S(1)}, u32[]{:S(2)}, u32[]{:S(2)}) collective-permute-start(f32[2048]{0:T(1024)S(1)} %log_add_fusion.1), channel_id=1, source_target_pairs={{0,8},{8,0},{16,24},{24,16},{1,9},{9,1},{17,25},{25,17},{2,10},{10... | collective-permute-start | bytes 24584 | tf_op jit(solution)/shard_map/ppermute | solution.py:10
  24.3 1.7 %copy-start.1 = (f32[2048]{0:T(1024)}, f32[2048]{0:T(1024)S(1)}, u32[]{:S(2)}) copy-start(f32[2048]{0:T(1024)S(1)} %log_add_fusion) | copy-start | bytes 24580
  26.2 11.0 %copy-start = (f32[32,1024]{1,0:T(8,128)S(1)}, f32[32,1024]{1,0:T(8,128)}, u32[]{:S(2)}) copy-start(f32[32,1024]{1,0:T(8,128)} %param.3) | copy-start | bytes 393220
  26.2 1.6 %collective-permute-start.7 = (bf16[128,1152]{1,0:T(8,128)(2,1)S(1)}, bf16[128,1152]{1,0:T(8,128)(2,1)S(1)}, u32[]{:S(2)}, u32[]{:S(2)}) collective-permute-start(bf16[128,1152]{1,0:T(8,128)(2,1)S(1)} %pad_maximum_fusion), channel_id=1, source_target_pairs={{0,1},{1,0},{2,3},{3,2},{4,5},{5,4},{6,7},{7,6},{8,9},{9,8},{10,11... | collective-permute-start | bytes 884744 | tf_op jit(solution)/shard_map/ppermute | solution.py:10
  28.4 4.9 %collective-permute-start.8 = (bf16[32,1152]{1,0:T(8,128)(2,1)S(1)}, bf16[32,1152]{1,0:T(8,128)(2,1)S(1)}, u32[]{:S(2)}, u32[]{:S(2)}) collective-permute-start(bf16[32,1152]{1,0:T(8,128)(2,1)S(1)} %get-tuple-element.7), channel_id=1, source_target_pairs={{0,2},{1,3},{2,0},{3,1},{4,6},{5,7},{6,4},{7,5},{8,10},{9,11},{10,... | collective-permute-start | bytes 221192 | tf_op jit(solution)/shard_map/ppermute | solution.py:10
  29.0 6.4 %collective-permute-start.10 = (bf16[32,1152]{1,0:T(8,128)(2,1)S(1)}, bf16[32,1152]{1,0:T(8,128)(2,1)S(1)}, u32[]{:S(2)}, u32[]{:S(2)}) collective-permute-start(bf16[32,1152]{1,0:T(8,128)(2,1)S(1)} %get-tuple-element.8), channel_id=1, source_target_pairs={{0,6},{1,7},{2,4},{3,5},{4,2},{5,3},{6,0},{7,1},{8,14},{9,15},{10,... | collective-permute-start | bytes 221192 | tf_op jit(solution)/shard_map/ppermute | solution.py:10
  31.5 5.0 %collective-permute-start.9 = (bf16[32,1152]{1,0:T(8,128)(2,1)S(1)}, bf16[32,1152]{1,0:T(8,128)(2,1)S(1)}, u32[]{:S(2)}, u32[]{:S(2)}) collective-permute-start(bf16[32,1152]{1,0:T(8,128)(2,1)S(1)} %get-tuple-element.9), channel_id=1, source_target_pairs={{0,4},{1,5},{2,6},{3,7},{4,0},{5,1},{6,2},{7,3},{8,12},{9,13},{10,... | collective-permute-start | bytes 221192 | tf_op jit(solution)/shard_map/ppermute | solution.py:10

commit v2 on v1

v2 whole, which is shorter than its diff:
```python
import math

import jax
import jax.numpy as jnp
from jax import lax
from jax.sharding import PartitionSpec as P


def make_body(n, g):
    def body(docs, centroids):
        rows, width = centroids.shape
        scale = 4.0 / math.sqrt(width)
        rounded = centroids.astype(jnp.bfloat16)
        table = lax.all_to_all(jnp.tile(rounded, (n, 1)), "dev", 0, 0, tiled=True)
        wide = table.astype(jnp.float32)
        norms = jnp.sum(wide * wide, axis=1)
        dots = lax.dot_general(
            docs, table, (((1,), (1,)), ((), ())), preferred_element_type=jnp.float32
        )
        scores = (dots - 0.5 * norms[None, :]) * scale
        top = jnp.max(scores, axis=1)
        group_lse = top + jnp.log(jnp.sum(jnp.exp(scores - top[:, None]), axis=1))
        everyone = jnp.tile(group_lse.reshape(1, -1, 128), (g, 1, 1))
        all_lse = lax.all_to_all(everyone, "cgrp", 0, 0, tiled=True).reshape(g, -1)
        best = jnp.max(all_lse, axis=0)
        doc_lse = best + jnp.log(jnp.sum(jnp.exp(all_lse - best), axis=0))
        resp = jnp.exp(scores - doc_lse[:, None])
        mass = jnp.sum(resp, axis=0)
        term = lax.dot_general(
            resp.astype(jnp.bfloat16), docs, (((0,), (0,)), ((), ())),
            preferred_element_type=jnp.float32,
        )
        lane = lax.broadcasted_iota(jnp.int32, (1, 128), 1)

        def pack(term, mass):
            high = mass.astype(jnp.bfloat16)
            low = (mass - high.astype(jnp.float32)).astype(jnp.bfloat16)
            extra = jnp.where(
                lane == 0, high[:, None], jnp.where(lane == 1, low[:, None], 0)
            ).astype(jnp.bfloat16)
            return jnp.concatenate([term.astype(jnp.bfloat16), extra], axis=1)

        def unpack(x):
            wide = x.astype(jnp.float32)
            return wide[:, :width], wide[:, width] + wide[:, width + 1]

        arrived = lax.all_to_all(pack(term, mass), "dev", 0, 0, tiled=True)
        arrived_term, arrived_mass = unpack(arrived)
        weighted = jnp.sum(arrived_term.reshape(n, rows, width), axis=0)
        mass = jnp.sum(arrived_mass.reshape(n, rows), axis=0)
        return ((weighted + centroids) / (mass[:, None] + 1.0), mass, doc_lse)

    return body


def solution(mesh):
    in_specs = (P("dev", None), P(("cgrp", "dev"), None))
    out_specs = (P(("cgrp", "dev"), None), P(("cgrp", "dev")), P("dev"))
    return jax.shard_map(
        make_body(mesh.shape["dev"], mesh.shape["cgrp"]),
        mesh=mesh, in_specs=in_specs, out_specs=out_specs, check_vma=False,
    )
```

time: 38.1 us -> 50.6 us (1.33)
  blocking collectives: 0 us -> 27.5 us
  waiting for transfers between devices: 15.2 us -> 5.65 us
  starting transfers between devices: 12.7 us -> 4.87 us
  matrix products: 4.84 us -> 6.93 us
  local copies, waits for them, and re-layouts: 0.19 us -> 1.35 us
  other arithmetic: 4.11 us -> 3.14 us
    all_to_all x0 -> x2, blocking collectives: none -> 27.5 us  [the longest x1 14.7 us: body(): table = lax.all_to_all(jnp.tile(rounded, (n, 1)), 'dev', 0, 0, tiled=True)]
    ppermute x11 -> x0, waiting for transfers between devices: 15.2 us -> none  [swap(): return lax.ppermute(x, axis, [(i, i ^ mask) for i in range(size)])]
    ppermute x11 -> x0, starting transfers between devices: 12.7 us -> none  [swap(): return lax.ppermute(x, axis, [(i, i ^ mask) for i in range(size)])]
    all_to_all x0 -> x1, waiting for transfers between devices: none -> 5.65 us  [body(): all_lse = lax.all_to_all(everyone, 'cgrp', 0, 0, tiled=True).reshape(g, -1)]
    all_to_all x0 -> x1, starting transfers between devices: none -> 4.87 us  [body(): all_lse = lax.all_to_all(everyone, 'cgrp', 0, 0, tiled=True).reshape(g, -1)]
    dot_general x1, matrix products: 1.3 us -> 3.44 us  [body(): lax.dot_general(resp.astype(jnp.bfloat16), docs, (((0,), (0,)), ((), ()))...]
    unnamed x1 -> x0, other arithmetic: 0.92 us -> none
    convert_element_type x0 -> x1, other arithmetic: none -> 0.92 us  [body(): rounded = centroids.astype(jnp.bfloat16)]
  transfers between devices with their start and end apart: 11 -> 1, of which waited for: 10 -> 1; matrix products, arithmetic and copies ran while one was open for 1% -> 0% of each run, Pallas kernels for 0% -> 0%
where the time goes in v2:
time: 50.6 us; the launch traced here: 50.3 us
  blocking collectives  27.5 us (54%)
  matrix products  6.93 us (14%)
  waiting for transfers between devices  5.65 us (11%)
  starting transfers between devices  4.87 us (10%)
  other arithmetic  3.14 us (6%)
  local copies, waits for them, and re-layouts  1.35 us (3%)
  between operations  0.77 us (2%)
    all_to_all x1, blocking collectives, body(): table = lax.all_to_all(jnp.tile(rounded, (n, 1)), 'dev', 0, 0, tiled=True)  14.7 us
    all_to_all x1, blocking collectives, body(): arrived = lax.all_to_all(pack(term, mass), 'dev', 0, 0, tiled=True)  12.8 us
    all_to_all x1, waiting for transfers between devices, body(): all_lse = lax.all_to_all(everyone, 'cgrp', 0, 0, tiled=True).reshape(g, -1)  5.65 us
    all_to_all x1, starting transfers between devices, body(): all_lse = lax.all_to_all(everyone, 'cgrp', 0, 0, tiled=True).reshape(g, -1)  4.87 us
    dot_general x1, matrix products, body(): lax.dot_general(docs, table, (((1,), (1,)), ((), ())), preferred_element_...  3.49 us
    dot_general x1, matrix products, body(): lax.dot_general(resp.astype(jnp.bfloat16), docs, (((0,), (0,)), ((), ()))...  3.44 us
  transfers between devices with their start and end apart: 1, of which 1 were waited for; matrix products, arithmetic and copies ran while one was open for 0% of the time, Pallas kernels for 0%

profile of v2, /device:TPU:0, one launch (start us, length us, event | category | flops | bytes accessed | tf_op | source)
XLA Modules:
  0.0 50.3 jit_solution(10686366536771781952)
XLA Ops:
  0.6 0.9 %convert_element_type.45 = bf16[32,1024]{1,0:T(8,128)(2,1)S(1)} convert(f32[32,1024]{1,0:T(8,128)} %param.3) | non-fusion elementwise | flops 32768 | bytes 196608 | tf_op jit(solution)/shard_map/convert_element_type | solution.py:13
  1.6 14.7 %all_to_all.23 = bf16[8,32,1024]{2,1,0:T(8,128)(2,1)S(1)} all-to-all(bf16[8,32,1024]{2,1,0:T(8,128)(2,1)S(1)} %tile.4), channel_id=1, replica_groups=mesh['cgrp'=4,'dev'=8] {'dev'}, dimensions={0} | all-to-all | bytes 1048576 | tf_op jit(solution)/shard_map/all_to_all | solution.py:14
  16.3 0.2 multiply_reduce_fusion
  16.5 0.1 mul.27
  16.6 3.5 %fusion.6 = (f32[2048]{0:T(1024)S(1)}, f32[2048,256]{0,1:T(8,128)S(1)}) fusion(f32[256]{0:T(256)S(1)} %mul.27, bf16[2048,1024]{1,0:T(8,128)(2,1)} %param.2, bf16[256,1024]{1,0:T(8,128)(2,1)S(1)} %bitcast.15), kind=kOutput, calls=%fused_computation.23 | convolution fusion | flops 1075312640 | bytes 6824960 | tf_op jit(solution)/shard_map/dot_general | solution.py:17
  20.1 0.3 exponential_reduce_fusion
  20.4 0.6 %tile.5 = f32[4,16,128]{2,1,0:T(8,128)} broadcast(f32[16,128]{1,0:T(8,128)S(1)} %add_bitcast_fusion.1), dimensions={1,2} | broadcast | bytes 40960 | tf_op jit(solution)/shard_map/tile | solution.py:23
  21.0 4.9 %all-to-all-start.1 = ((f32[4,16,128]{2,1,0:T(8,128)}), f32[4,16,128]{2,1,0:T(8,128)S(1)}, u32[]{:S(2)}, u32[]{:S(2)}) async-start(f32[4,16,128]{2,1,0:T(8,128)} %tile.5), calls=%async_computation.1 | async-start | bytes 65536 | tf_op jit(solution)/shard_map/all_to_all | solution.py:24
  25.9 5.7 %all-to-all-done.1 = f32[4,16,128]{2,1,0:T(8,128)S(1)} async-done(((f32[4,16,128]{2,1,0:T(8,128)}), f32[4,16,128]{2,1,0:T(8,128)S(1)}, u32[]{:S(2)}, u32[]{:S(2)}) %all-to-all-start.1) | async-done | bytes 32800 | tf_op jit(solution)/shard_map/all_to_all | solution.py:24
  31.6 0.0 copy-start.1
  31.6 3.4 %convolution_convert_fusion = bf16[256,1024]{1,0:T(8,128)(2,1)S(1)} fusion(bf16[2048,1024]{1,0:T(8,128)(2,1)} %param.2, f32[2048,256]{0,1:T(8,128)S(1)} %get-tuple-element.6, f32[2048]{0:T(1024)S(1)} %add_bitcast_fusion), kind=kOutput, calls=%fused_computation.6 | convolution fusion | flops 1075052544 | bytes 6823936 | tf_op jit(solution)/shard_map/dot_general | solution.py:29
  35.1 0.0 copy-done.1
  35.1 0.4 fusion.1
  35.4 0.1 select_select_fusion
  35.6 12.8 %all_to_all.24 = bf16[8,32,1152]{2,1,0:T(8,128)(2,1)S(1)} all-to-all(bf16[8,32,1152]{2,1,0:T(8,128)(2,1)S(1)} %bitcast.14), channel_id=1, replica_groups=mesh['cgrp'=4,'dev'=8] {'dev'}, dimensions={0} | all-to-all | bytes 1179648 | tf_op jit(solution)/shard_map/all_to_all | solution.py:47
  48.5 0.1 bitcast_convert_fusion
  48.6 0.0 copy-start
  48.6 0.1 slice.12
  48.7 0.2 fusion.5
  48.9 0.1 add.51
  49.0 0.1 reduce_sum.58
  49.1 0.0 copy-start.2
  49.1 0.4 copy-done
  49.5 0.7 %add_divide_fusion = f32[32,1024]{1,0:T(8,128)} fusion(f32[32,1024]{1,0:T(8,128)S(1)} %reduce_sum.58, f32[32,1024]{1,0:T(8,128)S(1)} %copy-done, f32[32]{0:T(128)S(1)} %broadcast_add_fusion), kind=kLoop, calls=%fused_computation.13 | loop fusion | flops 65536 | bytes 393344 | tf_op jit(solution)/shard_map/div | solution.py:51
  50.3 0.0 copy-done.2
  (11 shorter events, 0.2 us)
Async XLA Ops:
  21.0 10.5 %all-to-all-start.1 = ((f32[4,16,128]{2,1,0:T(8,128)}), f32[4,16,128]{2,1,0:T(8,128)S(1)}, u32[]{:S(2)}, u32[]{:S(2)}) async-start(f32[4,16,128]{2,1,0:T(8,128)} %tile.5), calls=%async_computation.1 | async-start | bytes 65536 | tf_op jit(solution)/shard_map/all_to_all | solution.py:24
  31.6 3.5 %copy-start.1 = (f32[2048]{0:T(1024)}, f32[2048]{0:T(1024)S(1)}, u32[]{:S(2)}) copy-start(f32[2048]{0:T(1024)S(1)} %add_bitcast_fusion) | copy-start | bytes 24580
  48.6 0.9 %copy-start = (f32[32,1024]{1,0:T(8,128)S(1)}, f32[32,1024]{1,0:T(8,128)}, u32[]{:S(2)}) copy-start(f32[32,1024]{1,0:T(8,128)} %param.3) | copy-start | bytes 393220
  49.1 1.2 %copy-start.2 = (f32[32]{0:T(128)}, f32[32]{0:T(128)S(1)}, u32[]{:S(2)}) copy-start(f32[32]{0:T(128)S(1)} %reduce_sum.59) | copy-start | bytes 388

commit v3 on v2

v3 whole, which is shorter than its diff:
```python
import math

import jax
import jax.numpy as jnp
from jax import lax
from jax.sharding import PartitionSpec as P


def chip_step(x, n, step):
    bits = (n // 2).bit_length() - 1
    pairs = []
    for i in range(n):
        bit = step if i % 2 == 0 else bits - 1 - step
        pairs.append((i, i ^ (2 << bit)))
    return lax.ppermute(x, "dev", pairs)


def core_swap(x, n):
    return lax.ppermute(x, "dev", [(i, i ^ 1) for i in range(n)])


def group_swap(x, g, mask):
    return lax.ppermute(x, "cgrp", [(i, i ^ mask) for i in range(g)])


def log_add(a, b):
    top = jnp.maximum(a, b)
    return top + jnp.log(jnp.exp(a - top) + jnp.exp(b - top))


def make_body(n, g):
    steps = (n // 2).bit_length() - 1

    def body(docs, centroids):
        rows, width = centroids.shape
        scale = 4.0 / math.sqrt(width)
        mine = centroids.astype(jnp.bfloat16)
        for step in range(steps):
            mine = jnp.concatenate([mine, chip_step(mine, n, step)], axis=0)
        table = jnp.concatenate([mine, core_swap(mine, n)], axis=0)
        wide = table.astype(jnp.float32)
        norms = jnp.sum(wide * wide, axis=1)
        dots = lax.dot_general(
            docs, table, (((1,), (1,)), ((), ())), preferred_element_type=jnp.float32
        )
        scores = (dots - 0.5 * norms[None, :]) * scale
        top = jnp.max(scores, axis=1)
        doc_lse = top + jnp.log(jnp.sum(jnp.exp(scores - top[:, None]), axis=1))
        mask = 1
        while mask < g:
            doc_lse = log_add(doc_lse, group_swap(doc_lse, g, mask))
            mask *= 2
        resp = jnp.exp(scores - doc_lse[:, None])
        mass = jnp.sum(resp, axis=0)
        term = lax.dot_general(
            resp.astype(jnp.bfloat16), docs, (((0,), (0,)), ((), ())),
            preferred_element_type=jnp.float32,
        )
        lane = lax.broadcasted_iota(jnp.int32, (1, 128), 1)

        def pack(term, mass):
            high = mass.astype(jnp.bfloat16)
            low = (mass - high.astype(jnp.float32)).astype(jnp.bfloat16)
            extra = jnp.where(
                lane == 0, high[:, None], jnp.where(lane == 1, low[:, None], 0)
            ).astype(jnp.bfloat16)
            return jnp.concatenate([term.astype(jnp.bfloat16), extra], axis=1)

        def fold(term, mass, swap):
            half = term.shape[0] // 2
            got = swap(pack(term[half:], mass[half:])).astype(jnp.float32)
            term = term[:half] + got[:, :width]
            mass = mass[:half] + (got[:, width] + got[:, width + 1])
            return term, mass

        term, mass = fold(term, mass, lambda x: core_swap(x, n))
        for step in reversed(range(steps)):
            term, mass = fold(term, mass, lambda x: chip_step(x, n, step))
        return ((term + centroids) / (mass[:, None] + 1.0), mass, doc_lse)

    return body


def solution(mesh):
    in_specs = (P("dev", None), P(("cgrp", "dev"), None))
    out_specs = (P(("cgrp", "dev"), None), P(("cgrp", "dev")), P("dev"))
    return jax.shard_map(
        make_body(mesh.shape["dev"], mesh.shape["cgrp"]),
        mesh=mesh, in_specs=in_specs, out_specs=out_specs, check_vma=False,
    )
```

time: 50.6 us -> 42 us (0.83)
  blocking collectives: 27.5 us -> 0 us
  waiting for transfers between devices: 5.65 us -> 17.4 us
  starting transfers between devices: 4.87 us -> 14.3 us
  matrix products: 6.93 us -> 4.79 us
  other arithmetic: 3.14 us -> 4.3 us
  local copies, waits for them, and re-layouts: 1.35 us -> 0.23 us
    all_to_all x2 -> x0, blocking collectives: 27.5 us -> none  [the longest x1 14.7 us: body(): table = lax.all_to_all(jnp.tile(rounded, (n, 1)), 'dev', 0, 0, tiled=True)]
    ppermute x0 -> x8, waiting for transfers between devices: none -> 17.4 us  [the longest x4 11 us: chip_step(): return lax.ppermute(x, 'dev', pairs)]
    ppermute x0 -> x8, starting transfers between devices: none -> 14.3 us  [the longest x4 8.91 us: chip_step(): return lax.ppermute(x, 'dev', pairs)]
    all_to_all x1 -> x0, waiting for transfers between devices: 5.65 us -> none  [body(): all_lse = lax.all_to_all(everyone, 'cgrp', 0, 0, tiled=True).reshape(g, -1)]
    all_to_all x1 -> x0, starting transfers between devices: 4.87 us -> none  [body(): all_lse = lax.all_to_all(everyone, 'cgrp', 0, 0, tiled=True).reshape(g, -1)]
    dot_general x1, matrix products: 3.44 us -> 1.31 us  [body(): lax.dot_general(resp.astype(jnp.bfloat16), docs, (((0,), (0,)), ((), ()))...]
    add x4 -> x11, other arithmetic: 0.2 us -> 1.21 us  [the longest x5 0.53 us: fold(): mass = mass[:half] + (got[:, width] + got[:, width + 1])]
    another operation x2 -> x0, local copies, waits for them, and re-layouts: 0.67 us -> none  [the longest x1 0.62 us: body(): everyone = jnp.tile(group_lse.reshape(1, -1, 128), (g, 1, 1))]
  transfers between devices with their start and end apart: 1 -> 8, of which waited for: 1 -> 8; matrix products, arithmetic and copies ran while one was open for 0% -> 0% of each run, Pallas kernels for 0% -> 0%
where the time goes in v3:
time: 42 us; the launch traced here: 41.8 us
  waiting for transfers between devices  17.4 us (41%)
  starting transfers between devices  14.3 us (34%)
  matrix products  4.79 us (11%)
  other arithmetic  4.3 us (10%)
  between operations  0.84 us (2%)
    ppermute x4, waiting for transfers between devices, chip_step(): return lax.ppermute(x, 'dev', pairs)  11 us
    ppermute x4, starting transfers between devices, chip_step(): return lax.ppermute(x, 'dev', pairs)  8.91 us
    ppermute x2, starting transfers between devices, group_swap(): return lax.ppermute(x, 'cgrp', [(i, i ^ mask) for i in range(g)])  5.24 us
    dot_general x1, matrix products, body(): lax.dot_general(docs, table, (((1,), (1,)), ((), ())), preferred_element_...  3.49 us
    ppermute x2, waiting for transfers between devices, group_swap(): return lax.ppermute(x, 'cgrp', [(i, i ^ mask) for i in range(g)])  3.26 us
    ppermute x2, waiting for transfers between devices, core_swap(): return lax.ppermute(x, 'dev', [(i, i ^ 1) for i in range(n)])  3.09 us
    dot_general x1, matrix products, body(): lax.dot_general(resp.astype(jnp.bfloat16), docs, (((0,), (0,)), ((), ()))...  1.31 us
    convert_element_type x1, other arithmetic, body(): mine = centroids.astype(jnp.bfloat16)  0.92 us
  transfers between devices with their start and end apart: 8, of which 8 were waited for; matrix products, arithmetic and copies ran while one was open for 0% of the time, Pallas kernels for 0%

profile of v3, /device:TPU:0, one launch (start us, length us, event | category | flops | bytes accessed | tf_op | source)
XLA Modules:
  0.0 41.8 jit_solution(13235618873024909332)
XLA Ops:
  0.6 0.9 %convert_element_type.52 = bf16[32,1024]{1,0:T(8,128)(2,1)S(1)} convert(f32[32,1024]{1,0:T(8,128)} %param.3) | non-fusion elementwise | flops 32768 | bytes 196608 | tf_op jit(solution)/shard_map/convert_element_type | solution.py:37
  1.5 3.0 %collective-permute-start = (bf16[32,1024]{1,0:T(8,128)(2,1)S(1)}, bf16[32,1024]{1,0:T(8,128)(2,1)S(1)}, u32[]{:S(2)}, u32[]{:S(2)}) collective-permute-start(bf16[32,1024]{1,0:T(8,128)(2,1)S(1)} %convert_element_type.52), channel_id=1, source_target_pairs={{0,2},{1,5},{2,0},{3,7},{4,6},{5,1},{6,4},{7,3},{8,10},{9,13},{10,... | collective-permute-start | bytes 196616 | tf_op jit(solution)/shard_map/ppermute | solution.py:15
  4.5 2.2 %collective-permute-done = bf16[32,1024]{1,0:T(8,128)(2,1)S(1)} collective-permute-done((bf16[32,1024]{1,0:T(8,128)(2,1)S(1)}, bf16[32,1024]{1,0:T(8,128)(2,1)S(1)}, u32[]{:S(2)}, u32[]{:S(2)}) %collective-permute-start) | collective-permute-done | bytes 65568 | tf_op jit(solution)/shard_map/ppermute | solution.py:15
  6.8 2.1 %collective-permute-start.1 = (bf16[64,1024]{1,0:T(8,128)(2,1)S(1)}, bf16[64,1024]{1,0:T(8,128)(2,1)S(1)}, u32[]{:S(2)}, u32[]{:S(2)}) collective-permute-start(bf16[64,1024]{1,0:T(8,128)(2,1)S(1)} %pad_maximum_fusion.4), channel_id=1, source_target_pairs={{0,4},{1,3},{2,6},{3,1},{4,0},{5,7},{6,2},{7,5},{8,12},{9,11},{10,... | collective-permute-start | bytes 393224 | tf_op jit(solution)/shard_map/ppermute | solution.py:15
  8.9 2.9 %collective-permute-done.1 = bf16[64,1024]{1,0:T(8,128)(2,1)S(1)} collective-permute-done((bf16[64,1024]{1,0:T(8,128)(2,1)S(1)}, bf16[64,1024]{1,0:T(8,128)(2,1)S(1)}, u32[]{:S(2)}, u32[]{:S(2)}) %collective-permute-start.1) | collective-permute-done | bytes 131104 | tf_op jit(solution)/shard_map/ppermute | solution.py:15
  11.9 0.1 collective-permute-start.2
  12.0 1.5 %collective-permute-done.2 = bf16[128,1024]{1,0:T(8,128)(2,1)S(1)} collective-permute-done((bf16[128,1024]{1,0:T(8,128)(2,1)S(1)}, bf16[128,1024]{1,0:T(8,128)(2,1)S(1)}, u32[]{:S(2)}, u32[]{:S(2)}) %collective-permute-start.2) | collective-permute-done | bytes 262176 | tf_op jit(solution)/shard_map/ppermute | solution.py:19
  13.5 0.2 multiply_reduce_fusion
  13.7 3.5 %fusion.14 = (f32[2048]{0:T(1024)S(1)}, f32[256,2048]{1,0:T(8,128)S(1)}) fusion(f32[256]{0:T(256)S(1)} %broadcast_multiply_fusion, bf16[2048,1024]{1,0:T(8,128)(2,1)} %param.2, bf16[128,1024]{1,0:T(8,128)(2,1)S(1)} %collective-permute-done.2, bf16[64,1024]{1,0:T(8,128)(2,1)S(1)} %collective-permute-done.1, bf16[32,1024]{1,0:T(8,128)(2,1)S(1)} %collective-permute-done, ...), kind=kOutput, calls=%fused_computation.53 | convolution fusion | flops 1077409792 | bytes 6824960 | tf_op jit(solution)/shard_map/dot_general | solution.py:43
  17.2 0.0 copy-start.2
  17.2 0.3 exponential_reduce_fusion
  17.5 2.1 %collective-permute-start.3 = (f32[2048]{0:T(1024)S(1)}, f32[2048]{0:T(1024)S(1)}, u32[]{:S(2)}, u32[]{:S(2)}) collective-permute-start(f32[2048]{0:T(1024)S(1)} %log_add_fusion.2), channel_id=1, source_target_pairs={{0,8},{8,0},{16,24},{24,16},{1,9},{9,1},{17,25},{25,17},{2,10},{10... | collective-permute-start | bytes 24584 | tf_op jit(solution)/shard_map/ppermute | solution.py:23
  19.7 1.6 %collective-permute-done.3 = f32[2048]{0:T(1024)S(1)} collective-permute-done((f32[2048]{0:T(1024)S(1)}, f32[2048]{0:T(1024)S(1)}, u32[]{:S(2)}, u32[]{:S(2)}) %collective-permute-start.3) | collective-permute-done | bytes 8224 | tf_op jit(solution)/shard_map/ppermute | solution.py:23
  21.3 3.1 %collective-permute-start.4 = (f32[2048]{0:T(1024)S(1)}, f32[2048]{0:T(1024)S(1)}, u32[]{:S(2)}, u32[]{:S(2)}) collective-permute-start(f32[2048]{0:T(1024)S(1)} %log_add_fusion.1), channel_id=1, source_target_pairs={{0,16},{8,24},{16,0},{24,8},{1,17},{9,25},{17,1},{25,9},{2,18},{10... | collective-permute-start | bytes 24584 | tf_op jit(solution)/shard_map/ppermute | solution.py:23
  24.4 1.6 %collective-permute-done.4 = f32[2048]{0:T(1024)S(1)} collective-permute-done((f32[2048]{0:T(1024)S(1)}, f32[2048]{0:T(1024)S(1)}, u32[]{:S(2)}, u32[]{:S(2)}) %collective-permute-start.4) | collective-permute-done | bytes 8224 | tf_op jit(solution)/shard_map/ppermute | solution.py:23
  26.0 0.0 copy-start.1
  26.1 0.4 fusion.1
  26.4 0.0 copy-done.2
  26.4 1.3 %fusion.3 = f32[256,1024]{1,0:T(8,128)S(1)} fusion(bf16[2048,1024]{1,0:T(8,128)(2,1)S(1)} %copy-done.2, f32[256,2048]{1,0:T(8,128)S(1)} %get-tuple-element.6, f32[2048]{0:T(1024)S(1)} %log_add_fusion), kind=kOutput, calls=%fused_computation.6 | convolution fusion | flops 1074790400 | bytes 7348224 | tf_op jit(solution)/shard_map/dot_general | solution.py:55
  27.8 0.0 copy-done.1
  27.8 0.1 select_select_fusion
  28.0 0.1 collective-permute-start.5
  28.1 1.6 %collective-permute-done.5 = bf16[128,1152]{1,0:T(8,128)(2,1)S(1)} collective-permute-done((bf16[128,1152]{1,0:T(8,128)(2,1)S(1)}, bf16[128,1152]{1,0:T(8,128)(2,1)S(1)}, u32[]{:S(2)}, u32[]{:S(2)}) %collective-permute-start.5) | collective-permute-done | bytes 294944 | tf_op jit(solution)/shard_map/ppermute | solution.py:19
  29.7 0.0 copy-start
  29.7 0.1 slice_add_fusion
  29.8 0.2 fusion.8
  30.0 0.1 subtract_convert_fusion.1
  30.0 0.1 slice.146
  30.1 0.1 select_select_fusion.1
  30.2 1.9 %collective-permute-start.6 = (bf16[64,1152]{1,0:T(8,128)(2,1)S(1)}, bf16[64,1152]{1,0:T(8,128)(2,1)S(1)}, u32[]{:S(2)}, u32[]{:S(2)}) collective-permute-start(bf16[64,1152]{1,0:T(8,128)(2,1)S(1)} %pad_maximum_fusion.3), channel_id=1, source_target_pairs={{0,4},{1,3},{2,6},{3,1},{4,0},{5,7},{6,2},{7,5},{8,12},{9,11},{10,... | collective-permute-start | bytes 442376 | tf_op jit(solution)/shard_map/ppermute | solution.py:15
  32.1 3.3 %collective-permute-done.6 = bf16[64,1152]{1,0:T(8,128)(2,1)S(1)} collective-permute-done((bf16[64,1152]{1,0:T(8,128)(2,1)S(1)}, bf16[64,1152]{1,0:T(8,128)(2,1)S(1)}, u32[]{:S(2)}, u32[]{:S(2)}) %collective-permute-start.6) | collective-permute-done | bytes 147488 | tf_op jit(solution)/shard_map/ppermute | solution.py:15
  35.5 0.2 fusion.9
  35.7 0.1 subtract_convert_fusion
  35.8 0.1 slice.145
  35.9 0.1 select_select_fusion.2
  36.0 1.9 %collective-permute-start.7 = (bf16[32,1152]{1,0:T(8,128)(2,1)S(1)}, bf16[32,1152]{1,0:T(8,128)(2,1)S(1)}, u32[]{:S(2)}, u32[]{:S(2)}) collective-permute-start(bf16[32,1152]{1,0:T(8,128)(2,1)S(1)} %pad_maximum_fusion.6), channel_id=1, source_target_pairs={{0,2},{1,5},{2,0},{3,7},{4,6},{5,1},{6,4},{7,3},{8,10},{9,13},{10,... | collective-permute-start | bytes 221192 | tf_op jit(solution)/shard_map/ppermute | solution.py:15
  37.8 2.5 %collective-permute-done.7 = bf16[32,1152]{1,0:T(8,128)(2,1)S(1)} collective-permute-done((bf16[32,1152]{1,0:T(8,128)(2,1)S(1)}, bf16[32,1152]{1,0:T(8,128)(2,1)S(1)}, u32[]{:S(2)}, u32[]{:S(2)}) %collective-permute-start.7) | collective-permute-done | bytes 73760 | tf_op jit(solution)/shard_map/ppermute | solution.py:15
  40.4 0.2 fusion.10
  40.6 0.5 %broadcast_add_fusion = (f32[32]{0:T(128)S(1)}, f32[32]{0:T(128)}) fusion(f32[32]{0:T(128)S(1)} %fusion.10, f32[64]{0:T(128)S(1)} %slice_add_fusion.7), kind=kLoop, calls=%fused_computation.51 | loop fusion | flops 64 | bytes 512 | tf_op jit(solution)/shard_map/add | solution.py:79
  41.1 0.0 copy-done
  41.1 0.7 %fusion.7 = f32[32,1024]{1,0:T(8,128)} fusion(f32[32,1024]{1,0:T(8,128)S(1)} %copy-done, f32[32,1152]{1,0:T(8,128)S(1)} %convert_element_type.65, f32[64,1024]{1,0:T(8,128)S(1)} %slice_add_fusion.1, f32[32]{0:T(128)S(1)} %get-tuple-element.3), kind=kLoop, calls=%fused_computation.19 | loop fusion | flops 98304 | bytes 524416 | tf_op jit(solution)/shard_map/div | solution.py:79
  (21 shorter events, 0.3 us)
Async XLA Ops:
  1.5 5.2 %collective-permute-start = (bf16[32,1024]{1,0:T(8,128)(2,1)S(1)}, bf16[32,1024]{1,0:T(8,128)(2,1)S(1)}, u32[]{:S(2)}, u32[]{:S(2)}) collective-permute-start(bf16[32,1024]{1,0:T(8,128)(2,1)S(1)} %convert_element_type.52), channel_id=1, source_target_pairs={{0,2},{1,5},{2,0},{3,7},{4,6},{5,1},{6,4},{7,3},{8,10},{9,13},{10,... | collective-permute-start | bytes 196616 | tf_op jit(solution)/shard_map/ppermute | solution.py:15
  6.8 5.1 %collective-permute-start.1 = (bf16[64,1024]{1,0:T(8,128)(2,1)S(1)}, bf16[64,1024]{1,0:T(8,128)(2,1)S(1)}, u32[]{:S(2)}, u32[]{:S(2)}) collective-permute-start(bf16[64,1024]{1,0:T(8,128)(2,1)S(1)} %pad_maximum_fusion.4), channel_id=1, source_target_pairs={{0,4},{1,3},{2,6},{3,1},{4,0},{5,7},{6,2},{7,5},{8,12},{9,11},{10,... | collective-permute-start | bytes 393224 | tf_op jit(solution)/shard_map/ppermute | solution.py:15
  11.9 1.6 %collective-permute-start.2 = (bf16[128,1024]{1,0:T(8,128)(2,1)S(1)}, bf16[128,1024]{1,0:T(8,128)(2,1)S(1)}, u32[]{:S(2)}, u32[]{:S(2)}) collective-permute-start(bf16[128,1024]{1,0:T(8,128)(2,1)S(1)} %pad_maximum_fusion.2), channel_id=1, source_target_pairs={{0,1},{1,0},{2,3},{3,2},{4,5},{5,4},{6,7},{7,6},{8,9},{9,8},{10,11... | collective-permute-start | bytes 786440 | tf_op jit(solution)/shard_map/ppermute | solution.py:19
  17.2 9.3 %copy-start.2 = (bf16[2048,1024]{1,0:T(8,128)(2,1)S(1)}, bf16[2048,1024]{1,0:T(8,128)(2,1)}, u32[]{:S(2)}) copy-start(bf16[2048,1024]{1,0:T(8,128)(2,1)} %param.2) | copy-start | bytes 12582916
  17.5 3.8 %collective-permute-start.3 = (f32[2048]{0:T(1024)S(1)}, f32[2048]{0:T(1024)S(1)}, u32[]{:S(2)}, u32[]{:S(2)}) collective-permute-start(f32[2048]{0:T(1024)S(1)} %log_add_fusion.2), channel_id=1, source_target_pairs={{0,8},{8,0},{16,24},{24,16},{1,9},{9,1},{17,25},{25,17},{2,10},{10... | collective-permute-start | bytes 24584 | tf_op jit(solution)/shard_map/ppermute | solution.py:23
  21.3 4.7 %collective-permute-start.4 = (f32[2048]{0:T(1024)S(1)}, f32[2048]{0:T(1024)S(1)}, u32[]{:S(2)}, u32[]{:S(2)}) collective-permute-start(f32[2048]{0:T(1024)S(1)} %log_add_fusion.1), channel_id=1, source_target_pairs={{0,16},{8,24},{16,0},{24,8},{1,17},{9,25},{17,1},{25,9},{2,18},{10... | collective-permute-start | bytes 24584 | tf_op jit(solution)/shard_map/ppermute | solution.py:23
  26.0 1.7 %copy-start.1 = (f32[2048]{0:T(1024)}, f32[2048]{0:T(1024)S(1)}, u32[]{:S(2)}) copy-start(f32[2048]{0:T(1024)S(1)} %log_add_fusion) | copy-start | bytes 24580
  28.0 1.6 %collective-permute-start.5 = (bf16[128,1152]{1,0:T(8,128)(2,1)S(1)}, bf16[128,1152]{1,0:T(8,128)(2,1)S(1)}, u32[]{:S(2)}, u32[]{:S(2)}) collective-permute-start(bf16[128,1152]{1,0:T(8,128)(2,1)S(1)} %pad_maximum_fusion.1), channel_id=1, source_target_pairs={{0,1},{1,0},{2,3},{3,2},{4,5},{5,4},{6,7},{7,6},{8,9},{9,8},{10,11... | collective-permute-start | bytes 884744 | tf_op jit(solution)/shard_map/ppermute | solution.py:19
  29.7 11.4 %copy-start = (f32[32,1024]{1,0:T(8,128)S(1)}, f32[32,1024]{1,0:T(8,128)}, u32[]{:S(2)}) copy-start(f32[32,1024]{1,0:T(8,128)} %param.3) | copy-start | bytes 393220
  30.2 5.2 %collective-permute-start.6 = (bf16[64,1152]{1,0:T(8,128)(2,1)S(1)}, bf16[64,1152]{1,0:T(8,128)(2,1)S(1)}, u32[]{:S(2)}, u32[]{:S(2)}) collective-permute-start(bf16[64,1152]{1,0:T(8,128)(2,1)S(1)} %pad_maximum_fusion.3), channel_id=1, source_target_pairs={{0,4},{1,3},{2,6},{3,1},{4,0},{5,7},{6,2},{7,5},{8,12},{9,11},{10,... | collective-permute-start | bytes 442376 | tf_op jit(solution)/shard_map/ppermute | solution.py:15
  36.0 4.4 %collective-permute-start.7 = (bf16[32,1152]{1,0:T(8,128)(2,1)S(1)}, bf16[32,1152]{1,0:T(8,128)(2,1)S(1)}, u32[]{:S(2)}, u32[]{:S(2)}) collective-permute-start(bf16[32,1152]{1,0:T(8,128)(2,1)S(1)} %pad_maximum_fusion.6), channel_id=1, source_target_pairs={{0,2},{1,5},{2,0},{3,7},{4,6},{5,1},{6,4},{7,3},{8,10},{9,13},{10,... | collective-permute-start | bytes 221192 | tf_op jit(solution)/shard_map/ppermute | solution.py:15

commit v4 on v1

v4 whole, which is shorter than its diff:
```python
import functools
import math

import jax
import jax.numpy as jnp
from jax import lax
from jax.experimental import pallas as pl
from jax.experimental.pallas import tpu as pltpu
from jax.sharding import PartitionSpec as P

LANES = 128
VMEM = pl.BlockSpec(memory_space=pltpu.VMEM)
PARAMS = pltpu.CompilerParams(vmem_limit_bytes=40 * 1024 * 1024)


def swap(x, axis, size, mask):
    return lax.ppermute(x, axis, [(i, i ^ mask) for i in range(size)])


def tree(parts, op):
    while len(parts) > 1:
        parts = [op(parts[i], parts[i + 1]) for i in range(0, len(parts), 2)]
    return parts[0]


def scores_kernel(chunk, docs_ref, mine_ref, theirs_ref, part_ref, top_ref, lse_ref):
    count, width = docs_ref.shape
    scale = 4.0 / math.sqrt(width)
    table = jnp.concatenate([mine_ref[...], theirs_ref[...]], axis=0)
    wide = table.astype(jnp.float32)
    half_norms = 0.5 * jnp.sum(wide * wide, axis=1, keepdims=True)
    for start in range(0, count, chunk):
        cols = slice(start, start + chunk)
        dots = lax.dot_general(
            table, docs_ref[cols, :], (((1,), (1,)), ((), ())),
            preferred_element_type=jnp.float32,
        )
        scores = (dots - half_norms) * scale
        top = jnp.max(scores, axis=0, keepdims=True)
        part = jnp.exp(scores - top)
        part_ref[:, cols] = part
        top_ref[:, cols] = top
        lse_ref[:, cols] = top + jnp.log(jnp.sum(part, axis=0, keepdims=True))


def with_mass(term, mass):
    high = mass.astype(jnp.bfloat16).astype(jnp.float32)
    lane = lax.broadcasted_iota(jnp.int32, (term.shape[0], LANES), 1)
    extra = jnp.where(lane == 0, high, jnp.where(lane == 1, mass - high, 0.0))
    return jnp.concatenate([term, extra], axis=1).astype(jnp.bfloat16)


def read_rows(rows, width):
    wide = rows.astype(jnp.float32)
    return wide[:, :width], wide[:, width:width + 1] + wide[:, width + 1:width + 2]


def weights_kernel(groups, chunk, *refs):
    lse_refs = refs[:groups]
    docs_ref, part_ref, top_ref = refs[groups:groups + 3]
    doc_lse_ref, keep_ref, keep_mass_ref, send_ref, resp_ref = refs[groups + 3:]
    parts = [r[...] for r in lse_refs]
    best = tree(parts, jnp.maximum)
    doc_lse = best + jnp.log(tree([jnp.exp(x - best) for x in parts], jnp.add))
    doc_lse_ref[...] = doc_lse
    factor = jnp.exp(top_ref[...] - doc_lse)
    rows, count = part_ref.shape
    half, width = keep_ref.shape
    mass = jnp.zeros((rows, 1), jnp.float32)
    for start in range(0, count, chunk):
        cols = slice(start, start + chunk)
        resp = part_ref[:, cols] * factor[:, cols]
        mass += jnp.sum(resp, axis=1, keepdims=True)
        resp_ref[:, cols] = resp.astype(jnp.bfloat16)
    keep_mass_ref[...] = jnp.broadcast_to(mass[:half], keep_mass_ref.shape)
    high = mass[half:].astype(jnp.bfloat16).astype(jnp.float32)
    lane = lax.broadcasted_iota(jnp.int32, (half, LANES), 1)
    extra = jnp.where(lane == 0, high, jnp.where(lane == 1, mass[half:] - high, 0.0))
    send_ref[:, width:] = extra.astype(jnp.bfloat16)
    for start in range(0, width, chunk):
        cols = slice(start, start + chunk)
        term = jnp.dot(resp_ref[...], docs_ref[:, cols], preferred_element_type=jnp.float32)
        keep_ref[:, cols] = term[:half]
        send_ref[:, cols] = term[half:].astype(jnp.bfloat16)


def fold_kernel(keep_ref, keep_mass_ref, got_ref, own_ref, own_mass_ref, *send_refs):
    rows, width = own_ref.shape
    for slot in range(keep_ref.shape[0] // rows):
        here = slice(slot * rows, (slot + 1) * rows)
        got, got_mass = read_rows(got_ref[here], width)
        term = keep_ref[here] + got
        mass = keep_mass_ref[here, :1] + got_mass
        if slot == 0:
            own_ref[...] = term
            own_mass_ref[...] = jnp.broadcast_to(mass, own_mass_ref.shape)
        else:
            send_refs[slot - 1][...] = with_mass(term, mass)


def final_kernel(own_ref, own_mass_ref, cent_ref, *refs):
    *got_refs, next_ref, mass_ref = refs
    width = own_ref.shape[1]
    got = [read_rows(r[...], width) for r in got_refs]
    term = tree([own_ref[...]] + [a for a, _ in got], jnp.add)
    mass = tree([own_mass_ref[:, :1]] + [b for _, b in got], jnp.add)
    next_ref[...] = (term + cent_ref[...]) / (mass + 1.0)
    mass_ref[...] = mass


def shape(dims, dtype=jnp.float32):
    return jax.ShapeDtypeStruct(dims, dtype)


def call(kernel, outs, *args, scratch=()):
    return pl.pallas_call(
        kernel,
        out_shape=outs,
        in_specs=[VMEM] * len(args),
        out_specs=[VMEM] * len(outs),
        scratch_shapes=scratch,
        compiler_params=PARAMS,
    )(*args)


def make_body(n, g):
    def body(docs, centroids):
        rows, width = centroids.shape
        count = docs.shape[0]
        group, half = rows * n, rows * n // 2
        chunk = 256
        rounded = centroids.astype(jnp.bfloat16)
        mine = jnp.concatenate(
            [rounded] + [swap(rounded, "dev", n, m) for m in range(2, n, 2)], axis=0
        )
        theirs = swap(mine, "dev", n, 1)
        part, top, lse = call(
            functools.partial(scores_kernel, chunk),
            [shape((group, count)), shape((1, count)), shape((1, count))],
            docs, mine, theirs,
        )
        all_lse = [lse] + [swap(lse, "cgrp", g, m) for m in range(1, g)]
        doc_lse, keep, keep_mass, send = call(
            functools.partial(weights_kernel, g, chunk),
            [shape((1, count)), shape((half, width)), shape((half, LANES)),
             shape((half, width + LANES), jnp.bfloat16)],
            *all_lse, docs, part, top,
            scratch=[pltpu.VMEM((group, count), jnp.bfloat16)],
        )
        got = swap(send, "dev", n, 1)
        own, own_mass, *sends = call(
            fold_kernel,
            [shape((rows, width)), shape((rows, LANES))]
            + [shape((rows, width + LANES), jnp.bfloat16)] * (n // 2 - 1),
            keep, keep_mass, got,
        )
        arrived = [swap(x, "dev", n, 2 * (j + 1)) for j, x in enumerate(sends)]
        result, mass = call(
            final_kernel, [shape((rows, width)), shape((rows, 1))],
            own, own_mass, centroids, *arrived,
        )
        return (result, mass.reshape(rows), doc_lse.reshape(count))

    return body


def solution(mesh):
    in_specs = (P("dev", None), P(("cgrp", "dev"), None))
    out_specs = (P(("cgrp", "dev"), None), P(("cgrp", "dev")), P("dev"))
    return jax.shard_map(
        make_body(mesh.shape["dev"], mesh.shape["cgrp"]),
        mesh=mesh, in_specs=in_specs, out_specs=out_specs, check_vma=False,
    )
```

time: 38.1 us -> 36.5 us (0.958)
  matrix products: 4.84 us -> 0 us
  Pallas kernels: 0 us -> 4.4 us
  other arithmetic: 4.11 us -> 1.56 us
  local copies, waits for them, and re-layouts: 0.19 us -> 2.19 us
  waiting for transfers between devices: 15.2 us -> 14.8 us
    dot_general x2 -> x0, matrix products: 4.84 us -> none  [the longest x1 3.54 us: body(): lax.dot_general(docs, table, (((1,), (1,)), ((), ())), preferred_element_...]
    pallas_call x0 -> x4, Pallas kernels: none -> 4.4 us  [call(): pl.pallas_call(kernel, out_shape=outs, in_specs=[VMEM] * len(args), out_s...]
    unnamed x9 -> x4, local copies, waits for them, and re-layouts: 0.04 us -> 2.19 us
    add x8 -> x0, other arithmetic: 1.18 us -> none  [the longest x1 0.52 us: body(): return ((weighted + centroids) / (mass[:, None] + 1.0), mass, doc_lse)]
    unnamed x1 -> x0, other arithmetic: 0.92 us -> none
    reduce_sum x3 -> x0, other arithmetic: 0.86 us -> none  [the longest x1 0.37 us: body(): mass = jnp.sum(resp, axis=0)]
    convert_element_type x6 -> x1, other arithmetic: 0.16 us -> 0.92 us  [body(): rounded = centroids.astype(jnp.bfloat16)]
    div x1 -> x0, other arithmetic: 0.74 us -> none  [body(): return ((weighted + centroids) / (mass[:, None] + 1.0), mass, doc_lse)]
  transfers between devices with their start and end apart: 11 -> 11, of which waited for: 10 -> 10; matrix products, arithmetic and copies ran while one was open for 1% -> 0% of each run, Pallas kernels for 0% -> 0%
where the time goes in v4:
time: 36.5 us; the launch traced here: 36.3 us
  waiting for transfers between devices  14.8 us (41%)
  starting transfers between devices  12.7 us (35%)
  Pallas kernels  4.4 us (12%)
  local copies, waits for them, and re-layouts  2.19 us (6%)
  other arithmetic  1.56 us (4%)
  between operations  0.67 us (2%)
    ppermute x11, waiting for transfers between devices, swap(): return lax.ppermute(x, axis, [(i, i ^ mask) for i in range(size)])  14.8 us
    ppermute x11, starting transfers between devices, swap(): return lax.ppermute(x, axis, [(i, i ^ mask) for i in range(size)])  12.7 us
    pallas_call x4, Pallas kernels, call(): pl.pallas_call(kernel, out_shape=outs, in_specs=[VMEM] * len(args), out_s...  4.4 us
    unnamed x4, local copies, waits for them, and re-layouts  2.19 us
    convert_element_type x1, other arithmetic, body(): rounded = centroids.astype(jnp.bfloat16)  0.92 us
  transfers between devices with their start and end apart: 11, of which 10 were waited for; matrix products, arithmetic and copies ran while one was open for 0% of the time, Pallas kernels for 0%

profile of v4, /device:TPU:0, one launch (start us, length us, event | category | flops | bytes accessed | tf_op | source)
XLA Modules:
  0.0 36.3 jit_solution(8542606100651490496)
XLA Ops:
  0.6 0.9 %convert_element_type.3 = bf16[32,1024]{1,0:T(8,128)(2,1)S(1)} convert(f32[32,1024]{1,0:T(8,128)} %cent_ref.1) | non-fusion elementwise | flops 32768 | bytes 196608 | tf_op jit(solution)/shard_map/convert_element_type | solution.py:132
  1.5 4.0 %collective-permute-start.2 = (bf16[32,1024]{1,0:T(8,128)(2,1)S(1)}, bf16[32,1024]{1,0:T(8,128)(2,1)S(1)}, u32[]{:S(2)}, u32[]{:S(2)}) collective-permute-start(bf16[32,1024]{1,0:T(8,128)(2,1)S(1)} %convert_element_type.3), channel_id=1, source_target_pairs={{0,6},{1,7},{2,4},{3,5},{4,2},{5,3},{6,0},{7,1},{8,14},{9,15},{10,... | collective-permute-start | bytes 196616 | tf_op jit(solution)/shard_map/ppermute | solution.py:17
  5.5 0.5 %collective-permute-start.1 = (bf16[32,1024]{1,0:T(8,128)(2,1)S(1)}, bf16[32,1024]{1,0:T(8,128)(2,1)S(1)}, u32[]{:S(2)}, u32[]{:S(2)}) collective-permute-start(bf16[32,1024]{1,0:T(8,128)(2,1)S(1)} %convert_element_type.3), channel_id=1, source_target_pairs={{0,4},{1,5},{2,6},{3,7},{4,0},{5,1},{6,2},{7,3},{8,12},{9,13},{10,... | collective-permute-start | bytes 196616 | tf_op jit(solution)/shard_map/ppermute | solution.py:17
  6.0 0.1 collective-permute-start
  6.1 1.6 %collective-permute-done.2 = bf16[32,1024]{1,0:T(8,128)(2,1)S(1)} collective-permute-done((bf16[32,1024]{1,0:T(8,128)(2,1)S(1)}, bf16[32,1024]{1,0:T(8,128)(2,1)S(1)}, u32[]{:S(2)}, u32[]{:S(2)}) %collective-permute-start.2) | collective-permute-done | bytes 65568 | tf_op jit(solution)/shard_map/ppermute | solution.py:17
  7.8 2.0 %collective-permute-done.1 = bf16[32,1024]{1,0:T(8,128)(2,1)S(1)} collective-permute-done((bf16[32,1024]{1,0:T(8,128)(2,1)S(1)}, bf16[32,1024]{1,0:T(8,128)(2,1)S(1)}, u32[]{:S(2)}, u32[]{:S(2)}) %collective-permute-start.1) | collective-permute-done | bytes 65568 | tf_op jit(solution)/shard_map/ppermute | solution.py:17
  9.8 0.5 %collective-permute-done = bf16[32,1024]{1,0:T(8,128)(2,1)S(1)} collective-permute-done((bf16[32,1024]{1,0:T(8,128)(2,1)S(1)}, bf16[32,1024]{1,0:T(8,128)(2,1)S(1)}, u32[]{:S(2)}, u32[]{:S(2)}) %collective-permute-start) | collective-permute-done | bytes 65568 | tf_op jit(solution)/shard_map/ppermute | solution.py:17
  10.3 0.1 collective-permute-start.3
  10.4 1.5 %collective-permute-done.3.theirs_ref = bf16[128,1024]{1,0:T(8,128)(2,1)S(1)} collective-permute-done((bf16[128,1024]{1,0:T(8,128)(2,1)S(1)}, bf16[128,1024]{1,0:T(8,128)(2,1)S(1)}, u32[]{:S(2)}, u32[]{:S(2)}) %collective-permute-start.3) | collective-permute-done | bytes 262176 | tf_op jit(solution)/shard_map/ppermute | solution.py:17
  11.9 0.0 copy-start
  11.9 2.2 %copy-done = bf16[2048,1024]{1,0:T(8,128)(2,1)S(1)} copy-done((bf16[2048,1024]{1,0:T(8,128)(2,1)S(1)}, bf16[2048,1024]{1,0:T(8,128)(2,1)}, u32[]{:S(2)}) %copy-start) | copy-done | bytes 4194328
  14.1 1.8 %shard_map.49 = (f32[256,2048]{1,0:T(8,128)S(1)}, f32[1,2048]{1,0:T(1,128)S(1)}, f32[1,2048]{1,0:T(1,128)S(1)}) custom-call(bf16[2048,1024]{1,0:T(8,128)(2,1)S(1)} %copy-done, bf16[128,1024]{1,0:T(8,128)(2,1)S(1)} %pad_maximum_fusion.mine_ref, bf16[128,1024]{1,0:T(8,128)(2,1)S(1)} %collective-permute-done.3.theirs_ref), custom_call_target="tpu_custom_call" | custom-call | tf_op jit(solution)/shard_map/pallas_call | solution.py:116
  15.8 0.0 copy-start.1
  15.9 3.7 %collective-permute-start.6 = (f32[1,2048]{1,0:T(1,128)S(1)}, f32[1,2048]{1,0:T(1,128)S(1)}, u32[]{:S(2)}, u32[]{:S(2)}) collective-permute-start(f32[1,2048]{1,0:T(1,128)S(1)} %get-tuple-element.17.refs_0_), channel_id=1, source_target_pairs={{0,24},{8,16},{16,8},{24,0},{1,25},{9,17},{17,9},{25,1},{2,26},{10... | collective-permute-start | bytes 24584 | tf_op jit(solution)/shard_map/ppermute | solution.py:17
  19.5 0.0 collective-permute-start.5
  19.5 0.8 %collective-permute-start.4 = (f32[1,2048]{1,0:T(1,128)S(1)}, f32[1,2048]{1,0:T(1,128)S(1)}, u32[]{:S(2)}, u32[]{:S(2)}) collective-permute-start(f32[1,2048]{1,0:T(1,128)S(1)} %get-tuple-element.17.refs_0_), channel_id=1, source_target_pairs={{0,8},{8,0},{16,24},{24,16},{1,9},{9,1},{17,25},{25,17},{2,10},{10... | collective-permute-start | bytes 24584 | tf_op jit(solution)/shard_map/ppermute | solution.py:17
  20.3 1.1 %collective-permute-done.6.refs_3_ = f32[1,2048]{1,0:T(1,128)S(1)} collective-permute-done((f32[1,2048]{1,0:T(1,128)S(1)}, f32[1,2048]{1,0:T(1,128)S(1)}, u32[]{:S(2)}, u32[]{:S(2)}) %collective-permute-start.6) | collective-permute-done | bytes 8224 | tf_op jit(solution)/shard_map/ppermute | solution.py:17
  21.4 2.7 %collective-permute-done.5.refs_2_ = f32[1,2048]{1,0:T(1,128)S(1)} collective-permute-done((f32[1,2048]{1,0:T(1,128)S(1)}, f32[1,2048]{1,0:T(1,128)S(1)}, u32[]{:S(2)}, u32[]{:S(2)}) %collective-permute-start.5) | collective-permute-done | bytes 8224 | tf_op jit(solution)/shard_map/ppermute | solution.py:17
  24.1 0.0 collective-permute-done.4.refs_1_
  24.1 1.7 %shard_map.50 = (f32[1,2048]{1,0:T(1,128)}, f32[128,1024]{1,0:T(8,128)S(1)}, f32[128,128]{1,0:T(8,128)S(1)}, bf16[128,1152]{1,0:T(8,128)(2,1)S(1)}) custom-call(f32[1,2048]{1,0:T(1,128)S(1)} %get-tuple-element.17.refs_0_, f32[1,2048]{1,0:T(1,128)S(1)} %collective-permute-done.4.refs_1_, f32[1,2048]{1,0:T(1,128)S(1)} %collective-permute-done.5.refs_2_, ...), custom_call_target="tpu_custom_call" | custom-call | tf_op jit(solution)/shard_map/pallas_call | solution.py:116
  25.7 0.0 collective-permute-start.7
  25.7 1.6 %collective-permute-done.7.got_ref = bf16[128,1152]{1,0:T(8,128)(2,1)S(1)} collective-permute-done((bf16[128,1152]{1,0:T(8,128)(2,1)S(1)}, bf16[128,1152]{1,0:T(8,128)(2,1)S(1)}, u32[]{:S(2)}, u32[]{:S(2)}) %collective-permute-start.7) | collective-permute-done | bytes 294944 | tf_op jit(solution)/shard_map/ppermute | solution.py:17
  27.3 0.2 shard_map.51
  27.5 0.6 %collective-permute-start.8 = (bf16[32,1152]{1,0:T(8,128)(2,1)S(1)}, bf16[32,1152]{1,0:T(8,128)(2,1)S(1)}, u32[]{:S(2)}, u32[]{:S(2)}) collective-permute-start(bf16[32,1152]{1,0:T(8,128)(2,1)S(1)} %get-tuple-element.25), channel_id=1, source_target_pairs={{0,2},{1,3},{2,0},{3,1},{4,6},{5,7},{6,4},{7,5},{8,10},{9,11},{10,... | collective-permute-start | bytes 221192 | tf_op jit(solution)/shard_map/ppermute | solution.py:17
  28.1 1.5 %collective-permute-start.9 = (bf16[32,1152]{1,0:T(8,128)(2,1)S(1)}, bf16[32,1152]{1,0:T(8,128)(2,1)S(1)}, u32[]{:S(2)}, u32[]{:S(2)}) collective-permute-start(bf16[32,1152]{1,0:T(8,128)(2,1)S(1)} %get-tuple-element.26), channel_id=1, source_target_pairs={{0,4},{1,5},{2,6},{3,7},{4,0},{5,1},{6,2},{7,3},{8,12},{9,13},{10,... | collective-permute-start | bytes 221192 | tf_op jit(solution)/shard_map/ppermute | solution.py:17
  29.6 1.4 %collective-permute-start.10 = (bf16[32,1152]{1,0:T(8,128)(2,1)S(1)}, bf16[32,1152]{1,0:T(8,128)(2,1)S(1)}, u32[]{:S(2)}, u32[]{:S(2)}) collective-permute-start(bf16[32,1152]{1,0:T(8,128)(2,1)S(1)} %get-tuple-element.27), channel_id=1, source_target_pairs={{0,6},{1,7},{2,4},{3,5},{4,2},{5,3},{6,0},{7,1},{8,14},{9,15},{10,... | collective-permute-start | bytes 221192 | tf_op jit(solution)/shard_map/ppermute | solution.py:17
  31.0 1.1 %collective-permute-done.8.refs_0_ = bf16[32,1152]{1,0:T(8,128)(2,1)S(1)} collective-permute-done((bf16[32,1152]{1,0:T(8,128)(2,1)S(1)}, bf16[32,1152]{1,0:T(8,128)(2,1)S(1)}, u32[]{:S(2)}, u32[]{:S(2)}) %collective-permute-start.8) | collective-permute-done | bytes 73760 | tf_op jit(solution)/shard_map/ppermute | solution.py:17
  32.1 0.3 collective-permute-done.9.refs_1_
  32.4 2.4 %collective-permute-done.10.refs_2_ = bf16[32,1152]{1,0:T(8,128)(2,1)S(1)} collective-permute-done((bf16[32,1152]{1,0:T(8,128)(2,1)S(1)}, bf16[32,1152]{1,0:T(8,128)(2,1)S(1)}, u32[]{:S(2)}, u32[]{:S(2)}) %collective-permute-start.10) | collective-permute-done | bytes 73760 | tf_op jit(solution)/shard_map/ppermute | solution.py:17
  34.9 0.0 copy-done.1
  34.9 0.8 %shard_map.52 = (f32[32,1024]{1,0:T(8,128)}, f32[32,1]{1,0:T(8,128)S(1)}) custom-call(f32[32,1024]{1,0:T(8,128)S(1)} %get-tuple-element.23.own_ref, f32[32,128]{1,0:T(8,128)S(1)} %get-tuple-element.24.own_mass_ref, f32[32,1024]{1,0:T(8,128)S(1)} %copy-done.1, bf16[32,1152]{1,0:T(8,128)(2,1)S(1)} %collective-permute-done.8.refs_0_, ...), custom_call_target="tpu_custom_call" | custom-call | tf_op jit(solution)/shard_map/pallas_call | solution.py:116
  35.7 0.6 %reduce = f32[32]{0:T(128)} reduce(f32[32,1]{1,0:T(8,128)S(1)} %get-tuple-element.29, f32[]{:T(128)} %constant), dimensions={1}, to_apply=%get-tuple-element.29.reduce_sub_computation | reduce | bytes 260 | tf_op jit(solution)/shard_map/pallas_call | solution.py:116
  (1 shorter events, 0.0 us)
Async XLA Ops:
  1.5 6.2 %collective-permute-start.2 = (bf16[32,1024]{1,0:T(8,128)(2,1)S(1)}, bf16[32,1024]{1,0:T(8,128)(2,1)S(1)}, u32[]{:S(2)}, u32[]{:S(2)}) collective-permute-start(bf16[32,1024]{1,0:T(8,128)(2,1)S(1)} %convert_element_type.3), channel_id=1, source_target_pairs={{0,6},{1,7},{2,4},{3,5},{4,2},{5,3},{6,0},{7,1},{8,14},{9,15},{10,... | collective-permute-start | bytes 196616 | tf_op jit(solution)/shard_map/ppermute | solution.py:17
  5.5 4.3 %collective-permute-start.1 = (bf16[32,1024]{1,0:T(8,128)(2,1)S(1)}, bf16[32,1024]{1,0:T(8,128)(2,1)S(1)}, u32[]{:S(2)}, u32[]{:S(2)}) collective-permute-start(bf16[32,1024]{1,0:T(8,128)(2,1)S(1)} %convert_element_type.3), channel_id=1, source_target_pairs={{0,4},{1,5},{2,6},{3,7},{4,0},{5,1},{6,2},{7,3},{8,12},{9,13},{10,... | collective-permute-start | bytes 196616 | tf_op jit(solution)/shard_map/ppermute | solution.py:17
  6.0 4.3 %collective-permute-start = (bf16[32,1024]{1,0:T(8,128)(2,1)S(1)}, bf16[32,1024]{1,0:T(8,128)(2,1)S(1)}, u32[]{:S(2)}, u32[]{:S(2)}) collective-permute-start(bf16[32,1024]{1,0:T(8,128)(2,1)S(1)} %convert_element_type.3), channel_id=1, source_target_pairs={{0,2},{1,3},{2,0},{3,1},{4,6},{5,7},{6,4},{7,5},{8,10},{9,11},{10,... | collective-permute-start | bytes 196616 | tf_op jit(solution)/shard_map/ppermute | solution.py:17
  10.3 1.6 %collective-permute-start.3 = (bf16[128,1024]{1,0:T(8,128)(2,1)S(1)}, bf16[128,1024]{1,0:T(8,128)(2,1)S(1)}, u32[]{:S(2)}, u32[]{:S(2)}) collective-permute-start(bf16[128,1024]{1,0:T(8,128)(2,1)S(1)} %pad_maximum_fusion.mine_ref), channel_id=1, source_target_pairs={{0,1},{1,0},{2,3},{3,2},{4,5},{5,4},{6,7},{7,6},{8,9},{9,8},{10,11... | collective-permute-start | bytes 786440 | tf_op jit(solution)/shard_map/ppermute | solution.py:17
  11.9 2.2 %copy-start = (bf16[2048,1024]{1,0:T(8,128)(2,1)S(1)}, bf16[2048,1024]{1,0:T(8,128)(2,1)}, u32[]{:S(2)}) copy-start(bf16[2048,1024]{1,0:T(8,128)(2,1)} %refs_4_.1) | copy-start | bytes 12582916
  15.8 19.0 %copy-start.1 = (f32[32,1024]{1,0:T(8,128)S(1)}, f32[32,1024]{1,0:T(8,128)}, u32[]{:S(2)}) copy-start(f32[32,1024]{1,0:T(8,128)} %cent_ref.1) | copy-start | bytes 393220
  15.9 5.5 %collective-permute-start.6 = (f32[1,2048]{1,0:T(1,128)S(1)}, f32[1,2048]{1,0:T(1,128)S(1)}, u32[]{:S(2)}, u32[]{:S(2)}) collective-permute-start(f32[1,2048]{1,0:T(1,128)S(1)} %get-tuple-element.17.refs_0_), channel_id=1, source_target_pairs={{0,24},{8,16},{16,8},{24,0},{1,25},{9,17},{17,9},{25,1},{2,26},{10... | collective-permute-start | bytes 24584 | tf_op jit(solution)/shard_map/ppermute | solution.py:17
  19.5 4.5 %collective-permute-start.5 = (f32[1,2048]{1,0:T(1,128)S(1)}, f32[1,2048]{1,0:T(1,128)S(1)}, u32[]{:S(2)}, u32[]{:S(2)}) collective-permute-start(f32[1,2048]{1,0:T(1,128)S(1)} %get-tuple-element.17.refs_0_), channel_id=1, source_target_pairs={{0,16},{8,24},{16,0},{24,8},{1,17},{9,25},{17,1},{25,9},{2,18},{10... | collective-permute-start | bytes 24584 | tf_op jit(solution)/shard_map/ppermute | solution.py:17
  19.5 4.5 %collective-permute-start.4 = (f32[1,2048]{1,0:T(1,128)S(1)}, f32[1,2048]{1,0:T(1,128)S(1)}, u32[]{:S(2)}, u32[]{:S(2)}) collective-permute-start(f32[1,2048]{1,0:T(1,128)S(1)} %get-tuple-element.17.refs_0_), channel_id=1, source_target_pairs={{0,8},{8,0},{16,24},{24,16},{1,9},{9,1},{17,25},{25,17},{2,10},{10... | collective-permute-start | bytes 24584 | tf_op jit(solution)/shard_map/ppermute | solution.py:17
  25.7 1.6 %collective-permute-start.7 = (bf16[128,1152]{1,0:T(8,128)(2,1)S(1)}, bf16[128,1152]{1,0:T(8,128)(2,1)S(1)}, u32[]{:S(2)}, u32[]{:S(2)}) collective-permute-start(bf16[128,1152]{1,0:T(8,128)(2,1)S(1)} %get-tuple-element.22), channel_id=1, source_target_pairs={{0,1},{1,0},{2,3},{3,2},{4,5},{5,4},{6,7},{7,6},{8,9},{9,8},{10,11... | collective-permute-start | bytes 884744 | tf_op jit(solution)/shard_map/ppermute | solution.py:17
  27.5 4.7 %collective-permute-start.8 = (bf16[32,1152]{1,0:T(8,128)(2,1)S(1)}, bf16[32,1152]{1,0:T(8,128)(2,1)S(1)}, u32[]{:S(2)}, u32[]{:S(2)}) collective-permute-start(bf16[32,1152]{1,0:T(8,128)(2,1)S(1)} %get-tuple-element.25), channel_id=1, source_target_pairs={{0,2},{1,3},{2,0},{3,1},{4,6},{5,7},{6,4},{7,5},{8,10},{9,11},{10,... | collective-permute-start | bytes 221192 | tf_op jit(solution)/shard_map/ppermute | solution.py:17
  28.1 4.4 %collective-permute-start.9 = (bf16[32,1152]{1,0:T(8,128)(2,1)S(1)}, bf16[32,1152]{1,0:T(8,128)(2,1)S(1)}, u32[]{:S(2)}, u32[]{:S(2)}) collective-permute-start(bf16[32,1152]{1,0:T(8,128)(2,1)S(1)} %get-tuple-element.26), channel_id=1, source_target_pairs={{0,4},{1,5},{2,6},{3,7},{4,0},{5,1},{6,2},{7,3},{8,12},{9,13},{10,... | collective-permute-start | bytes 221192 | tf_op jit(solution)/shard_map/ppermute | solution.py:17
  29.6 5.3 %collective-permute-start.10 = (bf16[32,1152]{1,0:T(8,128)(2,1)S(1)}, bf16[32,1152]{1,0:T(8,128)(2,1)S(1)}, u32[]{:S(2)}, u32[]{:S(2)}) collective-permute-start(bf16[32,1152]{1,0:T(8,128)(2,1)S(1)} %get-tuple-element.27), channel_id=1, source_target_pairs={{0,6},{1,7},{2,4},{3,5},{4,2},{5,3},{6,0},{7,1},{8,14},{9,15},{10,... | collective-permute-start | bytes 221192 | tf_op jit(solution)/shard_map/ppermute | solution.py:17

commit v5 on v4

--- a/solution.py
+++ b/solution.py
@@ -10,11 +10,28 @@
 
 LANES = 128
 VMEM = pl.BlockSpec(memory_space=pltpu.VMEM)
+SMEM = pl.BlockSpec(memory_space=pltpu.SMEM)
 PARAMS = pltpu.CompilerParams(vmem_limit_bytes=40 * 1024 * 1024)
 
 
 def swap(x, axis, size, mask):
     return lax.ppermute(x, axis, [(i, i ^ mask) for i in range(size)])
+
+
+def exchange(x, axis, plan):
+    return [lax.ppermute(x, axis, pairs) for pairs in plan]
+
+
+def group_plan(g):
+    if g == 4:
+        return [
+            [(0, 2), (2, 3)],
+            [(0, 1), (1, 3), (3, 2)],
+            [(0, 3), (1, 2), (2, 0), (3, 1)],
+            [(3, 0)],
+            [(1, 0), (2, 1)],
+        ]
+    return [[(i, i ^ m) for i in range(g)] for m in range(1, g)]
 
 
 def tree(parts, op):
@@ -55,11 +72,16 @@
     return wide[:, :width], wide[:, width:width + 1] + wide[:, width + 1:width + 2]
 
 
-def weights_kernel(groups, chunk, *refs):
-    lse_refs = refs[:groups]
-    docs_ref, part_ref, top_ref = refs[groups:groups + 3]
-    doc_lse_ref, keep_ref, keep_mass_ref, send_ref, resp_ref = refs[groups + 3:]
-    parts = [r[...] for r in lse_refs]
+def weights_kernel(groups, plan, chunk, me_ref, own_ref, *refs):
+    got_refs = refs[:len(plan)]
+    docs_ref, part_ref, top_ref = refs[len(plan):len(plan) + 3]
+    doc_lse_ref, keep_ref, keep_mass_ref, send_ref, resp_ref = refs[len(plan) + 3:]
+    me = me_ref[0]
+    parts = [own_ref[...]] * groups
+    for got_ref, pairs in zip(got_refs, plan):
+        got = got_ref[...]
+        for source, target in pairs:
+            parts[source] = jnp.where(me == target, got, parts[source])
     best = tree(parts, jnp.maximum)
     doc_lse = best + jnp.log(tree([jnp.exp(x - best) for x in parts], jnp.add))
     doc_lse_ref[...] = doc_lse
@@ -105,7 +127,16 @@
     term = tree([own_ref[...]] + [a for a, _ in got], jnp.add)
     mass = tree([own_mass_ref[:, :1]] + [b for _, b in got], jnp.add)
     next_ref[...] = (term + cent_ref[...]) / (mass + 1.0)
-    mass_ref[...] = mass
+    mass_ref[...] = jnp.broadcast_to(mass, (mass.shape[0], LANES)).T[:1]
+
+
+def after_docs_kernel(docs_ref, rounded_ref, own_ref):
+    own_ref[...] = rounded_ref[...]
+
+
+def after_docs(docs, rounded):
+    own, = call(after_docs_kernel, [shape(rounded.shape, rounded.dtype)], docs, rounded)
+    return own
 
 
 def shape(dims, dtype=jnp.float32):
@@ -116,7 +147,7 @@
     return pl.pallas_call(
         kernel,
         out_shape=outs,
-        in_specs=[VMEM] * len(args),
+        in_specs=[SMEM if x.dtype == jnp.int32 else VMEM for x in args],
         out_specs=[VMEM] * len(outs),
         scratch_shapes=scratch,
         compiler_params=PARAMS,
@@ -129,22 +160,23 @@
         count = docs.shape[0]
         group, half = rows * n, rows * n // 2
         chunk = 256
+        plan = group_plan(g)
         rounded = centroids.astype(jnp.bfloat16)
-        mine = jnp.concatenate(
-            [rounded] + [swap(rounded, "dev", n, m) for m in range(2, n, 2)], axis=0
-        )
+        blocks = [swap(rounded, "dev", n, m) for m in range(2, n, 2)]
+        rounded = after_docs(docs, rounded)
+        mine = jnp.concatenate([rounded] + blocks, axis=0)
         theirs = swap(mine, "dev", n, 1)
         part, top, lse = call(
             functools.partial(scores_kernel, chunk),
             [shape((group, count)), shape((1, count)), shape((1, count))],
             docs, mine, theirs,
         )
-        all_lse = [lse] + [swap(lse, "cgrp", g, m) for m in range(1, g)]
+        others = exchange(lse, "cgrp", plan)
         doc_lse, keep, keep_mass, send = call(
-            functools.partial(weights_kernel, g, chunk),
+            functools.partial(weights_kernel, g, plan, chunk),
             [shape((1, count)), shape((half, width)), shape((half, LANES)),
              shape((half, width + LANES), jnp.bfloat16)],
-            *all_lse, docs, part, top,
+            lax.axis_index("cgrp").reshape(1), lse, *others, docs, part, top,
             scratch=[pltpu.VMEM((group, count), jnp.bfloat16)],
         )
         got = swap(send, "dev", n, 1)
@@ -156,7 +188,7 @@
         )
         arrived = [swap(x, "dev", n, 2 * (j + 1)) for j, x in enumerate(sends)]
         result, mass = call(
-            final_kernel, [shape((rows, width)), shape((rows, 1))],
+            final_kernel, [shape((rows, width)), shape((1, rows))],
             own, own_mass, centroids, *arrived,
         )
         return (result, mass.reshape(rows), doc_lse.reshape(count))

time: 36.5 us -> 38.7 us (1.060)
  starting transfers between devices: 12.7 us -> 17.9 us
  waiting for transfers between devices: 14.8 us -> 10.2 us
  local copies, waits for them, and re-layouts: 2.19 us -> 4.38 us
  other arithmetic: 1.56 us -> 0.93 us
    ppermute x0 -> x5, starting transfers between devices: none -> 9.64 us  [exchange(): return [lax.ppermute(x, axis, pairs) for pairs in plan]]
    ppermute x11 -> x8, waiting for transfers between devices: 14.8 us -> 8.85 us  [swap(): return lax.ppermute(x, axis, [(i, i ^ mask) for i in range(size)])]
    ppermute x11 -> x8, starting transfers between devices: 12.7 us -> 8.22 us  [swap(): return lax.ppermute(x, axis, [(i, i ^ mask) for i in range(size)])]
    unnamed x4 -> x6, local copies, waits for them, and re-layouts: 2.19 us -> 4.38 us
    ppermute x0 -> x5, waiting for transfers between devices: none -> 1.32 us  [exchange(): return [lax.ppermute(x, axis, pairs) for pairs in plan]]
    pallas_call x1 -> x0, other arithmetic: 0.63 us -> none  [call(): pl.pallas_call(kernel, out_shape=outs, in_specs=[VMEM] * len(args), out_s...]
    pallas_call x4 -> x5, Pallas kernels: 4.4 us -> 4.38 us  [call(): pl.pallas_call(kernel, out_shape=outs, in_specs=[SMEM if x.dtype == jnp.i...]
  transfers between devices with their start and end apart: 11 -> 13, of which waited for: 10 -> 8; matrix products, arithmetic and copies ran while one was open for 0% -> 0% of each run, Pallas kernels for 0% -> 0%
where the time goes in v5:
time: 38.7 us; the launch traced here: 38.5 us
  starting transfers between devices  17.9 us (46%)
  waiting for transfers between devices  10.2 us (26%)
  local copies, waits for them, and re-layouts  4.38 us (11%)
  Pallas kernels  4.38 us (11%)
  other arithmetic  0.93 us (2%)
  between operations  0.72 us (2%)
    ppermute x5, starting transfers between devices, exchange(): return [lax.ppermute(x, axis, pairs) for pairs in plan]  9.64 us
    ppermute x8, waiting for transfers between devices, swap(): return lax.ppermute(x, axis, [(i, i ^ mask) for i in range(size)])  8.85 us
    ppermute x8, starting transfers between devices, swap(): return lax.ppermute(x, axis, [(i, i ^ mask) for i in range(size)])  8.22 us
    pallas_call x5, Pallas kernels, call(): pl.pallas_call(kernel, out_shape=outs, in_specs=[SMEM if x.dtype == jnp.i...  4.38 us
    unnamed x6, local copies, waits for them, and re-layouts  4.38 us
    ppermute x5, waiting for transfers between devices, exchange(): return [lax.ppermute(x, axis, pairs) for pairs in plan]  1.32 us
    convert_element_type x1, other arithmetic, body(): rounded = centroids.astype(jnp.bfloat16)  0.92 us
  transfers between devices with their start and end apart: 13, of which 8 were waited for; matrix products, arithmetic and copies ran while one was open for 0% of the time, Pallas kernels for 0%

profile of v5, /device:TPU:0, one launch (start us, length us, event | category | flops | bytes accessed | tf_op | source)
XLA Modules:
  0.0 38.5 jit_solution(4431185645981314100)
XLA Ops:
  0.6 0.9 %convert_element_type.3.rounded_ref = bf16[32,1024]{1,0:T(8,128)(2,1)S(1)} convert(f32[32,1024]{1,0:T(8,128)} %cent_ref.1) | non-fusion elementwise | flops 32768 | bytes 196608 | tf_op jit(solution)/shard_map/convert_element_type | solution.py:164
  1.5 4.0 %collective-permute-start.2 = (bf16[32,1024]{1,0:T(8,128)(2,1)S(1)}, bf16[32,1024]{1,0:T(8,128)(2,1)S(1)}, u32[]{:S(2)}, u32[]{:S(2)}) collective-permute-start(bf16[32,1024]{1,0:T(8,128)(2,1)S(1)} %convert_element_type.3.rounded_ref), channel_id=1, source_target_pairs={{0,6},{1,7},{2,4},{3,5},{4,2},{5,3},{6,0},{7,1},{8,14},{9,15},{10,... | collective-permute-start | bytes 196616 | tf_op jit(solution)/shard_map/ppermute | solution.py:18
  5.5 0.5 %collective-permute-start.1 = (bf16[32,1024]{1,0:T(8,128)(2,1)S(1)}, bf16[32,1024]{1,0:T(8,128)(2,1)S(1)}, u32[]{:S(2)}, u32[]{:S(2)}) collective-permute-start(bf16[32,1024]{1,0:T(8,128)(2,1)S(1)} %convert_element_type.3.rounded_ref), channel_id=1, source_target_pairs={{0,4},{1,5},{2,6},{3,7},{4,0},{5,1},{6,2},{7,3},{8,12},{9,13},{10,... | collective-permute-start | bytes 196616 | tf_op jit(solution)/shard_map/ppermute | solution.py:18
  6.0 0.1 collective-permute-start
  6.1 0.0 copy-start
  6.1 2.2 %copy-done = bf16[2048,1024]{1,0:T(8,128)(2,1)S(1)} copy-done((bf16[2048,1024]{1,0:T(8,128)(2,1)S(1)}, bf16[2048,1024]{1,0:T(8,128)(2,1)}, u32[]{:S(2)}) %copy-start) | copy-done | bytes 4194328
  8.3 0.0 collective-permute-done.2
  8.3 1.4 %collective-permute-done.1 = bf16[32,1024]{1,0:T(8,128)(2,1)S(1)} collective-permute-done((bf16[32,1024]{1,0:T(8,128)(2,1)S(1)}, bf16[32,1024]{1,0:T(8,128)(2,1)S(1)}, u32[]{:S(2)}, u32[]{:S(2)}) %collective-permute-start.1) | collective-permute-done | bytes 65568 | tf_op jit(solution)/shard_map/ppermute | solution.py:18
  9.8 0.5 %collective-permute-done = bf16[32,1024]{1,0:T(8,128)(2,1)S(1)} collective-permute-done((bf16[32,1024]{1,0:T(8,128)(2,1)S(1)}, bf16[32,1024]{1,0:T(8,128)(2,1)S(1)}, u32[]{:S(2)}, u32[]{:S(2)}) %collective-permute-start) | collective-permute-done | bytes 65568 | tf_op jit(solution)/shard_map/ppermute | solution.py:18
  10.3 0.1 collective-permute-start.3
  10.4 1.5 %collective-permute-done.3.theirs_ref = bf16[128,1024]{1,0:T(8,128)(2,1)S(1)} collective-permute-done((bf16[128,1024]{1,0:T(8,128)(2,1)S(1)}, bf16[128,1024]{1,0:T(8,128)(2,1)S(1)}, u32[]{:S(2)}, u32[]{:S(2)}) %collective-permute-start.3) | collective-permute-done | bytes 262176 | tf_op jit(solution)/shard_map/ppermute | solution.py:18
  11.9 0.0 copy-start.2
  11.9 1.7 %shard_map.50 = (f32[256,2048]{1,0:T(8,128)S(1)}, f32[1,2048]{1,0:T(1,128)S(1)}, f32[1,2048]{1,0:T(1,128)S(1)}) custom-call(bf16[2048,1024]{1,0:T(8,128)(2,1)S(1)} %copy-done, bf16[128,1024]{1,0:T(8,128)(2,1)S(1)} %pad_maximum_fusion.mine_ref, bf16[128,1024]{1,0:T(8,128)(2,1)S(1)} %collective-permute-done.3.theirs_ref), custom_call_target="tpu_custom_call" | custom-call | tf_op jit(solution)/shard_map/pallas_call | solution.py:147
  13.6 1.3 %collective-permute-start.8 = (f32[1,2048]{1,0:T(1,128)S(1)}, f32[1,2048]{1,0:T(1,128)S(1)}, u32[]{:S(2)}, u32[]{:S(2)}) collective-permute-start(f32[1,2048]{1,0:T(1,128)S(1)} %get-tuple-element.17.own_ref), channel_id=1, source_target_pairs={{8,0},{16,8},{9,1},{17,9},{10,2},{18,10},{11,3},{19,11},{12,4},{20... | collective-permute-start | bytes 24584 | tf_op jit(solution)/shard_map/ppermute | solution.py:22
  14.9 1.3 %collective-permute-start.7 = (f32[1,2048]{1,0:T(1,128)S(1)}, f32[1,2048]{1,0:T(1,128)S(1)}, u32[]{:S(2)}, u32[]{:S(2)}) collective-permute-start(f32[1,2048]{1,0:T(1,128)S(1)} %get-tuple-element.17.own_ref), channel_id=1, source_target_pairs={{24,0},{25,1},{26,2},{27,3},{28,4},{29,5},{30,6},{31,7}} | collective-permute-start | bytes 24584 | tf_op jit(solution)/shard_map/ppermute | solution.py:22
  16.2 4.5 %collective-permute-start.6 = (f32[1,2048]{1,0:T(1,128)S(1)}, f32[1,2048]{1,0:T(1,128)S(1)}, u32[]{:S(2)}, u32[]{:S(2)}) collective-permute-start(f32[1,2048]{1,0:T(1,128)S(1)} %get-tuple-element.17.own_ref), channel_id=1, source_target_pairs={{0,24},{8,16},{16,0},{24,8},{1,25},{9,17},{17,1},{25,9},{2,26},{10... | collective-permute-start | bytes 24584 | tf_op jit(solution)/shard_map/ppermute | solution.py:22
  20.7 1.3 %collective-permute-start.5 = (f32[1,2048]{1,0:T(1,128)S(1)}, f32[1,2048]{1,0:T(1,128)S(1)}, u32[]{:S(2)}, u32[]{:S(2)}) collective-permute-start(f32[1,2048]{1,0:T(1,128)S(1)} %get-tuple-element.17.own_ref), channel_id=1, source_target_pairs={{0,8},{8,24},{24,16},{1,9},{9,25},{25,17},{2,10},{10,26},{26,18},{... | collective-permute-start | bytes 24584 | tf_op jit(solution)/shard_map/ppermute | solution.py:22
  22.0 1.3 %collective-permute-start.4 = (f32[1,2048]{1,0:T(1,128)S(1)}, f32[1,2048]{1,0:T(1,128)S(1)}, u32[]{:S(2)}, u32[]{:S(2)}) collective-permute-start(f32[1,2048]{1,0:T(1,128)S(1)} %get-tuple-element.17.own_ref), channel_id=1, source_target_pairs={{0,16},{16,24},{1,17},{17,25},{2,18},{18,26},{3,19},{19,27},{4,20}... | collective-permute-start | bytes 24584 | tf_op jit(solution)/shard_map/ppermute | solution.py:22
  23.3 0.0 collective-permute-done.8.refs_4_
  23.3 0.0 collective-permute-done.7.refs_3_
  23.3 0.0 collective-permute-done.6.refs_2_
  23.4 0.0 collective-permute-done.5.refs_1_
  23.4 1.3 %collective-permute-done.4.refs_0_ = f32[1,2048]{1,0:T(1,128)S(1)} collective-permute-done((f32[1,2048]{1,0:T(1,128)S(1)}, f32[1,2048]{1,0:T(1,128)S(1)}, u32[]{:S(2)}, u32[]{:S(2)}) %collective-permute-start.4) | collective-permute-done | bytes 8224 | tf_op jit(solution)/shard_map/ppermute | solution.py:22
  24.7 0.0 copy-start.1
  24.7 2.2 %copy-done.1 = bf16[2048,1024]{1,0:T(8,128)(2,1)S(1)} copy-done((bf16[2048,1024]{1,0:T(8,128)(2,1)S(1)}, bf16[2048,1024]{1,0:T(8,128)(2,1)}, u32[]{:S(2)}) %copy-start.1) | copy-done | bytes 4194328
  26.9 1.6 %shard_map.51 = (f32[1,2048]{1,0:T(1,128)}, f32[128,1024]{1,0:T(8,128)S(1)}, f32[128,128]{1,0:T(8,128)S(1)}, bf16[128,1152]{1,0:T(8,128)(2,1)S(1)}) custom-call(s32[1]{0:T(128)} %bitcast.me_ref, f32[1,2048]{1,0:T(1,128)S(1)} %get-tuple-element.17.own_ref, f32[1,2048]{1,0:T(1,128)S(1)} %collective-permute-done.4.refs_0_, ...), custom_call_target="tpu_custom_call" | custom-call | tf_op jit(solution)/shard_map/pallas_call | solution.py:147
  28.5 0.0 collective-permute-start.9
  28.5 1.6 %collective-permute-done.9.got_ref = bf16[128,1152]{1,0:T(8,128)(2,1)S(1)} collective-permute-done((bf16[128,1152]{1,0:T(8,128)(2,1)S(1)}, bf16[128,1152]{1,0:T(8,128)(2,1)S(1)}, u32[]{:S(2)}, u32[]{:S(2)}) %collective-permute-start.9) | collective-permute-done | bytes 294944 | tf_op jit(solution)/shard_map/ppermute | solution.py:18
  30.1 0.2 shard_map.52
  30.2 0.5 %collective-permute-start.10 = (bf16[32,1152]{1,0:T(8,128)(2,1)S(1)}, bf16[32,1152]{1,0:T(8,128)(2,1)S(1)}, u32[]{:S(2)}, u32[]{:S(2)}) collective-permute-start(bf16[32,1152]{1,0:T(8,128)(2,1)S(1)} %get-tuple-element.25), channel_id=1, source_target_pairs={{0,2},{1,3},{2,0},{3,1},{4,6},{5,7},{6,4},{7,5},{8,10},{9,11},{10,... | collective-permute-start | bytes 221192 | tf_op jit(solution)/shard_map/ppermute | solution.py:18
  30.8 1.6 %collective-permute-start.11 = (bf16[32,1152]{1,0:T(8,128)(2,1)S(1)}, bf16[32,1152]{1,0:T(8,128)(2,1)S(1)}, u32[]{:S(2)}, u32[]{:S(2)}) collective-permute-start(bf16[32,1152]{1,0:T(8,128)(2,1)S(1)} %get-tuple-element.26), channel_id=1, source_target_pairs={{0,4},{1,5},{2,6},{3,7},{4,0},{5,1},{6,2},{7,3},{8,12},{9,13},{10,... | collective-permute-start | bytes 221192 | tf_op jit(solution)/shard_map/ppermute | solution.py:18
  32.4 1.4 %collective-permute-start.12 = (bf16[32,1152]{1,0:T(8,128)(2,1)S(1)}, bf16[32,1152]{1,0:T(8,128)(2,1)S(1)}, u32[]{:S(2)}, u32[]{:S(2)}) collective-permute-start(bf16[32,1152]{1,0:T(8,128)(2,1)S(1)} %get-tuple-element.27), channel_id=1, source_target_pairs={{0,6},{1,7},{2,4},{3,5},{4,2},{5,3},{6,0},{7,1},{8,14},{9,15},{10,... | collective-permute-start | bytes 221192 | tf_op jit(solution)/shard_map/ppermute | solution.py:18
  33.8 1.2 %collective-permute-done.10.refs_0_ = bf16[32,1152]{1,0:T(8,128)(2,1)S(1)} collective-permute-done((bf16[32,1152]{1,0:T(8,128)(2,1)S(1)}, bf16[32,1152]{1,0:T(8,128)(2,1)S(1)}, u32[]{:S(2)}, u32[]{:S(2)}) %collective-permute-start.10) | collective-permute-done | bytes 73760 | tf_op jit(solution)/shard_map/ppermute | solution.py:18
  35.0 0.2 collective-permute-done.11.refs_1_
  35.1 2.5 %collective-permute-done.12.refs_2_ = bf16[32,1152]{1,0:T(8,128)(2,1)S(1)} collective-permute-done((bf16[32,1152]{1,0:T(8,128)(2,1)S(1)}, bf16[32,1152]{1,0:T(8,128)(2,1)S(1)}, u32[]{:S(2)}, u32[]{:S(2)}) %collective-permute-start.12) | collective-permute-done | bytes 73760 | tf_op jit(solution)/shard_map/ppermute | solution.py:18
  37.6 0.0 copy-done.2
  37.6 0.8 %shard_map.53 = (f32[32,1024]{1,0:T(8,128)}, f32[1,32]{1,0:T(1,128)}) custom-call(f32[32,1024]{1,0:T(8,128)S(1)} %get-tuple-element.23.own_ref, f32[32,128]{1,0:T(8,128)S(1)} %get-tuple-element.24.own_mass_ref, f32[32,1024]{1,0:T(8,128)S(1)} %copy-done.2, bf16[32,1152]{1,0:T(8,128)(2,1)S(1)} %collective-permute-done.10.refs_0_, ...), custom_call_target="tpu_custom_call" | custom-call | tf_op jit(solution)/shard_map/pallas_call | solution.py:147
  (2 shorter events, 0.0 us)
Async XLA Ops:
  1.5 6.8 %collective-permute-start.2 = (bf16[32,1024]{1,0:T(8,128)(2,1)S(1)}, bf16[32,1024]{1,0:T(8,128)(2,1)S(1)}, u32[]{:S(2)}, u32[]{:S(2)}) collective-permute-start(bf16[32,1024]{1,0:T(8,128)(2,1)S(1)} %convert_element_type.3.rounded_ref), channel_id=1, source_target_pairs={{0,6},{1,7},{2,4},{3,5},{4,2},{5,3},{6,0},{7,1},{8,14},{9,15},{10,... | collective-permute-start | bytes 196616 | tf_op jit(solution)/shard_map/ppermute | solution.py:18
  5.5 4.3 %collective-permute-start.1 = (bf16[32,1024]{1,0:T(8,128)(2,1)S(1)}, bf16[32,1024]{1,0:T(8,128)(2,1)S(1)}, u32[]{:S(2)}, u32[]{:S(2)}) collective-permute-start(bf16[32,1024]{1,0:T(8,128)(2,1)S(1)} %convert_element_type.3.rounded_ref), channel_id=1, source_target_pairs={{0,4},{1,5},{2,6},{3,7},{4,0},{5,1},{6,2},{7,3},{8,12},{9,13},{10,... | collective-permute-start | bytes 196616 | tf_op jit(solution)/shard_map/ppermute | solution.py:18
  6.0 4.3 %collective-permute-start = (bf16[32,1024]{1,0:T(8,128)(2,1)S(1)}, bf16[32,1024]{1,0:T(8,128)(2,1)S(1)}, u32[]{:S(2)}, u32[]{:S(2)}) collective-permute-start(bf16[32,1024]{1,0:T(8,128)(2,1)S(1)} %convert_element_type.3.rounded_ref), channel_id=1, source_target_pairs={{0,2},{1,3},{2,0},{3,1},{4,6},{5,7},{6,4},{7,5},{8,10},{9,11},{10,... | collective-permute-start | bytes 196616 | tf_op jit(solution)/shard_map/ppermute | solution.py:18
  6.1 2.2 %copy-start = (bf16[2048,1024]{1,0:T(8,128)(2,1)S(1)}, bf16[2048,1024]{1,0:T(8,128)(2,1)}, u32[]{:S(2)}) copy-start(bf16[2048,1024]{1,0:T(8,128)(2,1)} %refs_5_.1) | copy-start | bytes 12582916
  10.3 1.6 %collective-permute-start.3 = (bf16[128,1024]{1,0:T(8,128)(2,1)S(1)}, bf16[128,1024]{1,0:T(8,128)(2,1)S(1)}, u32[]{:S(2)}, u32[]{:S(2)}) collective-permute-start(bf16[128,1024]{1,0:T(8,128)(2,1)S(1)} %pad_maximum_fusion.mine_ref), channel_id=1, source_target_pairs={{0,1},{1,0},{2,3},{3,2},{4,5},{5,4},{6,7},{7,6},{8,9},{9,8},{10,11... | collective-permute-start | bytes 786440 | tf_op jit(solution)/shard_map/ppermute | solution.py:18
  11.9 25.7 %copy-start.2 = (f32[32,1024]{1,0:T(8,128)S(1)}, f32[32,1024]{1,0:T(8,128)}, u32[]{:S(2)}) copy-start(f32[32,1024]{1,0:T(8,128)} %cent_ref.1) | copy-start | bytes 393220
  13.6 9.7 %collective-permute-start.8 = (f32[1,2048]{1,0:T(1,128)S(1)}, f32[1,2048]{1,0:T(1,128)S(1)}, u32[]{:S(2)}, u32[]{:S(2)}) collective-permute-start(f32[1,2048]{1,0:T(1,128)S(1)} %get-tuple-element.17.own_ref), channel_id=1, source_target_pairs={{8,0},{16,8},{9,1},{17,9},{10,2},{18,10},{11,3},{19,11},{12,4},{20... | collective-permute-start | bytes 24584 | tf_op jit(solution)/shard_map/ppermute | solution.py:22
  14.9 8.4 %collective-permute-start.7 = (f32[1,2048]{1,0:T(1,128)S(1)}, f32[1,2048]{1,0:T(1,128)S(1)}, u32[]{:S(2)}, u32[]{:S(2)}) collective-permute-start(f32[1,2048]{1,0:T(1,128)S(1)} %get-tuple-element.17.own_ref), channel_id=1, source_target_pairs={{24,0},{25,1},{26,2},{27,3},{28,4},{29,5},{30,6},{31,7}} | collective-permute-start | bytes 24584 | tf_op jit(solution)/shard_map/ppermute | solution.py:22
  16.2 7.1 %collective-permute-start.6 = (f32[1,2048]{1,0:T(1,128)S(1)}, f32[1,2048]{1,0:T(1,128)S(1)}, u32[]{:S(2)}, u32[]{:S(2)}) collective-permute-start(f32[1,2048]{1,0:T(1,128)S(1)} %get-tuple-element.17.own_ref), channel_id=1, source_target_pairs={{0,24},{8,16},{16,0},{24,8},{1,25},{9,17},{17,1},{25,9},{2,26},{10... | collective-permute-start | bytes 24584 | tf_op jit(solution)/shard_map/ppermute | solution.py:22
  20.7 2.6 %collective-permute-start.5 = (f32[1,2048]{1,0:T(1,128)S(1)}, f32[1,2048]{1,0:T(1,128)S(1)}, u32[]{:S(2)}, u32[]{:S(2)}) collective-permute-start(f32[1,2048]{1,0:T(1,128)S(1)} %get-tuple-element.17.own_ref), channel_id=1, source_target_pairs={{0,8},{8,24},{24,16},{1,9},{9,25},{25,17},{2,10},{10,26},{26,18},{... | collective-permute-start | bytes 24584 | tf_op jit(solution)/shard_map/ppermute | solution.py:22
  22.0 2.6 %collective-permute-start.4 = (f32[1,2048]{1,0:T(1,128)S(1)}, f32[1,2048]{1,0:T(1,128)S(1)}, u32[]{:S(2)}, u32[]{:S(2)}) collective-permute-start(f32[1,2048]{1,0:T(1,128)S(1)} %get-tuple-element.17.own_ref), channel_id=1, source_target_pairs={{0,16},{16,24},{1,17},{17,25},{2,18},{18,26},{3,19},{19,27},{4,20}... | collective-permute-start | bytes 24584 | tf_op jit(solution)/shard_map/ppermute | solution.py:22
  24.7 2.2 %copy-start.1 = (bf16[2048,1024]{1,0:T(8,128)(2,1)S(1)}, bf16[2048,1024]{1,0:T(8,128)(2,1)}, u32[]{:S(2)}) copy-start(bf16[2048,1024]{1,0:T(8,128)(2,1)} %refs_5_.1) | copy-start | bytes 12582916
  28.5 1.6 %collective-permute-start.9 = (bf16[128,1152]{1,0:T(8,128)(2,1)S(1)}, bf16[128,1152]{1,0:T(8,128)(2,1)S(1)}, u32[]{:S(2)}, u32[]{:S(2)}) collective-permute-start(bf16[128,1152]{1,0:T(8,128)(2,1)S(1)} %get-tuple-element.22), channel_id=1, source_target_pairs={{0,1},{1,0},{2,3},{3,2},{4,5},{5,4},{6,7},{7,6},{8,9},{9,8},{10,11... | collective-permute-start | bytes 884744 | tf_op jit(solution)/shard_map/ppermute | solution.py:18
  30.2 4.7 %collective-permute-start.10 = (bf16[32,1152]{1,0:T(8,128)(2,1)S(1)}, bf16[32,1152]{1,0:T(8,128)(2,1)S(1)}, u32[]{:S(2)}, u32[]{:S(2)}) collective-permute-start(bf16[32,1152]{1,0:T(8,128)(2,1)S(1)} %get-tuple-element.25), channel_id=1, source_target_pairs={{0,2},{1,3},{2,0},{3,1},{4,6},{5,7},{6,4},{7,5},{8,10},{9,11},{10,... | collective-permute-start | bytes 221192 | tf_op jit(solution)/shard_map/ppermute | solution.py:18
  30.8 4.4 %collective-permute-start.11 = (bf16[32,1152]{1,0:T(8,128)(2,1)S(1)}, bf16[32,1152]{1,0:T(8,128)(2,1)S(1)}, u32[]{:S(2)}, u32[]{:S(2)}) collective-permute-start(bf16[32,1152]{1,0:T(8,128)(2,1)S(1)} %get-tuple-element.26), channel_id=1, source_target_pairs={{0,4},{1,5},{2,6},{3,7},{4,0},{5,1},{6,2},{7,3},{8,12},{9,13},{10,... | collective-permute-start | bytes 221192 | tf_op jit(solution)/shard_map/ppermute | solution.py:18
  32.4 5.3 %collective-permute-start.12 = (bf16[32,1152]{1,0:T(8,128)(2,1)S(1)}, bf16[32,1152]{1,0:T(8,128)(2,1)S(1)}, u32[]{:S(2)}, u32[]{:S(2)}) collective-permute-start(bf16[32,1152]{1,0:T(8,128)(2,1)S(1)} %get-tuple-element.27), channel_id=1, source_target_pairs={{0,6},{1,7},{2,4},{3,5},{4,2},{5,3},{6,0},{7,1},{8,14},{9,15},{10,... | collective-permute-start | bytes 221192 | tf_op jit(solution)/shard_map/ppermute | solution.py:18

commit v6 on v5

v6 whole, which is shorter than its diff:
```python
import functools
import math

import jax
import jax.numpy as jnp
from jax import lax
from jax.experimental import pallas as pl
from jax.experimental.pallas import tpu as pltpu
from jax.sharding import PartitionSpec as P

LANES = 128
VMEM = pl.BlockSpec(memory_space=pltpu.VMEM)
SMEM = pl.BlockSpec(memory_space=pltpu.SMEM)


def swap(x, axis, size, mask):
    return lax.ppermute(x, axis, [(i, i ^ mask) for i in range(size)])


def group_plan(g):
    if g == 4:
        return [
            [(0, 1), (1, 0), (2, 3), (3, 2)],
            [(0, 3), (1, 2), (2, 0), (3, 1)],
            [(0, 2), (1, 3), (2, 1), (3, 0)],
        ]
    return [[(i, i ^ m) for i in range(g)] for m in range(1, g)]


def tree(parts, op):
    while len(parts) > 1:
        parts = [op(parts[i], parts[i + 1]) for i in range(0, len(parts), 2)]
    return parts[0]


def after_docs_kernel(docs_ref, rounded_ref, own_ref):
    own_ref[...] = rounded_ref[...]


def scores_kernel(chunk, docs_ref, table_ref, part_ref, top_ref, sum_ref):
    count, width = docs_ref.shape
    scale = 4.0 / math.sqrt(width)
    table = table_ref[...]
    wide = table.astype(jnp.float32)
    half_norms = 0.5 * jnp.sum(wide * wide, axis=1, keepdims=True)
    for start in range(0, count, chunk):
        cols = slice(start, start + chunk)
        dots = lax.dot_general(
            table, docs_ref[cols, :], (((1,), (1,)), ((), ())),
            preferred_element_type=jnp.float32,
        )
        scores = (dots - half_norms) * scale
        top = jnp.max(scores, axis=0, keepdims=True)
        part = jnp.exp(scores - top)
        part_ref[:, cols] = part
        top_ref[:, cols] = top
        sum_ref[:, cols] = jnp.sum(part, axis=0, keepdims=True)


def last_scores_kernel(
    chunk, docs_ref, table_ref, first_top_ref, first_sum_ref, part_ref, top_ref, lse_ref
):
    scores_kernel(chunk, docs_ref, table_ref, part_ref, top_ref, lse_ref)
    top = jnp.maximum(first_top_ref[...], top_ref[...])
    total = first_sum_ref[...] * jnp.exp(first_top_ref[...] - top)
    total += lse_ref[...] * jnp.exp(top_ref[...] - top)
    lse_ref[...] = top + jnp.log(total)


def weighted_sums(chunk, factor, docs_ref, part_ref, resp_ref, store):
    rows, count = part_ref.shape
    mass = jnp.zeros((rows, 1), jnp.float32)
    for start in range(0, count, chunk):
        cols = slice(start, start + chunk)
        resp = part_ref[:, cols] * factor[:, cols]
        mass += jnp.sum(resp, axis=1, keepdims=True)
        resp_ref[:, cols] = resp.astype(jnp.bfloat16)
    for start in range(0, docs_ref.shape[1], chunk):
        cols = slice(start, start + chunk)
        store(cols, jnp.dot(resp_ref[...], docs_ref[:, cols], preferred_element_type=jnp.float32))
    return mass


def mass_lanes(mass):
    high = mass.astype(jnp.bfloat16).astype(jnp.float32)
    lane = lax.broadcasted_iota(jnp.int32, (mass.shape[0], LANES), 1)
    lanes = jnp.where(lane == 0, high, jnp.where(lane == 1, mass - high, 0.0))
    return lanes.astype(jnp.bfloat16)


def read_rows(rows, width):
    wide = rows.astype(jnp.float32)
    return wide[:, :width], wide[:, width:width + 1] + wide[:, width + 1:width + 2]


def send_kernel(groups, plan, chunk, me_ref, lse_ref, *refs):
    got_refs = refs[:len(plan)]
    docs_ref, part_ref, top_ref, keep_top_ref = refs[len(plan):len(plan) + 4]
    doc_lse_ref, factor_ref, send_ref, resp_ref = refs[len(plan) + 4:]
    me = me_ref[0]
    parts = [lse_ref[...]] * groups
    for got_ref, pairs in zip(got_refs, plan):
        got = got_ref[...]
        for source, target in pairs:
            parts[source] = jnp.where(me == target, got, parts[source])
    best = tree(parts, jnp.maximum)
    doc_lse = best + jnp.log(tree([jnp.exp(x - best) for x in parts], jnp.add))
    doc_lse_ref[...] = doc_lse
    factor_ref[...] = jnp.exp(keep_top_ref[...] - doc_lse)
    factor = jnp.exp(top_ref[...] - doc_lse)

    def store(cols, term):
        send_ref[:, cols] = term.astype(jnp.bfloat16)

    mass = weighted_sums(chunk, factor, docs_ref, part_ref, resp_ref, store)
    send_ref[:, docs_ref.shape[1]:] = mass_lanes(mass)


def keep_kernel(chunk, factor_ref, docs_ref, part_ref, keep_ref, keep_mass_ref, resp_ref):
    def store(cols, term):
        keep_ref[:, cols] = term

    mass = weighted_sums(chunk, factor_ref[...], docs_ref, part_ref, resp_ref, store)
    keep_mass_ref[...] = jnp.broadcast_to(mass, keep_mass_ref.shape)


def fold_kernel(keep_ref, keep_mass_ref, got_ref, own_ref, own_mass_ref, *send_refs):
    rows, width = own_ref.shape
    for slot in range(keep_ref.shape[0] // rows):
        here = slice(slot * rows, (slot + 1) * rows)
        got, got_mass = read_rows(got_ref[here], width)
        term = keep_ref[here] + got
        mass = keep_mass_ref[here, :1] + got_mass
        if slot == 0:
            own_ref[...] = term
            own_mass_ref[...] = jnp.broadcast_to(mass, own_mass_ref.shape)
        else:
            send_refs[slot - 1][:, :width] = term.astype(jnp.bfloat16)
            send_refs[slot - 1][:, width:] = mass_lanes(mass)


def final_kernel(own_ref, own_mass_ref, cent_ref, *refs):
    *got_refs, next_ref, mass_ref = refs
    width = own_ref.shape[1]
    got = [read_rows(r[...], width) for r in got_refs]
    term = tree([own_ref[...]] + [a for a, _ in got], jnp.add)
    mass = tree([own_mass_ref[:, :1]] + [b for _, b in got], jnp.add)
    next_ref[...] = (term + cent_ref[...]) / (mass + 1.0)
    mass_ref[...] = jnp.broadcast_to(mass, (mass.shape[0], LANES)).T[:1]


def shape(dims, dtype=jnp.float32):
    return jax.ShapeDtypeStruct(dims, dtype)


def make_body(n, g):
    def body(docs, centroids):
        rows, width = centroids.shape
        count = docs.shape[0]
        half = rows * n // 2
        chunk = 256
        plan = group_plan(g)
        limit = (4 << 20) + half * (48 << 10)

        def call(kernel, outs, *args, scratch=(), flops=0):
            nbytes = sum(x.nbytes for x in args)
            return pl.pallas_call(
                kernel,
                out_shape=outs,
                in_specs=[SMEM if x.dtype == jnp.int32 else VMEM for x in args],
                out_specs=[VMEM] * len(outs),
                scratch_shapes=scratch,
                compiler_params=pltpu.CompilerParams(vmem_limit_bytes=limit),
                cost_estimate=pl.CostEstimate(
                    flops=flops, bytes_accessed=nbytes, transcendentals=0
                ),
            )(*args)

        flops = 2 * half * count * width
        stats = [shape((half, count)), shape((1, count)), shape((1, count))]
        resp = [pltpu.VMEM((half, count), jnp.bfloat16)]
        rounded = centroids.astype(jnp.bfloat16)
        blocks = [swap(rounded, "dev", n, m) for m in range(2, n, 2)]
        own, = call(after_docs_kernel, [shape(rounded.shape, rounded.dtype)], docs, rounded)
        mine = jnp.concatenate([own] + blocks, axis=0)
        theirs = swap(mine, "dev", n, 1)
        part, top, total = call(
            functools.partial(scores_kernel, chunk), stats, docs, mine, flops=flops
        )
        other_part, other_top, lse = call(
            functools.partial(last_scores_kernel, chunk), stats,
            docs, theirs, top, total, flops=flops,
        )
        others = [lax.ppermute(lse, "cgrp", pairs) for pairs in plan]
        doc_lse, factor, send = call(
            functools.partial(send_kernel, g, plan, chunk),
            [shape((1, count)), shape((1, count)), shape((half, width + LANES), jnp.bfloat16)],
            lax.axis_index("cgrp").reshape(1), lse, *others, docs, other_part, other_top, top,
            scratch=resp, flops=flops,
        )
        got = swap(send, "dev", n, 1)
        keep, keep_mass = call(
            functools.partial(keep_kernel, chunk),
            [shape((half, width)), shape((half, LANES))],
            factor, docs, part, scratch=resp, flops=flops,
        )
        own, own_mass, *sends = call(
            fold_kernel,
            [shape((rows, width)), shape((rows, LANES))]
            + [shape((rows, width + LANES), jnp.bfloat16)] * (n // 2 - 1),
            keep, keep_mass, got,
        )
        far_first = sorted(range(1, n // 2), key=lambda j: (-j.bit_count(), j))
        arrived = [swap(sends[j - 1], "dev", n, 2 * j) for j in far_first]
        result, mass = call(
            final_kernel, [shape((rows, width)), shape((1, rows))],
            own, own_mass, centroids, *arrived,
        )
        return (result, mass.reshape(rows), doc_lse.reshape(count))

    return body


def solution(mesh):
    in_specs = (P("dev", None), P(("cgrp", "dev"), None))
    out_specs = (P(("cgrp", "dev"), None), P(("cgrp", "dev")), P("dev"))
    return jax.shard_map(
        make_body(mesh.shape["dev"], mesh.shape["cgrp"]),
        mesh=mesh, in_specs=in_specs, out_specs=out_specs, check_vma=False,
    )
```

time: 38.7 us -> 35 us (0.904)
  starting transfers between devices: 17.9 us -> 12.9 us
  Pallas kernels: 4.38 us -> 5.72 us
    ppermute x5 -> x3, starting transfers between devices: 9.64 us -> 4.61 us  [body(): others = [lax.ppermute(lse, 'cgrp', pairs) for pairs in plan]]
    ppermute x8, waiting for transfers between devices: 8.85 us -> 6.77 us  [swap(): return lax.ppermute(x, axis, [(i, i ^ mask) for i in range(size)])]
    ppermute x5 -> x3, waiting for transfers between devices: 1.32 us -> 3.15 us  [body(): others = [lax.ppermute(lse, 'cgrp', pairs) for pairs in plan]]
    pallas_call x5 -> x7, Pallas kernels: 4.38 us -> 5.72 us  [call(): pl.pallas_call(kernel, out_shape=outs, in_specs=[SMEM if x.dtype == jnp.i...]
    unnamed x6 -> x8, local copies, waits for them, and re-layouts: 4.38 us -> 4.53 us
  transfers between devices with their start and end apart: 13 -> 11, of which waited for: 8 -> 9; matrix products, arithmetic and copies ran while one was open for 0% -> 0% of each run, Pallas kernels for 0% -> 7%
where the time goes in v6:
time: 35 us; the launch traced here: 34.7 us
  starting transfers between devices  12.9 us (37%)
  waiting for transfers between devices  9.92 us (28%)
  Pallas kernels  5.72 us (16%)
  local copies, waits for them, and re-layouts  4.53 us (13%)
  other arithmetic  0.93 us (3%)
  between operations  0.7 us (2%)
    ppermute x8, starting transfers between devices, swap(): return lax.ppermute(x, axis, [(i, i ^ mask) for i in range(size)])  8.29 us
    ppermute x8, waiting for transfers between devices, swap(): return lax.ppermute(x, axis, [(i, i ^ mask) for i in range(size)])  6.77 us
    pallas_call x7, Pallas kernels, call(): pl.pallas_call(kernel, out_shape=outs, in_specs=[SMEM if x.dtype == jnp.i...  5.72 us
    ppermute x3, starting transfers between devices, body(): others = [lax.ppermute(lse, 'cgrp', pairs) for pairs in plan]  4.61 us
    unnamed x8, local copies, waits for them, and re-layouts  4.53 us
    ppermute x3, waiting for transfers between devices, body(): others = [lax.ppermute(lse, 'cgrp', pairs) for pairs in plan]  3.15 us
    convert_element_type x1, other arithmetic, body(): rounded = centroids.astype(jnp.bfloat16)  0.92 us
  transfers between devices with their start and end apart: 11, of which 9 were waited for; matrix products, arithmetic and copies ran while one was open for 0% of the time, Pallas kernels for 7%

profile of v6, /device:TPU:0, one launch (start us, length us, event | category | flops | bytes accessed | tf_op | source)
XLA Modules:
  0.0 34.7 jit_solution(18117410140150401126)
XLA Ops:
  0.6 0.9 %convert_element_type.3.rounded_ref = bf16[32,1024]{1,0:T(8,128)(2,1)S(1)} convert(f32[32,1024]{1,0:T(8,128)} %cent_ref.1) | non-fusion elementwise | flops 32768 | bytes 196608 | tf_op jit(solution)/shard_map/convert_element_type | solution.py:182
  1.5 4.0 %collective-permute-start.2 = (bf16[32,1024]{1,0:T(8,128)(2,1)S(1)}, bf16[32,1024]{1,0:T(8,128)(2,1)S(1)}, u32[]{:S(2)}, u32[]{:S(2)}) collective-permute-start(bf16[32,1024]{1,0:T(8,128)(2,1)S(1)} %convert_element_type.3.rounded_ref), channel_id=1, source_target_pairs={{0,6},{1,7},{2,4},{3,5},{4,2},{5,3},{6,0},{7,1},{8,14},{9,15},{10,... | collective-permute-start | bytes 196616 | tf_op jit(solution)/shard_map/ppermute | solution.py:17
  5.5 0.5 %collective-permute-start.1 = (bf16[32,1024]{1,0:T(8,128)(2,1)S(1)}, bf16[32,1024]{1,0:T(8,128)(2,1)S(1)}, u32[]{:S(2)}, u32[]{:S(2)}) collective-permute-start(bf16[32,1024]{1,0:T(8,128)(2,1)S(1)} %convert_element_type.3.rounded_ref), channel_id=1, source_target_pairs={{0,4},{1,5},{2,6},{3,7},{4,0},{5,1},{6,2},{7,3},{8,12},{9,13},{10,... | collective-permute-start | bytes 196616 | tf_op jit(solution)/shard_map/ppermute | solution.py:17
  6.0 0.1 collective-permute-start
  6.1 0.0 copy-start
  6.1 2.2 %copy-done = bf16[2048,1024]{1,0:T(8,128)(2,1)S(1)} copy-done((bf16[2048,1024]{1,0:T(8,128)(2,1)S(1)}, bf16[2048,1024]{1,0:T(8,128)(2,1)}, u32[]{:S(2)}) %copy-start) | copy-done | bytes 4194328
  8.3 0.0 copy-start.1
  8.3 0.0 collective-permute-done.2
  8.3 1.4 %collective-permute-done.1 = bf16[32,1024]{1,0:T(8,128)(2,1)S(1)} collective-permute-done((bf16[32,1024]{1,0:T(8,128)(2,1)S(1)}, bf16[32,1024]{1,0:T(8,128)(2,1)S(1)}, u32[]{:S(2)}, u32[]{:S(2)}) %collective-permute-start.1) | collective-permute-done | bytes 65568 | tf_op jit(solution)/shard_map/ppermute | solution.py:17
  9.8 0.5 %collective-permute-done = bf16[32,1024]{1,0:T(8,128)(2,1)S(1)} collective-permute-done((bf16[32,1024]{1,0:T(8,128)(2,1)S(1)}, bf16[32,1024]{1,0:T(8,128)(2,1)S(1)}, u32[]{:S(2)}, u32[]{:S(2)}) %collective-permute-start) | collective-permute-done | bytes 65568 | tf_op jit(solution)/shard_map/ppermute | solution.py:17
  10.3 0.1 collective-permute-start.3
  10.4 0.1 copy-done.1
  10.5 1.6 %shard_map.50 = (f32[128,2048]{1,0:T(8,128)S(1)}, f32[1,2048]{1,0:T(1,128)S(1)}, f32[1,2048]{1,0:T(1,128)S(1)}) custom-call(bf16[2048,1024]{1,0:T(8,128)(2,1)S(1)} %copy-done.1, bf16[128,1024]{1,0:T(8,128)(2,1)S(1)} %pad_maximum_fusion.table_ref), custom_call_target="tpu_custom_call" | custom-call | flops 536870912 | bytes 4456448 | tf_op jit(solution)/shard_map/pallas_call | solution.py:167
  12.2 0.0 collective-permute-done.3.table_ref
  12.2 1.6 %shard_map.51 = (f32[128,2048]{1,0:T(8,128)S(1)}, f32[1,2048]{1,0:T(1,128)S(1)}, f32[1,2048]{1,0:T(1,128)S(1)}) custom-call(bf16[2048,1024]{1,0:T(8,128)(2,1)S(1)} %copy-done.1, bf16[128,1024]{1,0:T(8,128)(2,1)S(1)} %collective-permute-done.3.table_ref, f32[1,2048]{1,0:T(1,128)S(1)} %get-tuple-element.21.first_top_ref.refs_6_, ...), custom_call_target="tpu_custom_call" | custom-call | flops 536870912 | bytes 4472832 | tf_op jit(solution)/shard_map/pallas_call | solution.py:167
  13.8 3.0 %collective-permute-start.6 = (f32[1,2048]{1,0:T(1,128)S(1)}, f32[1,2048]{1,0:T(1,128)S(1)}, u32[]{:S(2)}, u32[]{:S(2)}) collective-permute-start(f32[1,2048]{1,0:T(1,128)S(1)} %get-tuple-element.23.lse_ref), channel_id=1, source_target_pairs={{0,16},{8,24},{16,8},{24,0},{1,17},{9,25},{17,9},{25,1},{2,18},{10... | collective-permute-start | bytes 24584 | tf_op jit(solution)/shard_map/ppermute | solution.py:194
  16.8 1.1 %collective-permute-start.5 = (f32[1,2048]{1,0:T(1,128)S(1)}, f32[1,2048]{1,0:T(1,128)S(1)}, u32[]{:S(2)}, u32[]{:S(2)}) collective-permute-start(f32[1,2048]{1,0:T(1,128)S(1)} %get-tuple-element.23.lse_ref), channel_id=1, source_target_pairs={{0,24},{8,16},{16,0},{24,8},{1,25},{9,17},{17,1},{25,9},{2,26},{10... | collective-permute-start | bytes 24584 | tf_op jit(solution)/shard_map/ppermute | solution.py:194
  17.9 0.5 %collective-permute-start.4 = (f32[1,2048]{1,0:T(1,128)S(1)}, f32[1,2048]{1,0:T(1,128)S(1)}, u32[]{:S(2)}, u32[]{:S(2)}) collective-permute-start(f32[1,2048]{1,0:T(1,128)S(1)} %get-tuple-element.23.lse_ref), channel_id=1, source_target_pairs={{0,8},{8,0},{16,24},{24,16},{1,9},{9,1},{17,25},{25,17},{2,10},{10... | collective-permute-start | bytes 24584 | tf_op jit(solution)/shard_map/ppermute | solution.py:194
  18.4 1.1 %collective-permute-done.6.refs_2_ = f32[1,2048]{1,0:T(1,128)S(1)} collective-permute-done((f32[1,2048]{1,0:T(1,128)S(1)}, f32[1,2048]{1,0:T(1,128)S(1)}, u32[]{:S(2)}, u32[]{:S(2)}) %collective-permute-start.6) | collective-permute-done | bytes 8224 | tf_op jit(solution)/shard_map/ppermute | solution.py:194
  19.5 1.9 %collective-permute-done.5.refs_1_ = f32[1,2048]{1,0:T(1,128)S(1)} collective-permute-done((f32[1,2048]{1,0:T(1,128)S(1)}, f32[1,2048]{1,0:T(1,128)S(1)}, u32[]{:S(2)}, u32[]{:S(2)}) %collective-permute-start.5) | collective-permute-done | bytes 8224 | tf_op jit(solution)/shard_map/ppermute | solution.py:194
  21.4 0.2 collective-permute-done.4.refs_0_
  21.6 0.0 copy-start.2
  21.6 2.2 %copy-done.2 = bf16[2048,1024]{1,0:T(8,128)(2,1)S(1)} copy-done((bf16[2048,1024]{1,0:T(8,128)(2,1)S(1)}, bf16[2048,1024]{1,0:T(8,128)(2,1)}, u32[]{:S(2)}) %copy-start.2) | copy-done | bytes 4194328
  23.8 0.7 %shard_map.52 = (f32[1,2048]{1,0:T(1,128)}, f32[1,2048]{1,0:T(1,128)S(1)}, bf16[128,1152]{1,0:T(8,128)(2,1)S(1)}) custom-call(s32[1]{0:T(128)} %bitcast.me_ref, f32[1,2048]{1,0:T(1,128)S(1)} %get-tuple-element.23.lse_ref, f32[1,2048]{1,0:T(1,128)S(1)} %collective-permute-done.4.refs_0_, f32[1,2048]{1,0:T(1,128)S(1)} %collective-permute-done.5.refs_1_, ...), custom_call_target="tpu_custom_call" | custom-call | flops 536870912 | bytes 5292036 | tf_op jit(solution)/shard_map/pallas_call | solution.py:167
  24.5 0.0 copy-start.3
  24.5 0.1 collective-permute-start.7
  24.6 0.7 %shard_map.53 = (f32[128,1024]{1,0:T(8,128)S(1)}, f32[128,128]{1,0:T(8,128)S(1)}) custom-call(f32[1,2048]{1,0:T(1,128)S(1)} %get-tuple-element.26.factor_ref, bf16[2048,1024]{1,0:T(8,128)(2,1)S(1)} %copy-done.2, f32[128,2048]{1,0:T(8,128)S(1)} %get-tuple-element.27.part_ref), custom_call_target="tpu_custom_call" | custom-call | flops 536870912 | bytes 5251072 | tf_op jit(solution)/shard_map/pallas_call | solution.py:167
  25.3 0.8 %collective-permute-done.7.got_ref = bf16[128,1152]{1,0:T(8,128)(2,1)S(1)} collective-permute-done((bf16[128,1152]{1,0:T(8,128)(2,1)S(1)}, bf16[128,1152]{1,0:T(8,128)(2,1)S(1)}, u32[]{:S(2)}, u32[]{:S(2)}) %collective-permute-start.7) | collective-permute-done | bytes 294944 | tf_op jit(solution)/shard_map/ppermute | solution.py:17
  26.2 0.2 shard_map.54
  26.3 2.7 %collective-permute-start.8 = (bf16[32,1152]{1,0:T(8,128)(2,1)S(1)}, bf16[32,1152]{1,0:T(8,128)(2,1)S(1)}, u32[]{:S(2)}, u32[]{:S(2)}) collective-permute-start(bf16[32,1152]{1,0:T(8,128)(2,1)S(1)} %get-tuple-element.33), channel_id=1, source_target_pairs={{0,6},{1,7},{2,4},{3,5},{4,2},{5,3},{6,0},{7,1},{8,14},{9,15},{10,... | collective-permute-start | bytes 221192 | tf_op jit(solution)/shard_map/ppermute | solution.py:17
  29.0 0.5 %collective-permute-start.9 = (bf16[32,1152]{1,0:T(8,128)(2,1)S(1)}, bf16[32,1152]{1,0:T(8,128)(2,1)S(1)}, u32[]{:S(2)}, u32[]{:S(2)}) collective-permute-start(bf16[32,1152]{1,0:T(8,128)(2,1)S(1)} %get-tuple-element.34), channel_id=1, source_target_pairs={{0,2},{1,3},{2,0},{3,1},{4,6},{5,7},{6,4},{7,5},{8,10},{9,11},{10,... | collective-permute-start | bytes 221192 | tf_op jit(solution)/shard_map/ppermute | solution.py:17
  29.5 0.3 %collective-permute-start.10 = (bf16[32,1152]{1,0:T(8,128)(2,1)S(1)}, bf16[32,1152]{1,0:T(8,128)(2,1)S(1)}, u32[]{:S(2)}, u32[]{:S(2)}) collective-permute-start(bf16[32,1152]{1,0:T(8,128)(2,1)S(1)} %get-tuple-element.35), channel_id=1, source_target_pairs={{0,4},{1,5},{2,6},{3,7},{4,0},{5,1},{6,2},{7,3},{8,12},{9,13},{10,... | collective-permute-start | bytes 221192 | tf_op jit(solution)/shard_map/ppermute | solution.py:17
  29.9 2.1 %collective-permute-done.8.refs_0_ = bf16[32,1152]{1,0:T(8,128)(2,1)S(1)} collective-permute-done((bf16[32,1152]{1,0:T(8,128)(2,1)S(1)}, bf16[32,1152]{1,0:T(8,128)(2,1)S(1)}, u32[]{:S(2)}, u32[]{:S(2)}) %collective-permute-start.8) | collective-permute-done | bytes 73760 | tf_op jit(solution)/shard_map/ppermute | solution.py:17
  32.0 1.5 %collective-permute-done.9.refs_1_ = bf16[32,1152]{1,0:T(8,128)(2,1)S(1)} collective-permute-done((bf16[32,1152]{1,0:T(8,128)(2,1)S(1)}, bf16[32,1152]{1,0:T(8,128)(2,1)S(1)}, u32[]{:S(2)}, u32[]{:S(2)}) %collective-permute-start.9) | collective-permute-done | bytes 73760 | tf_op jit(solution)/shard_map/ppermute | solution.py:17
  33.4 0.4 %collective-permute-done.10.refs_2_ = bf16[32,1152]{1,0:T(8,128)(2,1)S(1)} collective-permute-done((bf16[32,1152]{1,0:T(8,128)(2,1)S(1)}, bf16[32,1152]{1,0:T(8,128)(2,1)S(1)}, u32[]{:S(2)}, u32[]{:S(2)}) %collective-permute-start.10) | collective-permute-done | bytes 73760 | tf_op jit(solution)/shard_map/ppermute | solution.py:17
  33.9 0.0 copy-done.3
  33.9 0.8 %shard_map.55 = (f32[32,1024]{1,0:T(8,128)}, f32[1,32]{1,0:T(1,128)}) custom-call(f32[32,1024]{1,0:T(8,128)S(1)} %get-tuple-element.31.own_ref, f32[32,128]{1,0:T(8,128)S(1)} %get-tuple-element.32.own_mass_ref, f32[32,1024]{1,0:T(8,128)S(1)} %copy-done.3, bf16[32,1152]{1,0:T(8,128)(2,1)S(1)} %collective-permute-done.8.refs_0_, ...), custom_call_target="tpu_custom_call" | custom-call | bytes 499712 | tf_op jit(solution)/shard_map/pallas_call | solution.py:167
  (2 shorter events, 0.0 us)
Async XLA Ops:
  1.5 6.8 %collective-permute-start.2 = (bf16[32,1024]{1,0:T(8,128)(2,1)S(1)}, bf16[32,1024]{1,0:T(8,128)(2,1)S(1)}, u32[]{:S(2)}, u32[]{:S(2)}) collective-permute-start(bf16[32,1024]{1,0:T(8,128)(2,1)S(1)} %convert_element_type.3.rounded_ref), channel_id=1, source_target_pairs={{0,6},{1,7},{2,4},{3,5},{4,2},{5,3},{6,0},{7,1},{8,14},{9,15},{10,... | collective-permute-start | bytes 196616 | tf_op jit(solution)/shard_map/ppermute | solution.py:17
  5.5 4.3 %collective-permute-start.1 = (bf16[32,1024]{1,0:T(8,128)(2,1)S(1)}, bf16[32,1024]{1,0:T(8,128)(2,1)S(1)}, u32[]{:S(2)}, u32[]{:S(2)}) collective-permute-start(bf16[32,1024]{1,0:T(8,128)(2,1)S(1)} %convert_element_type.3.rounded_ref), channel_id=1, source_target_pairs={{0,4},{1,5},{2,6},{3,7},{4,0},{5,1},{6,2},{7,3},{8,12},{9,13},{10,... | collective-permute-start | bytes 196616 | tf_op jit(solution)/shard_map/ppermute | solution.py:17
  6.0 4.3 %collective-permute-start = (bf16[32,1024]{1,0:T(8,128)(2,1)S(1)}, bf16[32,1024]{1,0:T(8,128)(2,1)S(1)}, u32[]{:S(2)}, u32[]{:S(2)}) collective-permute-start(bf16[32,1024]{1,0:T(8,128)(2,1)S(1)} %convert_element_type.3.rounded_ref), channel_id=1, source_target_pairs={{0,2},{1,3},{2,0},{3,1},{4,6},{5,7},{6,4},{7,5},{8,10},{9,11},{10,... | collective-permute-start | bytes 196616 | tf_op jit(solution)/shard_map/ppermute | solution.py:17
  6.1 2.2 %copy-start = (bf16[2048,1024]{1,0:T(8,128)(2,1)S(1)}, bf16[2048,1024]{1,0:T(8,128)(2,1)}, u32[]{:S(2)}) copy-start(bf16[2048,1024]{1,0:T(8,128)(2,1)} %docs_ref.7) | copy-start | bytes 12582916
  8.3 2.2 %copy-start.1 = (bf16[2048,1024]{1,0:T(8,128)(2,1)S(1)}, bf16[2048,1024]{1,0:T(8,128)(2,1)}, u32[]{:S(2)}) copy-start(bf16[2048,1024]{1,0:T(8,128)(2,1)} %docs_ref.7) | copy-start | bytes 12582916
  10.3 1.9 %collective-permute-start.3 = (bf16[128,1024]{1,0:T(8,128)(2,1)S(1)}, bf16[128,1024]{1,0:T(8,128)(2,1)S(1)}, u32[]{:S(2)}, u32[]{:S(2)}) collective-permute-start(bf16[128,1024]{1,0:T(8,128)(2,1)S(1)} %pad_maximum_fusion.table_ref), channel_id=1, source_target_pairs={{0,1},{1,0},{2,3},{3,2},{4,5},{5,4},{6,7},{7,6},{8,9},{9,8},{10,11... | collective-permute-start | bytes 786440 | tf_op jit(solution)/shard_map/ppermute | solution.py:17
  13.8 5.7 %collective-permute-start.6 = (f32[1,2048]{1,0:T(1,128)S(1)}, f32[1,2048]{1,0:T(1,128)S(1)}, u32[]{:S(2)}, u32[]{:S(2)}) collective-permute-start(f32[1,2048]{1,0:T(1,128)S(1)} %get-tuple-element.23.lse_ref), channel_id=1, source_target_pairs={{0,16},{8,24},{16,8},{24,0},{1,17},{9,25},{17,9},{25,1},{2,18},{10... | collective-permute-start | bytes 24584 | tf_op jit(solution)/shard_map/ppermute | solution.py:194
  16.8 4.5 %collective-permute-start.5 = (f32[1,2048]{1,0:T(1,128)S(1)}, f32[1,2048]{1,0:T(1,128)S(1)}, u32[]{:S(2)}, u32[]{:S(2)}) collective-permute-start(f32[1,2048]{1,0:T(1,128)S(1)} %get-tuple-element.23.lse_ref), channel_id=1, source_target_pairs={{0,24},{8,16},{16,0},{24,8},{1,25},{9,17},{17,1},{25,9},{2,26},{10... | collective-permute-start | bytes 24584 | tf_op jit(solution)/shard_map/ppermute | solution.py:194
  17.9 3.7 %collective-permute-start.4 = (f32[1,2048]{1,0:T(1,128)S(1)}, f32[1,2048]{1,0:T(1,128)S(1)}, u32[]{:S(2)}, u32[]{:S(2)}) collective-permute-start(f32[1,2048]{1,0:T(1,128)S(1)} %get-tuple-element.23.lse_ref), channel_id=1, source_target_pairs={{0,8},{8,0},{16,24},{24,16},{1,9},{9,1},{17,25},{25,17},{2,10},{10... | collective-permute-start | bytes 24584 | tf_op jit(solution)/shard_map/ppermute | solution.py:194
  21.6 2.2 %copy-start.2 = (bf16[2048,1024]{1,0:T(8,128)(2,1)S(1)}, bf16[2048,1024]{1,0:T(8,128)(2,1)}, u32[]{:S(2)}) copy-start(bf16[2048,1024]{1,0:T(8,128)(2,1)} %docs_ref.7) | copy-start | bytes 12582916
  24.5 9.4 %copy-start.3 = (f32[32,1024]{1,0:T(8,128)S(1)}, f32[32,1024]{1,0:T(8,128)}, u32[]{:S(2)}) copy-start(f32[32,1024]{1,0:T(8,128)} %cent_ref.1) | copy-start | bytes 393220
  24.5 1.6 %collective-permute-start.7 = (bf16[128,1152]{1,0:T(8,128)(2,1)S(1)}, bf16[128,1152]{1,0:T(8,128)(2,1)S(1)}, u32[]{:S(2)}, u32[]{:S(2)}) collective-permute-start(bf16[128,1152]{1,0:T(8,128)(2,1)S(1)} %get-tuple-element.30), channel_id=1, source_target_pairs={{0,1},{1,0},{2,3},{3,2},{4,5},{5,4},{6,7},{7,6},{8,9},{9,8},{10,11... | collective-permute-start | bytes 884744 | tf_op jit(solution)/shard_map/ppermute | solution.py:17
  26.3 5.6 %collective-permute-start.8 = (bf16[32,1152]{1,0:T(8,128)(2,1)S(1)}, bf16[32,1152]{1,0:T(8,128)(2,1)S(1)}, u32[]{:S(2)}, u32[]{:S(2)}) collective-permute-start(bf16[32,1152]{1,0:T(8,128)(2,1)S(1)} %get-tuple-element.33), channel_id=1, source_target_pairs={{0,6},{1,7},{2,4},{3,5},{4,2},{5,3},{6,0},{7,1},{8,14},{9,15},{10,... | collective-permute-start | bytes 221192 | tf_op jit(solution)/shard_map/ppermute | solution.py:17
  29.0 4.4 %collective-permute-start.9 = (bf16[32,1152]{1,0:T(8,128)(2,1)S(1)}, bf16[32,1152]{1,0:T(8,128)(2,1)S(1)}, u32[]{:S(2)}, u32[]{:S(2)}) collective-permute-start(bf16[32,1152]{1,0:T(8,128)(2,1)S(1)} %get-tuple-element.34), channel_id=1, source_target_pairs={{0,2},{1,3},{2,0},{3,1},{4,6},{5,7},{6,4},{7,5},{8,10},{9,11},{10,... | collective-permute-start | bytes 221192 | tf_op jit(solution)/shard_map/ppermute | solution.py:17
  29.5 4.4 %collective-permute-start.10 = (bf16[32,1152]{1,0:T(8,128)(2,1)S(1)}, bf16[32,1152]{1,0:T(8,128)(2,1)S(1)}, u32[]{:S(2)}, u32[]{:S(2)}) collective-permute-start(bf16[32,1152]{1,0:T(8,128)(2,1)S(1)} %get-tuple-element.35), channel_id=1, source_target_pairs={{0,4},{1,5},{2,6},{3,7},{4,0},{5,1},{6,2},{7,3},{8,12},{9,13},{10,... | collective-permute-start | bytes 221192 | tf_op jit(solution)/shard_map/ppermute | solution.py:17

commit v7 on v6

--- a/solution.py
+++ b/solution.py
@@ -33,23 +33,38 @@
     return parts[0]
 
 
-def after_docs_kernel(docs_ref, rounded_ref, own_ref):
+def load_kernel(source_ref, rounded_ref, docs_ref, own_ref, sem):
+    copy = pltpu.make_async_copy(source_ref, docs_ref, sem)
+    copy.start()
     own_ref[...] = rounded_ref[...]
+    copy.wait()
+
+
+def load(source, rounded):
+    outs = [shape(source.shape, source.dtype), shape(rounded.shape, rounded.dtype)]
+    return pl.pallas_call(
+        load_kernel,
+        out_shape=outs,
+        in_specs=[pl.BlockSpec(memory_space=pltpu.HBM), VMEM],
+        out_specs=[VMEM, VMEM],
+        scratch_shapes=[pltpu.SemaphoreType.DMA],
+        compiler_params=pltpu.CompilerParams(vmem_limit_bytes=4 << 20),
+        cost_estimate=pl.CostEstimate(
+            flops=0, bytes_accessed=2 * source.nbytes, transcendentals=0
+        ),
+    )(pltpu.with_memory_space_constraint(source, pltpu.HBM), rounded)
 
 
 def scores_kernel(chunk, docs_ref, table_ref, part_ref, top_ref, sum_ref):
     count, width = docs_ref.shape
     scale = 4.0 / math.sqrt(width)
-    table = table_ref[...]
+    table = table_ref[...].T
     wide = table.astype(jnp.float32)
-    half_norms = 0.5 * jnp.sum(wide * wide, axis=1, keepdims=True)
+    half_norms = 0.5 * jnp.sum(wide * wide, axis=0, keepdims=True)
     for start in range(0, count, chunk):
         cols = slice(start, start + chunk)
-        dots = lax.dot_general(
-            table, docs_ref[cols, :], (((1,), (1,)), ((), ())),
-            preferred_element_type=jnp.float32,
-        )
-        scores = (dots - half_norms) * scale
+        dots = jnp.dot(docs_ref[cols, :], table, preferred_element_type=jnp.float32)
+        scores = ((dots - half_norms) * scale).T
         top = jnp.max(scores, axis=0, keepdims=True)
         part = jnp.exp(scores - top)
         part_ref[:, cols] = part
@@ -181,14 +196,14 @@
         resp = [pltpu.VMEM((half, count), jnp.bfloat16)]
         rounded = centroids.astype(jnp.bfloat16)
         blocks = [swap(rounded, "dev", n, m) for m in range(2, n, 2)]
-        own, = call(after_docs_kernel, [shape(rounded.shape, rounded.dtype)], docs, rounded)
+        docs, own = load(docs, rounded)
         mine = jnp.concatenate([own] + blocks, axis=0)
         theirs = swap(mine, "dev", n, 1)
         part, top, total = call(
-            functools.partial(scores_kernel, chunk), stats, docs, mine, flops=flops
+            functools.partial(scores_kernel, 2 * chunk), stats, docs, mine, flops=flops
         )
         other_part, other_top, lse = call(
-            functools.partial(last_scores_kernel, chunk), stats,
+            functools.partial(last_scores_kernel, 2 * chunk), stats,
             docs, theirs, top, total, flops=flops,
         )
         others = [lax.ppermute(lse, "cgrp", pairs) for pairs in plan]

time: 35 us -> 34.1 us (0.974)
  local copies, waits for them, and re-layouts: 4.53 us -> 2.22 us
  Pallas kernels: 5.72 us -> 7.58 us
  starting transfers between devices: 12.9 us -> 12.5 us
    unnamed x8 -> x9, local copies, waits for them, and re-layouts: 4.53 us -> 2.22 us
    pallas_call x0 -> x1, Pallas kernels: none -> 2.2 us  [load(): pl.pallas_call(load_kernel, out_shape=outs, in_specs=[pl.BlockSpec(memory...]
    ppermute x3, starting transfers between devices: 4.61 us -> 4.22 us  [body(): others = [lax.ppermute(lse, 'cgrp', pairs) for pairs in plan]]
    pallas_call x7 -> x6, Pallas kernels: 5.72 us -> 5.38 us  [call(): pl.pallas_call(kernel, out_shape=outs, in_specs=[SMEM if x.dtype == jnp.i...]
  transfers between devices with their start and end apart: 11 -> 11, of which waited for: 9 -> 9; matrix products, arithmetic and copies ran while one was open for 0% -> 0% of each run, Pallas kernels for 7% -> 13%
where the time goes in v7:
time: 34.1 us; the launch traced here: 33.9 us
  starting transfers between devices  12.5 us (37%)
  waiting for transfers between devices  9.96 us (29%)
  Pallas kernels  7.58 us (22%)
  local copies, waits for them, and re-layouts  2.22 us (7%)
  other arithmetic  0.92 us (3%)
  between operations  0.74 us (2%)
    ppermute x8, starting transfers between devices, swap(): return lax.ppermute(x, axis, [(i, i ^ mask) for i in range(size)])  8.29 us
    ppermute x8, waiting for transfers between devices, swap(): return lax.ppermute(x, axis, [(i, i ^ mask) for i in range(size)])  6.65 us
    pallas_call x6, Pallas kernels, call(): pl.pallas_call(kernel, out_shape=outs, in_specs=[SMEM if x.dtype == jnp.i...  5.38 us
    ppermute x3, starting transfers between devices, body(): others = [lax.ppermute(lse, 'cgrp', pairs) for pairs in plan]  4.22 us
    ppermute x3, waiting for transfers between devices, body(): others = [lax.ppermute(lse, 'cgrp', pairs) for pairs in plan]  3.31 us
    unnamed x9, local copies, waits for them, and re-layouts  2.22 us
    pallas_call x1, Pallas kernels, load(): pl.pallas_call(load_kernel, out_shape=outs, in_specs=[pl.BlockSpec(memory...  2.2 us
    convert_element_type x1, other arithmetic, body(): rounded = centroids.astype(jnp.bfloat16)  0.92 us
  transfers between devices with their start and end apart: 11, of which 9 were waited for; matrix products, arithmetic and copies ran while one was open for 0% of the time, Pallas kernels for 13%

profile of v7, /device:TPU:0, one launch (start us, length us, event | category | flops | bytes accessed | tf_op | source)
XLA Modules:
  0.0 33.9 jit_solution(3907038362746942258)
XLA Ops:
  0.6 0.9 %convert_element_type.3.rounded_ref = bf16[32,1024]{1,0:T(8,128)(2,1)S(1)} convert(f32[32,1024]{1,0:T(8,128)} %cent_ref.1) | non-fusion elementwise | flops 32768 | bytes 196608 | tf_op jit(solution)/shard_map/convert_element_type | solution.py:197
  1.5 4.0 %collective-permute-start.2 = (bf16[32,1024]{1,0:T(8,128)(2,1)S(1)}, bf16[32,1024]{1,0:T(8,128)(2,1)S(1)}, u32[]{:S(2)}, u32[]{:S(2)}) collective-permute-start(bf16[32,1024]{1,0:T(8,128)(2,1)S(1)} %convert_element_type.3.rounded_ref), channel_id=1, source_target_pairs={{0,6},{1,7},{2,4},{3,5},{4,2},{5,3},{6,0},{7,1},{8,14},{9,15},{10,... | collective-permute-start | bytes 196616 | tf_op jit(solution)/shard_map/ppermute | solution.py:17
  5.5 0.5 %collective-permute-start.1 = (bf16[32,1024]{1,0:T(8,128)(2,1)S(1)}, bf16[32,1024]{1,0:T(8,128)(2,1)S(1)}, u32[]{:S(2)}, u32[]{:S(2)}) collective-permute-start(bf16[32,1024]{1,0:T(8,128)(2,1)S(1)} %convert_element_type.3.rounded_ref), channel_id=1, source_target_pairs={{0,4},{1,5},{2,6},{3,7},{4,0},{5,1},{6,2},{7,3},{8,12},{9,13},{10,... | collective-permute-start | bytes 196616 | tf_op jit(solution)/shard_map/ppermute | solution.py:17
  6.0 0.1 collective-permute-start
  6.1 2.2 %shard_map.49 = (bf16[2048,1024]{1,0:T(8,128)(2,1)S(1)}, bf16[32,1024]{1,0:T(8,128)(2,1)S(1)}) custom-call(bf16[2048,1024]{1,0:T(8,128)(2,1)} %source_ref.1, bf16[32,1024]{1,0:T(8,128)(2,1)S(1)} %convert_element_type.3.rounded_ref), custom_call_target="tpu_custom_call" | custom-call | bytes 8388608 | tf_op jit(solution)/shard_map/pallas_call | solution.py:45
  8.3 0.0 copy-start
  8.4 1.9 %collective-permute-done = bf16[32,1024]{1,0:T(8,128)(2,1)S(1)} collective-permute-done((bf16[32,1024]{1,0:T(8,128)(2,1)S(1)}, bf16[32,1024]{1,0:T(8,128)(2,1)S(1)}, u32[]{:S(2)}, u32[]{:S(2)}) %collective-permute-start) | collective-permute-done | bytes 65568 | tf_op jit(solution)/shard_map/ppermute | solution.py:17
  10.3 0.0 collective-permute-done.1
  10.3 0.0 collective-permute-done.2
  10.3 0.1 collective-permute-start.3
  10.4 1.5 %shard_map.50 = (f32[128,2048]{1,0:T(8,128)S(1)}, f32[1,2048]{1,0:T(1,128)S(1)}, f32[1,2048]{1,0:T(1,128)S(1)}) custom-call(bf16[2048,1024]{1,0:T(8,128)(2,1)S(1)} %get-tuple-element.23.docs_ref.refs_3_, bf16[128,1024]{1,0:T(8,128)(2,1)S(1)} %constant_dynamic-update-slice_fusion.table_ref), custom_call_target="tpu_custom_call" | custom-call | flops 536870912 | bytes 4456448 | tf_op jit(solution)/shard_map/pallas_call | solution.py:182
  11.9 0.1 collective-permute-done.3.table_ref
  11.9 1.5 %shard_map.51 = (f32[128,2048]{1,0:T(8,128)S(1)}, f32[1,2048]{1,0:T(1,128)S(1)}, f32[1,2048]{1,0:T(1,128)S(1)}) custom-call(bf16[2048,1024]{1,0:T(8,128)(2,1)S(1)} %get-tuple-element.23.docs_ref.refs_3_, bf16[128,1024]{1,0:T(8,128)(2,1)S(1)} %collective-permute-done.3.table_ref, f32[1,2048]{1,0:T(1,128)S(1)} %get-tuple-element.25.first_top_ref.refs_6_, ...), custom_call_target="tpu_custom_call" | custom-call | flops 536870912 | bytes 4472832 | tf_op jit(solution)/shard_map/pallas_call | solution.py:182
  13.4 0.0 copy-done
  13.4 2.6 %collective-permute-start.6 = (f32[1,2048]{1,0:T(1,128)S(1)}, f32[1,2048]{1,0:T(1,128)S(1)}, u32[]{:S(2)}, u32[]{:S(2)}) collective-permute-start(f32[1,2048]{1,0:T(1,128)S(1)} %get-tuple-element.27.lse_ref), channel_id=1, source_target_pairs={{0,16},{8,24},{16,8},{24,0},{1,17},{9,25},{17,9},{25,1},{2,18},{10... | collective-permute-start | bytes 24584 | tf_op jit(solution)/shard_map/ppermute | solution.py:209
  16.0 1.2 %collective-permute-start.5 = (f32[1,2048]{1,0:T(1,128)S(1)}, f32[1,2048]{1,0:T(1,128)S(1)}, u32[]{:S(2)}, u32[]{:S(2)}) collective-permute-start(f32[1,2048]{1,0:T(1,128)S(1)} %get-tuple-element.27.lse_ref), channel_id=1, source_target_pairs={{0,24},{8,16},{16,0},{24,8},{1,25},{9,17},{17,1},{25,9},{2,26},{10... | collective-permute-start | bytes 24584 | tf_op jit(solution)/shard_map/ppermute | solution.py:209
  17.3 0.3 %collective-permute-start.4 = (f32[1,2048]{1,0:T(1,128)S(1)}, f32[1,2048]{1,0:T(1,128)S(1)}, u32[]{:S(2)}, u32[]{:S(2)}) collective-permute-start(f32[1,2048]{1,0:T(1,128)S(1)} %get-tuple-element.27.lse_ref), channel_id=1, source_target_pairs={{0,8},{8,0},{16,24},{24,16},{1,9},{9,1},{17,25},{25,17},{2,10},{10... | collective-permute-start | bytes 24584 | tf_op jit(solution)/shard_map/ppermute | solution.py:209
  17.6 1.3 %collective-permute-done.6.refs_2_ = f32[1,2048]{1,0:T(1,128)S(1)} collective-permute-done((f32[1,2048]{1,0:T(1,128)S(1)}, f32[1,2048]{1,0:T(1,128)S(1)}, u32[]{:S(2)}, u32[]{:S(2)}) %collective-permute-start.6) | collective-permute-done | bytes 8224 | tf_op jit(solution)/shard_map/ppermute | solution.py:209
  18.9 1.7 %collective-permute-done.5.refs_1_ = f32[1,2048]{1,0:T(1,128)S(1)} collective-permute-done((f32[1,2048]{1,0:T(1,128)S(1)}, f32[1,2048]{1,0:T(1,128)S(1)}, u32[]{:S(2)}, u32[]{:S(2)}) %collective-permute-start.5) | collective-permute-done | bytes 8224 | tf_op jit(solution)/shard_map/ppermute | solution.py:209
  20.6 0.3 collective-permute-done.4.refs_0_
  20.9 0.0 copy-start.1
  20.9 2.2 %copy-done.1 = bf16[2048,1024]{1,0:T(8,128)(2,1)S(1)} copy-done((bf16[2048,1024]{1,0:T(8,128)(2,1)S(1)}, bf16[2048,1024]{1,0:T(8,128)(2,1)}, u32[]{:S(2)}) %copy-start.1) | copy-done | bytes 4194328
  23.1 0.7 %shard_map.52 = (f32[1,2048]{1,0:T(1,128)}, f32[1,2048]{1,0:T(1,128)S(1)}, bf16[128,1152]{1,0:T(8,128)(2,1)S(1)}) custom-call(s32[1]{0:T(128)} %bitcast.me_ref, f32[1,2048]{1,0:T(1,128)S(1)} %get-tuple-element.27.lse_ref, f32[1,2048]{1,0:T(1,128)S(1)} %collective-permute-done.4.refs_0_, f32[1,2048]{1,0:T(1,128)S(1)} %collective-permute-done.5.refs_1_, ...), custom_call_target="tpu_custom_call" | custom-call | flops 536870912 | bytes 5292036 | tf_op jit(solution)/shard_map/pallas_call | solution.py:182
  23.9 0.0 copy-start.2
  23.9 0.1 collective-permute-start.7
  24.0 0.7 %shard_map.53 = (f32[128,1024]{1,0:T(8,128)S(1)}, f32[128,128]{1,0:T(8,128)S(1)}) custom-call(f32[1,2048]{1,0:T(1,128)S(1)} %get-tuple-element.30.factor_ref, bf16[2048,1024]{1,0:T(8,128)(2,1)S(1)} %copy-done.1, f32[128,2048]{1,0:T(8,128)S(1)} %get-tuple-element.31.part_ref), custom_call_target="tpu_custom_call" | custom-call | flops 536870912 | bytes 5251072 | tf_op jit(solution)/shard_map/pallas_call | solution.py:182
  24.7 0.8 %collective-permute-done.7.got_ref = bf16[128,1152]{1,0:T(8,128)(2,1)S(1)} collective-permute-done((bf16[128,1152]{1,0:T(8,128)(2,1)S(1)}, bf16[128,1152]{1,0:T(8,128)(2,1)S(1)}, u32[]{:S(2)}, u32[]{:S(2)}) %collective-permute-start.7) | collective-permute-done | bytes 294944 | tf_op jit(solution)/shard_map/ppermute | solution.py:17
  25.5 0.2 shard_map.54
  25.7 1.6 %collective-permute-start.8 = (bf16[32,1152]{1,0:T(8,128)(2,1)S(1)}, bf16[32,1152]{1,0:T(8,128)(2,1)S(1)}, u32[]{:S(2)}, u32[]{:S(2)}) collective-permute-start(bf16[32,1152]{1,0:T(8,128)(2,1)S(1)} %get-tuple-element.37), channel_id=1, source_target_pairs={{0,6},{1,7},{2,4},{3,5},{4,2},{5,3},{6,0},{7,1},{8,14},{9,15},{10,... | collective-permute-start | bytes 221192 | tf_op jit(solution)/shard_map/ppermute | solution.py:17
  27.3 1.5 %collective-permute-start.9 = (bf16[32,1152]{1,0:T(8,128)(2,1)S(1)}, bf16[32,1152]{1,0:T(8,128)(2,1)S(1)}, u32[]{:S(2)}, u32[]{:S(2)}) collective-permute-start(bf16[32,1152]{1,0:T(8,128)(2,1)S(1)} %get-tuple-element.38), channel_id=1, source_target_pairs={{0,2},{1,3},{2,0},{3,1},{4,6},{5,7},{6,4},{7,5},{8,10},{9,11},{10,... | collective-permute-start | bytes 221192 | tf_op jit(solution)/shard_map/ppermute | solution.py:17
  28.7 0.5 %collective-permute-start.10 = (bf16[32,1152]{1,0:T(8,128)(2,1)S(1)}, bf16[32,1152]{1,0:T(8,128)(2,1)S(1)}, u32[]{:S(2)}, u32[]{:S(2)}) collective-permute-start(bf16[32,1152]{1,0:T(8,128)(2,1)S(1)} %get-tuple-element.39), channel_id=1, source_target_pairs={{0,4},{1,5},{2,6},{3,7},{4,0},{5,1},{6,2},{7,3},{8,12},{9,13},{10,... | collective-permute-start | bytes 221192 | tf_op jit(solution)/shard_map/ppermute | solution.py:17
  29.2 2.6 %collective-permute-done.8.refs_0_ = bf16[32,1152]{1,0:T(8,128)(2,1)S(1)} collective-permute-done((bf16[32,1152]{1,0:T(8,128)(2,1)S(1)}, bf16[32,1152]{1,0:T(8,128)(2,1)S(1)}, u32[]{:S(2)}, u32[]{:S(2)}) %collective-permute-start.8) | collective-permute-done | bytes 73760 | tf_op jit(solution)/shard_map/ppermute | solution.py:17
  31.9 0.7 %collective-permute-done.9.refs_1_ = bf16[32,1152]{1,0:T(8,128)(2,1)S(1)} collective-permute-done((bf16[32,1152]{1,0:T(8,128)(2,1)S(1)}, bf16[32,1152]{1,0:T(8,128)(2,1)S(1)}, u32[]{:S(2)}, u32[]{:S(2)}) %collective-permute-start.9) | collective-permute-done | bytes 73760 | tf_op jit(solution)/shard_map/ppermute | solution.py:17
  32.6 0.5 %collective-permute-done.10.refs_2_ = bf16[32,1152]{1,0:T(8,128)(2,1)S(1)} collective-permute-done((bf16[32,1152]{1,0:T(8,128)(2,1)S(1)}, bf16[32,1152]{1,0:T(8,128)(2,1)S(1)}, u32[]{:S(2)}, u32[]{:S(2)}) %collective-permute-start.10) | collective-permute-done | bytes 73760 | tf_op jit(solution)/shard_map/ppermute | solution.py:17
  33.1 0.0 copy-done.2
  33.1 0.8 %shard_map.55 = (f32[32,1024]{1,0:T(8,128)}, f32[1,32]{1,0:T(1,128)}) custom-call(f32[32,1024]{1,0:T(8,128)S(1)} %get-tuple-element.35.own_ref, f32[32,128]{1,0:T(8,128)S(1)} %get-tuple-element.36.own_mass_ref, f32[32,1024]{1,0:T(8,128)S(1)} %copy-done.2, bf16[32,1152]{1,0:T(8,128)(2,1)S(1)} %collective-permute-done.8.refs_0_, ...), custom_call_target="tpu_custom_call" | custom-call | bytes 499712 | tf_op jit(solution)/shard_map/pallas_call | solution.py:182
  (4 shorter events, 0.0 us)
Async XLA Ops:
  1.5 8.8 %collective-permute-start.2 = (bf16[32,1024]{1,0:T(8,128)(2,1)S(1)}, bf16[32,1024]{1,0:T(8,128)(2,1)S(1)}, u32[]{:S(2)}, u32[]{:S(2)}) collective-permute-start(bf16[32,1024]{1,0:T(8,128)(2,1)S(1)} %convert_element_type.3.rounded_ref), channel_id=1, source_target_pairs={{0,6},{1,7},{2,4},{3,5},{4,2},{5,3},{6,0},{7,1},{8,14},{9,15},{10,... | collective-permute-start | bytes 196616 | tf_op jit(solution)/shard_map/ppermute | solution.py:17
  5.5 4.8 %collective-permute-start.1 = (bf16[32,1024]{1,0:T(8,128)(2,1)S(1)}, bf16[32,1024]{1,0:T(8,128)(2,1)S(1)}, u32[]{:S(2)}, u32[]{:S(2)}) collective-permute-start(bf16[32,1024]{1,0:T(8,128)(2,1)S(1)} %convert_element_type.3.rounded_ref), channel_id=1, source_target_pairs={{0,4},{1,5},{2,6},{3,7},{4,0},{5,1},{6,2},{7,3},{8,12},{9,13},{10,... | collective-permute-start | bytes 196616 | tf_op jit(solution)/shard_map/ppermute | solution.py:17
  6.0 4.3 %collective-permute-start = (bf16[32,1024]{1,0:T(8,128)(2,1)S(1)}, bf16[32,1024]{1,0:T(8,128)(2,1)S(1)}, u32[]{:S(2)}, u32[]{:S(2)}) collective-permute-start(bf16[32,1024]{1,0:T(8,128)(2,1)S(1)} %convert_element_type.3.rounded_ref), channel_id=1, source_target_pairs={{0,2},{1,3},{2,0},{3,1},{4,6},{5,7},{6,4},{7,5},{8,10},{9,11},{10,... | collective-permute-start | bytes 196616 | tf_op jit(solution)/shard_map/ppermute | solution.py:17
  8.3 5.1 %copy-start = (bf16[2048,1024]{1,0:T(8,128)(2,1)}, bf16[2048,1024]{1,0:T(8,128)(2,1)S(1)}, u32[]{:S(2)}) copy-start(bf16[2048,1024]{1,0:T(8,128)(2,1)S(1)} %get-tuple-element.23.docs_ref.refs_3_) | copy-start | bytes 12582916
  10.3 1.6 %collective-permute-start.3 = (bf16[128,1024]{1,0:T(8,128)(2,1)S(1)}, bf16[128,1024]{1,0:T(8,128)(2,1)S(1)}, u32[]{:S(2)}, u32[]{:S(2)}) collective-permute-start(bf16[128,1024]{1,0:T(8,128)(2,1)S(1)} %constant_dynamic-update-slice_fusion.table_ref), channel_id=1, source_target_pairs={{0,1},{1,0},{2,3},{3,2},{4,5},{5,4},{6,7},{7,6},{8,9},{9,8},{10,11... | collective-permute-start | bytes 786440 | tf_op jit(solution)/shard_map/ppermute | solution.py:17
  13.4 5.5 %collective-permute-start.6 = (f32[1,2048]{1,0:T(1,128)S(1)}, f32[1,2048]{1,0:T(1,128)S(1)}, u32[]{:S(2)}, u32[]{:S(2)}) collective-permute-start(f32[1,2048]{1,0:T(1,128)S(1)} %get-tuple-element.27.lse_ref), channel_id=1, source_target_pairs={{0,16},{8,24},{16,8},{24,0},{1,17},{9,25},{17,9},{25,1},{2,18},{10... | collective-permute-start | bytes 24584 | tf_op jit(solution)/shard_map/ppermute | solution.py:209
  16.0 4.5 %collective-permute-start.5 = (f32[1,2048]{1,0:T(1,128)S(1)}, f32[1,2048]{1,0:T(1,128)S(1)}, u32[]{:S(2)}, u32[]{:S(2)}) collective-permute-start(f32[1,2048]{1,0:T(1,128)S(1)} %get-tuple-element.27.lse_ref), channel_id=1, source_target_pairs={{0,24},{8,16},{16,0},{24,8},{1,25},{9,17},{17,1},{25,9},{2,26},{10... | collective-permute-start | bytes 24584 | tf_op jit(solution)/shard_map/ppermute | solution.py:209
  17.3 3.7 %collective-permute-start.4 = (f32[1,2048]{1,0:T(1,128)S(1)}, f32[1,2048]{1,0:T(1,128)S(1)}, u32[]{:S(2)}, u32[]{:S(2)}) collective-permute-start(f32[1,2048]{1,0:T(1,128)S(1)} %get-tuple-element.27.lse_ref), channel_id=1, source_target_pairs={{0,8},{8,0},{16,24},{24,16},{1,9},{9,1},{17,25},{25,17},{2,10},{10... | collective-permute-start | bytes 24584 | tf_op jit(solution)/shard_map/ppermute | solution.py:209
  20.9 2.2 %copy-start.1 = (bf16[2048,1024]{1,0:T(8,128)(2,1)S(1)}, bf16[2048,1024]{1,0:T(8,128)(2,1)}, u32[]{:S(2)}) copy-start(bf16[2048,1024]{1,0:T(8,128)(2,1)} %copy-done) | copy-start | bytes 12582916
  23.9 9.2 %copy-start.2 = (f32[32,1024]{1,0:T(8,128)S(1)}, f32[32,1024]{1,0:T(8,128)}, u32[]{:S(2)}) copy-start(f32[32,1024]{1,0:T(8,128)} %cent_ref.1) | copy-start | bytes 393220
  23.9 1.6 %collective-permute-start.7 = (bf16[128,1152]{1,0:T(8,128)(2,1)S(1)}, bf16[128,1152]{1,0:T(8,128)(2,1)S(1)}, u32[]{:S(2)}, u32[]{:S(2)}) collective-permute-start(bf16[128,1152]{1,0:T(8,128)(2,1)S(1)} %get-tuple-element.34), channel_id=1, source_target_pairs={{0,1},{1,0},{2,3},{3,2},{4,5},{5,4},{6,7},{7,6},{8,9},{9,8},{10,11... | collective-permute-start | bytes 884744 | tf_op jit(solution)/shard_map/ppermute | solution.py:17
  25.7 6.2 %collective-permute-start.8 = (bf16[32,1152]{1,0:T(8,128)(2,1)S(1)}, bf16[32,1152]{1,0:T(8,128)(2,1)S(1)}, u32[]{:S(2)}, u32[]{:S(2)}) collective-permute-start(bf16[32,1152]{1,0:T(8,128)(2,1)S(1)} %get-tuple-element.37), channel_id=1, source_target_pairs={{0,6},{1,7},{2,4},{3,5},{4,2},{5,3},{6,0},{7,1},{8,14},{9,15},{10,... | collective-permute-start | bytes 221192 | tf_op jit(solution)/shard_map/ppermute | solution.py:17
  27.3 5.4 %collective-permute-start.9 = (bf16[32,1152]{1,0:T(8,128)(2,1)S(1)}, bf16[32,1152]{1,0:T(8,128)(2,1)S(1)}, u32[]{:S(2)}, u32[]{:S(2)}) collective-permute-start(bf16[32,1152]{1,0:T(8,128)(2,1)S(1)} %get-tuple-element.38), channel_id=1, source_target_pairs={{0,2},{1,3},{2,0},{3,1},{4,6},{5,7},{6,4},{7,5},{8,10},{9,11},{10,... | collective-permute-start | bytes 221192 | tf_op jit(solution)/shard_map/ppermute | solution.py:17
  28.7 4.4 %collective-permute-start.10 = (bf16[32,1152]{1,0:T(8,128)(2,1)S(1)}, bf16[32,1152]{1,0:T(8,128)(2,1)S(1)}, u32[]{:S(2)}, u32[]{:S(2)}) collective-permute-start(bf16[32,1152]{1,0:T(8,128)(2,1)S(1)} %get-tuple-element.39), channel_id=1, source_target_pairs={{0,4},{1,5},{2,6},{3,7},{4,0},{5,1},{6,2},{7,3},{8,12},{9,13},{10,... | collective-permute-start | bytes 221192 | tf_op jit(solution)/shard_map/ppermute | solution.py:17

commit v8 on v6

--- a/solution.py
+++ b/solution.py
@@ -33,22 +33,59 @@
     return parts[0]
 
 
-def after_docs_kernel(docs_ref, rounded_ref, own_ref):
-    own_ref[...] = rounded_ref[...]
+def transpose_kernel(chunk, source_ref, follow_ref, docs_ref, own_ref, landing, sems):
+    copies = []
+    for i, start in enumerate(range(0, source_ref.shape[0], chunk)):
+        here = pl.ds(start, chunk)
+        copies.append(pltpu.make_async_copy(source_ref.at[here], landing.at[here], sems.at[i]))
+        copies[-1].start()
+    own_ref[...] = follow_ref[...]
+    for i, copy in enumerate(copies):
+        copy.wait()
+        here = slice(i * chunk, (i + 1) * chunk)
+        docs_ref[:, here] = landing[here, :].T
+
+
+def load_kernel(source_ref, follow_ref, docs_ref, own_ref, sem):
+    copy = pltpu.make_async_copy(source_ref, docs_ref, sem)
+    copy.start()
+    own_ref[...] = follow_ref[...]
+    copy.wait()
+
+
+def load(source, follow, chunk=0):
+    count, width = source.shape
+    kernel, dims, scratch = load_kernel, (count, width), [pltpu.SemaphoreType.DMA]
+    if chunk:
+        kernel, dims = functools.partial(transpose_kernel, chunk), (width, count)
+        scratch = [
+            pltpu.VMEM((count, width), source.dtype),
+            pltpu.SemaphoreType.DMA((count // chunk,)),
+        ]
+    return pl.pallas_call(
+        kernel,
+        out_shape=[shape(dims, source.dtype), shape(follow.shape, follow.dtype)],
+        in_specs=[pl.BlockSpec(memory_space=pltpu.HBM), VMEM],
+        out_specs=[VMEM, VMEM],
+        scratch_shapes=scratch,
+        compiler_params=pltpu.CompilerParams(
+            vmem_limit_bytes=(4 << 20) + (2 * source.nbytes if chunk else 0)
+        ),
+        cost_estimate=pl.CostEstimate(
+            flops=0, bytes_accessed=2 * source.nbytes, transcendentals=0
+        ),
+    )(pltpu.with_memory_space_constraint(source, pltpu.HBM), follow)
 
 
 def scores_kernel(chunk, docs_ref, table_ref, part_ref, top_ref, sum_ref):
-    count, width = docs_ref.shape
+    width, count = docs_ref.shape
     scale = 4.0 / math.sqrt(width)
     table = table_ref[...]
     wide = table.astype(jnp.float32)
     half_norms = 0.5 * jnp.sum(wide * wide, axis=1, keepdims=True)
     for start in range(0, count, chunk):
         cols = slice(start, start + chunk)
-        dots = lax.dot_general(
-            table, docs_ref[cols, :], (((1,), (1,)), ((), ())),
-            preferred_element_type=jnp.float32,
-        )
+        dots = jnp.dot(table, docs_ref[:, cols], preferred_element_type=jnp.float32)
         scores = (dots - half_norms) * scale
         top = jnp.max(scores, axis=0, keepdims=True)
         part = jnp.exp(scores - top)
@@ -181,17 +218,18 @@
         resp = [pltpu.VMEM((half, count), jnp.bfloat16)]
         rounded = centroids.astype(jnp.bfloat16)
         blocks = [swap(rounded, "dev", n, m) for m in range(2, n, 2)]
-        own, = call(after_docs_kernel, [shape(rounded.shape, rounded.dtype)], docs, rounded)
+        docs_t, own = load(docs, rounded, chunk)
         mine = jnp.concatenate([own] + blocks, axis=0)
         theirs = swap(mine, "dev", n, 1)
         part, top, total = call(
-            functools.partial(scores_kernel, chunk), stats, docs, mine, flops=flops
+            functools.partial(scores_kernel, chunk), stats, docs_t, mine, flops=flops
         )
         other_part, other_top, lse = call(
             functools.partial(last_scores_kernel, chunk), stats,
-            docs, theirs, top, total, flops=flops,
+            docs_t, theirs, top, total, flops=flops,
         )
         others = [lax.ppermute(lse, "cgrp", pairs) for pairs in plan]
+        docs, lse = load(docs, lse)
         doc_lse, factor, send = call(
             functools.partial(send_kernel, g, plan, chunk),
             [shape((1, count)), shape((1, count)), shape((half, width + LANES), jnp.bfloat16)],

time: 35 us -> 31.4 us (0.90)
  local copies, waits for them, and re-layouts: 4.53 us -> 0.03 us
  Pallas kernels: 5.72 us -> 9.36 us
  waiting for transfers between devices: 9.92 us -> 7.7 us
  starting transfers between devices: 12.9 us -> 12.5 us
    pallas_call x0 -> x2, Pallas kernels: none -> 4.93 us  [load(): pl.pallas_call(kernel, out_shape=[shape(dims, source.dtype), shape(follow...]
    unnamed x8 -> x5, local copies, waits for them, and re-layouts: 4.53 us -> 0.02 us
    ppermute x3, waiting for transfers between devices: 3.15 us -> 1.1 us  [body(): others = [lax.ppermute(lse, 'cgrp', pairs) for pairs in plan]]
    pallas_call x7 -> x6, Pallas kernels: 5.72 us -> 4.43 us  [call(): pl.pallas_call(kernel, out_shape=outs, in_specs=[SMEM if x.dtype == jnp.i...]
    ppermute x3, starting transfers between devices: 4.61 us -> 4.21 us  [body(): others = [lax.ppermute(lse, 'cgrp', pairs) for pairs in plan]]
  transfers between devices with their start and end apart: 11 -> 11, of which waited for: 9 -> 8; matrix products, arithmetic and copies ran while one was open for 0% -> 0% of each run, Pallas kernels for 7% -> 21%
where the time goes in v8:
time: 31.4 us; the launch traced here: 31.3 us
  starting transfers between devices  12.5 us (40%)
  Pallas kernels  9.36 us (30%)
  waiting for transfers between devices  7.7 us (25%)
  other arithmetic  0.92 us (3%)
  between operations  0.74 us (2%)
    ppermute x8, starting transfers between devices, swap(): return lax.ppermute(x, axis, [(i, i ^ mask) for i in range(size)])  8.29 us
    ppermute x8, waiting for transfers between devices, swap(): return lax.ppermute(x, axis, [(i, i ^ mask) for i in range(size)])  6.6 us
    pallas_call x2, Pallas kernels, load(): pl.pallas_call(kernel, out_shape=[shape(dims, source.dtype), shape(follow...  4.93 us
    pallas_call x6, Pallas kernels, call(): pl.pallas_call(kernel, out_shape=outs, in_specs=[SMEM if x.dtype == jnp.i...  4.43 us
    ppermute x3, starting transfers between devices, body(): others = [lax.ppermute(lse, 'cgrp', pairs) for pairs in plan]  4.21 us
    ppermute x3, waiting for transfers between devices, body(): others = [lax.ppermute(lse, 'cgrp', pairs) for pairs in plan]  1.1 us
    convert_element_type x1, other arithmetic, body(): rounded = centroids.astype(jnp.bfloat16)  0.92 us
  transfers between devices with their start and end apart: 11, of which 8 were waited for; matrix products, arithmetic and copies ran while one was open for 0% of the time, Pallas kernels for 21%

profile of v8, /device:TPU:0, one launch (start us, length us, event | category | flops | bytes accessed | tf_op | source)
XLA Modules:
  0.0 31.3 jit_solution(9562055034447020288)
XLA Ops:
  0.6 0.9 %convert_element_type.3.follow_ref = bf16[32,1024]{1,0:T(8,128)(2,1)S(1)} convert(f32[32,1024]{1,0:T(8,128)} %cent_ref.1) | non-fusion elementwise | flops 32768 | bytes 196608 | tf_op jit(solution)/shard_map/convert_element_type | solution.py:219
  1.5 4.0 %collective-permute-start.2 = (bf16[32,1024]{1,0:T(8,128)(2,1)S(1)}, bf16[32,1024]{1,0:T(8,128)(2,1)S(1)}, u32[]{:S(2)}, u32[]{:S(2)}) collective-permute-start(bf16[32,1024]{1,0:T(8,128)(2,1)S(1)} %convert_element_type.3.follow_ref), channel_id=1, source_target_pairs={{0,6},{1,7},{2,4},{3,5},{4,2},{5,3},{6,0},{7,1},{8,14},{9,15},{10,... | collective-permute-start | bytes 196616 | tf_op jit(solution)/shard_map/ppermute | solution.py:17
  5.5 0.5 %collective-permute-start.1 = (bf16[32,1024]{1,0:T(8,128)(2,1)S(1)}, bf16[32,1024]{1,0:T(8,128)(2,1)S(1)}, u32[]{:S(2)}, u32[]{:S(2)}) collective-permute-start(bf16[32,1024]{1,0:T(8,128)(2,1)S(1)} %convert_element_type.3.follow_ref), channel_id=1, source_target_pairs={{0,4},{1,5},{2,6},{3,7},{4,0},{5,1},{6,2},{7,3},{8,12},{9,13},{10,... | collective-permute-start | bytes 196616 | tf_op jit(solution)/shard_map/ppermute | solution.py:17
  6.0 0.1 collective-permute-start
  6.1 2.7 %shard_map.49 = (bf16[1024,2048]{1,0:T(8,128)(2,1)S(1)}, bf16[32,1024]{1,0:T(8,128)(2,1)S(1)}) custom-call(bf16[2048,1024]{1,0:T(8,128)(2,1)} %source_ref.3, bf16[32,1024]{1,0:T(8,128)(2,1)S(1)} %convert_element_type.3.follow_ref), custom_call_target="tpu_custom_call" | custom-call | bytes 8388608 | tf_op jit(solution)/shard_map/pallas_call | solution.py:65
  8.9 1.4 %collective-permute-done = bf16[32,1024]{1,0:T(8,128)(2,1)S(1)} collective-permute-done((bf16[32,1024]{1,0:T(8,128)(2,1)S(1)}, bf16[32,1024]{1,0:T(8,128)(2,1)S(1)}, u32[]{:S(2)}, u32[]{:S(2)}) %collective-permute-start) | collective-permute-done | bytes 65568 | tf_op jit(solution)/shard_map/ppermute | solution.py:17
  10.3 0.0 collective-permute-done.1
  10.3 0.0 collective-permute-done.2
  10.3 0.1 collective-permute-start.3
  10.4 0.9 %shard_map.50 = (f32[128,2048]{1,0:T(8,128)S(1)}, f32[1,2048]{1,0:T(1,128)S(1)}, f32[1,2048]{1,0:T(1,128)S(1)}) custom-call(bf16[1024,2048]{1,0:T(8,128)(2,1)S(1)} %get-tuple-element.25.docs_ref, bf16[128,1024]{1,0:T(8,128)(2,1)S(1)} %constant_dynamic-update-slice_fusion.table_ref), custom_call_target="tpu_custom_call" | custom-call | flops 536870912 | bytes 4456448 | tf_op jit(solution)/shard_map/pallas_call | solution.py:204
  11.3 0.6 %collective-permute-done.3.table_ref = bf16[128,1024]{1,0:T(8,128)(2,1)S(1)} collective-permute-done((bf16[128,1024]{1,0:T(8,128)(2,1)S(1)}, bf16[128,1024]{1,0:T(8,128)(2,1)S(1)}, u32[]{:S(2)}, u32[]{:S(2)}) %collective-permute-start.3) | collective-permute-done | bytes 262176 | tf_op jit(solution)/shard_map/ppermute | solution.py:17
  11.9 0.9 %shard_map.51 = (f32[128,2048]{1,0:T(8,128)S(1)}, f32[1,2048]{1,0:T(1,128)S(1)}, f32[1,2048]{1,0:T(1,128)S(1)}) custom-call(bf16[1024,2048]{1,0:T(8,128)(2,1)S(1)} %get-tuple-element.25.docs_ref, bf16[128,1024]{1,0:T(8,128)(2,1)S(1)} %collective-permute-done.3.table_ref, f32[1,2048]{1,0:T(1,128)S(1)} %get-tuple-element.27.first_top_ref.refs_6_, ...), custom_call_target="tpu_custom_call" | custom-call | flops 536870912 | bytes 4472832 | tf_op jit(solution)/shard_map/pallas_call | solution.py:204
  12.9 2.6 %collective-permute-start.6 = (f32[1,2048]{1,0:T(1,128)S(1)}, f32[1,2048]{1,0:T(1,128)S(1)}, u32[]{:S(2)}, u32[]{:S(2)}) collective-permute-start(f32[1,2048]{1,0:T(1,128)S(1)} %get-tuple-element.29.follow_ref), channel_id=1, source_target_pairs={{0,16},{8,24},{16,8},{24,0},{1,17},{9,25},{17,9},{25,1},{2,18},{10... | collective-permute-start | bytes 24584 | tf_op jit(solution)/shard_map/ppermute | solution.py:231
  15.5 1.2 %collective-permute-start.5 = (f32[1,2048]{1,0:T(1,128)S(1)}, f32[1,2048]{1,0:T(1,128)S(1)}, u32[]{:S(2)}, u32[]{:S(2)}) collective-permute-start(f32[1,2048]{1,0:T(1,128)S(1)} %get-tuple-element.29.follow_ref), channel_id=1, source_target_pairs={{0,24},{8,16},{16,0},{24,8},{1,25},{9,17},{17,1},{25,9},{2,26},{10... | collective-permute-start | bytes 24584 | tf_op jit(solution)/shard_map/ppermute | solution.py:231
  16.7 0.3 %collective-permute-start.4 = (f32[1,2048]{1,0:T(1,128)S(1)}, f32[1,2048]{1,0:T(1,128)S(1)}, u32[]{:S(2)}, u32[]{:S(2)}) collective-permute-start(f32[1,2048]{1,0:T(1,128)S(1)} %get-tuple-element.29.follow_ref), channel_id=1, source_target_pairs={{0,8},{8,0},{16,24},{24,16},{1,9},{9,1},{17,25},{25,17},{2,10},{10... | collective-permute-start | bytes 24584 | tf_op jit(solution)/shard_map/ppermute | solution.py:231
  17.1 2.2 %shard_map.52 = (bf16[2048,1024]{1,0:T(8,128)(2,1)S(1)}, f32[1,2048]{1,0:T(1,128)S(1)}) custom-call(bf16[2048,1024]{1,0:T(8,128)(2,1)} %source_ref.3, f32[1,2048]{1,0:T(1,128)S(1)} %get-tuple-element.29.follow_ref), custom_call_target="tpu_custom_call" | custom-call | bytes 8388608 | tf_op jit(solution)/shard_map/pallas_call | solution.py:65
  19.3 0.0 collective-permute-done.6.refs_2_
  19.3 0.8 %collective-permute-done.5.refs_1_ = f32[1,2048]{1,0:T(1,128)S(1)} collective-permute-done((f32[1,2048]{1,0:T(1,128)S(1)}, f32[1,2048]{1,0:T(1,128)S(1)}, u32[]{:S(2)}, u32[]{:S(2)}) %collective-permute-start.5) | collective-permute-done | bytes 8224 | tf_op jit(solution)/shard_map/ppermute | solution.py:231
  20.1 0.3 %collective-permute-done.4.refs_0_ = f32[1,2048]{1,0:T(1,128)S(1)} collective-permute-done((f32[1,2048]{1,0:T(1,128)S(1)}, f32[1,2048]{1,0:T(1,128)S(1)}, u32[]{:S(2)}, u32[]{:S(2)}) %collective-permute-start.4) | collective-permute-done | bytes 8224 | tf_op jit(solution)/shard_map/ppermute | solution.py:231
  20.4 0.8 %shard_map.53 = (f32[1,2048]{1,0:T(1,128)}, f32[1,2048]{1,0:T(1,128)S(1)}, bf16[128,1152]{1,0:T(8,128)(2,1)S(1)}) custom-call(s32[1]{0:T(128)} %bitcast.me_ref, f32[1,2048]{1,0:T(1,128)S(1)} %get-tuple-element.30.lse_ref, f32[1,2048]{1,0:T(1,128)S(1)} %collective-permute-done.4.refs_0_, f32[1,2048]{1,0:T(1,128)S(1)} %collective-permute-done.5.refs_1_, ...), custom_call_target="tpu_custom_call" | custom-call | flops 536870912 | bytes 5292036 | tf_op jit(solution)/shard_map/pallas_call | solution.py:204
  21.2 0.0 copy-start
  21.2 0.1 collective-permute-start.7
  21.3 0.8 %shard_map.54 = (f32[128,1024]{1,0:T(8,128)S(1)}, f32[128,128]{1,0:T(8,128)S(1)}) custom-call(f32[1,2048]{1,0:T(1,128)S(1)} %get-tuple-element.34.factor_ref, bf16[2048,1024]{1,0:T(8,128)(2,1)S(1)} %get-tuple-element.31.refs_3_.docs_ref, f32[128,2048]{1,0:T(8,128)S(1)} %get-tuple-element.35.part_ref), custom_call_target="tpu_custom_call" | custom-call | flops 536870912 | bytes 5251072 | tf_op jit(solution)/shard_map/pallas_call | solution.py:204
  22.1 0.8 %collective-permute-done.7.got_ref = bf16[128,1152]{1,0:T(8,128)(2,1)S(1)} collective-permute-done((bf16[128,1152]{1,0:T(8,128)(2,1)S(1)}, bf16[128,1152]{1,0:T(8,128)(2,1)S(1)}, u32[]{:S(2)}, u32[]{:S(2)}) %collective-permute-start.7) | collective-permute-done | bytes 294944 | tf_op jit(solution)/shard_map/ppermute | solution.py:17
  22.9 0.2 shard_map.55
  23.0 1.6 %collective-permute-start.8 = (bf16[32,1152]{1,0:T(8,128)(2,1)S(1)}, bf16[32,1152]{1,0:T(8,128)(2,1)S(1)}, u32[]{:S(2)}, u32[]{:S(2)}) collective-permute-start(bf16[32,1152]{1,0:T(8,128)(2,1)S(1)} %get-tuple-element.41), channel_id=1, source_target_pairs={{0,6},{1,7},{2,4},{3,5},{4,2},{5,3},{6,0},{7,1},{8,14},{9,15},{10,... | collective-permute-start | bytes 221192 | tf_op jit(solution)/shard_map/ppermute | solution.py:17
  24.6 1.5 %collective-permute-start.9 = (bf16[32,1152]{1,0:T(8,128)(2,1)S(1)}, bf16[32,1152]{1,0:T(8,128)(2,1)S(1)}, u32[]{:S(2)}, u32[]{:S(2)}) collective-permute-start(bf16[32,1152]{1,0:T(8,128)(2,1)S(1)} %get-tuple-element.42), channel_id=1, source_target_pairs={{0,2},{1,3},{2,0},{3,1},{4,6},{5,7},{6,4},{7,5},{8,10},{9,11},{10,... | collective-permute-start | bytes 221192 | tf_op jit(solution)/shard_map/ppermute | solution.py:17
  26.1 0.5 %collective-permute-start.10 = (bf16[32,1152]{1,0:T(8,128)(2,1)S(1)}, bf16[32,1152]{1,0:T(8,128)(2,1)S(1)}, u32[]{:S(2)}, u32[]{:S(2)}) collective-permute-start(bf16[32,1152]{1,0:T(8,128)(2,1)S(1)} %get-tuple-element.43), channel_id=1, source_target_pairs={{0,4},{1,5},{2,6},{3,7},{4,0},{5,1},{6,2},{7,3},{8,12},{9,13},{10,... | collective-permute-start | bytes 221192 | tf_op jit(solution)/shard_map/ppermute | solution.py:17
  26.6 2.6 %collective-permute-done.8.refs_0_ = bf16[32,1152]{1,0:T(8,128)(2,1)S(1)} collective-permute-done((bf16[32,1152]{1,0:T(8,128)(2,1)S(1)}, bf16[32,1152]{1,0:T(8,128)(2,1)S(1)}, u32[]{:S(2)}, u32[]{:S(2)}) %collective-permute-start.8) | collective-permute-done | bytes 73760 | tf_op jit(solution)/shard_map/ppermute | solution.py:17
  29.2 0.7 %collective-permute-done.9.refs_1_ = bf16[32,1152]{1,0:T(8,128)(2,1)S(1)} collective-permute-done((bf16[32,1152]{1,0:T(8,128)(2,1)S(1)}, bf16[32,1152]{1,0:T(8,128)(2,1)S(1)}, u32[]{:S(2)}, u32[]{:S(2)}) %collective-permute-start.9) | collective-permute-done | bytes 73760 | tf_op jit(solution)/shard_map/ppermute | solution.py:17
  29.9 0.5 %collective-permute-done.10.refs_2_ = bf16[32,1152]{1,0:T(8,128)(2,1)S(1)} collective-permute-done((bf16[32,1152]{1,0:T(8,128)(2,1)S(1)}, bf16[32,1152]{1,0:T(8,128)(2,1)S(1)}, u32[]{:S(2)}, u32[]{:S(2)}) %collective-permute-start.10) | collective-permute-done | bytes 73760 | tf_op jit(solution)/shard_map/ppermute | solution.py:17
  30.4 0.0 copy-done
  30.4 0.8 %shard_map.56 = (f32[32,1024]{1,0:T(8,128)}, f32[1,32]{1,0:T(1,128)}) custom-call(f32[32,1024]{1,0:T(8,128)S(1)} %get-tuple-element.39.own_ref, f32[32,128]{1,0:T(8,128)S(1)} %get-tuple-element.40.own_mass_ref, f32[32,1024]{1,0:T(8,128)S(1)} %copy-done, bf16[32,1152]{1,0:T(8,128)(2,1)S(1)} %collective-permute-done.8.refs_0_, ...), custom_call_target="tpu_custom_call" | custom-call | bytes 499712 | tf_op jit(solution)/shard_map/pallas_call | solution.py:204
  (4 shorter events, 0.0 us)
Async XLA Ops:
  1.5 8.8 %collective-permute-start.2 = (bf16[32,1024]{1,0:T(8,128)(2,1)S(1)}, bf16[32,1024]{1,0:T(8,128)(2,1)S(1)}, u32[]{:S(2)}, u32[]{:S(2)}) collective-permute-start(bf16[32,1024]{1,0:T(8,128)(2,1)S(1)} %convert_element_type.3.follow_ref), channel_id=1, source_target_pairs={{0,6},{1,7},{2,4},{3,5},{4,2},{5,3},{6,0},{7,1},{8,14},{9,15},{10,... | collective-permute-start | bytes 196616 | tf_op jit(solution)/shard_map/ppermute | solution.py:17
  5.5 4.8 %collective-permute-start.1 = (bf16[32,1024]{1,0:T(8,128)(2,1)S(1)}, bf16[32,1024]{1,0:T(8,128)(2,1)S(1)}, u32[]{:S(2)}, u32[]{:S(2)}) collective-permute-start(bf16[32,1024]{1,0:T(8,128)(2,1)S(1)} %convert_element_type.3.follow_ref), channel_id=1, source_target_pairs={{0,4},{1,5},{2,6},{3,7},{4,0},{5,1},{6,2},{7,3},{8,12},{9,13},{10,... | collective-permute-start | bytes 196616 | tf_op jit(solution)/shard_map/ppermute | solution.py:17
  6.0 4.3 %collective-permute-start = (bf16[32,1024]{1,0:T(8,128)(2,1)S(1)}, bf16[32,1024]{1,0:T(8,128)(2,1)S(1)}, u32[]{:S(2)}, u32[]{:S(2)}) collective-permute-start(bf16[32,1024]{1,0:T(8,128)(2,1)S(1)} %convert_element_type.3.follow_ref), channel_id=1, source_target_pairs={{0,2},{1,3},{2,0},{3,1},{4,6},{5,7},{6,4},{7,5},{8,10},{9,11},{10,... | collective-permute-start | bytes 196616 | tf_op jit(solution)/shard_map/ppermute | solution.py:17
  10.3 1.6 %collective-permute-start.3 = (bf16[128,1024]{1,0:T(8,128)(2,1)S(1)}, bf16[128,1024]{1,0:T(8,128)(2,1)S(1)}, u32[]{:S(2)}, u32[]{:S(2)}) collective-permute-start(bf16[128,1024]{1,0:T(8,128)(2,1)S(1)} %constant_dynamic-update-slice_fusion.table_ref), channel_id=1, source_target_pairs={{0,1},{1,0},{2,3},{3,2},{4,5},{5,4},{6,7},{7,6},{8,9},{9,8},{10,11... | collective-permute-start | bytes 786440 | tf_op jit(solution)/shard_map/ppermute | solution.py:17
  12.9 6.4 %collective-permute-start.6 = (f32[1,2048]{1,0:T(1,128)S(1)}, f32[1,2048]{1,0:T(1,128)S(1)}, u32[]{:S(2)}, u32[]{:S(2)}) collective-permute-start(f32[1,2048]{1,0:T(1,128)S(1)} %get-tuple-element.29.follow_ref), channel_id=1, source_target_pairs={{0,16},{8,24},{16,8},{24,0},{1,17},{9,25},{17,9},{25,1},{2,18},{10... | collective-permute-start | bytes 24584 | tf_op jit(solution)/shard_map/ppermute | solution.py:231
  15.5 4.5 %collective-permute-start.5 = (f32[1,2048]{1,0:T(1,128)S(1)}, f32[1,2048]{1,0:T(1,128)S(1)}, u32[]{:S(2)}, u32[]{:S(2)}) collective-permute-start(f32[1,2048]{1,0:T(1,128)S(1)} %get-tuple-element.29.follow_ref), channel_id=1, source_target_pairs={{0,24},{8,16},{16,0},{24,8},{1,25},{9,17},{17,1},{25,9},{2,26},{10... | collective-permute-start | bytes 24584 | tf_op jit(solution)/shard_map/ppermute | solution.py:231
  16.7 3.7 %collective-permute-start.4 = (f32[1,2048]{1,0:T(1,128)S(1)}, f32[1,2048]{1,0:T(1,128)S(1)}, u32[]{:S(2)}, u32[]{:S(2)}) collective-permute-start(f32[1,2048]{1,0:T(1,128)S(1)} %get-tuple-element.29.follow_ref), channel_id=1, source_target_pairs={{0,8},{8,0},{16,24},{24,16},{1,9},{9,1},{17,25},{25,17},{2,10},{10... | collective-permute-start | bytes 24584 | tf_op jit(solution)/shard_map/ppermute | solution.py:231
  21.2 9.2 %copy-start = (f32[32,1024]{1,0:T(8,128)S(1)}, f32[32,1024]{1,0:T(8,128)}, u32[]{:S(2)}) copy-start(f32[32,1024]{1,0:T(8,128)} %cent_ref.1) | copy-start | bytes 393220
  21.2 1.6 %collective-permute-start.7 = (bf16[128,1152]{1,0:T(8,128)(2,1)S(1)}, bf16[128,1152]{1,0:T(8,128)(2,1)S(1)}, u32[]{:S(2)}, u32[]{:S(2)}) collective-permute-start(bf16[128,1152]{1,0:T(8,128)(2,1)S(1)} %get-tuple-element.38), channel_id=1, source_target_pairs={{0,1},{1,0},{2,3},{3,2},{4,5},{5,4},{6,7},{7,6},{8,9},{9,8},{10,11... | collective-permute-start | bytes 884744 | tf_op jit(solution)/shard_map/ppermute | solution.py:17
  23.0 6.2 %collective-permute-start.8 = (bf16[32,1152]{1,0:T(8,128)(2,1)S(1)}, bf16[32,1152]{1,0:T(8,128)(2,1)S(1)}, u32[]{:S(2)}, u32[]{:S(2)}) collective-permute-start(bf16[32,1152]{1,0:T(8,128)(2,1)S(1)} %get-tuple-element.41), channel_id=1, source_target_pairs={{0,6},{1,7},{2,4},{3,5},{4,2},{5,3},{6,0},{7,1},{8,14},{9,15},{10,... | collective-permute-start | bytes 221192 | tf_op jit(solution)/shard_map/ppermute | solution.py:17
  24.6 5.3 %collective-permute-start.9 = (bf16[32,1152]{1,0:T(8,128)(2,1)S(1)}, bf16[32,1152]{1,0:T(8,128)(2,1)S(1)}, u32[]{:S(2)}, u32[]{:S(2)}) collective-permute-start(bf16[32,1152]{1,0:T(8,128)(2,1)S(1)} %get-tuple-element.42), channel_id=1, source_target_pairs={{0,2},{1,3},{2,0},{3,1},{4,6},{5,7},{6,4},{7,5},{8,10},{9,11},{10,... | collective-permute-start | bytes 221192 | tf_op jit(solution)/shard_map/ppermute | solution.py:17
  26.1 4.4 %collective-permute-start.10 = (bf16[32,1152]{1,0:T(8,128)(2,1)S(1)}, bf16[32,1152]{1,0:T(8,128)(2,1)S(1)}, u32[]{:S(2)}, u32[]{:S(2)}) collective-permute-start(bf16[32,1152]{1,0:T(8,128)(2,1)S(1)} %get-tuple-element.43), channel_id=1, source_target_pairs={{0,4},{1,5},{2,6},{3,7},{4,0},{5,1},{6,2},{7,3},{8,12},{9,13},{10,... | collective-permute-start | bytes 221192 | tf_op jit(solution)/shard_map/ppermute | solution.py:17

commit v9 on v8

--- a/solution.py
+++ b/solution.py
@@ -31,6 +31,23 @@
     while len(parts) > 1:
         parts = [op(parts[i], parts[i + 1]) for i in range(0, len(parts), 2)]
     return parts[0]
+
+
+def round_kernel(source_ref, out_ref, landing, sem):
+    copy = pltpu.make_async_copy(source_ref, landing, sem)
+    copy.start()
+    copy.wait()
+    out_ref[...] = landing[...].astype(out_ref.dtype)
+
+
+def round_rows(x):
+    return pl.pallas_call(
+        round_kernel,
+        out_shape=shape(x.shape, jnp.bfloat16),
+        in_specs=[pl.BlockSpec(memory_space=pltpu.HBM)],
+        out_specs=VMEM,
+        scratch_shapes=[pltpu.VMEM(x.shape, x.dtype), pltpu.SemaphoreType.DMA],
+    )(pltpu.with_memory_space_constraint(x, pltpu.HBM))
 
 
 def transpose_kernel(chunk, source_ref, follow_ref, docs_ref, own_ref, landing, sems):
@@ -104,18 +121,22 @@
     lse_ref[...] = top + jnp.log(total)
 
 
-def weighted_sums(chunk, factor, docs_ref, part_ref, resp_ref, store):
-    rows, count = part_ref.shape
-    mass = jnp.zeros((rows, 1), jnp.float32)
-    for start in range(0, count, chunk):
-        cols = slice(start, start + chunk)
-        resp = part_ref[:, cols] * factor[:, cols]
-        mass += jnp.sum(resp, axis=1, keepdims=True)
-        resp_ref[:, cols] = resp.astype(jnp.bfloat16)
+def weighted_sums(chunk, pieces, docs_ref, resp_ref, store):
+    masses, at = [], 0
+    for part_ref, here, factor in pieces:
+        rows = here.stop - here.start
+        mass = jnp.zeros((rows, 1), jnp.float32)
+        for start in range(0, part_ref.shape[1], chunk):
+            cols = slice(start, start + chunk)
+            resp = part_ref[here, cols] * factor[:, cols]
+            mass += jnp.sum(resp, axis=1, keepdims=True)
+            resp_ref[at:at + rows, cols] = resp.astype(jnp.bfloat16)
+        masses.append(mass)
+        at += rows
     for start in range(0, docs_ref.shape[1], chunk):
         cols = slice(start, start + chunk)
         store(cols, jnp.dot(resp_ref[...], docs_ref[:, cols], preferred_element_type=jnp.float32))
-    return mass
+    return jnp.concatenate(masses, axis=0)
 
 
 def mass_lanes(mass):
@@ -132,8 +153,8 @@
 
 def send_kernel(groups, plan, chunk, me_ref, lse_ref, *refs):
     got_refs = refs[:len(plan)]
-    docs_ref, part_ref, top_ref, keep_top_ref = refs[len(plan):len(plan) + 4]
-    doc_lse_ref, factor_ref, send_ref, resp_ref = refs[len(plan) + 4:]
+    docs_ref, part_ref, top_ref, keep_part_ref, keep_top_ref = refs[len(plan):len(plan) + 5]
+    doc_lse_ref, factor_ref, send_ref, resp_ref = refs[len(plan) + 5:]
     me = me_ref[0]
     parts = [lse_ref[...]] * groups
     for got_ref, pairs in zip(got_refs, plan):
@@ -143,13 +164,18 @@
     best = tree(parts, jnp.maximum)
     doc_lse = best + jnp.log(tree([jnp.exp(x - best) for x in parts], jnp.add))
     doc_lse_ref[...] = doc_lse
-    factor_ref[...] = jnp.exp(keep_top_ref[...] - doc_lse)
-    factor = jnp.exp(top_ref[...] - doc_lse)
+    keep_factor = jnp.exp(keep_top_ref[...] - doc_lse)
+    factor_ref[...] = keep_factor
 
     def store(cols, term):
         send_ref[:, cols] = term.astype(jnp.bfloat16)
 
-    mass = weighted_sums(chunk, factor, docs_ref, part_ref, resp_ref, store)
+    half, rows = part_ref.shape[0], send_ref.shape[0] - part_ref.shape[0]
+    pieces = [
+        (part_ref, slice(0, half), jnp.exp(top_ref[...] - doc_lse)),
+        (keep_part_ref, slice(half - rows, half), keep_factor),
+    ]
+    mass = weighted_sums(chunk, pieces, docs_ref, resp_ref, store)
     send_ref[:, docs_ref.shape[1]:] = mass_lanes(mass)
 
 
@@ -157,29 +183,42 @@
     def store(cols, term):
         keep_ref[:, cols] = term
 
-    mass = weighted_sums(chunk, factor_ref[...], docs_ref, part_ref, resp_ref, store)
+    pieces = [(part_ref, slice(0, keep_ref.shape[0]), factor_ref[...])]
+    mass = weighted_sums(chunk, pieces, docs_ref, resp_ref, store)
     keep_mass_ref[...] = jnp.broadcast_to(mass, keep_mass_ref.shape)
 
 
-def fold_kernel(keep_ref, keep_mass_ref, got_ref, own_ref, own_mass_ref, *send_refs):
+def fold_kernel(keep_ref, keep_mass_ref, sent_ref, got_ref, own_ref, own_mass_ref, *send_refs):
     rows, width = own_ref.shape
-    for slot in range(keep_ref.shape[0] // rows):
-        here = slice(slot * rows, (slot + 1) * rows)
-        got, got_mass = read_rows(got_ref[here], width)
+    *near_refs, far_ref = send_refs
+    last = len(near_refs) + 1
+
+    def slot(ref, i):
+        return read_rows(ref[i * rows:(i + 1) * rows], width)
+
+    for i in range(last):
+        here = slice(i * rows, (i + 1) * rows)
+        got, got_mass = slot(got_ref, i)
         term = keep_ref[here] + got
         mass = keep_mass_ref[here, :1] + got_mass
-        if slot == 0:
+        if i == 0:
             own_ref[...] = term
             own_mass_ref[...] = jnp.broadcast_to(mass, own_mass_ref.shape)
         else:
-            send_refs[slot - 1][:, :width] = term.astype(jnp.bfloat16)
-            send_refs[slot - 1][:, width:] = mass_lanes(mass)
-
-
-def final_kernel(own_ref, own_mass_ref, cent_ref, *refs):
-    *got_refs, next_ref, mass_ref = refs
-    width = own_ref.shape[1]
-    got = [read_rows(r[...], width) for r in got_refs]
+            near_refs[i - 1][:, :width] = term.astype(jnp.bfloat16)
+            near_refs[i - 1][:, width:] = mass_lanes(mass)
+    for i, (mine, theirs) in enumerate(((last + 1, last), (last, last + 1))):
+        here = slice(i * rows, (i + 1) * rows)
+        (a, a_mass), (b, b_mass) = slot(sent_ref, mine), slot(got_ref, theirs)
+        far_ref[here, :width] = (a + b).astype(jnp.bfloat16)
+        far_ref[here, width:] = mass_lanes(a_mass + b_mass)
+
+
+def final_kernel(odd_ref, own_ref, own_mass_ref, cent_ref, far_ref, passed_ref, *refs):
+    *near_refs, next_ref, mass_ref = refs
+    rows, width = own_ref.shape
+    far = jnp.where(odd_ref[0] == 1, far_ref[:rows], passed_ref[...])
+    got = [read_rows(x, width) for x in [r[...] for r in near_refs] + [far]]
     term = tree([own_ref[...]] + [a for a, _ in got], jnp.add)
     mass = tree([own_mass_ref[:, :1]] + [b for _, b in got], jnp.add)
     next_ref[...] = (term + cent_ref[...]) / (mass + 1.0)
@@ -215,8 +254,7 @@
 
         flops = 2 * half * count * width
         stats = [shape((half, count)), shape((1, count)), shape((1, count))]
-        resp = [pltpu.VMEM((half, count), jnp.bfloat16)]
-        rounded = centroids.astype(jnp.bfloat16)
+        rounded = round_rows(centroids)
         blocks = [swap(rounded, "dev", n, m) for m in range(2, n, 2)]
         docs_t, own = load(docs, rounded, chunk)
         mine = jnp.concatenate([own] + blocks, axis=0)
@@ -230,29 +268,36 @@
         )
         others = [lax.ppermute(lse, "cgrp", pairs) for pairs in plan]
         docs, lse = load(docs, lse)
+        sent = half + rows
         doc_lse, factor, send = call(
             functools.partial(send_kernel, g, plan, chunk),
-            [shape((1, count)), shape((1, count)), shape((half, width + LANES), jnp.bfloat16)],
-            lax.axis_index("cgrp").reshape(1), lse, *others, docs, other_part, other_top, top,
-            scratch=resp, flops=flops,
+            [shape((1, count)), shape((1, count)), shape((sent, width + LANES), jnp.bfloat16)],
+            lax.axis_index("cgrp").reshape(1), lse, *others,
+            docs, other_part, other_top, part, top,
+            scratch=[pltpu.VMEM((sent, count), jnp.bfloat16)], flops=flops,
         )
         got = swap(send, "dev", n, 1)
+        kept = half - rows
         keep, keep_mass = call(
             functools.partial(keep_kernel, chunk),
-            [shape((half, width)), shape((half, LANES))],
-            factor, docs, part, scratch=resp, flops=flops,
-        )
-        own, own_mass, *sends = call(
+            [shape((kept, width)), shape((kept, LANES))],
+            factor, docs, part,
+            scratch=[pltpu.VMEM((kept, count), jnp.bfloat16)], flops=flops,
+        )
+        own, own_mass, *sends, far = call(
             fold_kernel,
             [shape((rows, width)), shape((rows, LANES))]
-            + [shape((rows, width + LANES), jnp.bfloat16)] * (n // 2 - 1),
-            keep, keep_mass, got,
-        )
-        far_first = sorted(range(1, n // 2), key=lambda j: (-j.bit_count(), j))
-        arrived = [swap(sends[j - 1], "dev", n, 2 * j) for j in far_first]
+            + [shape((rows, width + LANES), jnp.bfloat16)] * (n // 2 - 2)
+            + [shape((2 * rows, width + LANES), jnp.bfloat16)],
+            keep, keep_mass, send, got,
+        )
+        far = lax.ppermute(far, "dev", [(i, i ^ (n - 2)) for i in range(1, n, 2)])
+        passed = swap(far[rows:], "dev", n, 1)
+        arrived = [swap(x, "dev", n, 2 * (j + 1)) for j, x in enumerate(sends)]
         result, mass = call(
             final_kernel, [shape((rows, width)), shape((1, rows))],
-            own, own_mass, centroids, *arrived,
+            (lax.axis_index("dev") % 2).reshape(1),
+            own, own_mass, centroids, far, passed, *arrived,
         )
         return (result, mass.reshape(rows), doc_lse.reshape(count))
 

time: 31.4 us -> 33.7 us (1.073)
  starting transfers between devices: 12.5 us -> 16.4 us
  waiting for transfers between devices: 7.7 us -> 4.21 us
  Pallas kernels: 9.36 us -> 11.1 us
  other arithmetic: 0.92 us -> 0 us
  local copies, waits for them, and re-layouts: 0.03 us -> 0.91 us
    ppermute x8, waiting for transfers between devices: 6.6 us -> 3.12 us  [swap(): return lax.ppermute(x, axis, [(i, i ^ mask) for i in range(size)])]
    ppermute x8, starting transfers between devices: 8.29 us -> 11.6 us  [swap(): return lax.ppermute(x, axis, [(i, i ^ mask) for i in range(size)])]
    pallas_call x0 -> x1, Pallas kernels: none -> 1.55 us  [round_rows(): pl.pallas_call(round_kernel, out_shape=shape(x.shape, jnp.bfloat16), in_s...]
    convert_element_type x1 -> x0, other arithmetic: 0.92 us -> none  [body(): rounded = centroids.astype(jnp.bfloat16)]
    unnamed x5 -> x7, local copies, waits for them, and re-layouts: 0.02 us -> 0.89 us
    ppermute x0 -> x1, starting transfers between devices: none -> 0.67 us  [body(): far = lax.ppermute(far, 'dev', [(i, i ^ n - 2) for i in range(1, n, 2)])]
  transfers between devices with their start and end apart: 11 -> 12, of which waited for: 8 -> 7; matrix products, arithmetic and copies ran while one was open for 0% -> 0% of each run, Pallas kernels for 21% -> 20%
where the time goes in v9:
time: 33.7 us; the launch traced here: 33.5 us
  starting transfers between devices  16.4 us (49%)
  Pallas kernels  11.1 us (33%)
  waiting for transfers between devices  4.21 us (12%)
  local copies, waits for them, and re-layouts  0.91 us (3%)
  between operations  0.74 us (2%)
    ppermute x8, starting transfers between devices, swap(): return lax.ppermute(x, axis, [(i, i ^ mask) for i in range(size)])  11.6 us
    pallas_call x2, Pallas kernels, load(): pl.pallas_call(kernel, out_shape=[shape(dims, source.dtype), shape(follow...  4.93 us
    pallas_call x6, Pallas kernels, call(): pl.pallas_call(kernel, out_shape=outs, in_specs=[SMEM if x.dtype == jnp.i...  4.66 us
    ppermute x3, starting transfers between devices, body(): others = [lax.ppermute(lse, 'cgrp', pairs) for pairs in plan]  4.22 us
    ppermute x8, waiting for transfers between devices, swap(): return lax.ppermute(x, axis, [(i, i ^ mask) for i in range(size)])  3.12 us
    pallas_call x1, Pallas kernels, round_rows(): pl.pallas_call(round_kernel, out_shape=shape(x.shape, jnp.bfloat16), in_s...  1.55 us
    ppermute x3, waiting for transfers between devices, body(): others = [lax.ppermute(lse, 'cgrp', pairs) for pairs in plan]  1.09 us
    unnamed x7, local copies, waits for them, and re-layouts  0.89 us
  transfers between devices with their start and end apart: 12, of which 7 were waited for; matrix products, arithmetic and copies ran while one was open for 0% of the time, Pallas kernels for 20%

profile of v9, /device:TPU:0, one launch (start us, length us, event | category | flops | bytes accessed | tf_op | source)
XLA Modules:
  0.0 33.5 jit_solution(1500235384392820489)
XLA Ops:
  0.6 1.6 %shard_map.49.follow_ref = bf16[32,1024]{1,0:T(8,128)(2,1)} custom-call(f32[32,1024]{1,0:T(8,128)} %cent_ref.1), custom_call_target="tpu_custom_call" | custom-call | tf_op jit(solution)/shard_map/pallas_call | solution.py:44
  2.2 4.0 %collective-permute-start.2 = (bf16[32,1024]{1,0:T(8,128)(2,1)}, bf16[32,1024]{1,0:T(8,128)(2,1)S(1)}, u32[]{:S(2)}, u32[]{:S(2)}) collective-permute-start(bf16[32,1024]{1,0:T(8,128)(2,1)} %shard_map.49.follow_ref), channel_id=1, source_target_pairs={{0,6},{1,7},{2,4},{3,5},{4,2},{5,3},{6,0},{7,1},{8,14},{9,15},{10,... | collective-permute-start | bytes 196616 | tf_op jit(solution)/shard_map/ppermute | solution.py:17
  6.1 0.5 %collective-permute-start.1 = (bf16[32,1024]{1,0:T(8,128)(2,1)}, bf16[32,1024]{1,0:T(8,128)(2,1)S(1)}, u32[]{:S(2)}, u32[]{:S(2)}) collective-permute-start(bf16[32,1024]{1,0:T(8,128)(2,1)} %shard_map.49.follow_ref), channel_id=1, source_target_pairs={{0,4},{1,5},{2,6},{3,7},{4,0},{5,1},{6,2},{7,3},{8,12},{9,13},{10,... | collective-permute-start | bytes 196616 | tf_op jit(solution)/shard_map/ppermute | solution.py:17
  6.7 0.1 collective-permute-start
  6.8 0.0 copy-start.1
  6.8 0.9 %copy-done.1 = bf16[32,1024]{1,0:T(8,128)(2,1)S(1)} copy-done((bf16[32,1024]{1,0:T(8,128)(2,1)S(1)}, bf16[32,1024]{1,0:T(8,128)(2,1)}, u32[]{:S(2)}) %copy-start.1) | copy-done | bytes 65560
  7.7 2.7 %shard_map.50 = (bf16[1024,2048]{1,0:T(8,128)(2,1)S(1)}, bf16[32,1024]{1,0:T(8,128)(2,1)S(1)}) custom-call(bf16[2048,1024]{1,0:T(8,128)(2,1)} %source_ref.5, bf16[32,1024]{1,0:T(8,128)(2,1)S(1)} %copy-done.1), custom_call_target="tpu_custom_call" | custom-call | bytes 8388608 | tf_op jit(solution)/shard_map/pallas_call | solution.py:82
  10.4 0.7 %collective-permute-done = bf16[32,1024]{1,0:T(8,128)(2,1)S(1)} collective-permute-done((bf16[32,1024]{1,0:T(8,128)(2,1)}, bf16[32,1024]{1,0:T(8,128)(2,1)S(1)}, u32[]{:S(2)}, u32[]{:S(2)}) %collective-permute-start) | collective-permute-done | bytes 65568 | tf_op jit(solution)/shard_map/ppermute | solution.py:17
  11.1 0.0 collective-permute-done.1
  11.2 0.0 collective-permute-done.2
  11.2 0.1 collective-permute-start.3
  11.3 0.9 %shard_map.51 = (f32[128,2048]{1,0:T(8,128)S(1)}, f32[1,2048]{1,0:T(1,128)S(1)}, f32[1,2048]{1,0:T(1,128)S(1)}) custom-call(bf16[1024,2048]{1,0:T(8,128)(2,1)S(1)} %get-tuple-element.25.docs_ref, bf16[128,1024]{1,0:T(8,128)(2,1)S(1)} %constant_dynamic-update-slice_fusion.table_ref), custom_call_target="tpu_custom_call" | custom-call | flops 536870912 | bytes 4456448 | tf_op jit(solution)/shard_map/pallas_call | solution.py:243
  12.2 0.6 %collective-permute-done.3.table_ref = bf16[128,1024]{1,0:T(8,128)(2,1)S(1)} collective-permute-done((bf16[128,1024]{1,0:T(8,128)(2,1)S(1)}, bf16[128,1024]{1,0:T(8,128)(2,1)S(1)}, u32[]{:S(2)}, u32[]{:S(2)}) %collective-permute-start.3) | collective-permute-done | bytes 262176 | tf_op jit(solution)/shard_map/ppermute | solution.py:17
  12.8 0.9 %shard_map.52 = (f32[128,2048]{1,0:T(8,128)S(1)}, f32[1,2048]{1,0:T(1,128)S(1)}, f32[1,2048]{1,0:T(1,128)S(1)}) custom-call(bf16[1024,2048]{1,0:T(8,128)(2,1)S(1)} %get-tuple-element.25.docs_ref, bf16[128,1024]{1,0:T(8,128)(2,1)S(1)} %collective-permute-done.3.table_ref, f32[1,2048]{1,0:T(1,128)S(1)} %get-tuple-element.27.first_top_ref.refs_7_, ...), custom_call_target="tpu_custom_call" | custom-call | flops 536870912 | bytes 4472832 | tf_op jit(solution)/shard_map/pallas_call | solution.py:243
  13.7 2.6 %collective-permute-start.6 = (f32[1,2048]{1,0:T(1,128)S(1)}, f32[1,2048]{1,0:T(1,128)S(1)}, u32[]{:S(2)}, u32[]{:S(2)}) collective-permute-start(f32[1,2048]{1,0:T(1,128)S(1)} %get-tuple-element.29.follow_ref), channel_id=1, source_target_pairs={{0,16},{8,24},{16,8},{24,0},{1,17},{9,25},{17,9},{25,1},{2,18},{10... | collective-permute-start | bytes 24584 | tf_op jit(solution)/shard_map/ppermute | solution.py:269
  16.4 1.2 %collective-permute-start.5 = (f32[1,2048]{1,0:T(1,128)S(1)}, f32[1,2048]{1,0:T(1,128)S(1)}, u32[]{:S(2)}, u32[]{:S(2)}) collective-permute-start(f32[1,2048]{1,0:T(1,128)S(1)} %get-tuple-element.29.follow_ref), channel_id=1, source_target_pairs={{0,24},{8,16},{16,0},{24,8},{1,25},{9,17},{17,1},{25,9},{2,26},{10... | collective-permute-start | bytes 24584 | tf_op jit(solution)/shard_map/ppermute | solution.py:269
  17.6 0.3 %collective-permute-start.4 = (f32[1,2048]{1,0:T(1,128)S(1)}, f32[1,2048]{1,0:T(1,128)S(1)}, u32[]{:S(2)}, u32[]{:S(2)}) collective-permute-start(f32[1,2048]{1,0:T(1,128)S(1)} %get-tuple-element.29.follow_ref), channel_id=1, source_target_pairs={{0,8},{8,0},{16,24},{24,16},{1,9},{9,1},{17,25},{25,17},{2,10},{10... | collective-permute-start | bytes 24584 | tf_op jit(solution)/shard_map/ppermute | solution.py:269
  17.9 2.2 %shard_map.53 = (bf16[2048,1024]{1,0:T(8,128)(2,1)S(1)}, f32[1,2048]{1,0:T(1,128)S(1)}) custom-call(bf16[2048,1024]{1,0:T(8,128)(2,1)} %source_ref.5, f32[1,2048]{1,0:T(1,128)S(1)} %get-tuple-element.29.follow_ref), custom_call_target="tpu_custom_call" | custom-call | bytes 8388608 | tf_op jit(solution)/shard_map/pallas_call | solution.py:82
  20.1 0.0 collective-permute-done.6.refs_2_
  20.2 0.8 %collective-permute-done.5.refs_1_ = f32[1,2048]{1,0:T(1,128)S(1)} collective-permute-done((f32[1,2048]{1,0:T(1,128)S(1)}, f32[1,2048]{1,0:T(1,128)S(1)}, u32[]{:S(2)}, u32[]{:S(2)}) %collective-permute-start.5) | collective-permute-done | bytes 8224 | tf_op jit(solution)/shard_map/ppermute | solution.py:269
  20.9 0.3 collective-permute-done.4.refs_0_
  21.2 1.0 %shard_map.54 = (f32[1,2048]{1,0:T(1,128)}, f32[1,2048]{1,0:T(1,128)S(1)}, bf16[160,1152]{1,0:T(8,128)(2,1)S(1)}) custom-call(s32[1]{0:T(128)} %bitcast.1.me_ref, f32[1,2048]{1,0:T(1,128)S(1)} %get-tuple-element.30.lse_ref, f32[1,2048]{1,0:T(1,128)S(1)} %collective-permute-done.4.refs_0_, f32[1,2048]{1,0:T(1,128)S(1)} %collective-permute-done.5.refs_1_, ...), custom_call_target="tpu_custom_call" | custom-call | flops 536870912 | bytes 6340612 | tf_op jit(solution)/shard_map/pallas_call | solution.py:243
  22.3 0.0 copy-start
  22.3 0.0 collective-permute-start.7
  22.3 0.8 %shard_map.55 = (f32[96,1024]{1,0:T(8,128)S(1)}, f32[96,128]{1,0:T(8,128)S(1)}) custom-call(f32[1,2048]{1,0:T(1,128)S(1)} %get-tuple-element.35.factor_ref, bf16[2048,1024]{1,0:T(8,128)(2,1)S(1)} %get-tuple-element.31.refs_3_.docs_ref, f32[128,2048]{1,0:T(8,128)S(1)} %get-tuple-element.34.refs_6_.part_ref), custom_call_target="tpu_custom_call" | custom-call | flops 536870912 | bytes 5251072 | tf_op jit(solution)/shard_map/pallas_call | solution.py:243
  23.1 0.9 %collective-permute-done.7.got_ref = bf16[160,1152]{1,0:T(8,128)(2,1)S(1)} collective-permute-done((bf16[160,1152]{1,0:T(8,128)(2,1)S(1)}, bf16[160,1152]{1,0:T(8,128)(2,1)S(1)}, u32[]{:S(2)}, u32[]{:S(2)}) %collective-permute-start.7) | collective-permute-done | bytes 368672 | tf_op jit(solution)/shard_map/ppermute | solution.py:17
  23.9 0.2 shard_map.56
  24.1 0.7 %collective-permute-start.8 = (bf16[64,1152]{1,0:T(8,128)(2,1)S(1)}, bf16[64,1152]{1,0:T(8,128)(2,1)S(1)}, u32[]{:S(2)}, u32[]{:S(2)}) collective-permute-start(bf16[64,1152]{1,0:T(8,128)(2,1)S(1)} %get-tuple-element.41), channel_id=1, source_target_pairs={{1,7},{3,5},{5,3},{7,1},{9,15},{11,13},{13,11},{15,9},{17,23},{19,... | collective-permute-start | bytes 442376 | tf_op jit(solution)/shard_map/ppermute | solution.py:294
  24.8 1.3 %collective-permute-start.10 = (bf16[32,1152]{1,0:T(8,128)(2,1)S(1)}, bf16[32,1152]{1,0:T(8,128)(2,1)S(1)}, u32[]{:S(2)}, u32[]{:S(2)}) collective-permute-start(bf16[32,1152]{1,0:T(8,128)(2,1)S(1)} %get-tuple-element.42), channel_id=1, source_target_pairs={{0,2},{1,3},{2,0},{3,1},{4,6},{5,7},{6,4},{7,5},{8,10},{9,11},{10,... | collective-permute-start | bytes 221192 | tf_op jit(solution)/shard_map/ppermute | solution.py:17
  26.1 1.5 %collective-permute-start.11 = (bf16[32,1152]{1,0:T(8,128)(2,1)S(1)}, bf16[32,1152]{1,0:T(8,128)(2,1)S(1)}, u32[]{:S(2)}, u32[]{:S(2)}) collective-permute-start(bf16[32,1152]{1,0:T(8,128)(2,1)S(1)} %get-tuple-element.43), channel_id=1, source_target_pairs={{0,4},{1,5},{2,6},{3,7},{4,0},{5,1},{6,2},{7,3},{8,12},{9,13},{10,... | collective-permute-start | bytes 221192 | tf_op jit(solution)/shard_map/ppermute | solution.py:17
  27.6 0.0 collective-permute-done.8.far_ref
  27.6 4.1 %collective-permute-start.9 = (bf16[32,1152]{1,0:T(8,128)(2,1)S(1)}, bf16[32,1152]{1,0:T(8,128)(2,1)S(1)}, u32[]{:S(2)}, u32[]{:S(2)}) collective-permute-start(bf16[32,1152]{1,0:T(8,128)(2,1)S(1)} %slice.4), channel_id=1, source_target_pairs={{0,1},{1,0},{2,3},{3,2},{4,5},{5,4},{6,7},{7,6},{8,9},{9,8},{10,11... | collective-permute-start | bytes 221192 | tf_op jit(solution)/shard_map/ppermute | solution.py:17
  31.7 0.0 collective-permute-done.10.refs_0_
  31.7 0.4 %collective-permute-done.11.refs_1_ = bf16[32,1152]{1,0:T(8,128)(2,1)S(1)} collective-permute-done((bf16[32,1152]{1,0:T(8,128)(2,1)S(1)}, bf16[32,1152]{1,0:T(8,128)(2,1)S(1)}, u32[]{:S(2)}, u32[]{:S(2)}) %collective-permute-start.11) | collective-permute-done | bytes 73760 | tf_op jit(solution)/shard_map/ppermute | solution.py:17
  32.1 0.5 %collective-permute-done.9.passed_ref = bf16[32,1152]{1,0:T(8,128)(2,1)S(1)} collective-permute-done((bf16[32,1152]{1,0:T(8,128)(2,1)S(1)}, bf16[32,1152]{1,0:T(8,128)(2,1)S(1)}, u32[]{:S(2)}, u32[]{:S(2)}) %collective-permute-start.9) | collective-permute-done | bytes 73760 | tf_op jit(solution)/shard_map/ppermute | solution.py:17
  32.6 0.0 copy-done
  32.6 0.8 %shard_map.57 = (f32[32,1024]{1,0:T(8,128)}, f32[1,32]{1,0:T(1,128)}) custom-call(s32[1]{0:T(128)} %bitcast.odd_ref, f32[32,1024]{1,0:T(8,128)S(1)} %get-tuple-element.39.own_ref, f32[32,128]{1,0:T(8,128)S(1)} %get-tuple-element.40.own_mass_ref, f32[32,1024]{1,0:T(8,128)S(1)} %copy-done, bf16[64,1152]{1,0:T(8,128)(2,1)S(1)} %collective-permute-done.8.far_ref, ...), custom_call_target="tpu_custom_call" | custom-call | bytes 647172 | tf_op jit(solution)/shard_map/pallas_call | solution.py:243
  (5 shorter events, 0.0 us)
Async XLA Ops:
  2.2 9.0 %collective-permute-start.2 = (bf16[32,1024]{1,0:T(8,128)(2,1)}, bf16[32,1024]{1,0:T(8,128)(2,1)S(1)}, u32[]{:S(2)}, u32[]{:S(2)}) collective-permute-start(bf16[32,1024]{1,0:T(8,128)(2,1)} %shard_map.49.follow_ref), channel_id=1, source_target_pairs={{0,6},{1,7},{2,4},{3,5},{4,2},{5,3},{6,0},{7,1},{8,14},{9,15},{10,... | collective-permute-start | bytes 196616 | tf_op jit(solution)/shard_map/ppermute | solution.py:17
  6.1 5.0 %collective-permute-start.1 = (bf16[32,1024]{1,0:T(8,128)(2,1)}, bf16[32,1024]{1,0:T(8,128)(2,1)S(1)}, u32[]{:S(2)}, u32[]{:S(2)}) collective-permute-start(bf16[32,1024]{1,0:T(8,128)(2,1)} %shard_map.49.follow_ref), channel_id=1, source_target_pairs={{0,4},{1,5},{2,6},{3,7},{4,0},{5,1},{6,2},{7,3},{8,12},{9,13},{10,... | collective-permute-start | bytes 196616 | tf_op jit(solution)/shard_map/ppermute | solution.py:17
  6.7 4.5 %collective-permute-start = (bf16[32,1024]{1,0:T(8,128)(2,1)}, bf16[32,1024]{1,0:T(8,128)(2,1)S(1)}, u32[]{:S(2)}, u32[]{:S(2)}) collective-permute-start(bf16[32,1024]{1,0:T(8,128)(2,1)} %shard_map.49.follow_ref), channel_id=1, source_target_pairs={{0,2},{1,3},{2,0},{3,1},{4,6},{5,7},{6,4},{7,5},{8,10},{9,11},{10,... | collective-permute-start | bytes 196616 | tf_op jit(solution)/shard_map/ppermute | solution.py:17
  6.8 0.9 %copy-start.1 = (bf16[32,1024]{1,0:T(8,128)(2,1)S(1)}, bf16[32,1024]{1,0:T(8,128)(2,1)}, u32[]{:S(2)}) copy-start(bf16[32,1024]{1,0:T(8,128)(2,1)} %shard_map.49.follow_ref) | copy-start | bytes 196612
  11.2 1.6 %collective-permute-start.3 = (bf16[128,1024]{1,0:T(8,128)(2,1)S(1)}, bf16[128,1024]{1,0:T(8,128)(2,1)S(1)}, u32[]{:S(2)}, u32[]{:S(2)}) collective-permute-start(bf16[128,1024]{1,0:T(8,128)(2,1)S(1)} %constant_dynamic-update-slice_fusion.table_ref), channel_id=1, source_target_pairs={{0,1},{1,0},{2,3},{3,2},{4,5},{5,4},{6,7},{7,6},{8,9},{9,8},{10,11... | collective-permute-start | bytes 786440 | tf_op jit(solution)/shard_map/ppermute | solution.py:17
  13.7 6.4 %collective-permute-start.6 = (f32[1,2048]{1,0:T(1,128)S(1)}, f32[1,2048]{1,0:T(1,128)S(1)}, u32[]{:S(2)}, u32[]{:S(2)}) collective-permute-start(f32[1,2048]{1,0:T(1,128)S(1)} %get-tuple-element.29.follow_ref), channel_id=1, source_target_pairs={{0,16},{8,24},{16,8},{24,0},{1,17},{9,25},{17,9},{25,1},{2,18},{10... | collective-permute-start | bytes 24584 | tf_op jit(solution)/shard_map/ppermute | solution.py:269
  16.4 4.5 %collective-permute-start.5 = (f32[1,2048]{1,0:T(1,128)S(1)}, f32[1,2048]{1,0:T(1,128)S(1)}, u32[]{:S(2)}, u32[]{:S(2)}) collective-permute-start(f32[1,2048]{1,0:T(1,128)S(1)} %get-tuple-element.29.follow_ref), channel_id=1, source_target_pairs={{0,24},{8,16},{16,0},{24,8},{1,25},{9,17},{17,1},{25,9},{2,26},{10... | collective-permute-start | bytes 24584 | tf_op jit(solution)/shard_map/ppermute | solution.py:269
  17.6 3.7 %collective-permute-start.4 = (f32[1,2048]{1,0:T(1,128)S(1)}, f32[1,2048]{1,0:T(1,128)S(1)}, u32[]{:S(2)}, u32[]{:S(2)}) collective-permute-start(f32[1,2048]{1,0:T(1,128)S(1)} %get-tuple-element.29.follow_ref), channel_id=1, source_target_pairs={{0,8},{8,0},{16,24},{24,16},{1,9},{9,1},{17,25},{25,17},{2,10},{10... | collective-permute-start | bytes 24584 | tf_op jit(solution)/shard_map/ppermute | solution.py:269
  22.3 10.4 %copy-start = (f32[32,1024]{1,0:T(8,128)S(1)}, f32[32,1024]{1,0:T(8,128)}, u32[]{:S(2)}) copy-start(f32[32,1024]{1,0:T(8,128)} %cent_ref.1) | copy-start | bytes 393220
  22.3 1.7 %collective-permute-start.7 = (bf16[160,1152]{1,0:T(8,128)(2,1)S(1)}, bf16[160,1152]{1,0:T(8,128)(2,1)S(1)}, u32[]{:S(2)}, u32[]{:S(2)}) collective-permute-start(bf16[160,1152]{1,0:T(8,128)(2,1)S(1)} %get-tuple-element.38.sent_ref), channel_id=1, source_target_pairs={{0,1},{1,0},{2,3},{3,2},{4,5},{5,4},{6,7},{7,6},{8,9},{9,8},{10,11... | collective-permute-start | bytes 1105928 | tf_op jit(solution)/shard_map/ppermute | solution.py:17
  24.1 3.5 %collective-permute-start.8 = (bf16[64,1152]{1,0:T(8,128)(2,1)S(1)}, bf16[64,1152]{1,0:T(8,128)(2,1)S(1)}, u32[]{:S(2)}, u32[]{:S(2)}) collective-permute-start(bf16[64,1152]{1,0:T(8,128)(2,1)S(1)} %get-tuple-element.41), channel_id=1, source_target_pairs={{1,7},{3,5},{5,3},{7,1},{9,15},{11,13},{13,11},{15,9},{17,23},{19,... | collective-permute-start | bytes 442376 | tf_op jit(solution)/shard_map/ppermute | solution.py:294
  24.8 6.9 %collective-permute-start.10 = (bf16[32,1152]{1,0:T(8,128)(2,1)S(1)}, bf16[32,1152]{1,0:T(8,128)(2,1)S(1)}, u32[]{:S(2)}, u32[]{:S(2)}) collective-permute-start(bf16[32,1152]{1,0:T(8,128)(2,1)S(1)} %get-tuple-element.42), channel_id=1, source_target_pairs={{0,2},{1,3},{2,0},{3,1},{4,6},{5,7},{6,4},{7,5},{8,10},{9,11},{10,... | collective-permute-start | bytes 221192 | tf_op jit(solution)/shard_map/ppermute | solution.py:17
  26.1 6.0 %collective-permute-start.11 = (bf16[32,1152]{1,0:T(8,128)(2,1)S(1)}, bf16[32,1152]{1,0:T(8,128)(2,1)S(1)}, u32[]{:S(2)}, u32[]{:S(2)}) collective-permute-start(bf16[32,1152]{1,0:T(8,128)(2,1)S(1)} %get-tuple-element.43), channel_id=1, source_target_pairs={{0,4},{1,5},{2,6},{3,7},{4,0},{5,1},{6,2},{7,3},{8,12},{9,13},{10,... | collective-permute-start | bytes 221192 | tf_op jit(solution)/shard_map/ppermute | solution.py:17
  27.6 5.0 %collective-permute-start.9 = (bf16[32,1152]{1,0:T(8,128)(2,1)S(1)}, bf16[32,1152]{1,0:T(8,128)(2,1)S(1)}, u32[]{:S(2)}, u32[]{:S(2)}) collective-permute-start(bf16[32,1152]{1,0:T(8,128)(2,1)S(1)} %slice.4), channel_id=1, source_target_pairs={{0,1},{1,0},{2,3},{3,2},{4,5},{5,4},{6,7},{7,6},{8,9},{9,8},{10,11... | collective-permute-start | bytes 221192 | tf_op jit(solution)/shard_map/ppermute | solution.py:17

commit v10 on v9

--- a/solution.py
+++ b/solution.py
@@ -31,23 +31,6 @@
     while len(parts) > 1:
         parts = [op(parts[i], parts[i + 1]) for i in range(0, len(parts), 2)]
     return parts[0]
-
-
-def round_kernel(source_ref, out_ref, landing, sem):
-    copy = pltpu.make_async_copy(source_ref, landing, sem)
-    copy.start()
-    copy.wait()
-    out_ref[...] = landing[...].astype(out_ref.dtype)
-
-
-def round_rows(x):
-    return pl.pallas_call(
-        round_kernel,
-        out_shape=shape(x.shape, jnp.bfloat16),
-        in_specs=[pl.BlockSpec(memory_space=pltpu.HBM)],
-        out_specs=VMEM,
-        scratch_shapes=[pltpu.VMEM(x.shape, x.dtype), pltpu.SemaphoreType.DMA],
-    )(pltpu.with_memory_space_constraint(x, pltpu.HBM))
 
 
 def transpose_kernel(chunk, source_ref, follow_ref, docs_ref, own_ref, landing, sems):
@@ -188,37 +171,50 @@
     keep_mass_ref[...] = jnp.broadcast_to(mass, keep_mass_ref.shape)
 
 
-def fold_kernel(keep_ref, keep_mass_ref, sent_ref, got_ref, own_ref, own_mass_ref, *send_refs):
+def scatter_masks(n, core):
+    near = list(range(2, n - 2, 2))
+    return [n - 2] + near if core else near + [0]
+
+
+def fold_kernel(
+    odd_ref, keep_ref, keep_mass_ref, sent_ref, got_ref, own_ref, own_mass_ref, *send_refs
+):
     rows, width = own_ref.shape
-    *near_refs, far_ref = send_refs
-    last = len(near_refs) + 1
+    odd = odd_ref[0] == 1
+    last = len(send_refs)
 
     def slot(ref, i):
         return read_rows(ref[i * rows:(i + 1) * rows], width)
 
+    def put(ref, here, term, mass):
+        ref[here, :width] = term.astype(jnp.bfloat16)
+        ref[here, width:] = mass_lanes(mass)
+
+    near = []
     for i in range(last):
         here = slice(i * rows, (i + 1) * rows)
         got, got_mass = slot(got_ref, i)
-        term = keep_ref[here] + got
-        mass = keep_mass_ref[here, :1] + got_mass
-        if i == 0:
-            own_ref[...] = term
-            own_mass_ref[...] = jnp.broadcast_to(mass, own_mass_ref.shape)
-        else:
-            near_refs[i - 1][:, :width] = term.astype(jnp.bfloat16)
-            near_refs[i - 1][:, width:] = mass_lanes(mass)
-    for i, (mine, theirs) in enumerate(((last + 1, last), (last, last + 1))):
-        here = slice(i * rows, (i + 1) * rows)
+        near.append((keep_ref[here] + got, keep_mass_ref[here, :1] + got_mass))
+    far = []
+    for mine, theirs in ((last + 1, last), (last, last + 1)):
         (a, a_mass), (b, b_mass) = slot(sent_ref, mine), slot(got_ref, theirs)
-        far_ref[here, :width] = (a + b).astype(jnp.bfloat16)
-        far_ref[here, width:] = mass_lanes(a_mass + b_mass)
-
-
-def final_kernel(odd_ref, own_ref, own_mass_ref, cent_ref, far_ref, passed_ref, *refs):
-    *near_refs, next_ref, mass_ref = refs
+        far.append((a + b, a_mass + b_mass))
+    (own_ref[...], own_mass), *near = near
+    own_mass_ref[...] = jnp.broadcast_to(own_mass, own_mass_ref.shape)
+    for i, ref in enumerate(send_refs):
+        on_odd = near[i - 1] if i else far[0]
+        on_even = near[min(i, len(near) - 1)]
+        picked = [jnp.where(odd, x, y) for x, y in zip(on_odd, on_even)]
+        put(ref, slice(0, rows), *picked)
+    put(send_refs[0], slice(rows, 2 * rows), *far[1])
+
+
+def final_kernel(odd_ref, own_ref, own_mass_ref, cent_ref, passed_ref, *refs):
+    *got_refs, next_ref, mass_ref = refs
     rows, width = own_ref.shape
-    far = jnp.where(odd_ref[0] == 1, far_ref[:rows], passed_ref[...])
-    got = [read_rows(x, width) for x in [r[...] for r in near_refs] + [far]]
+    got = [r[:rows] for r in got_refs]
+    got[-1] = jnp.where(odd_ref[0] == 1, got[-1], passed_ref[...])
+    got = [read_rows(x, width) for x in got]
     term = tree([own_ref[...]] + [a for a, _ in got], jnp.add)
     mass = tree([own_mass_ref[:, :1]] + [b for _, b in got], jnp.add)
     next_ref[...] = (term + cent_ref[...]) / (mass + 1.0)
@@ -254,7 +250,7 @@
 
         flops = 2 * half * count * width
         stats = [shape((half, count)), shape((1, count)), shape((1, count))]
-        rounded = round_rows(centroids)
+        rounded = centroids.astype(jnp.bfloat16)
         blocks = [swap(rounded, "dev", n, m) for m in range(2, n, 2)]
         docs_t, own = load(docs, rounded, chunk)
         mine = jnp.concatenate([own] + blocks, axis=0)
@@ -284,20 +280,23 @@
             factor, docs, part,
             scratch=[pltpu.VMEM((kept, count), jnp.bfloat16)], flops=flops,
         )
-        own, own_mass, *sends, far = call(
+        odd = (lax.axis_index("dev") % 2).reshape(1)
+        own, own_mass, *sends = call(
             fold_kernel,
-            [shape((rows, width)), shape((rows, LANES))]
-            + [shape((rows, width + LANES), jnp.bfloat16)] * (n // 2 - 2)
-            + [shape((2 * rows, width + LANES), jnp.bfloat16)],
-            keep, keep_mass, send, got,
-        )
-        far = lax.ppermute(far, "dev", [(i, i ^ (n - 2)) for i in range(1, n, 2)])
-        passed = swap(far[rows:], "dev", n, 1)
-        arrived = [swap(x, "dev", n, 2 * (j + 1)) for j, x in enumerate(sends)]
+            [shape((rows, width)), shape((rows, LANES)),
+             shape((2 * rows, width + LANES), jnp.bfloat16)]
+            + [shape((rows, width + LANES), jnp.bfloat16)] * (n // 2 - 2),
+            odd, keep, keep_mass, send, got,
+        )
+        masks = list(zip(scatter_masks(n, 0), scatter_masks(n, 1)))
+        arrived = [
+            lax.ppermute(x, "dev", [(i, i ^ pair[i % 2]) for i in range(n)])
+            for x, pair in zip(sends, masks)
+        ]
+        passed = swap(arrived[0][rows:], "dev", n, 1)
         result, mass = call(
             final_kernel, [shape((rows, width)), shape((1, rows))],
-            (lax.axis_index("dev") % 2).reshape(1),
-            own, own_mass, centroids, far, passed, *arrived,
+            odd, own, own_mass, centroids, passed, *arrived,
         )
         return (result, mass.reshape(rows), doc_lse.reshape(count))
 

time: 33.7 us -> 35.2 us (1.045)
  starting transfers between devices: 16.4 us -> 11.9 us
  waiting for transfers between devices: 4.21 us -> 7.7 us
  local copies, waits for them, and re-layouts: 0.91 us -> 4.16 us
  Pallas kernels: 11.1 us -> 9.59 us
  other arithmetic: 0 us -> 0.92 us
    ppermute x8 -> x6, starting transfers between devices: 11.6 us -> 4.91 us  [swap(): return lax.ppermute(x, axis, [(i, i ^ mask) for i in range(size)])]
    ppermute x1 -> x3, waiting for transfers between devices: 0.01 us -> 3.58 us  [body(): lax.ppermute(x, 'dev', [(i, i ^ pair[i % 2]) for i in range(n)])]
    unnamed x7 -> x9, local copies, waits for them, and re-layouts: 0.89 us -> 4.15 us
    ppermute x1 -> x3, starting transfers between devices: 0.67 us -> 2.77 us  [body(): lax.ppermute(x, 'dev', [(i, i ^ pair[i % 2]) for i in range(n)])]
    pallas_call x1 -> x0, Pallas kernels: 1.55 us -> none  [round_rows(): pl.pallas_call(round_kernel, out_shape=shape(x.shape, jnp.bfloat16), in_s...]
    convert_element_type x0 -> x1, other arithmetic: none -> 0.92 us  [body(): rounded = centroids.astype(jnp.bfloat16)]
    ppermute x8 -> x6, waiting for transfers between devices: 3.12 us -> 3.02 us  [swap(): return lax.ppermute(x, axis, [(i, i ^ mask) for i in range(size)])]
  transfers between devices with their start and end apart: 12 -> 12, of which waited for: 7 -> 6; matrix products, arithmetic and copies ran while one was open for 0% -> 0% of each run, Pallas kernels for 20% -> 19%
where the time goes in v10:
time: 35.2 us; the launch traced here: 35 us
  starting transfers between devices  11.9 us (34%)
  Pallas kernels  9.59 us (27%)
  waiting for transfers between devices  7.7 us (22%)
  local copies, waits for them, and re-layouts  4.16 us (12%)
  other arithmetic  0.92 us (3%)
  between operations  0.74 us (2%)
    pallas_call x2, Pallas kernels, load(): pl.pallas_call(kernel, out_shape=[shape(dims, source.dtype), shape(follow...  4.93 us
    ppermute x6, starting transfers between devices, swap(): return lax.ppermute(x, axis, [(i, i ^ mask) for i in range(size)])  4.91 us
    pallas_call x6, Pallas kernels, call(): pl.pallas_call(kernel, out_shape=outs, in_specs=[SMEM if x.dtype == jnp.i...  4.66 us
    ppermute x3, starting transfers between devices, body(): others = [lax.ppermute(lse, 'cgrp', pairs) for pairs in plan]  4.21 us
    unnamed x9, local copies, waits for them, and re-layouts  4.15 us
    ppermute x3, waiting for transfers between devices, body(): lax.ppermute(x, 'dev', [(i, i ^ pair[i % 2]) for i in range(n)])  3.58 us
    ppermute x6, waiting for transfers between devices, swap(): return lax.ppermute(x, axis, [(i, i ^ mask) for i in range(size)])  3.02 us
    ppermute x3, starting transfers between devices, body(): lax.ppermute(x, 'dev', [(i, i ^ pair[i % 2]) for i in range(n)])  2.77 us
  transfers between devices with their start and end apart: 12, of which 6 were waited for; matrix products, arithmetic and copies ran while one was open for 0% of the time, Pallas kernels for 19%

profile of v10, /device:TPU:0, one launch (start us, length us, event | category | flops | bytes accessed | tf_op | source)
XLA Modules:
  0.0 35.0 jit_solution(5120719900747768381)
XLA Ops:
  0.6 0.9 %convert_element_type.3.follow_ref = bf16[32,1024]{1,0:T(8,128)(2,1)S(1)} convert(f32[32,1024]{1,0:T(8,128)} %cent_ref.1) | non-fusion elementwise | flops 32768 | bytes 196608 | tf_op jit(solution)/shard_map/convert_element_type | solution.py:253
  1.5 4.0 %collective-permute-start.2 = (bf16[32,1024]{1,0:T(8,128)(2,1)S(1)}, bf16[32,1024]{1,0:T(8,128)(2,1)S(1)}, u32[]{:S(2)}, u32[]{:S(2)}) collective-permute-start(bf16[32,1024]{1,0:T(8,128)(2,1)S(1)} %convert_element_type.3.follow_ref), channel_id=1, source_target_pairs={{0,6},{1,7},{2,4},{3,5},{4,2},{5,3},{6,0},{7,1},{8,14},{9,15},{10,... | collective-permute-start | bytes 196616 | tf_op jit(solution)/shard_map/ppermute | solution.py:17
  5.5 0.5 %collective-permute-start.1 = (bf16[32,1024]{1,0:T(8,128)(2,1)S(1)}, bf16[32,1024]{1,0:T(8,128)(2,1)S(1)}, u32[]{:S(2)}, u32[]{:S(2)}) collective-permute-start(bf16[32,1024]{1,0:T(8,128)(2,1)S(1)} %convert_element_type.3.follow_ref), channel_id=1, source_target_pairs={{0,4},{1,5},{2,6},{3,7},{4,0},{5,1},{6,2},{7,3},{8,12},{9,13},{10,... | collective-permute-start | bytes 196616 | tf_op jit(solution)/shard_map/ppermute | solution.py:17
  6.0 0.1 collective-permute-start
  6.1 2.7 %shard_map.49 = (bf16[1024,2048]{1,0:T(8,128)(2,1)S(1)}, bf16[32,1024]{1,0:T(8,128)(2,1)S(1)}) custom-call(bf16[2048,1024]{1,0:T(8,128)(2,1)} %source_ref.3, bf16[32,1024]{1,0:T(8,128)(2,1)S(1)} %convert_element_type.3.follow_ref), custom_call_target="tpu_custom_call" | custom-call | bytes 8388608 | tf_op jit(solution)/shard_map/pallas_call | solution.py:65
  8.9 1.4 %collective-permute-done = bf16[32,1024]{1,0:T(8,128)(2,1)S(1)} collective-permute-done((bf16[32,1024]{1,0:T(8,128)(2,1)S(1)}, bf16[32,1024]{1,0:T(8,128)(2,1)S(1)}, u32[]{:S(2)}, u32[]{:S(2)}) %collective-permute-start) | collective-permute-done | bytes 65568 | tf_op jit(solution)/shard_map/ppermute | solution.py:17
  10.3 0.0 collective-permute-done.1
  10.3 0.0 collective-permute-done.2
  10.3 0.1 collective-permute-start.3
  10.4 0.9 %shard_map.50 = (f32[128,2048]{1,0:T(8,128)S(1)}, f32[1,2048]{1,0:T(1,128)S(1)}, f32[1,2048]{1,0:T(1,128)S(1)}) custom-call(bf16[1024,2048]{1,0:T(8,128)(2,1)S(1)} %get-tuple-element.25.docs_ref, bf16[128,1024]{1,0:T(8,128)(2,1)S(1)} %constant_dynamic-update-slice_fusion.table_ref), custom_call_target="tpu_custom_call" | custom-call | flops 536870912 | bytes 4456448 | tf_op jit(solution)/shard_map/pallas_call | solution.py:239
  11.3 0.6 %collective-permute-done.3.table_ref = bf16[128,1024]{1,0:T(8,128)(2,1)S(1)} collective-permute-done((bf16[128,1024]{1,0:T(8,128)(2,1)S(1)}, bf16[128,1024]{1,0:T(8,128)(2,1)S(1)}, u32[]{:S(2)}, u32[]{:S(2)}) %collective-permute-start.3) | collective-permute-done | bytes 262176 | tf_op jit(solution)/shard_map/ppermute | solution.py:17
  11.9 0.9 %shard_map.51 = (f32[128,2048]{1,0:T(8,128)S(1)}, f32[1,2048]{1,0:T(1,128)S(1)}, f32[1,2048]{1,0:T(1,128)S(1)}) custom-call(bf16[1024,2048]{1,0:T(8,128)(2,1)S(1)} %get-tuple-element.25.docs_ref, bf16[128,1024]{1,0:T(8,128)(2,1)S(1)} %collective-permute-done.3.table_ref, f32[1,2048]{1,0:T(1,128)S(1)} %get-tuple-element.27.first_top_ref.refs_7_, ...), custom_call_target="tpu_custom_call" | custom-call | flops 536870912 | bytes 4472832 | tf_op jit(solution)/shard_map/pallas_call | solution.py:239
  12.9 2.6 %collective-permute-start.6 = (f32[1,2048]{1,0:T(1,128)S(1)}, f32[1,2048]{1,0:T(1,128)S(1)}, u32[]{:S(2)}, u32[]{:S(2)}) collective-permute-start(f32[1,2048]{1,0:T(1,128)S(1)} %get-tuple-element.29.follow_ref), channel_id=1, source_target_pairs={{0,16},{8,24},{16,8},{24,0},{1,17},{9,25},{17,9},{25,1},{2,18},{10... | collective-permute-start | bytes 24584 | tf_op jit(solution)/shard_map/ppermute | solution.py:265
  15.5 1.2 %collective-permute-start.5 = (f32[1,2048]{1,0:T(1,128)S(1)}, f32[1,2048]{1,0:T(1,128)S(1)}, u32[]{:S(2)}, u32[]{:S(2)}) collective-permute-start(f32[1,2048]{1,0:T(1,128)S(1)} %get-tuple-element.29.follow_ref), channel_id=1, source_target_pairs={{0,24},{8,16},{16,0},{24,8},{1,25},{9,17},{17,1},{25,9},{2,26},{10... | collective-permute-start | bytes 24584 | tf_op jit(solution)/shard_map/ppermute | solution.py:265
  16.7 0.3 collective-permute-start.4
  17.1 2.2 %shard_map.52 = (bf16[2048,1024]{1,0:T(8,128)(2,1)S(1)}, f32[1,2048]{1,0:T(1,128)S(1)}) custom-call(bf16[2048,1024]{1,0:T(8,128)(2,1)} %source_ref.3, f32[1,2048]{1,0:T(1,128)S(1)} %get-tuple-element.29.follow_ref), custom_call_target="tpu_custom_call" | custom-call | bytes 8388608 | tf_op jit(solution)/shard_map/pallas_call | solution.py:65
  19.3 0.0 collective-permute-done.6.refs_2_
  19.3 0.8 %collective-permute-done.5.refs_1_ = f32[1,2048]{1,0:T(1,128)S(1)} collective-permute-done((f32[1,2048]{1,0:T(1,128)S(1)}, f32[1,2048]{1,0:T(1,128)S(1)}, u32[]{:S(2)}, u32[]{:S(2)}) %collective-permute-start.5) | collective-permute-done | bytes 8224 | tf_op jit(solution)/shard_map/ppermute | solution.py:265
  20.1 0.3 collective-permute-done.4.refs_0_
  20.4 0.0 copy-start.2
  20.4 1.0 %shard_map.53 = (f32[1,2048]{1,0:T(1,128)}, f32[1,2048]{1,0:T(1,128)S(1)}, bf16[160,1152]{1,0:T(8,128)(2,1)S(1)}) custom-call(s32[1]{0:T(128)} %bitcast.1.me_ref, f32[1,2048]{1,0:T(1,128)S(1)} %get-tuple-element.30.lse_ref, f32[1,2048]{1,0:T(1,128)S(1)} %collective-permute-done.4.refs_0_, f32[1,2048]{1,0:T(1,128)S(1)} %collective-permute-done.5.refs_1_, ...), custom_call_target="tpu_custom_call" | custom-call | flops 536870912 | bytes 6340612 | tf_op jit(solution)/shard_map/pallas_call | solution.py:239
  21.4 0.0 copy-start
  21.4 1.9 %copy-done = bf16[2048,1024]{1,0:T(8,128)(2,1)} copy-done((bf16[2048,1024]{1,0:T(8,128)(2,1)}, bf16[2048,1024]{1,0:T(8,128)(2,1)S(1)}, u32[]{:S(2)}) %copy-start) | copy-done | bytes 4194328
  23.3 0.0 collective-permute-start.7
  23.3 0.0 copy-start.1
  23.3 2.2 %copy-done.1 = bf16[2048,1024]{1,0:T(8,128)(2,1)S(1)} copy-done((bf16[2048,1024]{1,0:T(8,128)(2,1)S(1)}, bf16[2048,1024]{1,0:T(8,128)(2,1)}, u32[]{:S(2)}) %copy-start.1) | copy-done | bytes 4194328
  25.5 0.8 %shard_map.54 = (f32[96,1024]{1,0:T(8,128)S(1)}, f32[96,128]{1,0:T(8,128)S(1)}) custom-call(f32[1,2048]{1,0:T(1,128)S(1)} %get-tuple-element.35.factor_ref, bf16[2048,1024]{1,0:T(8,128)(2,1)S(1)} %copy-done.1, f32[128,2048]{1,0:T(8,128)S(1)} %get-tuple-element.34.refs_6_.part_ref), custom_call_target="tpu_custom_call" | custom-call | flops 536870912 | bytes 5251072 | tf_op jit(solution)/shard_map/pallas_call | solution.py:239
  26.3 0.0 collective-permute-done.7.got_ref
  26.3 0.2 shard_map.55
  26.5 0.6 %collective-permute-start.8 = (bf16[64,1152]{1,0:T(8,128)(2,1)S(1)}, bf16[64,1152]{1,0:T(8,128)(2,1)S(1)}, u32[]{:S(2)}, u32[]{:S(2)}) collective-permute-start(bf16[64,1152]{1,0:T(8,128)(2,1)S(1)} %get-tuple-element.41), channel_id=1, source_target_pairs={{0,2},{1,7},{2,0},{3,5},{4,6},{5,3},{6,4},{7,1},{8,10},{9,15},{10,... | collective-permute-start | bytes 442376 | tf_op jit(solution)/shard_map/ppermute | solution.py:293
  27.1 1.5 %collective-permute-start.10 = (bf16[32,1152]{1,0:T(8,128)(2,1)S(1)}, bf16[32,1152]{1,0:T(8,128)(2,1)S(1)}, u32[]{:S(2)}, u32[]{:S(2)}) collective-permute-start(bf16[32,1152]{1,0:T(8,128)(2,1)S(1)} %get-tuple-element.42), channel_id=1, source_target_pairs={{0,4},{1,3},{2,6},{3,1},{4,0},{5,7},{6,2},{7,5},{8,12},{9,11},{10,... | collective-permute-start | bytes 221192 | tf_op jit(solution)/shard_map/ppermute | solution.py:293
  28.7 0.7 %collective-permute-start.11 = (bf16[32,1152]{1,0:T(8,128)(2,1)S(1)}, bf16[32,1152]{1,0:T(8,128)(2,1)S(1)}, u32[]{:S(2)}, u32[]{:S(2)}) collective-permute-start(bf16[32,1152]{1,0:T(8,128)(2,1)S(1)} %get-tuple-element.43), channel_id=1, source_target_pairs={{0,0},{1,5},{2,2},{3,7},{4,4},{5,1},{6,6},{7,3},{8,8},{9,13},{10,1... | collective-permute-start | bytes 221192 | tf_op jit(solution)/shard_map/ppermute | solution.py:293
  29.3 3.6 %collective-permute-done.8.refs_0_ = bf16[64,1152]{1,0:T(8,128)(2,1)S(1)} collective-permute-done((bf16[64,1152]{1,0:T(8,128)(2,1)S(1)}, bf16[64,1152]{1,0:T(8,128)(2,1)S(1)}, u32[]{:S(2)}, u32[]{:S(2)}) %collective-permute-start.8) | collective-permute-done | bytes 147488 | tf_op jit(solution)/shard_map/ppermute | solution.py:293
  32.9 0.2 collective-permute-start.9
  33.1 0.0 collective-permute-done.10.refs_1_
  33.1 0.0 collective-permute-done.11.refs_2_
  33.1 1.0 %collective-permute-done.9.passed_ref = bf16[32,1152]{1,0:T(8,128)(2,1)S(1)} collective-permute-done((bf16[32,1152]{1,0:T(8,128)(2,1)S(1)}, bf16[32,1152]{1,0:T(8,128)(2,1)S(1)}, u32[]{:S(2)}, u32[]{:S(2)}) %collective-permute-start.9) | collective-permute-done | bytes 73760 | tf_op jit(solution)/shard_map/ppermute | solution.py:17
  34.2 0.0 copy-done.2
  34.2 0.8 %shard_map.56 = (f32[32,1024]{1,0:T(8,128)}, f32[1,32]{1,0:T(1,128)}) custom-call(s32[1]{0:T(128)} %bitcast.odd_ref, f32[32,1024]{1,0:T(8,128)S(1)} %get-tuple-element.39.own_ref, f32[32,128]{1,0:T(8,128)S(1)} %get-tuple-element.40.own_mass_ref, f32[32,1024]{1,0:T(8,128)S(1)} %copy-done.2, bf16[32,1152]{1,0:T(8,128)(2,1)S(1)} %collective-permute-done.9.passed_ref, ...), custom_call_target="tpu_custom_call" | custom-call | bytes 647172 | tf_op jit(solution)/shard_map/pallas_call | solution.py:239
  (5 shorter events, 0.0 us)
Async XLA Ops:
  1.5 8.8 %collective-permute-start.2 = (bf16[32,1024]{1,0:T(8,128)(2,1)S(1)}, bf16[32,1024]{1,0:T(8,128)(2,1)S(1)}, u32[]{:S(2)}, u32[]{:S(2)}) collective-permute-start(bf16[32,1024]{1,0:T(8,128)(2,1)S(1)} %convert_element_type.3.follow_ref), channel_id=1, source_target_pairs={{0,6},{1,7},{2,4},{3,5},{4,2},{5,3},{6,0},{7,1},{8,14},{9,15},{10,... | collective-permute-start | bytes 196616 | tf_op jit(solution)/shard_map/ppermute | solution.py:17
  5.5 4.8 %collective-permute-start.1 = (bf16[32,1024]{1,0:T(8,128)(2,1)S(1)}, bf16[32,1024]{1,0:T(8,128)(2,1)S(1)}, u32[]{:S(2)}, u32[]{:S(2)}) collective-permute-start(bf16[32,1024]{1,0:T(8,128)(2,1)S(1)} %convert_element_type.3.follow_ref), channel_id=1, source_target_pairs={{0,4},{1,5},{2,6},{3,7},{4,0},{5,1},{6,2},{7,3},{8,12},{9,13},{10,... | collective-permute-start | bytes 196616 | tf_op jit(solution)/shard_map/ppermute | solution.py:17
  6.0 4.3 %collective-permute-start = (bf16[32,1024]{1,0:T(8,128)(2,1)S(1)}, bf16[32,1024]{1,0:T(8,128)(2,1)S(1)}, u32[]{:S(2)}, u32[]{:S(2)}) collective-permute-start(bf16[32,1024]{1,0:T(8,128)(2,1)S(1)} %convert_element_type.3.follow_ref), channel_id=1, source_target_pairs={{0,2},{1,3},{2,0},{3,1},{4,6},{5,7},{6,4},{7,5},{8,10},{9,11},{10,... | collective-permute-start | bytes 196616 | tf_op jit(solution)/shard_map/ppermute | solution.py:17
  10.3 1.6 %collective-permute-start.3 = (bf16[128,1024]{1,0:T(8,128)(2,1)S(1)}, bf16[128,1024]{1,0:T(8,128)(2,1)S(1)}, u32[]{:S(2)}, u32[]{:S(2)}) collective-permute-start(bf16[128,1024]{1,0:T(8,128)(2,1)S(1)} %constant_dynamic-update-slice_fusion.table_ref), channel_id=1, source_target_pairs={{0,1},{1,0},{2,3},{3,2},{4,5},{5,4},{6,7},{7,6},{8,9},{9,8},{10,11... | collective-permute-start | bytes 786440 | tf_op jit(solution)/shard_map/ppermute | solution.py:17
  12.9 6.4 %collective-permute-start.6 = (f32[1,2048]{1,0:T(1,128)S(1)}, f32[1,2048]{1,0:T(1,128)S(1)}, u32[]{:S(2)}, u32[]{:S(2)}) collective-permute-start(f32[1,2048]{1,0:T(1,128)S(1)} %get-tuple-element.29.follow_ref), channel_id=1, source_target_pairs={{0,16},{8,24},{16,8},{24,0},{1,17},{9,25},{17,9},{25,1},{2,18},{10... | collective-permute-start | bytes 24584 | tf_op jit(solution)/shard_map/ppermute | solution.py:265
  15.5 4.5 %collective-permute-start.5 = (f32[1,2048]{1,0:T(1,128)S(1)}, f32[1,2048]{1,0:T(1,128)S(1)}, u32[]{:S(2)}, u32[]{:S(2)}) collective-permute-start(f32[1,2048]{1,0:T(1,128)S(1)} %get-tuple-element.29.follow_ref), channel_id=1, source_target_pairs={{0,24},{8,16},{16,0},{24,8},{1,25},{9,17},{17,1},{25,9},{2,26},{10... | collective-permute-start | bytes 24584 | tf_op jit(solution)/shard_map/ppermute | solution.py:265
  16.7 3.7 %collective-permute-start.4 = (f32[1,2048]{1,0:T(1,128)S(1)}, f32[1,2048]{1,0:T(1,128)S(1)}, u32[]{:S(2)}, u32[]{:S(2)}) collective-permute-start(f32[1,2048]{1,0:T(1,128)S(1)} %get-tuple-element.29.follow_ref), channel_id=1, source_target_pairs={{0,8},{8,0},{16,24},{24,16},{1,9},{9,1},{17,25},{25,17},{2,10},{10... | collective-permute-start | bytes 24584 | tf_op jit(solution)/shard_map/ppermute | solution.py:265
  20.4 13.8 %copy-start.2 = (f32[32,1024]{1,0:T(8,128)S(1)}, f32[32,1024]{1,0:T(8,128)}, u32[]{:S(2)}) copy-start(f32[32,1024]{1,0:T(8,128)} %cent_ref.1) | copy-start | bytes 393220
  21.4 1.9 %copy-start = (bf16[2048,1024]{1,0:T(8,128)(2,1)}, bf16[2048,1024]{1,0:T(8,128)(2,1)S(1)}, u32[]{:S(2)}) copy-start(bf16[2048,1024]{1,0:T(8,128)(2,1)S(1)} %get-tuple-element.31.refs_3_.docs_ref) | copy-start | bytes 12582916
  23.3 3.0 %collective-permute-start.7 = (bf16[160,1152]{1,0:T(8,128)(2,1)S(1)}, bf16[160,1152]{1,0:T(8,128)(2,1)S(1)}, u32[]{:S(2)}, u32[]{:S(2)}) collective-permute-start(bf16[160,1152]{1,0:T(8,128)(2,1)S(1)} %get-tuple-element.38.sent_ref), channel_id=1, source_target_pairs={{0,1},{1,0},{2,3},{3,2},{4,5},{5,4},{6,7},{7,6},{8,9},{9,8},{10,11... | collective-permute-start | bytes 1105928 | tf_op jit(solution)/shard_map/ppermute | solution.py:17
  23.3 2.2 %copy-start.1 = (bf16[2048,1024]{1,0:T(8,128)(2,1)S(1)}, bf16[2048,1024]{1,0:T(8,128)(2,1)}, u32[]{:S(2)}) copy-start(bf16[2048,1024]{1,0:T(8,128)(2,1)} %copy-done) | copy-start | bytes 12582916
  26.5 6.4 %collective-permute-start.8 = (bf16[64,1152]{1,0:T(8,128)(2,1)S(1)}, bf16[64,1152]{1,0:T(8,128)(2,1)S(1)}, u32[]{:S(2)}, u32[]{:S(2)}) collective-permute-start(bf16[64,1152]{1,0:T(8,128)(2,1)S(1)} %get-tuple-element.41), channel_id=1, source_target_pairs={{0,2},{1,7},{2,0},{3,5},{4,6},{5,3},{6,4},{7,1},{8,10},{9,15},{10,... | collective-permute-start | bytes 442376 | tf_op jit(solution)/shard_map/ppermute | solution.py:293
  27.1 6.0 %collective-permute-start.10 = (bf16[32,1152]{1,0:T(8,128)(2,1)S(1)}, bf16[32,1152]{1,0:T(8,128)(2,1)S(1)}, u32[]{:S(2)}, u32[]{:S(2)}) collective-permute-start(bf16[32,1152]{1,0:T(8,128)(2,1)S(1)} %get-tuple-element.42), channel_id=1, source_target_pairs={{0,4},{1,3},{2,6},{3,1},{4,0},{5,7},{6,2},{7,5},{8,12},{9,11},{10,... | collective-permute-start | bytes 221192 | tf_op jit(solution)/shard_map/ppermute | solution.py:293
  28.7 4.5 %collective-permute-start.11 = (bf16[32,1152]{1,0:T(8,128)(2,1)S(1)}, bf16[32,1152]{1,0:T(8,128)(2,1)S(1)}, u32[]{:S(2)}, u32[]{:S(2)}) collective-permute-start(bf16[32,1152]{1,0:T(8,128)(2,1)S(1)} %get-tuple-element.43), channel_id=1, source_target_pairs={{0,0},{1,5},{2,2},{3,7},{4,4},{5,1},{6,6},{7,3},{8,8},{9,13},{10,1... | collective-permute-start | bytes 221192 | tf_op jit(solution)/shard_map/ppermute | solution.py:293
  32.9 1.3 %collective-permute-start.9 = (bf16[32,1152]{1,0:T(8,128)(2,1)S(1)}, bf16[32,1152]{1,0:T(8,128)(2,1)S(1)}, u32[]{:S(2)}, u32[]{:S(2)}) collective-permute-start(bf16[32,1152]{1,0:T(8,128)(2,1)S(1)} %slice.4), channel_id=1, source_target_pairs={{0,1},{1,0},{2,3},{3,2},{4,5},{5,4},{6,7},{7,6},{8,9},{9,8},{10,11... | collective-permute-start | bytes 221192 | tf_op jit(solution)/shard_map/ppermute | solution.py:17

commit v11 on v8

--- a/solution.py
+++ b/solution.py
@@ -20,9 +20,9 @@
 def group_plan(g):
     if g == 4:
         return [
-            [(0, 1), (1, 0), (2, 3), (3, 2)],
-            [(0, 3), (1, 2), (2, 0), (3, 1)],
-            [(0, 2), (1, 3), (2, 1), (3, 0)],
+            [(0, 2), (1, 0), (2, 3), (3, 1)],
+            [(0, 3), (1, 2), (2, 1), (3, 0)],
+            [(0, 1), (1, 3), (2, 0), (3, 2)],
         ]
     return [[(i, i ^ m) for i in range(g)] for m in range(1, g)]
 
@@ -83,9 +83,17 @@
     table = table_ref[...]
     wide = table.astype(jnp.float32)
     half_norms = 0.5 * jnp.sum(wide * wide, axis=1, keepdims=True)
+
+    def product(start):
+        cols = slice(start, start + chunk)
+        return jnp.dot(table, docs_ref[:, cols], preferred_element_type=jnp.float32)
+
+    ahead = product(0)
     for start in range(0, count, chunk):
+        dots = ahead
+        if start + chunk < count:
+            ahead = product(start + chunk)
         cols = slice(start, start + chunk)
-        dots = jnp.dot(table, docs_ref[:, cols], preferred_element_type=jnp.float32)
         scores = (dots - half_norms) * scale
         top = jnp.max(scores, axis=0, keepdims=True)
         part = jnp.exp(scores - top)
@@ -104,7 +112,7 @@
     lse_ref[...] = top + jnp.log(total)
 
 
-def weighted_sums(chunk, factor, docs_ref, part_ref, resp_ref, store):
+def responsibilities(chunk, factor, part_ref, resp_ref):
     rows, count = part_ref.shape
     mass = jnp.zeros((rows, 1), jnp.float32)
     for start in range(0, count, chunk):
@@ -112,10 +120,14 @@
         resp = part_ref[:, cols] * factor[:, cols]
         mass += jnp.sum(resp, axis=1, keepdims=True)
         resp_ref[:, cols] = resp.astype(jnp.bfloat16)
-    for start in range(0, docs_ref.shape[1], chunk):
-        cols = slice(start, start + chunk)
-        store(cols, jnp.dot(resp_ref[...], docs_ref[:, cols], preferred_element_type=jnp.float32))
     return mass
+
+
+def weighted_sums(chunk, resp_ref, docs_ref, first, out_ref, width):
+    for start in range(0, width, chunk):
+        cols = slice(first + start, first + start + chunk)
+        term = jnp.dot(resp_ref[...], docs_ref[:, cols], preferred_element_type=jnp.float32)
+        out_ref[:, start:start + chunk] = term.astype(out_ref.dtype)
 
 
 def mass_lanes(mass):
@@ -144,28 +156,29 @@
     doc_lse = best + jnp.log(tree([jnp.exp(x - best) for x in parts], jnp.add))
     doc_lse_ref[...] = doc_lse
     factor_ref[...] = jnp.exp(keep_top_ref[...] - doc_lse)
-    factor = jnp.exp(top_ref[...] - doc_lse)
-
-    def store(cols, term):
-        send_ref[:, cols] = term.astype(jnp.bfloat16)
-
-    mass = weighted_sums(chunk, factor, docs_ref, part_ref, resp_ref, store)
-    send_ref[:, docs_ref.shape[1]:] = mass_lanes(mass)
+    mass = responsibilities(chunk, jnp.exp(top_ref[...] - doc_lse), part_ref, resp_ref)
+    first = send_ref.shape[1] - LANES
+    weighted_sums(chunk, resp_ref, docs_ref, 0, send_ref, first)
+    send_ref[:, first:] = mass_lanes(mass)
+
+
+def send_rest_kernel(chunk, resp_ref, docs_ref, send_ref):
+    rest = send_ref.shape[1]
+    weighted_sums(chunk, resp_ref, docs_ref, docs_ref.shape[1] - rest, send_ref, rest)
 
 
 def keep_kernel(chunk, factor_ref, docs_ref, part_ref, keep_ref, keep_mass_ref, resp_ref):
-    def store(cols, term):
-        keep_ref[:, cols] = term
-
-    mass = weighted_sums(chunk, factor_ref[...], docs_ref, part_ref, resp_ref, store)
+    mass = responsibilities(chunk, factor_ref[...], part_ref, resp_ref)
+    weighted_sums(chunk, resp_ref, docs_ref, 0, keep_ref, docs_ref.shape[1])
     keep_mass_ref[...] = jnp.broadcast_to(mass, keep_mass_ref.shape)
 
 
-def fold_kernel(keep_ref, keep_mass_ref, got_ref, own_ref, own_mass_ref, *send_refs):
+def fold_kernel(keep_ref, keep_mass_ref, got_ref, rest_ref, own_ref, own_mass_ref, *send_refs):
     rows, width = own_ref.shape
     for slot in range(keep_ref.shape[0] // rows):
         here = slice(slot * rows, (slot + 1) * rows)
-        got, got_mass = read_rows(got_ref[here], width)
+        got, got_mass = read_rows(got_ref[here], got_ref.shape[1] - LANES)
+        got = jnp.concatenate([got, rest_ref[here].astype(jnp.float32)], axis=1)
         term = keep_ref[here] + got
         mass = keep_mass_ref[here, :1] + got_mass
         if slot == 0:
@@ -215,7 +228,6 @@
 
         flops = 2 * half * count * width
         stats = [shape((half, count)), shape((1, count)), shape((1, count))]
-        resp = [pltpu.VMEM((half, count), jnp.bfloat16)]
         rounded = centroids.astype(jnp.bfloat16)
         blocks = [swap(rounded, "dev", n, m) for m in range(2, n, 2)]
         docs_t, own = load(docs, rounded, chunk)
@@ -230,23 +242,30 @@
         )
         others = [lax.ppermute(lse, "cgrp", pairs) for pairs in plan]
         docs, lse = load(docs, lse)
-        doc_lse, factor, send = call(
+        first = width // 2
+        doc_lse, factor, send, resp = call(
             functools.partial(send_kernel, g, plan, chunk),
-            [shape((1, count)), shape((1, count)), shape((half, width + LANES), jnp.bfloat16)],
+            [shape((1, count)), shape((1, count)),
+             shape((half, first + LANES), jnp.bfloat16), shape((half, count), jnp.bfloat16)],
             lax.axis_index("cgrp").reshape(1), lse, *others, docs, other_part, other_top, top,
-            scratch=resp, flops=flops,
+            flops=flops // 2,
         )
         got = swap(send, "dev", n, 1)
+        rest, = call(
+            functools.partial(send_rest_kernel, chunk),
+            [shape((half, width - first), jnp.bfloat16)], resp, docs, flops=flops // 2,
+        )
+        rest = swap(rest, "dev", n, 1)
         keep, keep_mass = call(
             functools.partial(keep_kernel, chunk),
-            [shape((half, width)), shape((half, LANES))],
-            factor, docs, part, scratch=resp, flops=flops,
+            [shape((half, width)), shape((half, LANES))], factor, docs, part,
+            scratch=[pltpu.VMEM((half, count), jnp.bfloat16)], flops=flops,
         )
         own, own_mass, *sends = call(
             fold_kernel,
             [shape((rows, width)), shape((rows, LANES))]
             + [shape((rows, width + LANES), jnp.bfloat16)] * (n // 2 - 1),
-            keep, keep_mass, got,
+            keep, keep_mass, got, rest,
         )
         far_first = sorted(range(1, n // 2), key=lambda j: (-j.bit_count(), j))
         arrived = [swap(sends[j - 1], "dev", n, 2 * j) for j in far_first]

time: 31.4 us -> 32.2 us (1.025)
  starting transfers between devices: 12.5 us -> 14.5 us
  waiting for transfers between devices: 7.7 us -> 6.05 us
  Pallas kernels: 9.36 us -> 9.8 us
    ppermute x3, starting transfers between devices: 4.21 us -> 5.67 us  [body(): others = [lax.ppermute(lse, 'cgrp', pairs) for pairs in plan]]
    ppermute x3, waiting for transfers between devices: 1.1 us -> 0.01 us  [body(): others = [lax.ppermute(lse, 'cgrp', pairs) for pairs in plan]]
    ppermute x8 -> x9, waiting for transfers between devices: 6.6 us -> 6.04 us  [swap(): return lax.ppermute(x, axis, [(i, i ^ mask) for i in range(size)])]
    ppermute x8 -> x9, starting transfers between devices: 8.29 us -> 8.81 us  [swap(): return lax.ppermute(x, axis, [(i, i ^ mask) for i in range(size)])]
    pallas_call x6 -> x7, Pallas kernels: 4.43 us -> 4.87 us  [call(): pl.pallas_call(kernel, out_shape=outs, in_specs=[SMEM if x.dtype == jnp.i...]
  transfers between devices with their start and end apart: 11 -> 12, of which waited for: 8 -> 6; matrix products, arithmetic and copies ran while one was open for 0% -> 0% of each run, Pallas kernels for 21% -> 22%
where the time goes in v11:
time: 32.2 us; the launch traced here: 32 us
  starting transfers between devices  14.5 us (45%)
  Pallas kernels  9.8 us (30%)
  waiting for transfers between devices  6.05 us (19%)
  other arithmetic  0.92 us (3%)
  between operations  0.76 us (2%)
    ppermute x9, starting transfers between devices, swap(): return lax.ppermute(x, axis, [(i, i ^ mask) for i in range(size)])  8.81 us
    ppermute x9, waiting for transfers between devices, swap(): return lax.ppermute(x, axis, [(i, i ^ mask) for i in range(size)])  6.04 us
    ppermute x3, starting transfers between devices, body(): others = [lax.ppermute(lse, 'cgrp', pairs) for pairs in plan]  5.67 us
    pallas_call x2, Pallas kernels, load(): pl.pallas_call(kernel, out_shape=[shape(dims, source.dtype), shape(follow...  4.93 us
    pallas_call x7, Pallas kernels, call(): pl.pallas_call(kernel, out_shape=outs, in_specs=[SMEM if x.dtype == jnp.i...  4.87 us
    convert_element_type x1, other arithmetic, body(): rounded = centroids.astype(jnp.bfloat16)  0.92 us
  transfers between devices with their start and end apart: 12, of which 6 were waited for; matrix products, arithmetic and copies ran while one was open for 0% of the time, Pallas kernels for 22%

profile of v11, /device:TPU:0, one launch (start us, length us, event | category | flops | bytes accessed | tf_op | source)
XLA Modules:
  0.0 32.0 jit_solution(785960061579487225)
XLA Ops:
  0.6 0.9 %convert_element_type.3.follow_ref = bf16[32,1024]{1,0:T(8,128)(2,1)S(1)} convert(f32[32,1024]{1,0:T(8,128)} %cent_ref.1) | non-fusion elementwise | flops 32768 | bytes 196608 | tf_op jit(solution)/shard_map/convert_element_type | solution.py:231
  1.5 4.0 %collective-permute-start.2 = (bf16[32,1024]{1,0:T(8,128)(2,1)S(1)}, bf16[32,1024]{1,0:T(8,128)(2,1)S(1)}, u32[]{:S(2)}, u32[]{:S(2)}) collective-permute-start(bf16[32,1024]{1,0:T(8,128)(2,1)S(1)} %convert_element_type.3.follow_ref), channel_id=1, source_target_pairs={{0,6},{1,7},{2,4},{3,5},{4,2},{5,3},{6,0},{7,1},{8,14},{9,15},{10,... | collective-permute-start | bytes 196616 | tf_op jit(solution)/shard_map/ppermute | solution.py:17
  5.5 0.5 %collective-permute-start.1 = (bf16[32,1024]{1,0:T(8,128)(2,1)S(1)}, bf16[32,1024]{1,0:T(8,128)(2,1)S(1)}, u32[]{:S(2)}, u32[]{:S(2)}) collective-permute-start(bf16[32,1024]{1,0:T(8,128)(2,1)S(1)} %convert_element_type.3.follow_ref), channel_id=1, source_target_pairs={{0,4},{1,5},{2,6},{3,7},{4,0},{5,1},{6,2},{7,3},{8,12},{9,13},{10,... | collective-permute-start | bytes 196616 | tf_op jit(solution)/shard_map/ppermute | solution.py:17
  6.0 0.1 collective-permute-start
  6.1 2.7 %shard_map.49 = (bf16[1024,2048]{1,0:T(8,128)(2,1)S(1)}, bf16[32,1024]{1,0:T(8,128)(2,1)S(1)}) custom-call(bf16[2048,1024]{1,0:T(8,128)(2,1)} %source_ref.3, bf16[32,1024]{1,0:T(8,128)(2,1)S(1)} %convert_element_type.3.follow_ref), custom_call_target="tpu_custom_call" | custom-call | bytes 8388608 | tf_op jit(solution)/shard_map/pallas_call | solution.py:65
  8.9 1.4 %collective-permute-done = bf16[32,1024]{1,0:T(8,128)(2,1)S(1)} collective-permute-done((bf16[32,1024]{1,0:T(8,128)(2,1)S(1)}, bf16[32,1024]{1,0:T(8,128)(2,1)S(1)}, u32[]{:S(2)}, u32[]{:S(2)}) %collective-permute-start) | collective-permute-done | bytes 65568 | tf_op jit(solution)/shard_map/ppermute | solution.py:17
  10.3 0.0 collective-permute-done.1
  10.3 0.0 collective-permute-done.2
  10.3 0.1 collective-permute-start.3
  10.4 0.9 %shard_map.50 = (f32[128,2048]{1,0:T(8,128)S(1)}, f32[1,2048]{1,0:T(1,128)S(1)}, f32[1,2048]{1,0:T(1,128)S(1)}) custom-call(bf16[1024,2048]{1,0:T(8,128)(2,1)S(1)} %get-tuple-element.26.docs_ref, bf16[128,1024]{1,0:T(8,128)(2,1)S(1)} %constant_dynamic-update-slice_fusion.table_ref), custom_call_target="tpu_custom_call" | custom-call | flops 536870912 | bytes 4456448 | tf_op jit(solution)/shard_map/pallas_call | solution.py:217
  11.3 0.6 %collective-permute-done.3.table_ref = bf16[128,1024]{1,0:T(8,128)(2,1)S(1)} collective-permute-done((bf16[128,1024]{1,0:T(8,128)(2,1)S(1)}, bf16[128,1024]{1,0:T(8,128)(2,1)S(1)}, u32[]{:S(2)}, u32[]{:S(2)}) %collective-permute-start.3) | collective-permute-done | bytes 262176 | tf_op jit(solution)/shard_map/ppermute | solution.py:17
  11.9 0.9 %shard_map.51 = (f32[128,2048]{1,0:T(8,128)S(1)}, f32[1,2048]{1,0:T(1,128)S(1)}, f32[1,2048]{1,0:T(1,128)S(1)}) custom-call(bf16[1024,2048]{1,0:T(8,128)(2,1)S(1)} %get-tuple-element.26.docs_ref, bf16[128,1024]{1,0:T(8,128)(2,1)S(1)} %collective-permute-done.3.table_ref, f32[1,2048]{1,0:T(1,128)S(1)} %get-tuple-element.28.first_top_ref.refs_6_, ...), custom_call_target="tpu_custom_call" | custom-call | flops 536870912 | bytes 4472832 | tf_op jit(solution)/shard_map/pallas_call | solution.py:217
  12.9 1.6 %collective-permute-start.6 = (f32[1,2048]{1,0:T(1,128)S(1)}, f32[1,2048]{1,0:T(1,128)S(1)}, u32[]{:S(2)}, u32[]{:S(2)}) collective-permute-start(f32[1,2048]{1,0:T(1,128)S(1)} %get-tuple-element.30.follow_ref), channel_id=1, source_target_pairs={{0,8},{8,24},{16,0},{24,16},{1,9},{9,25},{17,1},{25,17},{2,10},{10... | collective-permute-start | bytes 24584 | tf_op jit(solution)/shard_map/ppermute | solution.py:243
  14.5 2.5 %collective-permute-start.5 = (f32[1,2048]{1,0:T(1,128)S(1)}, f32[1,2048]{1,0:T(1,128)S(1)}, u32[]{:S(2)}, u32[]{:S(2)}) collective-permute-start(f32[1,2048]{1,0:T(1,128)S(1)} %get-tuple-element.30.follow_ref), channel_id=1, source_target_pairs={{0,24},{8,16},{16,8},{24,0},{1,25},{9,17},{17,9},{25,1},{2,26},{10... | collective-permute-start | bytes 24584 | tf_op jit(solution)/shard_map/ppermute | solution.py:243
  17.0 1.6 %collective-permute-start.4 = (f32[1,2048]{1,0:T(1,128)S(1)}, f32[1,2048]{1,0:T(1,128)S(1)}, u32[]{:S(2)}, u32[]{:S(2)}) collective-permute-start(f32[1,2048]{1,0:T(1,128)S(1)} %get-tuple-element.30.follow_ref), channel_id=1, source_target_pairs={{0,16},{8,0},{16,24},{24,8},{1,17},{9,1},{17,25},{25,9},{2,18},{10... | collective-permute-start | bytes 24584 | tf_op jit(solution)/shard_map/ppermute | solution.py:243
  18.5 2.2 %shard_map.52 = (bf16[2048,1024]{1,0:T(8,128)(2,1)S(1)}, f32[1,2048]{1,0:T(1,128)S(1)}) custom-call(bf16[2048,1024]{1,0:T(8,128)(2,1)} %source_ref.3, f32[1,2048]{1,0:T(1,128)S(1)} %get-tuple-element.30.follow_ref), custom_call_target="tpu_custom_call" | custom-call | bytes 8388608 | tf_op jit(solution)/shard_map/pallas_call | solution.py:65
  20.7 0.0 collective-permute-done.6.refs_2_
  20.8 0.0 collective-permute-done.5.refs_1_
  20.8 0.0 collective-permute-done.4.refs_0_
  20.8 0.8 %shard_map.53 = (f32[1,2048]{1,0:T(1,128)}, f32[1,2048]{1,0:T(1,128)S(1)}, bf16[128,640]{1,0:T(8,128)(2,1)S(1)}, bf16[128,2048]{1,0:T(8,128)(2,1)S(1)}) custom-call(s32[1]{0:T(128)} %bitcast.me_ref, f32[1,2048]{1,0:T(1,128)S(1)} %get-tuple-element.31.lse_ref, f32[1,2048]{1,0:T(1,128)S(1)} %collective-permute-done.4.refs_0_, ...), custom_call_target="tpu_custom_call" | custom-call | flops 268435456 | bytes 5292036 | tf_op jit(solution)/shard_map/pallas_call | solution.py:217
  21.6 0.0 collective-permute-start.7
  21.6 0.5 %shard_map.55 = bf16[128,512]{1,0:T(8,128)(2,1)S(1)} custom-call(bf16[128,2048]{1,0:T(8,128)(2,1)S(1)} %get-tuple-element.40.resp_ref, bf16[2048,1024]{1,0:T(8,128)(2,1)S(1)} %get-tuple-element.32.refs_3_.docs_ref), custom_call_target="tpu_custom_call" | custom-call | flops 268435456 | bytes 4718592 | tf_op jit(solution)/shard_map/pallas_call | solution.py:217
  22.0 0.0 copy-start
  22.1 0.6 %collective-permute-start.8 = (bf16[128,512]{1,0:T(8,128)(2,1)S(1)}, bf16[128,512]{1,0:T(8,128)(2,1)S(1)}, u32[]{:S(2)}, u32[]{:S(2)}) collective-permute-start(bf16[128,512]{1,0:T(8,128)(2,1)S(1)} %shard_map.55), channel_id=1, source_target_pairs={{0,1},{1,0},{2,3},{3,2},{4,5},{5,4},{6,7},{7,6},{8,9},{9,8},{10,11... | collective-permute-start | bytes 393224 | tf_op jit(solution)/shard_map/ppermute | solution.py:17
  22.6 0.8 %shard_map.54 = (f32[128,1024]{1,0:T(8,128)S(1)}, f32[128,128]{1,0:T(8,128)S(1)}) custom-call(f32[1,2048]{1,0:T(1,128)S(1)} %get-tuple-element.35.factor_ref, bf16[2048,1024]{1,0:T(8,128)(2,1)S(1)} %get-tuple-element.32.refs_3_.docs_ref, f32[128,2048]{1,0:T(8,128)S(1)} %get-tuple-element.36.part_ref), custom_call_target="tpu_custom_call" | custom-call | flops 536870912 | bytes 5251072 | tf_op jit(solution)/shard_map/pallas_call | solution.py:217
  23.4 0.2 collective-permute-done.8.rest_ref
  23.6 0.0 collective-permute-done.7.got_ref
  23.6 0.2 shard_map.56
  23.8 1.6 %collective-permute-start.9 = (bf16[32,1152]{1,0:T(8,128)(2,1)S(1)}, bf16[32,1152]{1,0:T(8,128)(2,1)S(1)}, u32[]{:S(2)}, u32[]{:S(2)}) collective-permute-start(bf16[32,1152]{1,0:T(8,128)(2,1)S(1)} %get-tuple-element.43), channel_id=1, source_target_pairs={{0,6},{1,7},{2,4},{3,5},{4,2},{5,3},{6,0},{7,1},{8,14},{9,15},{10,... | collective-permute-start | bytes 221192 | tf_op jit(solution)/shard_map/ppermute | solution.py:17
  25.4 1.5 %collective-permute-start.10 = (bf16[32,1152]{1,0:T(8,128)(2,1)S(1)}, bf16[32,1152]{1,0:T(8,128)(2,1)S(1)}, u32[]{:S(2)}, u32[]{:S(2)}) collective-permute-start(bf16[32,1152]{1,0:T(8,128)(2,1)S(1)} %get-tuple-element.44), channel_id=1, source_target_pairs={{0,2},{1,3},{2,0},{3,1},{4,6},{5,7},{6,4},{7,5},{8,10},{9,11},{10,... | collective-permute-start | bytes 221192 | tf_op jit(solution)/shard_map/ppermute | solution.py:17
  26.8 0.5 %collective-permute-start.11 = (bf16[32,1152]{1,0:T(8,128)(2,1)S(1)}, bf16[32,1152]{1,0:T(8,128)(2,1)S(1)}, u32[]{:S(2)}, u32[]{:S(2)}) collective-permute-start(bf16[32,1152]{1,0:T(8,128)(2,1)S(1)} %get-tuple-element.45), channel_id=1, source_target_pairs={{0,4},{1,5},{2,6},{3,7},{4,0},{5,1},{6,2},{7,3},{8,12},{9,13},{10,... | collective-permute-start | bytes 221192 | tf_op jit(solution)/shard_map/ppermute | solution.py:17
  27.4 2.5 %collective-permute-done.9.refs_0_ = bf16[32,1152]{1,0:T(8,128)(2,1)S(1)} collective-permute-done((bf16[32,1152]{1,0:T(8,128)(2,1)S(1)}, bf16[32,1152]{1,0:T(8,128)(2,1)S(1)}, u32[]{:S(2)}, u32[]{:S(2)}) %collective-permute-start.9) | collective-permute-done | bytes 73760 | tf_op jit(solution)/shard_map/ppermute | solution.py:17
  29.9 1.1 %collective-permute-done.10.refs_1_ = bf16[32,1152]{1,0:T(8,128)(2,1)S(1)} collective-permute-done((bf16[32,1152]{1,0:T(8,128)(2,1)S(1)}, bf16[32,1152]{1,0:T(8,128)(2,1)S(1)}, u32[]{:S(2)}, u32[]{:S(2)}) %collective-permute-start.10) | collective-permute-done | bytes 73760 | tf_op jit(solution)/shard_map/ppermute | solution.py:17
  30.9 0.3 collective-permute-done.11.refs_2_
  31.2 0.0 copy-done
  31.2 0.8 %shard_map.57 = (f32[32,1024]{1,0:T(8,128)}, f32[1,32]{1,0:T(1,128)}) custom-call(f32[32,1024]{1,0:T(8,128)S(1)} %get-tuple-element.41.own_ref, f32[32,128]{1,0:T(8,128)S(1)} %get-tuple-element.42.own_mass_ref, f32[32,1024]{1,0:T(8,128)S(1)} %copy-done, bf16[32,1152]{1,0:T(8,128)(2,1)S(1)} %collective-permute-done.9.refs_0_, ...), custom_call_target="tpu_custom_call" | custom-call | bytes 499712 | tf_op jit(solution)/shard_map/pallas_call | solution.py:217
  (4 shorter events, 0.0 us)
Async XLA Ops:
  1.5 8.8 %collective-permute-start.2 = (bf16[32,1024]{1,0:T(8,128)(2,1)S(1)}, bf16[32,1024]{1,0:T(8,128)(2,1)S(1)}, u32[]{:S(2)}, u32[]{:S(2)}) collective-permute-start(bf16[32,1024]{1,0:T(8,128)(2,1)S(1)} %convert_element_type.3.follow_ref), channel_id=1, source_target_pairs={{0,6},{1,7},{2,4},{3,5},{4,2},{5,3},{6,0},{7,1},{8,14},{9,15},{10,... | collective-permute-start | bytes 196616 | tf_op jit(solution)/shard_map/ppermute | solution.py:17
  5.5 4.8 %collective-permute-start.1 = (bf16[32,1024]{1,0:T(8,128)(2,1)S(1)}, bf16[32,1024]{1,0:T(8,128)(2,1)S(1)}, u32[]{:S(2)}, u32[]{:S(2)}) collective-permute-start(bf16[32,1024]{1,0:T(8,128)(2,1)S(1)} %convert_element_type.3.follow_ref), channel_id=1, source_target_pairs={{0,4},{1,5},{2,6},{3,7},{4,0},{5,1},{6,2},{7,3},{8,12},{9,13},{10,... | collective-permute-start | bytes 196616 | tf_op jit(solution)/shard_map/ppermute | solution.py:17
  6.0 4.3 %collective-permute-start = (bf16[32,1024]{1,0:T(8,128)(2,1)S(1)}, bf16[32,1024]{1,0:T(8,128)(2,1)S(1)}, u32[]{:S(2)}, u32[]{:S(2)}) collective-permute-start(bf16[32,1024]{1,0:T(8,128)(2,1)S(1)} %convert_element_type.3.follow_ref), channel_id=1, source_target_pairs={{0,2},{1,3},{2,0},{3,1},{4,6},{5,7},{6,4},{7,5},{8,10},{9,11},{10,... | collective-permute-start | bytes 196616 | tf_op jit(solution)/shard_map/ppermute | solution.py:17
  10.3 1.6 %collective-permute-start.3 = (bf16[128,1024]{1,0:T(8,128)(2,1)S(1)}, bf16[128,1024]{1,0:T(8,128)(2,1)S(1)}, u32[]{:S(2)}, u32[]{:S(2)}) collective-permute-start(bf16[128,1024]{1,0:T(8,128)(2,1)S(1)} %constant_dynamic-update-slice_fusion.table_ref), channel_id=1, source_target_pairs={{0,1},{1,0},{2,3},{3,2},{4,5},{5,4},{6,7},{7,6},{8,9},{9,8},{10,11... | collective-permute-start | bytes 786440 | tf_op jit(solution)/shard_map/ppermute | solution.py:17
  12.9 7.9 %collective-permute-start.6 = (f32[1,2048]{1,0:T(1,128)S(1)}, f32[1,2048]{1,0:T(1,128)S(1)}, u32[]{:S(2)}, u32[]{:S(2)}) collective-permute-start(f32[1,2048]{1,0:T(1,128)S(1)} %get-tuple-element.30.follow_ref), channel_id=1, source_target_pairs={{0,8},{8,24},{16,0},{24,16},{1,9},{9,25},{17,1},{25,17},{2,10},{10... | collective-permute-start | bytes 24584 | tf_op jit(solution)/shard_map/ppermute | solution.py:243
  14.5 6.3 %collective-permute-start.5 = (f32[1,2048]{1,0:T(1,128)S(1)}, f32[1,2048]{1,0:T(1,128)S(1)}, u32[]{:S(2)}, u32[]{:S(2)}) collective-permute-start(f32[1,2048]{1,0:T(1,128)S(1)} %get-tuple-element.30.follow_ref), channel_id=1, source_target_pairs={{0,24},{8,16},{16,8},{24,0},{1,25},{9,17},{17,9},{25,1},{2,26},{10... | collective-permute-start | bytes 24584 | tf_op jit(solution)/shard_map/ppermute | solution.py:243
  17.0 3.8 %collective-permute-start.4 = (f32[1,2048]{1,0:T(1,128)S(1)}, f32[1,2048]{1,0:T(1,128)S(1)}, u32[]{:S(2)}, u32[]{:S(2)}) collective-permute-start(f32[1,2048]{1,0:T(1,128)S(1)} %get-tuple-element.30.follow_ref), channel_id=1, source_target_pairs={{0,16},{8,0},{16,24},{24,8},{1,17},{9,1},{17,25},{25,9},{2,18},{10... | collective-permute-start | bytes 24584 | tf_op jit(solution)/shard_map/ppermute | solution.py:243
  21.6 2.0 %collective-permute-start.7 = (bf16[128,640]{1,0:T(8,128)(2,1)S(1)}, bf16[128,640]{1,0:T(8,128)(2,1)S(1)}, u32[]{:S(2)}, u32[]{:S(2)}) collective-permute-start(bf16[128,640]{1,0:T(8,128)(2,1)S(1)} %get-tuple-element.39), channel_id=1, source_target_pairs={{0,1},{1,0},{2,3},{3,2},{4,5},{5,4},{6,7},{7,6},{8,9},{9,8},{10,11... | collective-permute-start | bytes 491528 | tf_op jit(solution)/shard_map/ppermute | solution.py:17
  22.0 9.2 %copy-start = (f32[32,1024]{1,0:T(8,128)S(1)}, f32[32,1024]{1,0:T(8,128)}, u32[]{:S(2)}) copy-start(f32[32,1024]{1,0:T(8,128)} %cent_ref.1) | copy-start | bytes 393220
  22.1 1.6 %collective-permute-start.8 = (bf16[128,512]{1,0:T(8,128)(2,1)S(1)}, bf16[128,512]{1,0:T(8,128)(2,1)S(1)}, u32[]{:S(2)}, u32[]{:S(2)}) collective-permute-start(bf16[128,512]{1,0:T(8,128)(2,1)S(1)} %shard_map.55), channel_id=1, source_target_pairs={{0,1},{1,0},{2,3},{3,2},{4,5},{5,4},{6,7},{7,6},{8,9},{9,8},{10,11... | collective-permute-start | bytes 393224 | tf_op jit(solution)/shard_map/ppermute | solution.py:17
  23.8 6.1 %collective-permute-start.9 = (bf16[32,1152]{1,0:T(8,128)(2,1)S(1)}, bf16[32,1152]{1,0:T(8,128)(2,1)S(1)}, u32[]{:S(2)}, u32[]{:S(2)}) collective-permute-start(bf16[32,1152]{1,0:T(8,128)(2,1)S(1)} %get-tuple-element.43), channel_id=1, source_target_pairs={{0,6},{1,7},{2,4},{3,5},{4,2},{5,3},{6,0},{7,1},{8,14},{9,15},{10,... | collective-permute-start | bytes 221192 | tf_op jit(solution)/shard_map/ppermute | solution.py:17
  25.4 5.6 %collective-permute-start.10 = (bf16[32,1152]{1,0:T(8,128)(2,1)S(1)}, bf16[32,1152]{1,0:T(8,128)(2,1)S(1)}, u32[]{:S(2)}, u32[]{:S(2)}) collective-permute-start(bf16[32,1152]{1,0:T(8,128)(2,1)S(1)} %get-tuple-element.44), channel_id=1, source_target_pairs={{0,2},{1,3},{2,0},{3,1},{4,6},{5,7},{6,4},{7,5},{8,10},{9,11},{10,... | collective-permute-start | bytes 221192 | tf_op jit(solution)/shard_map/ppermute | solution.py:17
  26.8 4.4 %collective-permute-start.11 = (bf16[32,1152]{1,0:T(8,128)(2,1)S(1)}, bf16[32,1152]{1,0:T(8,128)(2,1)S(1)}, u32[]{:S(2)}, u32[]{:S(2)}) collective-permute-start(bf16[32,1152]{1,0:T(8,128)(2,1)S(1)} %get-tuple-element.45), channel_id=1, source_target_pairs={{0,4},{1,5},{2,6},{3,7},{4,0},{5,1},{6,2},{7,3},{8,12},{9,13},{10,... | collective-permute-start | bytes 221192 | tf_op jit(solution)/shard_map/ppermute | solution.py:17

commit v12 on v8

--- a/solution.py
+++ b/solution.py
@@ -217,7 +217,7 @@
         stats = [shape((half, count)), shape((1, count)), shape((1, count))]
         resp = [pltpu.VMEM((half, count), jnp.bfloat16)]
         rounded = centroids.astype(jnp.bfloat16)
-        blocks = [swap(rounded, "dev", n, m) for m in range(2, n, 2)]
+        blocks = [swap(rounded, "dev", n, m + 1) for m in range(2, n, 2)]
         docs_t, own = load(docs, rounded, chunk)
         mine = jnp.concatenate([own] + blocks, axis=0)
         theirs = swap(mine, "dev", n, 1)
@@ -249,7 +249,7 @@
             keep, keep_mass, got,
         )
         far_first = sorted(range(1, n // 2), key=lambda j: (-j.bit_count(), j))
-        arrived = [swap(sends[j - 1], "dev", n, 2 * j) for j in far_first]
+        arrived = [swap(sends[j - 1], "dev", n, 2 * j + 1) for j in far_first]
         result, mass = call(
             final_kernel, [shape((rows, width)), shape((1, rows))],
             own, own_mass, centroids, *arrived,

time: 31.4 us -> 30.9 us (0.984)
  starting transfers between devices: 12.5 us -> 11.8 us
    ppermute x8, starting transfers between devices: 8.29 us -> 7.6 us  [swap(): return lax.ppermute(x, axis, [(i, i ^ mask) for i in range(size)])]
  transfers between devices with their start and end apart: 11 -> 11, of which waited for: 8 -> 8; matrix products, arithmetic and copies ran while one was open for 0% -> 0% of each run, Pallas kernels for 21% -> 22%
where the time goes in v12:
time: 30.9 us; the launch traced here: 30.7 us
  starting transfers between devices  11.8 us (38%)
  Pallas kernels  9.35 us (30%)
  waiting for transfers between devices  7.87 us (25%)
  other arithmetic  0.92 us (3%)
  between operations  0.74 us (2%)
    ppermute x8, starting transfers between devices, swap(): return lax.ppermute(x, axis, [(i, i ^ mask) for i in range(size)])  7.6 us
    ppermute x8, waiting for transfers between devices, swap(): return lax.ppermute(x, axis, [(i, i ^ mask) for i in range(size)])  6.78 us
    pallas_call x2, Pallas kernels, load(): pl.pallas_call(kernel, out_shape=[shape(dims, source.dtype), shape(follow...  4.93 us
    pallas_call x6, Pallas kernels, call(): pl.pallas_call(kernel, out_shape=outs, in_specs=[SMEM if x.dtype == jnp.i...  4.42 us
    ppermute x3, starting transfers between devices, body(): others = [lax.ppermute(lse, 'cgrp', pairs) for pairs in plan]  4.22 us
    ppermute x3, waiting for transfers between devices, body(): others = [lax.ppermute(lse, 'cgrp', pairs) for pairs in plan]  1.09 us
    convert_element_type x1, other arithmetic, body(): rounded = centroids.astype(jnp.bfloat16)  0.92 us
  transfers between devices with their start and end apart: 11, of which 8 were waited for; matrix products, arithmetic and copies ran while one was open for 0% of the time, Pallas kernels for 22%

profile of v12, /device:TPU:0, one launch (start us, length us, event | category | flops | bytes accessed | tf_op | source)
XLA Modules:
  0.0 30.7 jit_solution(13183425706879279914)
XLA Ops:
  0.6 0.9 %convert_element_type.3.follow_ref = bf16[32,1024]{1,0:T(8,128)(2,1)S(1)} convert(f32[32,1024]{1,0:T(8,128)} %cent_ref.1) | non-fusion elementwise | flops 32768 | bytes 196608 | tf_op jit(solution)/shard_map/convert_element_type | solution.py:219
  1.5 3.4 %collective-permute-start.2 = (bf16[32,1024]{1,0:T(8,128)(2,1)S(1)}, bf16[32,1024]{1,0:T(8,128)(2,1)S(1)}, u32[]{:S(2)}, u32[]{:S(2)}) collective-permute-start(bf16[32,1024]{1,0:T(8,128)(2,1)S(1)} %convert_element_type.3.follow_ref), channel_id=1, source_target_pairs={{0,7},{1,6},{2,5},{3,4},{4,3},{5,2},{6,1},{7,0},{8,15},{9,14},{10,... | collective-permute-start | bytes 196616 | tf_op jit(solution)/shard_map/ppermute | solution.py:17
  4.9 0.8 %collective-permute-start.1 = (bf16[32,1024]{1,0:T(8,128)(2,1)S(1)}, bf16[32,1024]{1,0:T(8,128)(2,1)S(1)}, u32[]{:S(2)}, u32[]{:S(2)}) collective-permute-start(bf16[32,1024]{1,0:T(8,128)(2,1)S(1)} %convert_element_type.3.follow_ref), channel_id=1, source_target_pairs={{0,5},{1,4},{2,7},{3,6},{4,1},{5,0},{6,3},{7,2},{8,13},{9,12},{10,... | collective-permute-start | bytes 196616 | tf_op jit(solution)/shard_map/ppermute | solution.py:17
  5.7 0.1 collective-permute-start
  5.9 2.7 %shard_map.49 = (bf16[1024,2048]{1,0:T(8,128)(2,1)S(1)}, bf16[32,1024]{1,0:T(8,128)(2,1)S(1)}) custom-call(bf16[2048,1024]{1,0:T(8,128)(2,1)} %source_ref.3, bf16[32,1024]{1,0:T(8,128)(2,1)S(1)} %convert_element_type.3.follow_ref), custom_call_target="tpu_custom_call" | custom-call | bytes 8388608 | tf_op jit(solution)/shard_map/pallas_call | solution.py:65
  8.6 1.4 %collective-permute-done = bf16[32,1024]{1,0:T(8,128)(2,1)S(1)} collective-permute-done((bf16[32,1024]{1,0:T(8,128)(2,1)S(1)}, bf16[32,1024]{1,0:T(8,128)(2,1)S(1)}, u32[]{:S(2)}, u32[]{:S(2)}) %collective-permute-start) | collective-permute-done | bytes 65568 | tf_op jit(solution)/shard_map/ppermute | solution.py:17
  10.1 0.0 collective-permute-done.1
  10.1 0.0 collective-permute-done.2
  10.1 0.2 collective-permute-start.3
  10.3 0.9 %shard_map.50 = (f32[128,2048]{1,0:T(8,128)S(1)}, f32[1,2048]{1,0:T(1,128)S(1)}, f32[1,2048]{1,0:T(1,128)S(1)}) custom-call(bf16[1024,2048]{1,0:T(8,128)(2,1)S(1)} %get-tuple-element.25.docs_ref, bf16[128,1024]{1,0:T(8,128)(2,1)S(1)} %constant_dynamic-update-slice_fusion.table_ref), custom_call_target="tpu_custom_call" | custom-call | flops 536870912 | bytes 4456448 | tf_op jit(solution)/shard_map/pallas_call | solution.py:204
  11.2 0.5 %collective-permute-done.3.table_ref = bf16[128,1024]{1,0:T(8,128)(2,1)S(1)} collective-permute-done((bf16[128,1024]{1,0:T(8,128)(2,1)S(1)}, bf16[128,1024]{1,0:T(8,128)(2,1)S(1)}, u32[]{:S(2)}, u32[]{:S(2)}) %collective-permute-start.3) | collective-permute-done | bytes 262176 | tf_op jit(solution)/shard_map/ppermute | solution.py:17
  11.7 0.9 %shard_map.51 = (f32[128,2048]{1,0:T(8,128)S(1)}, f32[1,2048]{1,0:T(1,128)S(1)}, f32[1,2048]{1,0:T(1,128)S(1)}) custom-call(bf16[1024,2048]{1,0:T(8,128)(2,1)S(1)} %get-tuple-element.25.docs_ref, bf16[128,1024]{1,0:T(8,128)(2,1)S(1)} %collective-permute-done.3.table_ref, f32[1,2048]{1,0:T(1,128)S(1)} %get-tuple-element.27.first_top_ref.refs_6_, ...), custom_call_target="tpu_custom_call" | custom-call | flops 536870912 | bytes 4472832 | tf_op jit(solution)/shard_map/pallas_call | solution.py:204
  12.6 2.6 %collective-permute-start.6 = (f32[1,2048]{1,0:T(1,128)S(1)}, f32[1,2048]{1,0:T(1,128)S(1)}, u32[]{:S(2)}, u32[]{:S(2)}) collective-permute-start(f32[1,2048]{1,0:T(1,128)S(1)} %get-tuple-element.29.follow_ref), channel_id=1, source_target_pairs={{0,16},{8,24},{16,8},{24,0},{1,17},{9,25},{17,9},{25,1},{2,18},{10... | collective-permute-start | bytes 24584 | tf_op jit(solution)/shard_map/ppermute | solution.py:231
  15.3 1.2 %collective-permute-start.5 = (f32[1,2048]{1,0:T(1,128)S(1)}, f32[1,2048]{1,0:T(1,128)S(1)}, u32[]{:S(2)}, u32[]{:S(2)}) collective-permute-start(f32[1,2048]{1,0:T(1,128)S(1)} %get-tuple-element.29.follow_ref), channel_id=1, source_target_pairs={{0,24},{8,16},{16,0},{24,8},{1,25},{9,17},{17,1},{25,9},{2,26},{10... | collective-permute-start | bytes 24584 | tf_op jit(solution)/shard_map/ppermute | solution.py:231
  16.5 0.3 %collective-permute-start.4 = (f32[1,2048]{1,0:T(1,128)S(1)}, f32[1,2048]{1,0:T(1,128)S(1)}, u32[]{:S(2)}, u32[]{:S(2)}) collective-permute-start(f32[1,2048]{1,0:T(1,128)S(1)} %get-tuple-element.29.follow_ref), channel_id=1, source_target_pairs={{0,8},{8,0},{16,24},{24,16},{1,9},{9,1},{17,25},{25,17},{2,10},{10... | collective-permute-start | bytes 24584 | tf_op jit(solution)/shard_map/ppermute | solution.py:231
  16.9 2.2 %shard_map.52 = (bf16[2048,1024]{1,0:T(8,128)(2,1)S(1)}, f32[1,2048]{1,0:T(1,128)S(1)}) custom-call(bf16[2048,1024]{1,0:T(8,128)(2,1)} %source_ref.3, f32[1,2048]{1,0:T(1,128)S(1)} %get-tuple-element.29.follow_ref), custom_call_target="tpu_custom_call" | custom-call | bytes 8388608 | tf_op jit(solution)/shard_map/pallas_call | solution.py:65
  19.1 0.0 collective-permute-done.6.refs_2_
  19.1 0.8 %collective-permute-done.5.refs_1_ = f32[1,2048]{1,0:T(1,128)S(1)} collective-permute-done((f32[1,2048]{1,0:T(1,128)S(1)}, f32[1,2048]{1,0:T(1,128)S(1)}, u32[]{:S(2)}, u32[]{:S(2)}) %collective-permute-start.5) | collective-permute-done | bytes 8224 | tf_op jit(solution)/shard_map/ppermute | solution.py:231
  19.8 0.3 %collective-permute-done.4.refs_0_ = f32[1,2048]{1,0:T(1,128)S(1)} collective-permute-done((f32[1,2048]{1,0:T(1,128)S(1)}, f32[1,2048]{1,0:T(1,128)S(1)}, u32[]{:S(2)}, u32[]{:S(2)}) %collective-permute-start.4) | collective-permute-done | bytes 8224 | tf_op jit(solution)/shard_map/ppermute | solution.py:231
  20.2 0.8 %shard_map.53 = (f32[1,2048]{1,0:T(1,128)}, f32[1,2048]{1,0:T(1,128)S(1)}, bf16[128,1152]{1,0:T(8,128)(2,1)S(1)}) custom-call(s32[1]{0:T(128)} %bitcast.me_ref, f32[1,2048]{1,0:T(1,128)S(1)} %get-tuple-element.30.lse_ref, f32[1,2048]{1,0:T(1,128)S(1)} %collective-permute-done.4.refs_0_, f32[1,2048]{1,0:T(1,128)S(1)} %collective-permute-done.5.refs_1_, ...), custom_call_target="tpu_custom_call" | custom-call | flops 536870912 | bytes 5292036 | tf_op jit(solution)/shard_map/pallas_call | solution.py:204
  21.0 0.0 copy-start
  21.0 0.1 collective-permute-start.7
  21.1 0.8 %shard_map.54 = (f32[128,1024]{1,0:T(8,128)S(1)}, f32[128,128]{1,0:T(8,128)S(1)}) custom-call(f32[1,2048]{1,0:T(1,128)S(1)} %get-tuple-element.34.factor_ref, bf16[2048,1024]{1,0:T(8,128)(2,1)S(1)} %get-tuple-element.31.refs_3_.docs_ref, f32[128,2048]{1,0:T(8,128)S(1)} %get-tuple-element.35.part_ref), custom_call_target="tpu_custom_call" | custom-call | flops 536870912 | bytes 5251072 | tf_op jit(solution)/shard_map/pallas_call | solution.py:204
  21.9 0.8 %collective-permute-done.7.got_ref = bf16[128,1152]{1,0:T(8,128)(2,1)S(1)} collective-permute-done((bf16[128,1152]{1,0:T(8,128)(2,1)S(1)}, bf16[128,1152]{1,0:T(8,128)(2,1)S(1)}, u32[]{:S(2)}, u32[]{:S(2)}) %collective-permute-start.7) | collective-permute-done | bytes 294944 | tf_op jit(solution)/shard_map/ppermute | solution.py:17
  22.6 0.2 shard_map.55
  22.8 1.3 %collective-permute-start.8 = (bf16[32,1152]{1,0:T(8,128)(2,1)S(1)}, bf16[32,1152]{1,0:T(8,128)(2,1)S(1)}, u32[]{:S(2)}, u32[]{:S(2)}) collective-permute-start(bf16[32,1152]{1,0:T(8,128)(2,1)S(1)} %get-tuple-element.41), channel_id=1, source_target_pairs={{0,7},{1,6},{2,5},{3,4},{4,3},{5,2},{6,1},{7,0},{8,15},{9,14},{10,... | collective-permute-start | bytes 221192 | tf_op jit(solution)/shard_map/ppermute | solution.py:17
  24.1 1.5 %collective-permute-start.9 = (bf16[32,1152]{1,0:T(8,128)(2,1)S(1)}, bf16[32,1152]{1,0:T(8,128)(2,1)S(1)}, u32[]{:S(2)}, u32[]{:S(2)}) collective-permute-start(bf16[32,1152]{1,0:T(8,128)(2,1)S(1)} %get-tuple-element.42), channel_id=1, source_target_pairs={{0,3},{1,2},{2,1},{3,0},{4,7},{5,6},{6,5},{7,4},{8,11},{9,10},{10,... | collective-permute-start | bytes 221192 | tf_op jit(solution)/shard_map/ppermute | solution.py:17
  25.6 0.2 collective-permute-start.10
  25.8 2.2 %collective-permute-done.8.refs_0_ = bf16[32,1152]{1,0:T(8,128)(2,1)S(1)} collective-permute-done((bf16[32,1152]{1,0:T(8,128)(2,1)S(1)}, bf16[32,1152]{1,0:T(8,128)(2,1)S(1)}, u32[]{:S(2)}, u32[]{:S(2)}) %collective-permute-start.8) | collective-permute-done | bytes 73760 | tf_op jit(solution)/shard_map/ppermute | solution.py:17
  28.0 1.7 %collective-permute-done.9.refs_1_ = bf16[32,1152]{1,0:T(8,128)(2,1)S(1)} collective-permute-done((bf16[32,1152]{1,0:T(8,128)(2,1)S(1)}, bf16[32,1152]{1,0:T(8,128)(2,1)S(1)}, u32[]{:S(2)}, u32[]{:S(2)}) %collective-permute-start.9) | collective-permute-done | bytes 73760 | tf_op jit(solution)/shard_map/ppermute | solution.py:17
  29.7 0.2 collective-permute-done.10.refs_2_
  29.9 0.0 copy-done
  29.9 0.8 %shard_map.56 = (f32[32,1024]{1,0:T(8,128)}, f32[1,32]{1,0:T(1,128)}) custom-call(f32[32,1024]{1,0:T(8,128)S(1)} %get-tuple-element.39.own_ref, f32[32,128]{1,0:T(8,128)S(1)} %get-tuple-element.40.own_mass_ref, f32[32,1024]{1,0:T(8,128)S(1)} %copy-done, bf16[32,1152]{1,0:T(8,128)(2,1)S(1)} %collective-permute-done.8.refs_0_, ...), custom_call_target="tpu_custom_call" | custom-call | bytes 499712 | tf_op jit(solution)/shard_map/pallas_call | solution.py:204
  (4 shorter events, 0.0 us)
Async XLA Ops:
  1.5 8.5 %collective-permute-start.2 = (bf16[32,1024]{1,0:T(8,128)(2,1)S(1)}, bf16[32,1024]{1,0:T(8,128)(2,1)S(1)}, u32[]{:S(2)}, u32[]{:S(2)}) collective-permute-start(bf16[32,1024]{1,0:T(8,128)(2,1)S(1)} %convert_element_type.3.follow_ref), channel_id=1, source_target_pairs={{0,7},{1,6},{2,5},{3,4},{4,3},{5,2},{6,1},{7,0},{8,15},{9,14},{10,... | collective-permute-start | bytes 196616 | tf_op jit(solution)/shard_map/ppermute | solution.py:17
  4.9 5.1 %collective-permute-start.1 = (bf16[32,1024]{1,0:T(8,128)(2,1)S(1)}, bf16[32,1024]{1,0:T(8,128)(2,1)S(1)}, u32[]{:S(2)}, u32[]{:S(2)}) collective-permute-start(bf16[32,1024]{1,0:T(8,128)(2,1)S(1)} %convert_element_type.3.follow_ref), channel_id=1, source_target_pairs={{0,5},{1,4},{2,7},{3,6},{4,1},{5,0},{6,3},{7,2},{8,13},{9,12},{10,... | collective-permute-start | bytes 196616 | tf_op jit(solution)/shard_map/ppermute | solution.py:17
  5.7 4.3 %collective-permute-start = (bf16[32,1024]{1,0:T(8,128)(2,1)S(1)}, bf16[32,1024]{1,0:T(8,128)(2,1)S(1)}, u32[]{:S(2)}, u32[]{:S(2)}) collective-permute-start(bf16[32,1024]{1,0:T(8,128)(2,1)S(1)} %convert_element_type.3.follow_ref), channel_id=1, source_target_pairs={{0,3},{1,2},{2,1},{3,0},{4,7},{5,6},{6,5},{7,4},{8,11},{9,10},{10,... | collective-permute-start | bytes 196616 | tf_op jit(solution)/shard_map/ppermute | solution.py:17
  10.1 1.6 %collective-permute-start.3 = (bf16[128,1024]{1,0:T(8,128)(2,1)S(1)}, bf16[128,1024]{1,0:T(8,128)(2,1)S(1)}, u32[]{:S(2)}, u32[]{:S(2)}) collective-permute-start(bf16[128,1024]{1,0:T(8,128)(2,1)S(1)} %constant_dynamic-update-slice_fusion.table_ref), channel_id=1, source_target_pairs={{0,1},{1,0},{2,3},{3,2},{4,5},{5,4},{6,7},{7,6},{8,9},{9,8},{10,11... | collective-permute-start | bytes 786440 | tf_op jit(solution)/shard_map/ppermute | solution.py:17
  12.6 6.4 %collective-permute-start.6 = (f32[1,2048]{1,0:T(1,128)S(1)}, f32[1,2048]{1,0:T(1,128)S(1)}, u32[]{:S(2)}, u32[]{:S(2)}) collective-permute-start(f32[1,2048]{1,0:T(1,128)S(1)} %get-tuple-element.29.follow_ref), channel_id=1, source_target_pairs={{0,16},{8,24},{16,8},{24,0},{1,17},{9,25},{17,9},{25,1},{2,18},{10... | collective-permute-start | bytes 24584 | tf_op jit(solution)/shard_map/ppermute | solution.py:231
  15.3 4.5 %collective-permute-start.5 = (f32[1,2048]{1,0:T(1,128)S(1)}, f32[1,2048]{1,0:T(1,128)S(1)}, u32[]{:S(2)}, u32[]{:S(2)}) collective-permute-start(f32[1,2048]{1,0:T(1,128)S(1)} %get-tuple-element.29.follow_ref), channel_id=1, source_target_pairs={{0,24},{8,16},{16,0},{24,8},{1,25},{9,17},{17,1},{25,9},{2,26},{10... | collective-permute-start | bytes 24584 | tf_op jit(solution)/shard_map/ppermute | solution.py:231
  16.5 3.7 %collective-permute-start.4 = (f32[1,2048]{1,0:T(1,128)S(1)}, f32[1,2048]{1,0:T(1,128)S(1)}, u32[]{:S(2)}, u32[]{:S(2)}) collective-permute-start(f32[1,2048]{1,0:T(1,128)S(1)} %get-tuple-element.29.follow_ref), channel_id=1, source_target_pairs={{0,8},{8,0},{16,24},{24,16},{1,9},{9,1},{17,25},{25,17},{2,10},{10... | collective-permute-start | bytes 24584 | tf_op jit(solution)/shard_map/ppermute | solution.py:231
  21.0 8.9 %copy-start = (f32[32,1024]{1,0:T(8,128)S(1)}, f32[32,1024]{1,0:T(8,128)}, u32[]{:S(2)}) copy-start(f32[32,1024]{1,0:T(8,128)} %cent_ref.1) | copy-start | bytes 393220
  21.0 1.6 %collective-permute-start.7 = (bf16[128,1152]{1,0:T(8,128)(2,1)S(1)}, bf16[128,1152]{1,0:T(8,128)(2,1)S(1)}, u32[]{:S(2)}, u32[]{:S(2)}) collective-permute-start(bf16[128,1152]{1,0:T(8,128)(2,1)S(1)} %get-tuple-element.38), channel_id=1, source_target_pairs={{0,1},{1,0},{2,3},{3,2},{4,5},{5,4},{6,7},{7,6},{8,9},{9,8},{10,11... | collective-permute-start | bytes 884744 | tf_op jit(solution)/shard_map/ppermute | solution.py:17
  22.8 5.2 %collective-permute-start.8 = (bf16[32,1152]{1,0:T(8,128)(2,1)S(1)}, bf16[32,1152]{1,0:T(8,128)(2,1)S(1)}, u32[]{:S(2)}, u32[]{:S(2)}) collective-permute-start(bf16[32,1152]{1,0:T(8,128)(2,1)S(1)} %get-tuple-element.41), channel_id=1, source_target_pairs={{0,7},{1,6},{2,5},{3,4},{4,3},{5,2},{6,1},{7,0},{8,15},{9,14},{10,... | collective-permute-start | bytes 221192 | tf_op jit(solution)/shard_map/ppermute | solution.py:17
  24.1 5.6 %collective-permute-start.9 = (bf16[32,1152]{1,0:T(8,128)(2,1)S(1)}, bf16[32,1152]{1,0:T(8,128)(2,1)S(1)}, u32[]{:S(2)}, u32[]{:S(2)}) collective-permute-start(bf16[32,1152]{1,0:T(8,128)(2,1)S(1)} %get-tuple-element.42), channel_id=1, source_target_pairs={{0,3},{1,2},{2,1},{3,0},{4,7},{5,6},{6,5},{7,4},{8,11},{9,10},{10,... | collective-permute-start | bytes 221192 | tf_op jit(solution)/shard_map/ppermute | solution.py:17
  25.6 4.3 %collective-permute-start.10 = (bf16[32,1152]{1,0:T(8,128)(2,1)S(1)}, bf16[32,1152]{1,0:T(8,128)(2,1)S(1)}, u32[]{:S(2)}, u32[]{:S(2)}) collective-permute-start(bf16[32,1152]{1,0:T(8,128)(2,1)S(1)} %get-tuple-element.43), channel_id=1, source_target_pairs={{0,5},{1,4},{2,7},{3,6},{4,1},{5,0},{6,3},{7,2},{8,13},{9,12},{10,... | collective-permute-start | bytes 221192 | tf_op jit(solution)/shard_map/ppermute | solution.py:17

commit v13 on v12

--- a/solution.py
+++ b/solution.py
@@ -15,6 +15,13 @@
 
 def swap(x, axis, size, mask):
     return lax.ppermute(x, axis, [(i, i ^ mask) for i in range(size)])
+
+
+def chip_plan(n):
+    near = list(range(2, n - 2, 2))
+    turned = near[len(near) // 2:] + near[:len(near) // 2]
+    masks = list(zip(near, turned)) + [(n - 2, n - 2)]
+    return [[(i, i ^ pair[i % 2] ^ 1) for i in range(n)] for pair in masks]
 
 
 def group_plan(g):
@@ -217,7 +224,8 @@
         stats = [shape((half, count)), shape((1, count)), shape((1, count))]
         resp = [pltpu.VMEM((half, count), jnp.bfloat16)]
         rounded = centroids.astype(jnp.bfloat16)
-        blocks = [swap(rounded, "dev", n, m + 1) for m in range(2, n, 2)]
+        routes = chip_plan(n)
+        blocks = [lax.ppermute(rounded, "dev", pairs) for pairs in routes]
         docs_t, own = load(docs, rounded, chunk)
         mine = jnp.concatenate([own] + blocks, axis=0)
         theirs = swap(mine, "dev", n, 1)
@@ -248,8 +256,10 @@
             + [shape((rows, width + LANES), jnp.bfloat16)] * (n // 2 - 1),
             keep, keep_mass, got,
         )
-        far_first = sorted(range(1, n // 2), key=lambda j: (-j.bit_count(), j))
-        arrived = [swap(sends[j - 1], "dev", n, 2 * j + 1) for j in far_first]
+        arrived = [
+            lax.ppermute(x, "dev", [(target, source) for source, target in pairs])
+            for x, pairs in zip(sends[-1:] + sends[:-1], routes[-1:] + routes[:-1])
+        ]
         result, mass = call(
             final_kernel, [shape((rows, width)), shape((1, rows))],
             own, own_mass, centroids, *arrived,

time: 30.9 us -> 30.9 us (level)
  starting transfers between devices: 11.8 us -> 13 us
  waiting for transfers between devices: 7.87 us -> 6.7 us
    ppermute x0 -> x6, starting transfers between devices: none -> 8.55 us  [the longest x3 5.14 us: body(): blocks = [lax.ppermute(rounded, 'dev', pairs) for pairs in routes]]
    ppermute x8 -> x2, starting transfers between devices: 7.6 us -> 0.23 us  [swap(): return lax.ppermute(x, axis, [(i, i ^ mask) for i in range(size)])]
    ppermute x8 -> x2, waiting for transfers between devices: 6.78 us -> 1.31 us  [swap(): return lax.ppermute(x, axis, [(i, i ^ mask) for i in range(size)])]
    ppermute x0 -> x6, waiting for transfers between devices: none -> 4.31 us  [the longest x3 3.7 us: body(): lax.ppermute(x, 'dev', [(target, source) for source, target in pairs])]
where the time goes in v13:
time: 30.9 us; the launch traced here: 30.7 us
  starting transfers between devices  13 us (42%)
  Pallas kernels  9.35 us (30%)
  waiting for transfers between devices  6.7 us (22%)
  other arithmetic  0.92 us (3%)
  between operations  0.74 us (2%)
    ppermute x3, starting transfers between devices, body(): blocks = [lax.ppermute(rounded, 'dev', pairs) for pairs in routes]  5.14 us
    pallas_call x2, Pallas kernels, load(): pl.pallas_call(kernel, out_shape=[shape(dims, source.dtype), shape(follow...  4.93 us
    pallas_call x6, Pallas kernels, call(): pl.pallas_call(kernel, out_shape=outs, in_specs=[SMEM if x.dtype == jnp.i...  4.42 us
    ppermute x3, starting transfers between devices, body(): others = [lax.ppermute(lse, 'cgrp', pairs) for pairs in plan]  4.22 us
    ppermute x3, waiting for transfers between devices, body(): lax.ppermute(x, 'dev', [(target, source) for source, target in pairs])  3.7 us
    ppermute x3, starting transfers between devices, body(): lax.ppermute(x, 'dev', [(target, source) for source, target in pairs])  3.41 us
    ppermute x2, waiting for transfers between devices, swap(): return lax.ppermute(x, axis, [(i, i ^ mask) for i in range(size)])  1.31 us
    ppermute x3, waiting for transfers between devices, body(): others = [lax.ppermute(lse, 'cgrp', pairs) for pairs in plan]  1.09 us
  transfers between devices with their start and end apart: 11, of which 8 were waited for; matrix products, arithmetic and copies ran while one was open for 0% of the time, Pallas kernels for 22%

profile of v13, /device:TPU:0, one launch (start us, length us, event | category | flops | bytes accessed | tf_op | source)
XLA Modules:
  0.0 30.7 jit_solution(10881843485788208310)
XLA Ops:
  0.6 0.9 %convert_element_type.3.follow_ref = bf16[32,1024]{1,0:T(8,128)(2,1)S(1)} convert(f32[32,1024]{1,0:T(8,128)} %cent_ref.1) | non-fusion elementwise | flops 32768 | bytes 196608 | tf_op jit(solution)/shard_map/convert_element_type | solution.py:226
  1.5 3.4 %collective-permute-start.2 = (bf16[32,1024]{1,0:T(8,128)(2,1)S(1)}, bf16[32,1024]{1,0:T(8,128)(2,1)S(1)}, u32[]{:S(2)}, u32[]{:S(2)}) collective-permute-start(bf16[32,1024]{1,0:T(8,128)(2,1)S(1)} %convert_element_type.3.follow_ref), channel_id=1, source_target_pairs={{0,7},{1,6},{2,5},{3,4},{4,3},{5,2},{6,1},{7,0},{8,15},{9,14},{10,... | collective-permute-start | bytes 196616 | tf_op jit(solution)/shard_map/ppermute | solution.py:228
  4.9 0.8 %collective-permute-start.1 = (bf16[32,1024]{1,0:T(8,128)(2,1)S(1)}, bf16[32,1024]{1,0:T(8,128)(2,1)S(1)}, u32[]{:S(2)}, u32[]{:S(2)}) collective-permute-start(bf16[32,1024]{1,0:T(8,128)(2,1)S(1)} %convert_element_type.3.follow_ref), channel_id=1, source_target_pairs={{0,5},{1,2},{2,7},{3,0},{4,1},{5,6},{6,3},{7,4},{8,13},{9,10},{10,... | collective-permute-start | bytes 196616 | tf_op jit(solution)/shard_map/ppermute | solution.py:228
  5.7 1.0 %collective-permute-start = (bf16[32,1024]{1,0:T(8,128)(2,1)S(1)}, bf16[32,1024]{1,0:T(8,128)(2,1)S(1)}, u32[]{:S(2)}, u32[]{:S(2)}) collective-permute-start(bf16[32,1024]{1,0:T(8,128)(2,1)S(1)} %convert_element_type.3.follow_ref), channel_id=1, source_target_pairs={{0,3},{1,4},{2,1},{3,6},{4,7},{5,0},{6,5},{7,2},{8,11},{9,12},{10,... | collective-permute-start | bytes 196616 | tf_op jit(solution)/shard_map/ppermute | solution.py:228
  6.7 2.7 %shard_map.49 = (bf16[1024,2048]{1,0:T(8,128)(2,1)S(1)}, bf16[32,1024]{1,0:T(8,128)(2,1)S(1)}) custom-call(bf16[2048,1024]{1,0:T(8,128)(2,1)} %source_ref.3, bf16[32,1024]{1,0:T(8,128)(2,1)S(1)} %convert_element_type.3.follow_ref), custom_call_target="tpu_custom_call" | custom-call | bytes 8388608 | tf_op jit(solution)/shard_map/pallas_call | solution.py:72
  9.4 0.6 %collective-permute-done = bf16[32,1024]{1,0:T(8,128)(2,1)S(1)} collective-permute-done((bf16[32,1024]{1,0:T(8,128)(2,1)S(1)}, bf16[32,1024]{1,0:T(8,128)(2,1)S(1)}, u32[]{:S(2)}, u32[]{:S(2)}) %collective-permute-start) | collective-permute-done | bytes 65568 | tf_op jit(solution)/shard_map/ppermute | solution.py:228
  10.1 0.0 collective-permute-done.1
  10.1 0.0 collective-permute-done.2
  10.1 0.2 collective-permute-start.3
  10.3 0.9 %shard_map.50 = (f32[128,2048]{1,0:T(8,128)S(1)}, f32[1,2048]{1,0:T(1,128)S(1)}, f32[1,2048]{1,0:T(1,128)S(1)}) custom-call(bf16[1024,2048]{1,0:T(8,128)(2,1)S(1)} %get-tuple-element.25.docs_ref, bf16[128,1024]{1,0:T(8,128)(2,1)S(1)} %constant_dynamic-update-slice_fusion.table_ref), custom_call_target="tpu_custom_call" | custom-call | flops 536870912 | bytes 4456448 | tf_op jit(solution)/shard_map/pallas_call | solution.py:211
  11.2 0.5 %collective-permute-done.3.table_ref = bf16[128,1024]{1,0:T(8,128)(2,1)S(1)} collective-permute-done((bf16[128,1024]{1,0:T(8,128)(2,1)S(1)}, bf16[128,1024]{1,0:T(8,128)(2,1)S(1)}, u32[]{:S(2)}, u32[]{:S(2)}) %collective-permute-start.3) | collective-permute-done | bytes 262176 | tf_op jit(solution)/shard_map/ppermute | solution.py:17
  11.7 0.9 %shard_map.51 = (f32[128,2048]{1,0:T(8,128)S(1)}, f32[1,2048]{1,0:T(1,128)S(1)}, f32[1,2048]{1,0:T(1,128)S(1)}) custom-call(bf16[1024,2048]{1,0:T(8,128)(2,1)S(1)} %get-tuple-element.25.docs_ref, bf16[128,1024]{1,0:T(8,128)(2,1)S(1)} %collective-permute-done.3.table_ref, f32[1,2048]{1,0:T(1,128)S(1)} %get-tuple-element.27.first_top_ref.refs_6_, ...), custom_call_target="tpu_custom_call" | custom-call | flops 536870912 | bytes 4472832 | tf_op jit(solution)/shard_map/pallas_call | solution.py:211
  12.6 2.6 %collective-permute-start.6 = (f32[1,2048]{1,0:T(1,128)S(1)}, f32[1,2048]{1,0:T(1,128)S(1)}, u32[]{:S(2)}, u32[]{:S(2)}) collective-permute-start(f32[1,2048]{1,0:T(1,128)S(1)} %get-tuple-element.29.follow_ref), channel_id=1, source_target_pairs={{0,16},{8,24},{16,8},{24,0},{1,17},{9,25},{17,9},{25,1},{2,18},{10... | collective-permute-start | bytes 24584 | tf_op jit(solution)/shard_map/ppermute | solution.py:239
  15.3 1.2 %collective-permute-start.5 = (f32[1,2048]{1,0:T(1,128)S(1)}, f32[1,2048]{1,0:T(1,128)S(1)}, u32[]{:S(2)}, u32[]{:S(2)}) collective-permute-start(f32[1,2048]{1,0:T(1,128)S(1)} %get-tuple-element.29.follow_ref), channel_id=1, source_target_pairs={{0,24},{8,16},{16,0},{24,8},{1,25},{9,17},{17,1},{25,9},{2,26},{10... | collective-permute-start | bytes 24584 | tf_op jit(solution)/shard_map/ppermute | solution.py:239
  16.5 0.3 %collective-permute-start.4 = (f32[1,2048]{1,0:T(1,128)S(1)}, f32[1,2048]{1,0:T(1,128)S(1)}, u32[]{:S(2)}, u32[]{:S(2)}) collective-permute-start(f32[1,2048]{1,0:T(1,128)S(1)} %get-tuple-element.29.follow_ref), channel_id=1, source_target_pairs={{0,8},{8,0},{16,24},{24,16},{1,9},{9,1},{17,25},{25,17},{2,10},{10... | collective-permute-start | bytes 24584 | tf_op jit(solution)/shard_map/ppermute | solution.py:239
  16.9 2.2 %shard_map.52 = (bf16[2048,1024]{1,0:T(8,128)(2,1)S(1)}, f32[1,2048]{1,0:T(1,128)S(1)}) custom-call(bf16[2048,1024]{1,0:T(8,128)(2,1)} %source_ref.3, f32[1,2048]{1,0:T(1,128)S(1)} %get-tuple-element.29.follow_ref), custom_call_target="tpu_custom_call" | custom-call | bytes 8388608 | tf_op jit(solution)/shard_map/pallas_call | solution.py:72
  19.1 0.0 collective-permute-done.6.refs_2_
  19.1 0.8 %collective-permute-done.5.refs_1_ = f32[1,2048]{1,0:T(1,128)S(1)} collective-permute-done((f32[1,2048]{1,0:T(1,128)S(1)}, f32[1,2048]{1,0:T(1,128)S(1)}, u32[]{:S(2)}, u32[]{:S(2)}) %collective-permute-start.5) | collective-permute-done | bytes 8224 | tf_op jit(solution)/shard_map/ppermute | solution.py:239
  19.8 0.3 %collective-permute-done.4.refs_0_ = f32[1,2048]{1,0:T(1,128)S(1)} collective-permute-done((f32[1,2048]{1,0:T(1,128)S(1)}, f32[1,2048]{1,0:T(1,128)S(1)}, u32[]{:S(2)}, u32[]{:S(2)}) %collective-permute-start.4) | collective-permute-done | bytes 8224 | tf_op jit(solution)/shard_map/ppermute | solution.py:239
  20.2 0.8 %shard_map.53 = (f32[1,2048]{1,0:T(1,128)}, f32[1,2048]{1,0:T(1,128)S(1)}, bf16[128,1152]{1,0:T(8,128)(2,1)S(1)}) custom-call(s32[1]{0:T(128)} %bitcast.me_ref, f32[1,2048]{1,0:T(1,128)S(1)} %get-tuple-element.30.lse_ref, f32[1,2048]{1,0:T(1,128)S(1)} %collective-permute-done.4.refs_0_, f32[1,2048]{1,0:T(1,128)S(1)} %collective-permute-done.5.refs_1_, ...), custom_call_target="tpu_custom_call" | custom-call | flops 536870912 | bytes 5292036 | tf_op jit(solution)/shard_map/pallas_call | solution.py:211
  21.0 0.0 copy-start
  21.0 0.1 collective-permute-start.7
  21.1 0.8 %shard_map.54 = (f32[128,1024]{1,0:T(8,128)S(1)}, f32[128,128]{1,0:T(8,128)S(1)}) custom-call(f32[1,2048]{1,0:T(1,128)S(1)} %get-tuple-element.34.factor_ref, bf16[2048,1024]{1,0:T(8,128)(2,1)S(1)} %get-tuple-element.31.refs_3_.docs_ref, f32[128,2048]{1,0:T(8,128)S(1)} %get-tuple-element.35.part_ref), custom_call_target="tpu_custom_call" | custom-call | flops 536870912 | bytes 5251072 | tf_op jit(solution)/shard_map/pallas_call | solution.py:211
  21.9 0.8 %collective-permute-done.7.got_ref = bf16[128,1152]{1,0:T(8,128)(2,1)S(1)} collective-permute-done((bf16[128,1152]{1,0:T(8,128)(2,1)S(1)}, bf16[128,1152]{1,0:T(8,128)(2,1)S(1)}, u32[]{:S(2)}, u32[]{:S(2)}) %collective-permute-start.7) | collective-permute-done | bytes 294944 | tf_op jit(solution)/shard_map/ppermute | solution.py:17
  22.6 0.2 shard_map.55
  22.8 1.7 %collective-permute-start.8 = (bf16[32,1152]{1,0:T(8,128)(2,1)S(1)}, bf16[32,1152]{1,0:T(8,128)(2,1)S(1)}, u32[]{:S(2)}, u32[]{:S(2)}) collective-permute-start(bf16[32,1152]{1,0:T(8,128)(2,1)S(1)} %get-tuple-element.41), channel_id=1, source_target_pairs={{7,0},{6,1},{5,2},{4,3},{3,4},{2,5},{1,6},{0,7},{15,8},{14,9},{13,... | collective-permute-start | bytes 221192 | tf_op jit(solution)/shard_map/ppermute | solution.py:260
  24.5 0.7 %collective-permute-start.9 = (bf16[32,1152]{1,0:T(8,128)(2,1)S(1)}, bf16[32,1152]{1,0:T(8,128)(2,1)S(1)}, u32[]{:S(2)}, u32[]{:S(2)}) collective-permute-start(bf16[32,1152]{1,0:T(8,128)(2,1)S(1)} %get-tuple-element.42), channel_id=1, source_target_pairs={{3,0},{4,1},{1,2},{6,3},{7,4},{0,5},{5,6},{2,7},{11,8},{12,9},{9,1... | collective-permute-start | bytes 221192 | tf_op jit(solution)/shard_map/ppermute | solution.py:260
  25.2 1.0 %collective-permute-start.10 = (bf16[32,1152]{1,0:T(8,128)(2,1)S(1)}, bf16[32,1152]{1,0:T(8,128)(2,1)S(1)}, u32[]{:S(2)}, u32[]{:S(2)}) collective-permute-start(bf16[32,1152]{1,0:T(8,128)(2,1)S(1)} %get-tuple-element.43), channel_id=1, source_target_pairs={{5,0},{2,1},{7,2},{0,3},{1,4},{6,5},{3,6},{4,7},{13,8},{10,9},{15,... | collective-permute-start | bytes 221192 | tf_op jit(solution)/shard_map/ppermute | solution.py:260
  26.2 1.8 %collective-permute-done.8.refs_0_ = bf16[32,1152]{1,0:T(8,128)(2,1)S(1)} collective-permute-done((bf16[32,1152]{1,0:T(8,128)(2,1)S(1)}, bf16[32,1152]{1,0:T(8,128)(2,1)S(1)}, u32[]{:S(2)}, u32[]{:S(2)}) %collective-permute-start.8) | collective-permute-done | bytes 73760 | tf_op jit(solution)/shard_map/ppermute | solution.py:260
  28.0 1.1 %collective-permute-done.9.refs_1_ = bf16[32,1152]{1,0:T(8,128)(2,1)S(1)} collective-permute-done((bf16[32,1152]{1,0:T(8,128)(2,1)S(1)}, bf16[32,1152]{1,0:T(8,128)(2,1)S(1)}, u32[]{:S(2)}, u32[]{:S(2)}) %collective-permute-start.9) | collective-permute-done | bytes 73760 | tf_op jit(solution)/shard_map/ppermute | solution.py:260
  29.1 0.8 %collective-permute-done.10.refs_2_ = bf16[32,1152]{1,0:T(8,128)(2,1)S(1)} collective-permute-done((bf16[32,1152]{1,0:T(8,128)(2,1)S(1)}, bf16[32,1152]{1,0:T(8,128)(2,1)S(1)}, u32[]{:S(2)}, u32[]{:S(2)}) %collective-permute-start.10) | collective-permute-done | bytes 73760 | tf_op jit(solution)/shard_map/ppermute | solution.py:260
  29.9 0.0 copy-done
  29.9 0.8 %shard_map.56 = (f32[32,1024]{1,0:T(8,128)}, f32[1,32]{1,0:T(1,128)}) custom-call(f32[32,1024]{1,0:T(8,128)S(1)} %get-tuple-element.39.own_ref, f32[32,128]{1,0:T(8,128)S(1)} %get-tuple-element.40.own_mass_ref, f32[32,1024]{1,0:T(8,128)S(1)} %copy-done, bf16[32,1152]{1,0:T(8,128)(2,1)S(1)} %collective-permute-done.8.refs_0_, ...), custom_call_target="tpu_custom_call" | custom-call | bytes 499712 | tf_op jit(solution)/shard_map/pallas_call | solution.py:211
  (4 shorter events, 0.0 us)
Async XLA Ops:
  1.5 8.5 %collective-permute-start.2 = (bf16[32,1024]{1,0:T(8,128)(2,1)S(1)}, bf16[32,1024]{1,0:T(8,128)(2,1)S(1)}, u32[]{:S(2)}, u32[]{:S(2)}) collective-permute-start(bf16[32,1024]{1,0:T(8,128)(2,1)S(1)} %convert_element_type.3.follow_ref), channel_id=1, source_target_pairs={{0,7},{1,6},{2,5},{3,4},{4,3},{5,2},{6,1},{7,0},{8,15},{9,14},{10,... | collective-permute-start | bytes 196616 | tf_op jit(solution)/shard_map/ppermute | solution.py:228
  4.9 5.1 %collective-permute-start.1 = (bf16[32,1024]{1,0:T(8,128)(2,1)S(1)}, bf16[32,1024]{1,0:T(8,128)(2,1)S(1)}, u32[]{:S(2)}, u32[]{:S(2)}) collective-permute-start(bf16[32,1024]{1,0:T(8,128)(2,1)S(1)} %convert_element_type.3.follow_ref), channel_id=1, source_target_pairs={{0,5},{1,2},{2,7},{3,0},{4,1},{5,6},{6,3},{7,4},{8,13},{9,10},{10,... | collective-permute-start | bytes 196616 | tf_op jit(solution)/shard_map/ppermute | solution.py:228
  5.7 4.3 %collective-permute-start = (bf16[32,1024]{1,0:T(8,128)(2,1)S(1)}, bf16[32,1024]{1,0:T(8,128)(2,1)S(1)}, u32[]{:S(2)}, u32[]{:S(2)}) collective-permute-start(bf16[32,1024]{1,0:T(8,128)(2,1)S(1)} %convert_element_type.3.follow_ref), channel_id=1, source_target_pairs={{0,3},{1,4},{2,1},{3,6},{4,7},{5,0},{6,5},{7,2},{8,11},{9,12},{10,... | collective-permute-start | bytes 196616 | tf_op jit(solution)/shard_map/ppermute | solution.py:228
  10.1 1.6 %collective-permute-start.3 = (bf16[128,1024]{1,0:T(8,128)(2,1)S(1)}, bf16[128,1024]{1,0:T(8,128)(2,1)S(1)}, u32[]{:S(2)}, u32[]{:S(2)}) collective-permute-start(bf16[128,1024]{1,0:T(8,128)(2,1)S(1)} %constant_dynamic-update-slice_fusion.table_ref), channel_id=1, source_target_pairs={{0,1},{1,0},{2,3},{3,2},{4,5},{5,4},{6,7},{7,6},{8,9},{9,8},{10,11... | collective-permute-start | bytes 786440 | tf_op jit(solution)/shard_map/ppermute | solution.py:17
  12.6 6.4 %collective-permute-start.6 = (f32[1,2048]{1,0:T(1,128)S(1)}, f32[1,2048]{1,0:T(1,128)S(1)}, u32[]{:S(2)}, u32[]{:S(2)}) collective-permute-start(f32[1,2048]{1,0:T(1,128)S(1)} %get-tuple-element.29.follow_ref), channel_id=1, source_target_pairs={{0,16},{8,24},{16,8},{24,0},{1,17},{9,25},{17,9},{25,1},{2,18},{10... | collective-permute-start | bytes 24584 | tf_op jit(solution)/shard_map/ppermute | solution.py:239
  15.3 4.5 %collective-permute-start.5 = (f32[1,2048]{1,0:T(1,128)S(1)}, f32[1,2048]{1,0:T(1,128)S(1)}, u32[]{:S(2)}, u32[]{:S(2)}) collective-permute-start(f32[1,2048]{1,0:T(1,128)S(1)} %get-tuple-element.29.follow_ref), channel_id=1, source_target_pairs={{0,24},{8,16},{16,0},{24,8},{1,25},{9,17},{17,1},{25,9},{2,26},{10... | collective-permute-start | bytes 24584 | tf_op jit(solution)/shard_map/ppermute | solution.py:239
  16.5 3.7 %collective-permute-start.4 = (f32[1,2048]{1,0:T(1,128)S(1)}, f32[1,2048]{1,0:T(1,128)S(1)}, u32[]{:S(2)}, u32[]{:S(2)}) collective-permute-start(f32[1,2048]{1,0:T(1,128)S(1)} %get-tuple-element.29.follow_ref), channel_id=1, source_target_pairs={{0,8},{8,0},{16,24},{24,16},{1,9},{9,1},{17,25},{25,17},{2,10},{10... | collective-permute-start | bytes 24584 | tf_op jit(solution)/shard_map/ppermute | solution.py:239
  21.0 8.9 %copy-start = (f32[32,1024]{1,0:T(8,128)S(1)}, f32[32,1024]{1,0:T(8,128)}, u32[]{:S(2)}) copy-start(f32[32,1024]{1,0:T(8,128)} %cent_ref.1) | copy-start | bytes 393220
  21.0 1.6 %collective-permute-start.7 = (bf16[128,1152]{1,0:T(8,128)(2,1)S(1)}, bf16[128,1152]{1,0:T(8,128)(2,1)S(1)}, u32[]{:S(2)}, u32[]{:S(2)}) collective-permute-start(bf16[128,1152]{1,0:T(8,128)(2,1)S(1)} %get-tuple-element.38), channel_id=1, source_target_pairs={{0,1},{1,0},{2,3},{3,2},{4,5},{5,4},{6,7},{7,6},{8,9},{9,8},{10,11... | collective-permute-start | bytes 884744 | tf_op jit(solution)/shard_map/ppermute | solution.py:17
  22.8 5.2 %collective-permute-start.8 = (bf16[32,1152]{1,0:T(8,128)(2,1)S(1)}, bf16[32,1152]{1,0:T(8,128)(2,1)S(1)}, u32[]{:S(2)}, u32[]{:S(2)}) collective-permute-start(bf16[32,1152]{1,0:T(8,128)(2,1)S(1)} %get-tuple-element.41), channel_id=1, source_target_pairs={{7,0},{6,1},{5,2},{4,3},{3,4},{2,5},{1,6},{0,7},{15,8},{14,9},{13,... | collective-permute-start | bytes 221192 | tf_op jit(solution)/shard_map/ppermute | solution.py:260
  24.5 4.6 %collective-permute-start.9 = (bf16[32,1152]{1,0:T(8,128)(2,1)S(1)}, bf16[32,1152]{1,0:T(8,128)(2,1)S(1)}, u32[]{:S(2)}, u32[]{:S(2)}) collective-permute-start(bf16[32,1152]{1,0:T(8,128)(2,1)S(1)} %get-tuple-element.42), channel_id=1, source_target_pairs={{3,0},{4,1},{1,2},{6,3},{7,4},{0,5},{5,6},{2,7},{11,8},{12,9},{9,1... | collective-permute-start | bytes 221192 | tf_op jit(solution)/shard_map/ppermute | solution.py:260
  25.2 4.7 %collective-permute-start.10 = (bf16[32,1152]{1,0:T(8,128)(2,1)S(1)}, bf16[32,1152]{1,0:T(8,128)(2,1)S(1)}, u32[]{:S(2)}, u32[]{:S(2)}) collective-permute-start(bf16[32,1152]{1,0:T(8,128)(2,1)S(1)} %get-tuple-element.43), channel_id=1, source_target_pairs={{5,0},{2,1},{7,2},{0,3},{1,4},{6,5},{3,6},{4,7},{13,8},{10,9},{15,... | collective-permute-start | bytes 221192 | tf_op jit(solution)/shard_map/ppermute | solution.py:260

commit v14 on v13

--- a/solution.py
+++ b/solution.py
@@ -20,16 +20,16 @@
 def chip_plan(n):
     near = list(range(2, n - 2, 2))
     turned = near[len(near) // 2:] + near[:len(near) // 2]
-    masks = list(zip(near, turned)) + [(n - 2, n - 2)]
+    masks = [(n - 2, n - 2)] + list(zip(near, turned))
     return [[(i, i ^ pair[i % 2] ^ 1) for i in range(n)] for pair in masks]
 
 
 def group_plan(g):
     if g == 4:
         return [
+            [(0, 2), (1, 3), (2, 1), (3, 0)],
+            [(0, 3), (1, 2), (2, 0), (3, 1)],
             [(0, 1), (1, 0), (2, 3), (3, 2)],
-            [(0, 3), (1, 2), (2, 0), (3, 1)],
-            [(0, 2), (1, 3), (2, 1), (3, 0)],
         ]
     return [[(i, i ^ m) for i in range(g)] for m in range(1, g)]
 
@@ -53,35 +53,43 @@
         docs_ref[:, here] = landing[here, :].T
 
 
-def load_kernel(source_ref, follow_ref, docs_ref, own_ref, sem):
-    copy = pltpu.make_async_copy(source_ref, docs_ref, sem)
-    copy.start()
+def load_kernel(*refs):
+    half = len(refs) // 2
+    sources, follow_ref = refs[:half - 1], refs[half - 1]
+    targets, own_ref, sems = refs[half:-2], refs[-2], refs[-1]
+    copies = [
+        pltpu.make_async_copy(source, target, sems.at[i])
+        for i, (source, target) in enumerate(zip(sources, targets))
+    ]
+    for copy in copies:
+        copy.start()
     own_ref[...] = follow_ref[...]
-    copy.wait()
-
-
-def load(source, follow, chunk=0):
-    count, width = source.shape
-    kernel, dims, scratch = load_kernel, (count, width), [pltpu.SemaphoreType.DMA]
+    for copy in copies:
+        copy.wait()
+
+
+def load(sources, follow, chunk=0):
+    kernel, dims = load_kernel, sources[0].shape
+    scratch = [pltpu.SemaphoreType.DMA((len(sources),))]
     if chunk:
-        kernel, dims = functools.partial(transpose_kernel, chunk), (width, count)
+        kernel, (count, width) = functools.partial(transpose_kernel, chunk), dims
+        dims = (width, count)
         scratch = [
-            pltpu.VMEM((count, width), source.dtype),
+            pltpu.VMEM((count, width), follow.dtype),
             pltpu.SemaphoreType.DMA((count // chunk,)),
         ]
+    size = sum(x.nbytes for x in sources)
     return pl.pallas_call(
         kernel,
-        out_shape=[shape(dims, source.dtype), shape(follow.shape, follow.dtype)],
-        in_specs=[pl.BlockSpec(memory_space=pltpu.HBM), VMEM],
-        out_specs=[VMEM, VMEM],
+        out_shape=[shape(dims, x.dtype) for x in sources] + [shape(follow.shape, follow.dtype)],
+        in_specs=[pl.BlockSpec(memory_space=pltpu.HBM)] * len(sources) + [VMEM],
+        out_specs=[VMEM] * (len(sources) + 1),
         scratch_shapes=scratch,
         compiler_params=pltpu.CompilerParams(
-            vmem_limit_bytes=(4 << 20) + (2 * source.nbytes if chunk else 0)
+            vmem_limit_bytes=(4 << 20) + (2 * size if chunk else 0)
         ),
-        cost_estimate=pl.CostEstimate(
-            flops=0, bytes_accessed=2 * source.nbytes, transcendentals=0
-        ),
-    )(pltpu.with_memory_space_constraint(source, pltpu.HBM), follow)
+        cost_estimate=pl.CostEstimate(flops=0, bytes_accessed=2 * size, transcendentals=0),
+    )(*[pltpu.with_memory_space_constraint(x, pltpu.HBM) for x in sources], follow)
 
 
 def scores_kernel(chunk, docs_ref, table_ref, part_ref, top_ref, sum_ref):
@@ -96,7 +104,7 @@
         scores = (dots - half_norms) * scale
         top = jnp.max(scores, axis=0, keepdims=True)
         part = jnp.exp(scores - top)
-        part_ref[:, cols] = part
+        part_ref[:, cols] = part.astype(part_ref.dtype)
         top_ref[:, cols] = top
         sum_ref[:, cols] = jnp.sum(part, axis=0, keepdims=True)
 
@@ -116,7 +124,7 @@
     mass = jnp.zeros((rows, 1), jnp.float32)
     for start in range(0, count, chunk):
         cols = slice(start, start + chunk)
-        resp = part_ref[:, cols] * factor[:, cols]
+        resp = part_ref[:, cols].astype(jnp.float32) * factor[:, cols]
         mass += jnp.sum(resp, axis=1, keepdims=True)
         resp_ref[:, cols] = resp.astype(jnp.bfloat16)
     for start in range(0, docs_ref.shape[1], chunk):
@@ -137,10 +145,9 @@
     return wide[:, :width], wide[:, width:width + 1] + wide[:, width + 1:width + 2]
 
 
-def send_kernel(groups, plan, chunk, me_ref, lse_ref, *refs):
+def factors_kernel(groups, plan, me_ref, lse_ref, *refs):
     got_refs = refs[:len(plan)]
-    docs_ref, part_ref, top_ref, keep_top_ref = refs[len(plan):len(plan) + 4]
-    doc_lse_ref, factor_ref, send_ref, resp_ref = refs[len(plan) + 4:]
+    top_ref, their_top_ref, doc_lse_ref, factor_ref, send_ref = refs[len(plan):]
     me = me_ref[0]
     parts = [lse_ref[...]] * groups
     for got_ref, pairs in zip(got_refs, plan):
@@ -150,37 +157,35 @@
     best = tree(parts, jnp.maximum)
     doc_lse = best + jnp.log(tree([jnp.exp(x - best) for x in parts], jnp.add))
     doc_lse_ref[...] = doc_lse
-    factor_ref[...] = jnp.exp(keep_top_ref[...] - doc_lse)
-    factor = jnp.exp(top_ref[...] - doc_lse)
-
+    factor_ref[...] = jnp.exp(top_ref[...] - doc_lse)
+    send_ref[...] = jnp.exp(their_top_ref[...] - doc_lse)
+
+
+def first_sums_kernel(chunk, factor_ref, docs_ref, part_ref, sum_ref, mass_ref, resp_ref):
     def store(cols, term):
-        send_ref[:, cols] = term.astype(jnp.bfloat16)
-
-    mass = weighted_sums(chunk, factor, docs_ref, part_ref, resp_ref, store)
-    send_ref[:, docs_ref.shape[1]:] = mass_lanes(mass)
-
-
-def keep_kernel(chunk, factor_ref, docs_ref, part_ref, keep_ref, keep_mass_ref, resp_ref):
+        sum_ref[:, cols] = term
+
+    mass = weighted_sums(chunk, factor_ref[...], docs_ref, part_ref, resp_ref, store)
+    mass_ref[...] = jnp.broadcast_to(mass, mass_ref.shape)
+
+
+def second_sums_kernel(
+    chunk, factor_ref, docs_ref, part_ref, sum_ref, mass_ref, own_ref, own_mass_ref, *refs
+):
+    *send_refs, resp_ref = refs
+    rows, width = own_ref.shape
+
     def store(cols, term):
-        keep_ref[:, cols] = term
+        if cols.start < width:
+            term += sum_ref[:, cols]
+            own_ref[:, cols] = term[:rows]
+        for slot, ref in enumerate(send_refs, 1):
+            ref[:, cols] = term[slot * rows:(slot + 1) * rows].astype(jnp.bfloat16)
 
     mass = weighted_sums(chunk, factor_ref[...], docs_ref, part_ref, resp_ref, store)
-    keep_mass_ref[...] = jnp.broadcast_to(mass, keep_mass_ref.shape)
-
-
-def fold_kernel(keep_ref, keep_mass_ref, got_ref, own_ref, own_mass_ref, *send_refs):
-    rows, width = own_ref.shape
-    for slot in range(keep_ref.shape[0] // rows):
-        here = slice(slot * rows, (slot + 1) * rows)
-        got, got_mass = read_rows(got_ref[here], width)
-        term = keep_ref[here] + got
-        mass = keep_mass_ref[here, :1] + got_mass
-        if slot == 0:
-            own_ref[...] = term
-            own_mass_ref[...] = jnp.broadcast_to(mass, own_mass_ref.shape)
-        else:
-            send_refs[slot - 1][:, :width] = term.astype(jnp.bfloat16)
-            send_refs[slot - 1][:, width:] = mass_lanes(mass)
+    mass += mass_ref[:, :1]
+    own_mass_ref[...] = jnp.broadcast_to(mass[:rows], own_mass_ref.shape)
+    store(slice(width, width + LANES), mass_lanes(mass))
 
 
 def final_kernel(own_ref, own_mass_ref, cent_ref, *refs):
@@ -221,44 +226,46 @@
             )(*args)
 
         flops = 2 * half * count * width
-        stats = [shape((half, count)), shape((1, count)), shape((1, count))]
+        stats = [shape((1, count)), shape((1, count))]
         resp = [pltpu.VMEM((half, count), jnp.bfloat16)]
         rounded = centroids.astype(jnp.bfloat16)
         routes = chip_plan(n)
         blocks = [lax.ppermute(rounded, "dev", pairs) for pairs in routes]
-        docs_t, own = load(docs, rounded, chunk)
+        their_docs = swap(docs, "dev", n, 1)
+        docs_t, own = load([docs], rounded, chunk)
         mine = jnp.concatenate([own] + blocks, axis=0)
         theirs = swap(mine, "dev", n, 1)
         part, top, total = call(
-            functools.partial(scores_kernel, chunk), stats, docs_t, mine, flops=flops
+            functools.partial(scores_kernel, chunk), [shape((half, count))] + stats,
+            docs_t, mine, flops=flops,
         )
         other_part, other_top, lse = call(
-            functools.partial(last_scores_kernel, chunk), stats,
+            functools.partial(last_scores_kernel, chunk),
+            [shape((half, count), jnp.bfloat16)] + stats,
             docs_t, theirs, top, total, flops=flops,
         )
         others = [lax.ppermute(lse, "cgrp", pairs) for pairs in plan]
-        docs, lse = load(docs, lse)
-        doc_lse, factor, send = call(
-            functools.partial(send_kernel, g, plan, chunk),
-            [shape((1, count)), shape((1, count)), shape((half, width + LANES), jnp.bfloat16)],
-            lax.axis_index("cgrp").reshape(1), lse, *others, docs, other_part, other_top, top,
-            scratch=resp, flops=flops,
-        )
-        got = swap(send, "dev", n, 1)
-        keep, keep_mass = call(
-            functools.partial(keep_kernel, chunk),
+        their_part = swap(other_part, "dev", n, 1)
+        docs, lse = load([docs], lse)
+        doc_lse, factor, their_factor = call(
+            functools.partial(factors_kernel, g, plan), [shape((1, count))] * 3,
+            lax.axis_index("cgrp").reshape(1), lse, *others, top, other_top,
+        )
+        their_factor = swap(their_factor, "dev", n, 1)
+        sums, mass = call(
+            functools.partial(first_sums_kernel, chunk),
             [shape((half, width)), shape((half, LANES))],
             factor, docs, part, scratch=resp, flops=flops,
         )
         own, own_mass, *sends = call(
-            fold_kernel,
+            functools.partial(second_sums_kernel, chunk),
             [shape((rows, width)), shape((rows, LANES))]
             + [shape((rows, width + LANES), jnp.bfloat16)] * (n // 2 - 1),
-            keep, keep_mass, got,
+            their_factor, their_docs, their_part, sums, mass, scratch=resp, flops=flops,
         )
         arrived = [
             lax.ppermute(x, "dev", [(target, source) for source, target in pairs])
-            for x, pairs in zip(sends[-1:] + sends[:-1], routes[-1:] + routes[:-1])
+            for x, pairs in zip(sends, routes)
         ]
         result, mass = call(
             final_kernel, [shape((rows, width)), shape((1, rows))],

time: 30.9 us -> 33.4 us (1.081)
  Pallas kernels: 9.35 us -> 11.9 us
    pallas_call x6, Pallas kernels: 4.42 us -> 6.95 us  [call(): pl.pallas_call(kernel, out_shape=outs, in_specs=[SMEM if x.dtype == jnp.i...]
    ppermute x3, starting transfers between devices: 3.41 us -> 2.66 us  [body(): lax.ppermute(x, 'dev', [(target, source) for source, target in pairs])]
    ppermute x3, waiting for transfers between devices: 3.7 us -> 4.45 us  [body(): lax.ppermute(x, 'dev', [(target, source) for source, target in pairs])]
    ppermute x2 -> x4, starting transfers between devices: 0.23 us -> 0.86 us  [swap(): return lax.ppermute(x, axis, [(i, i ^ mask) for i in range(size)])]
    ppermute x3, waiting for transfers between devices: 0.61 us -> 0.01 us  [body(): blocks = [lax.ppermute(rounded, 'dev', pairs) for pairs in routes]]
    ppermute x2 -> x4, waiting for transfers between devices: 1.31 us -> 1.01 us  [swap(): return lax.ppermute(x, axis, [(i, i ^ mask) for i in range(size)])]
  transfers between devices with their start and end apart: 11 -> 13, of which waited for: 8 -> 7; matrix products, arithmetic and copies ran while one was open for 0% -> 3% of each run, Pallas kernels for 22% -> 25%
where the time goes in v14:
time: 33.4 us; the launch traced here: 33.2 us
  starting transfers between devices  13.1 us (39%)
  Pallas kernels  11.9 us (36%)
  waiting for transfers between devices  6.57 us (20%)
  other arithmetic  0.91 us (3%)
  between operations  0.74 us (2%)
    pallas_call x6, Pallas kernels, call(): pl.pallas_call(kernel, out_shape=outs, in_specs=[SMEM if x.dtype == jnp.i...  6.95 us
    ppermute x3, starting transfers between devices, body(): blocks = [lax.ppermute(rounded, 'dev', pairs) for pairs in routes]  5.36 us
    pallas_call x2, Pallas kernels, load(): pl.pallas_call(kernel, out_shape=[shape(dims, x.dtype) for x in sources]...  4.93 us
    ppermute x3, waiting for transfers between devices, body(): lax.ppermute(x, 'dev', [(target, source) for source, target in pairs])  4.45 us
    ppermute x3, starting transfers between devices, body(): others = [lax.ppermute(lse, 'cgrp', pairs) for pairs in plan]  4.18 us
    ppermute x3, starting transfers between devices, body(): lax.ppermute(x, 'dev', [(target, source) for source, target in pairs])  2.66 us
    ppermute x3, waiting for transfers between devices, body(): others = [lax.ppermute(lse, 'cgrp', pairs) for pairs in plan]  1.1 us
    ppermute x4, waiting for transfers between devices, swap(): return lax.ppermute(x, axis, [(i, i ^ mask) for i in range(size)])  1.01 us
  transfers between devices with their start and end apart: 13, of which 7 were waited for; matrix products, arithmetic and copies ran while one was open for 3% of the time, Pallas kernels for 25%

profile of v14, /device:TPU:0, one launch (start us, length us, event | category | flops | bytes accessed | tf_op | source)
XLA Modules:
  0.0 33.2 jit_solution(4268534985418446980)
XLA Ops:
  0.6 0.5 %collective-permute-start.8 = (bf16[2048,1024]{1,0:T(8,128)(2,1)}, bf16[2048,1024]{1,0:T(8,128)(2,1)}, u32[]{:S(2)}, u32[]{:S(2)}) collective-permute-start(bf16[2048,1024]{1,0:T(8,128)(2,1)} %refs_0_.1), channel_id=1, source_target_pairs={{0,1},{1,0},{2,3},{3,2},{4,5},{5,4},{6,7},{7,6},{8,9},{9,8},{10,11... | collective-permute-start | bytes 12582920 | tf_op jit(solution)/shard_map/ppermute | solution.py:17
  1.1 0.9 %convert_element_type.3.follow_ref = bf16[32,1024]{1,0:T(8,128)(2,1)S(1)} convert(f32[32,1024]{1,0:T(8,128)} %cent_ref.1) | non-fusion elementwise | flops 32768 | bytes 196608 | tf_op jit(solution)/shard_map/convert_element_type | solution.py:231
  2.1 3.6 %collective-permute-start = (bf16[32,1024]{1,0:T(8,128)(2,1)S(1)}, bf16[32,1024]{1,0:T(8,128)(2,1)S(1)}, u32[]{:S(2)}, u32[]{:S(2)}) collective-permute-start(bf16[32,1024]{1,0:T(8,128)(2,1)S(1)} %convert_element_type.3.follow_ref), channel_id=1, source_target_pairs={{0,7},{1,6},{2,5},{3,4},{4,3},{5,2},{6,1},{7,0},{8,15},{9,14},{10,... | collective-permute-start | bytes 196616 | tf_op jit(solution)/shard_map/ppermute | solution.py:233
  5.7 0.2 collective-permute-start.1
  5.8 1.6 %collective-permute-start.2 = (bf16[32,1024]{1,0:T(8,128)(2,1)S(1)}, bf16[32,1024]{1,0:T(8,128)(2,1)S(1)}, u32[]{:S(2)}, u32[]{:S(2)}) collective-permute-start(bf16[32,1024]{1,0:T(8,128)(2,1)S(1)} %convert_element_type.3.follow_ref), channel_id=1, source_target_pairs={{0,5},{1,2},{2,7},{3,0},{4,1},{5,6},{6,3},{7,4},{8,13},{9,10},{10,... | collective-permute-start | bytes 196616 | tf_op jit(solution)/shard_map/ppermute | solution.py:233
  7.4 2.7 %shard_map.49 = (bf16[1024,2048]{1,0:T(8,128)(2,1)S(1)}, bf16[32,1024]{1,0:T(8,128)(2,1)S(1)}) custom-call(bf16[2048,1024]{1,0:T(8,128)(2,1)} %refs_0_.1, bf16[32,1024]{1,0:T(8,128)(2,1)S(1)} %convert_element_type.3.follow_ref), custom_call_target="tpu_custom_call" | custom-call | bytes 8388608 | tf_op jit(solution)/shard_map/pallas_call | solution.py:82
  10.2 0.0 collective-permute-done
  10.2 0.0 collective-permute-done.1
  10.2 0.0 collective-permute-done.2
  10.3 0.1 collective-permute-start.3
  10.4 0.9 %shard_map.50 = (f32[128,2048]{1,0:T(8,128)S(1)}, f32[1,2048]{1,0:T(1,128)S(1)}, f32[1,2048]{1,0:T(1,128)S(1)}) custom-call(bf16[1024,2048]{1,0:T(8,128)(2,1)S(1)} %get-tuple-element.25.docs_ref, bf16[128,1024]{1,0:T(8,128)(2,1)S(1)} %constant_dynamic-update-slice_fusion.table_ref), custom_call_target="tpu_custom_call" | custom-call | flops 536870912 | bytes 4456448 | tf_op jit(solution)/shard_map/pallas_call | solution.py:216
  11.3 0.6 %collective-permute-done.3.table_ref = bf16[128,1024]{1,0:T(8,128)(2,1)S(1)} collective-permute-done((bf16[128,1024]{1,0:T(8,128)(2,1)S(1)}, bf16[128,1024]{1,0:T(8,128)(2,1)S(1)}, u32[]{:S(2)}, u32[]{:S(2)}) %collective-permute-start.3) | collective-permute-done | bytes 262176 | tf_op jit(solution)/shard_map/ppermute | solution.py:17
  11.9 1.0 %shard_map.51 = (bf16[128,2048]{1,0:T(8,128)(2,1)S(1)}, f32[1,2048]{1,0:T(1,128)S(1)}, f32[1,2048]{1,0:T(1,128)S(1)}) custom-call(bf16[1024,2048]{1,0:T(8,128)(2,1)S(1)} %get-tuple-element.25.docs_ref, bf16[128,1024]{1,0:T(8,128)(2,1)S(1)} %collective-permute-done.3.table_ref, f32[1,2048]{1,0:T(1,128)S(1)} %get-tuple-element.27.first_top_ref.refs_3_, ...), custom_call_target="tpu_custom_call" | custom-call | flops 536870912 | bytes 4472832 | tf_op jit(solution)/shard_map/pallas_call | solution.py:216
  12.8 0.2 collective-permute-start.9
  13.0 2.6 %collective-permute-start.4 = (f32[1,2048]{1,0:T(1,128)S(1)}, f32[1,2048]{1,0:T(1,128)S(1)}, u32[]{:S(2)}, u32[]{:S(2)}) collective-permute-start(f32[1,2048]{1,0:T(1,128)S(1)} %get-tuple-element.29.refs_1_), channel_id=1, source_target_pairs={{0,16},{8,24},{16,8},{24,0},{1,17},{9,25},{17,9},{25,1},{2,18},{10... | collective-permute-start | bytes 24584 | tf_op jit(solution)/shard_map/ppermute | solution.py:247
  15.6 1.2 %collective-permute-start.5 = (f32[1,2048]{1,0:T(1,128)S(1)}, f32[1,2048]{1,0:T(1,128)S(1)}, u32[]{:S(2)}, u32[]{:S(2)}) collective-permute-start(f32[1,2048]{1,0:T(1,128)S(1)} %get-tuple-element.29.refs_1_), channel_id=1, source_target_pairs={{0,24},{8,16},{16,0},{24,8},{1,25},{9,17},{17,1},{25,9},{2,26},{10... | collective-permute-start | bytes 24584 | tf_op jit(solution)/shard_map/ppermute | solution.py:247
  16.9 0.3 %collective-permute-start.6 = (f32[1,2048]{1,0:T(1,128)S(1)}, f32[1,2048]{1,0:T(1,128)S(1)}, u32[]{:S(2)}, u32[]{:S(2)}) collective-permute-start(f32[1,2048]{1,0:T(1,128)S(1)} %get-tuple-element.29.refs_1_), channel_id=1, source_target_pairs={{0,8},{8,0},{16,24},{24,16},{1,9},{9,1},{17,25},{25,17},{2,10},{10... | collective-permute-start | bytes 24584 | tf_op jit(solution)/shard_map/ppermute | solution.py:247
  17.2 2.2 %shard_map.52 = (bf16[2048,1024]{1,0:T(8,128)(2,1)S(1)}, f32[1,2048]{1,0:T(1,128)S(1)}) custom-call(bf16[2048,1024]{1,0:T(8,128)(2,1)} %refs_0_.1, f32[1,2048]{1,0:T(1,128)S(1)} %get-tuple-element.29.refs_1_), custom_call_target="tpu_custom_call" | custom-call | bytes 8388608 | tf_op jit(solution)/shard_map/pallas_call | solution.py:82
  19.4 0.0 collective-permute-done.4.refs_0_
  19.4 0.8 %collective-permute-done.5.refs_1_ = f32[1,2048]{1,0:T(1,128)S(1)} collective-permute-done((f32[1,2048]{1,0:T(1,128)S(1)}, f32[1,2048]{1,0:T(1,128)S(1)}, u32[]{:S(2)}, u32[]{:S(2)}) %collective-permute-start.5) | collective-permute-done | bytes 8224 | tf_op jit(solution)/shard_map/ppermute | solution.py:247
  20.2 0.3 %collective-permute-done.6.refs_2_ = f32[1,2048]{1,0:T(1,128)S(1)} collective-permute-done((f32[1,2048]{1,0:T(1,128)S(1)}, f32[1,2048]{1,0:T(1,128)S(1)}, u32[]{:S(2)}, u32[]{:S(2)}) %collective-permute-start.6) | collective-permute-done | bytes 8224 | tf_op jit(solution)/shard_map/ppermute | solution.py:247
  20.5 0.6 %shard_map.53 = (f32[1,2048]{1,0:T(1,128)}, f32[1,2048]{1,0:T(1,128)S(1)}, f32[1,2048]{1,0:T(1,128)S(1)}) custom-call(s32[1]{0:T(128)} %bitcast.me_ref, f32[1,2048]{1,0:T(1,128)S(1)} %get-tuple-element.30.lse_ref, f32[1,2048]{1,0:T(1,128)S(1)} %collective-permute-done.4.refs_0_, f32[1,2048]{1,0:T(1,128)S(1)} %collective-permute-done.5.refs_1_, ...), custom_call_target="tpu_custom_call" | custom-call | bytes 49156 | tf_op jit(solution)/shard_map/pallas_call | solution.py:216
  21.1 0.0 collective-permute-start.7
  21.2 0.0 copy-start
  21.2 0.7 %shard_map.54 = (f32[128,1024]{1,0:T(8,128)S(1)}, f32[128,128]{1,0:T(8,128)S(1)}) custom-call(f32[1,2048]{1,0:T(1,128)S(1)} %get-tuple-element.34.factor_ref, bf16[2048,1024]{1,0:T(8,128)(2,1)S(1)} %get-tuple-element.35.docs_ref, f32[128,2048]{1,0:T(8,128)S(1)} %get-tuple-element.36.part_ref), custom_call_target="tpu_custom_call" | custom-call | flops 536870912 | bytes 5251072 | tf_op jit(solution)/shard_map/pallas_call | solution.py:216
  21.9 0.4 %collective-permute-done.7.factor_ref = f32[1,2048]{1,0:T(1,128)S(1)} collective-permute-done((f32[1,2048]{1,0:T(1,128)S(1)}, f32[1,2048]{1,0:T(1,128)S(1)}, u32[]{:S(2)}, u32[]{:S(2)}) %collective-permute-start.7) | collective-permute-done | bytes 8224 | tf_op jit(solution)/shard_map/ppermute | solution.py:17
  22.3 0.0 collective-permute-done.9.part_ref
  22.3 0.0 collective-permute-done.8.docs_ref
  22.3 2.9 %shard_map.55 = (f32[32,1024]{1,0:T(8,128)S(1)}, f32[32,128]{1,0:T(8,128)S(1)}, bf16[32,1152]{1,0:T(8,128)(2,1)S(1)}, bf16[32,1152]{1,0:T(8,128)(2,1)S(1)}, bf16[32,1152]{1,0:T(8,128)(2,1)S(1)}) custom-call(f32[1,2048]{1,0:T(1,128)S(1)} %collective-permute-done.7.factor_ref, bf16[2048,1024]{1,0:T(8,128)(2,1)} %collective-permute-done.8.docs_ref, ...), custom_call_target="tpu_custom_call" | custom-call | flops 536870912 | bytes 5316608 | tf_op jit(solution)/shard_map/pallas_call | solution.py:216
  25.3 0.9 %collective-permute-start.10 = (bf16[32,1152]{1,0:T(8,128)(2,1)S(1)}, bf16[32,1152]{1,0:T(8,128)(2,1)S(1)}, u32[]{:S(2)}, u32[]{:S(2)}) collective-permute-start(bf16[32,1152]{1,0:T(8,128)(2,1)S(1)} %get-tuple-element.41), channel_id=1, source_target_pairs={{7,0},{6,1},{5,2},{4,3},{3,4},{2,5},{1,6},{0,7},{15,8},{14,9},{13,... | collective-permute-start | bytes 221192 | tf_op jit(solution)/shard_map/ppermute | solution.py:267
  26.2 1.4 %collective-permute-start.11 = (bf16[32,1152]{1,0:T(8,128)(2,1)S(1)}, bf16[32,1152]{1,0:T(8,128)(2,1)S(1)}, u32[]{:S(2)}, u32[]{:S(2)}) collective-permute-start(bf16[32,1152]{1,0:T(8,128)(2,1)S(1)} %get-tuple-element.42), channel_id=1, source_target_pairs={{3,0},{4,1},{1,2},{6,3},{7,4},{0,5},{5,6},{2,7},{11,8},{12,9},{9,1... | collective-permute-start | bytes 221192 | tf_op jit(solution)/shard_map/ppermute | solution.py:267
  27.6 0.3 %collective-permute-start.12 = (bf16[32,1152]{1,0:T(8,128)(2,1)S(1)}, bf16[32,1152]{1,0:T(8,128)(2,1)S(1)}, u32[]{:S(2)}, u32[]{:S(2)}) collective-permute-start(bf16[32,1152]{1,0:T(8,128)(2,1)S(1)} %get-tuple-element.43), channel_id=1, source_target_pairs={{5,0},{2,1},{7,2},{0,3},{1,4},{6,5},{3,6},{4,7},{13,8},{10,9},{15,... | collective-permute-start | bytes 221192 | tf_op jit(solution)/shard_map/ppermute | solution.py:267
  27.9 2.7 %collective-permute-done.10.refs_0_ = bf16[32,1152]{1,0:T(8,128)(2,1)S(1)} collective-permute-done((bf16[32,1152]{1,0:T(8,128)(2,1)S(1)}, bf16[32,1152]{1,0:T(8,128)(2,1)S(1)}, u32[]{:S(2)}, u32[]{:S(2)}) %collective-permute-start.10) | collective-permute-done | bytes 73760 | tf_op jit(solution)/shard_map/ppermute | solution.py:267
  30.6 0.7 %collective-permute-done.11.refs_1_ = bf16[32,1152]{1,0:T(8,128)(2,1)S(1)} collective-permute-done((bf16[32,1152]{1,0:T(8,128)(2,1)S(1)}, bf16[32,1152]{1,0:T(8,128)(2,1)S(1)}, u32[]{:S(2)}, u32[]{:S(2)}) %collective-permute-start.11) | collective-permute-done | bytes 73760 | tf_op jit(solution)/shard_map/ppermute | solution.py:267
  31.4 1.0 %collective-permute-done.12.refs_2_ = bf16[32,1152]{1,0:T(8,128)(2,1)S(1)} collective-permute-done((bf16[32,1152]{1,0:T(8,128)(2,1)S(1)}, bf16[32,1152]{1,0:T(8,128)(2,1)S(1)}, u32[]{:S(2)}, u32[]{:S(2)}) %collective-permute-start.12) | collective-permute-done | bytes 73760 | tf_op jit(solution)/shard_map/ppermute | solution.py:267
  32.4 0.0 copy-done
  32.4 0.8 %shard_map.56 = (f32[32,1024]{1,0:T(8,128)}, f32[1,32]{1,0:T(1,128)}) custom-call(f32[32,1024]{1,0:T(8,128)S(1)} %get-tuple-element.39.own_ref, f32[32,128]{1,0:T(8,128)S(1)} %get-tuple-element.40.own_mass_ref, f32[32,1024]{1,0:T(8,128)S(1)} %copy-done, bf16[32,1152]{1,0:T(8,128)(2,1)S(1)} %collective-permute-done.10.refs_0_, ...), custom_call_target="tpu_custom_call" | custom-call | bytes 499712 | tf_op jit(solution)/shard_map/pallas_call | solution.py:216
  (4 shorter events, 0.0 us)
Async XLA Ops:
  0.6 21.7 %collective-permute-start.8 = (bf16[2048,1024]{1,0:T(8,128)(2,1)}, bf16[2048,1024]{1,0:T(8,128)(2,1)}, u32[]{:S(2)}, u32[]{:S(2)}) collective-permute-start(bf16[2048,1024]{1,0:T(8,128)(2,1)} %refs_0_.1), channel_id=1, source_target_pairs={{0,1},{1,0},{2,3},{3,2},{4,5},{5,4},{6,7},{7,6},{8,9},{9,8},{10,11... | collective-permute-start | bytes 12582920 | tf_op jit(solution)/shard_map/ppermute | solution.py:17
  2.1 8.1 %collective-permute-start = (bf16[32,1024]{1,0:T(8,128)(2,1)S(1)}, bf16[32,1024]{1,0:T(8,128)(2,1)S(1)}, u32[]{:S(2)}, u32[]{:S(2)}) collective-permute-start(bf16[32,1024]{1,0:T(8,128)(2,1)S(1)} %convert_element_type.3.follow_ref), channel_id=1, source_target_pairs={{0,7},{1,6},{2,5},{3,4},{4,3},{5,2},{6,1},{7,0},{8,15},{9,14},{10,... | collective-permute-start | bytes 196616 | tf_op jit(solution)/shard_map/ppermute | solution.py:233
  5.7 4.5 %collective-permute-start.1 = (bf16[32,1024]{1,0:T(8,128)(2,1)S(1)}, bf16[32,1024]{1,0:T(8,128)(2,1)S(1)}, u32[]{:S(2)}, u32[]{:S(2)}) collective-permute-start(bf16[32,1024]{1,0:T(8,128)(2,1)S(1)} %convert_element_type.3.follow_ref), channel_id=1, source_target_pairs={{0,3},{1,4},{2,1},{3,6},{4,7},{5,0},{6,5},{7,2},{8,11},{9,12},{10,... | collective-permute-start | bytes 196616 | tf_op jit(solution)/shard_map/ppermute | solution.py:233
  5.8 4.4 %collective-permute-start.2 = (bf16[32,1024]{1,0:T(8,128)(2,1)S(1)}, bf16[32,1024]{1,0:T(8,128)(2,1)S(1)}, u32[]{:S(2)}, u32[]{:S(2)}) collective-permute-start(bf16[32,1024]{1,0:T(8,128)(2,1)S(1)} %convert_element_type.3.follow_ref), channel_id=1, source_target_pairs={{0,5},{1,2},{2,7},{3,0},{4,1},{5,6},{6,3},{7,4},{8,13},{9,10},{10,... | collective-permute-start | bytes 196616 | tf_op jit(solution)/shard_map/ppermute | solution.py:233
  10.3 1.6 %collective-permute-start.3 = (bf16[128,1024]{1,0:T(8,128)(2,1)S(1)}, bf16[128,1024]{1,0:T(8,128)(2,1)S(1)}, u32[]{:S(2)}, u32[]{:S(2)}) collective-permute-start(bf16[128,1024]{1,0:T(8,128)(2,1)S(1)} %constant_dynamic-update-slice_fusion.table_ref), channel_id=1, source_target_pairs={{0,1},{1,0},{2,3},{3,2},{4,5},{5,4},{6,7},{7,6},{8,9},{9,8},{10,11... | collective-permute-start | bytes 786440 | tf_op jit(solution)/shard_map/ppermute | solution.py:17
  12.8 9.5 %collective-permute-start.9 = (bf16[128,2048]{1,0:T(8,128)(2,1)S(1)}, bf16[128,2048]{1,0:T(8,128)(2,1)S(1)}, u32[]{:S(2)}, u32[]{:S(2)}) collective-permute-start(bf16[128,2048]{1,0:T(8,128)(2,1)S(1)} %get-tuple-element.33), channel_id=1, source_target_pairs={{0,1},{1,0},{2,3},{3,2},{4,5},{5,4},{6,7},{7,6},{8,9},{9,8},{10,11... | collective-permute-start | bytes 1572872 | tf_op jit(solution)/shard_map/ppermute | solution.py:17
  13.0 6.4 %collective-permute-start.4 = (f32[1,2048]{1,0:T(1,128)S(1)}, f32[1,2048]{1,0:T(1,128)S(1)}, u32[]{:S(2)}, u32[]{:S(2)}) collective-permute-start(f32[1,2048]{1,0:T(1,128)S(1)} %get-tuple-element.29.refs_1_), channel_id=1, source_target_pairs={{0,16},{8,24},{16,8},{24,0},{1,17},{9,25},{17,9},{25,1},{2,18},{10... | collective-permute-start | bytes 24584 | tf_op jit(solution)/shard_map/ppermute | solution.py:247
  15.6 4.5 %collective-permute-start.5 = (f32[1,2048]{1,0:T(1,128)S(1)}, f32[1,2048]{1,0:T(1,128)S(1)}, u32[]{:S(2)}, u32[]{:S(2)}) collective-permute-start(f32[1,2048]{1,0:T(1,128)S(1)} %get-tuple-element.29.refs_1_), channel_id=1, source_target_pairs={{0,24},{8,16},{16,0},{24,8},{1,25},{9,17},{17,1},{25,9},{2,26},{10... | collective-permute-start | bytes 24584 | tf_op jit(solution)/shard_map/ppermute | solution.py:247
  16.9 3.7 %collective-permute-start.6 = (f32[1,2048]{1,0:T(1,128)S(1)}, f32[1,2048]{1,0:T(1,128)S(1)}, u32[]{:S(2)}, u32[]{:S(2)}) collective-permute-start(f32[1,2048]{1,0:T(1,128)S(1)} %get-tuple-element.29.refs_1_), channel_id=1, source_target_pairs={{0,8},{8,0},{16,24},{24,16},{1,9},{9,1},{17,25},{25,17},{2,10},{10... | collective-permute-start | bytes 24584 | tf_op jit(solution)/shard_map/ppermute | solution.py:247
  21.1 1.2 %collective-permute-start.7 = (f32[1,2048]{1,0:T(1,128)S(1)}, f32[1,2048]{1,0:T(1,128)S(1)}, u32[]{:S(2)}, u32[]{:S(2)}) collective-permute-start(f32[1,2048]{1,0:T(1,128)S(1)} %get-tuple-element.32), channel_id=1, source_target_pairs={{0,1},{1,0},{2,3},{3,2},{4,5},{5,4},{6,7},{7,6},{8,9},{9,8},{10,11... | collective-permute-start | bytes 24584 | tf_op jit(solution)/shard_map/ppermute | solution.py:17
  21.2 11.2 %copy-start = (f32[32,1024]{1,0:T(8,128)S(1)}, f32[32,1024]{1,0:T(8,128)}, u32[]{:S(2)}) copy-start(f32[32,1024]{1,0:T(8,128)} %cent_ref.1) | copy-start | bytes 393220
  25.3 5.4 %collective-permute-start.10 = (bf16[32,1152]{1,0:T(8,128)(2,1)S(1)}, bf16[32,1152]{1,0:T(8,128)(2,1)S(1)}, u32[]{:S(2)}, u32[]{:S(2)}) collective-permute-start(bf16[32,1152]{1,0:T(8,128)(2,1)S(1)} %get-tuple-element.41), channel_id=1, source_target_pairs={{7,0},{6,1},{5,2},{4,3},{3,4},{2,5},{1,6},{0,7},{15,8},{14,9},{13,... | collective-permute-start | bytes 221192 | tf_op jit(solution)/shard_map/ppermute | solution.py:267
  26.2 5.2 %collective-permute-start.11 = (bf16[32,1152]{1,0:T(8,128)(2,1)S(1)}, bf16[32,1152]{1,0:T(8,128)(2,1)S(1)}, u32[]{:S(2)}, u32[]{:S(2)}) collective-permute-start(bf16[32,1152]{1,0:T(8,128)(2,1)S(1)} %get-tuple-element.42), channel_id=1, source_target_pairs={{3,0},{4,1},{1,2},{6,3},{7,4},{0,5},{5,6},{2,7},{11,8},{12,9},{9,1... | collective-permute-start | bytes 221192 | tf_op jit(solution)/shard_map/ppermute | solution.py:267
  27.6 4.8 %collective-permute-start.12 = (bf16[32,1152]{1,0:T(8,128)(2,1)S(1)}, bf16[32,1152]{1,0:T(8,128)(2,1)S(1)}, u32[]{:S(2)}, u32[]{:S(2)}) collective-permute-start(bf16[32,1152]{1,0:T(8,128)(2,1)S(1)} %get-tuple-element.43), channel_id=1, source_target_pairs={{5,0},{2,1},{7,2},{0,3},{1,4},{6,5},{3,6},{4,7},{13,8},{10,9},{15,... | collective-permute-start | bytes 221192 | tf_op jit(solution)/shard_map/ppermute | solution.py:267

commit v15 on v13

--- a/solution.py
+++ b/solution.py
@@ -84,6 +84,12 @@
     )(pltpu.with_memory_space_constraint(source, pltpu.HBM), follow)
 
 
+def put_row(ref, start, row):
+    for i in range(row.shape[1] // LANES):
+        at = start // LANES + i
+        ref[at:at + 1, :] = row[:, i * LANES:(i + 1) * LANES]
+
+
 def scores_kernel(chunk, docs_ref, table_ref, part_ref, top_ref, sum_ref):
     width, count = docs_ref.shape
     scale = 4.0 / math.sqrt(width)
@@ -97,8 +103,8 @@
         top = jnp.max(scores, axis=0, keepdims=True)
         part = jnp.exp(scores - top)
         part_ref[:, cols] = part
-        top_ref[:, cols] = top
-        sum_ref[:, cols] = jnp.sum(part, axis=0, keepdims=True)
+        put_row(top_ref, start, top)
+        put_row(sum_ref, start, jnp.sum(part, axis=0, keepdims=True))
 
 
 def last_scores_kernel(
@@ -113,16 +119,16 @@
 
 def weighted_sums(chunk, factor, docs_ref, part_ref, resp_ref, store):
     rows, count = part_ref.shape
-    mass = jnp.zeros((rows, 1), jnp.float32)
-    for start in range(0, count, chunk):
-        cols = slice(start, start + chunk)
-        resp = part_ref[:, cols] * factor[:, cols]
-        mass += jnp.sum(resp, axis=1, keepdims=True)
+    mass = jnp.zeros((rows, LANES), jnp.float32)
+    for i in range(count // LANES):
+        cols = slice(i * LANES, (i + 1) * LANES)
+        resp = part_ref[:, cols] * factor[i:i + 1]
+        mass += resp
         resp_ref[:, cols] = resp.astype(jnp.bfloat16)
     for start in range(0, docs_ref.shape[1], chunk):
         cols = slice(start, start + chunk)
         store(cols, jnp.dot(resp_ref[...], docs_ref[:, cols], preferred_element_type=jnp.float32))
-    return mass
+    return jnp.sum(mass, axis=1, keepdims=True)
 
 
 def mass_lanes(mass):
@@ -221,7 +227,7 @@
             )(*args)
 
         flops = 2 * half * count * width
-        stats = [shape((half, count)), shape((1, count)), shape((1, count))]
+        stats = [shape((half, count)), shape((count // LANES, LANES)), shape((count // LANES, LANES))]
         resp = [pltpu.VMEM((half, count), jnp.bfloat16)]
         rounded = centroids.astype(jnp.bfloat16)
         routes = chip_plan(n)
@@ -240,7 +246,7 @@
         docs, lse = load(docs, lse)
         doc_lse, factor, send = call(
             functools.partial(send_kernel, g, plan, chunk),
-            [shape((1, count)), shape((1, count)), shape((half, width + LANES), jnp.bfloat16)],
+            [shape((count // LANES, LANES)), shape((count // LANES, LANES)), shape((half, width + LANES), jnp.bfloat16)],
             lax.axis_index("cgrp").reshape(1), lse, *others, docs, other_part, other_top, top,
             scratch=resp, flops=flops,
         )

time: 30.9 us -> 30.9 us (level)
  no operation moved by 1% of the time
where the time goes in v15:
time: 30.9 us; the launch traced here: 30.7 us
  starting transfers between devices  13 us (42%)
  Pallas kernels  9.31 us (30%)
  waiting for transfers between devices  6.73 us (22%)
  other arithmetic  0.92 us (3%)
  between operations  0.74 us (2%)
    ppermute x3, starting transfers between devices, body(): blocks = [lax.ppermute(rounded, 'dev', pairs) for pairs in routes]  5.14 us
    pallas_call x2, Pallas kernels, load(): pl.pallas_call(kernel, out_shape=[shape(dims, source.dtype), shape(follow...  4.93 us
    pallas_call x6, Pallas kernels, call(): pl.pallas_call(kernel, out_shape=outs, in_specs=[SMEM if x.dtype == jnp.i...  4.38 us
    ppermute x3, starting transfers between devices, body(): others = [lax.ppermute(lse, 'cgrp', pairs) for pairs in plan]  4.22 us
    ppermute x3, waiting for transfers between devices, body(): lax.ppermute(x, 'dev', [(target, source) for source, target in pairs])  3.7 us
    ppermute x3, starting transfers between devices, body(): lax.ppermute(x, 'dev', [(target, source) for source, target in pairs])  3.41 us
    ppermute x2, waiting for transfers between devices, swap(): return lax.ppermute(x, axis, [(i, i ^ mask) for i in range(size)])  1.33 us
    ppermute x3, waiting for transfers between devices, body(): others = [lax.ppermute(lse, 'cgrp', pairs) for pairs in plan]  1.09 us
  transfers between devices with their start and end apart: 11, of which 8 were waited for; matrix products, arithmetic and copies ran while one was open for 0% of the time, Pallas kernels for 22%

profile of v15, /device:TPU:0, one launch (start us, length us, event | category | flops | bytes accessed | tf_op | source)
XLA Modules:
  0.0 30.7 jit_solution(17633319305015475582)
XLA Ops:
  0.6 0.9 %convert_element_type.3.follow_ref = bf16[32,1024]{1,0:T(8,128)(2,1)S(1)} convert(f32[32,1024]{1,0:T(8,128)} %cent_ref.1) | non-fusion elementwise | flops 32768 | bytes 196608 | tf_op jit(solution)/shard_map/convert_element_type | solution.py:232
  1.5 3.4 %collective-permute-start.2 = (bf16[32,1024]{1,0:T(8,128)(2,1)S(1)}, bf16[32,1024]{1,0:T(8,128)(2,1)S(1)}, u32[]{:S(2)}, u32[]{:S(2)}) collective-permute-start(bf16[32,1024]{1,0:T(8,128)(2,1)S(1)} %convert_element_type.3.follow_ref), channel_id=1, source_target_pairs={{0,7},{1,6},{2,5},{3,4},{4,3},{5,2},{6,1},{7,0},{8,15},{9,14},{10,... | collective-permute-start | bytes 196616 | tf_op jit(solution)/shard_map/ppermute | solution.py:234
  4.9 0.8 %collective-permute-start.1 = (bf16[32,1024]{1,0:T(8,128)(2,1)S(1)}, bf16[32,1024]{1,0:T(8,128)(2,1)S(1)}, u32[]{:S(2)}, u32[]{:S(2)}) collective-permute-start(bf16[32,1024]{1,0:T(8,128)(2,1)S(1)} %convert_element_type.3.follow_ref), channel_id=1, source_target_pairs={{0,5},{1,2},{2,7},{3,0},{4,1},{5,6},{6,3},{7,4},{8,13},{9,10},{10,... | collective-permute-start | bytes 196616 | tf_op jit(solution)/shard_map/ppermute | solution.py:234
  5.7 1.0 %collective-permute-start = (bf16[32,1024]{1,0:T(8,128)(2,1)S(1)}, bf16[32,1024]{1,0:T(8,128)(2,1)S(1)}, u32[]{:S(2)}, u32[]{:S(2)}) collective-permute-start(bf16[32,1024]{1,0:T(8,128)(2,1)S(1)} %convert_element_type.3.follow_ref), channel_id=1, source_target_pairs={{0,3},{1,4},{2,1},{3,6},{4,7},{5,0},{6,5},{7,2},{8,11},{9,12},{10,... | collective-permute-start | bytes 196616 | tf_op jit(solution)/shard_map/ppermute | solution.py:234
  6.7 2.7 %shard_map.49 = (bf16[1024,2048]{1,0:T(8,128)(2,1)S(1)}, bf16[32,1024]{1,0:T(8,128)(2,1)S(1)}) custom-call(bf16[2048,1024]{1,0:T(8,128)(2,1)} %source_ref.3, bf16[32,1024]{1,0:T(8,128)(2,1)S(1)} %convert_element_type.3.follow_ref), custom_call_target="tpu_custom_call" | custom-call | bytes 8388608 | tf_op jit(solution)/shard_map/pallas_call | solution.py:72
  9.4 0.6 %collective-permute-done = bf16[32,1024]{1,0:T(8,128)(2,1)S(1)} collective-permute-done((bf16[32,1024]{1,0:T(8,128)(2,1)S(1)}, bf16[32,1024]{1,0:T(8,128)(2,1)S(1)}, u32[]{:S(2)}, u32[]{:S(2)}) %collective-permute-start) | collective-permute-done | bytes 65568 | tf_op jit(solution)/shard_map/ppermute | solution.py:234
  10.1 0.0 collective-permute-done.1
  10.1 0.0 collective-permute-done.2
  10.1 0.2 collective-permute-start.3
  10.3 0.9 %shard_map.50 = (f32[128,2048]{1,0:T(8,128)S(1)}, f32[16,128]{1,0:T(8,128)S(1)}, f32[16,128]{1,0:T(8,128)S(1)}) custom-call(bf16[1024,2048]{1,0:T(8,128)(2,1)S(1)} %get-tuple-element.25.docs_ref, bf16[128,1024]{1,0:T(8,128)(2,1)S(1)} %constant_dynamic-update-slice_fusion.table_ref), custom_call_target="tpu_custom_call" | custom-call | flops 536870912 | bytes 4456448 | tf_op jit(solution)/shard_map/pallas_call | solution.py:217
  11.2 0.6 %collective-permute-done.3.table_ref = bf16[128,1024]{1,0:T(8,128)(2,1)S(1)} collective-permute-done((bf16[128,1024]{1,0:T(8,128)(2,1)S(1)}, bf16[128,1024]{1,0:T(8,128)(2,1)S(1)}, u32[]{:S(2)}, u32[]{:S(2)}) %collective-permute-start.3) | collective-permute-done | bytes 262176 | tf_op jit(solution)/shard_map/ppermute | solution.py:17
  11.7 0.9 %shard_map.51 = (f32[128,2048]{1,0:T(8,128)S(1)}, f32[16,128]{1,0:T(8,128)S(1)}, f32[16,128]{1,0:T(8,128)S(1)}) custom-call(bf16[1024,2048]{1,0:T(8,128)(2,1)S(1)} %get-tuple-element.25.docs_ref, bf16[128,1024]{1,0:T(8,128)(2,1)S(1)} %collective-permute-done.3.table_ref, f32[16,128]{1,0:T(8,128)S(1)} %get-tuple-element.27.first_top_ref.refs_6_, ...), custom_call_target="tpu_custom_call" | custom-call | flops 536870912 | bytes 4472832 | tf_op jit(solution)/shard_map/pallas_call | solution.py:217
  12.6 2.6 %collective-permute-start.6 = (f32[16,128]{1,0:T(8,128)S(1)}, f32[16,128]{1,0:T(8,128)S(1)}, u32[]{:S(2)}, u32[]{:S(2)}) collective-permute-start(f32[16,128]{1,0:T(8,128)S(1)} %get-tuple-element.29.follow_ref), channel_id=1, source_target_pairs={{0,16},{8,24},{16,8},{24,0},{1,17},{9,25},{17,9},{25,1},{2,18},{10... | collective-permute-start | bytes 24584 | tf_op jit(solution)/shard_map/ppermute | solution.py:245
  15.2 1.2 %collective-permute-start.5 = (f32[16,128]{1,0:T(8,128)S(1)}, f32[16,128]{1,0:T(8,128)S(1)}, u32[]{:S(2)}, u32[]{:S(2)}) collective-permute-start(f32[16,128]{1,0:T(8,128)S(1)} %get-tuple-element.29.follow_ref), channel_id=1, source_target_pairs={{0,24},{8,16},{16,0},{24,8},{1,25},{9,17},{17,1},{25,9},{2,26},{10... | collective-permute-start | bytes 24584 | tf_op jit(solution)/shard_map/ppermute | solution.py:245
  16.5 0.3 %collective-permute-start.4 = (f32[16,128]{1,0:T(8,128)S(1)}, f32[16,128]{1,0:T(8,128)S(1)}, u32[]{:S(2)}, u32[]{:S(2)}) collective-permute-start(f32[16,128]{1,0:T(8,128)S(1)} %get-tuple-element.29.follow_ref), channel_id=1, source_target_pairs={{0,8},{8,0},{16,24},{24,16},{1,9},{9,1},{17,25},{25,17},{2,10},{10... | collective-permute-start | bytes 24584 | tf_op jit(solution)/shard_map/ppermute | solution.py:245
  16.8 2.2 %shard_map.52 = (bf16[2048,1024]{1,0:T(8,128)(2,1)S(1)}, f32[16,128]{1,0:T(8,128)S(1)}) custom-call(bf16[2048,1024]{1,0:T(8,128)(2,1)} %source_ref.3, f32[16,128]{1,0:T(8,128)S(1)} %get-tuple-element.29.follow_ref), custom_call_target="tpu_custom_call" | custom-call | bytes 8388608 | tf_op jit(solution)/shard_map/pallas_call | solution.py:72
  19.0 0.0 collective-permute-done.6.refs_2_
  19.0 0.8 %collective-permute-done.5.refs_1_ = f32[16,128]{1,0:T(8,128)S(1)} collective-permute-done((f32[16,128]{1,0:T(8,128)S(1)}, f32[16,128]{1,0:T(8,128)S(1)}, u32[]{:S(2)}, u32[]{:S(2)}) %collective-permute-start.5) | collective-permute-done | bytes 8224 | tf_op jit(solution)/shard_map/ppermute | solution.py:245
  19.8 0.3 %collective-permute-done.4.refs_0_ = f32[16,128]{1,0:T(8,128)S(1)} collective-permute-done((f32[16,128]{1,0:T(8,128)S(1)}, f32[16,128]{1,0:T(8,128)S(1)}, u32[]{:S(2)}, u32[]{:S(2)}) %collective-permute-start.4) | collective-permute-done | bytes 8224 | tf_op jit(solution)/shard_map/ppermute | solution.py:245
  20.1 0.8 %shard_map.53 = (f32[16,128]{1,0:T(8,128)}, f32[16,128]{1,0:T(8,128)S(1)}, bf16[128,1152]{1,0:T(8,128)(2,1)S(1)}) custom-call(s32[1]{0:T(128)} %bitcast.me_ref, f32[16,128]{1,0:T(8,128)S(1)} %get-tuple-element.30.lse_ref, f32[16,128]{1,0:T(8,128)S(1)} %collective-permute-done.4.refs_0_, f32[16,128]{1,0:T(8,128)S(1)} %collective-permute-done.5.refs_1_, ...), custom_call_target="tpu_custom_call" | custom-call | flops 536870912 | bytes 5292036 | tf_op jit(solution)/shard_map/pallas_call | solution.py:217
  21.0 0.0 copy-start
  21.0 0.1 collective-permute-start.7
  21.0 0.8 %shard_map.54 = (f32[128,1024]{1,0:T(8,128)S(1)}, f32[128,128]{1,0:T(8,128)S(1)}) custom-call(f32[16,128]{1,0:T(8,128)S(1)} %get-tuple-element.34.factor_ref, bf16[2048,1024]{1,0:T(8,128)(2,1)S(1)} %get-tuple-element.31.refs_3_.docs_ref, f32[128,2048]{1,0:T(8,128)S(1)} %get-tuple-element.35.part_ref), custom_call_target="tpu_custom_call" | custom-call | flops 536870912 | bytes 5251072 | tf_op jit(solution)/shard_map/pallas_call | solution.py:217
  21.8 0.8 %collective-permute-done.7.got_ref = bf16[128,1152]{1,0:T(8,128)(2,1)S(1)} collective-permute-done((bf16[128,1152]{1,0:T(8,128)(2,1)S(1)}, bf16[128,1152]{1,0:T(8,128)(2,1)S(1)}, u32[]{:S(2)}, u32[]{:S(2)}) %collective-permute-start.7) | collective-permute-done | bytes 294944 | tf_op jit(solution)/shard_map/ppermute | solution.py:17
  22.6 0.2 shard_map.55
  22.8 1.7 %collective-permute-start.8 = (bf16[32,1152]{1,0:T(8,128)(2,1)S(1)}, bf16[32,1152]{1,0:T(8,128)(2,1)S(1)}, u32[]{:S(2)}, u32[]{:S(2)}) collective-permute-start(bf16[32,1152]{1,0:T(8,128)(2,1)S(1)} %get-tuple-element.41), channel_id=1, source_target_pairs={{7,0},{6,1},{5,2},{4,3},{3,4},{2,5},{1,6},{0,7},{15,8},{14,9},{13,... | collective-permute-start | bytes 221192 | tf_op jit(solution)/shard_map/ppermute | solution.py:266
  24.5 0.7 %collective-permute-start.9 = (bf16[32,1152]{1,0:T(8,128)(2,1)S(1)}, bf16[32,1152]{1,0:T(8,128)(2,1)S(1)}, u32[]{:S(2)}, u32[]{:S(2)}) collective-permute-start(bf16[32,1152]{1,0:T(8,128)(2,1)S(1)} %get-tuple-element.42), channel_id=1, source_target_pairs={{3,0},{4,1},{1,2},{6,3},{7,4},{0,5},{5,6},{2,7},{11,8},{12,9},{9,1... | collective-permute-start | bytes 221192 | tf_op jit(solution)/shard_map/ppermute | solution.py:266
  25.2 1.0 %collective-permute-start.10 = (bf16[32,1152]{1,0:T(8,128)(2,1)S(1)}, bf16[32,1152]{1,0:T(8,128)(2,1)S(1)}, u32[]{:S(2)}, u32[]{:S(2)}) collective-permute-start(bf16[32,1152]{1,0:T(8,128)(2,1)S(1)} %get-tuple-element.43), channel_id=1, source_target_pairs={{5,0},{2,1},{7,2},{0,3},{1,4},{6,5},{3,6},{4,7},{13,8},{10,9},{15,... | collective-permute-start | bytes 221192 | tf_op jit(solution)/shard_map/ppermute | solution.py:266
  26.2 1.8 %collective-permute-done.8.refs_0_ = bf16[32,1152]{1,0:T(8,128)(2,1)S(1)} collective-permute-done((bf16[32,1152]{1,0:T(8,128)(2,1)S(1)}, bf16[32,1152]{1,0:T(8,128)(2,1)S(1)}, u32[]{:S(2)}, u32[]{:S(2)}) %collective-permute-start.8) | collective-permute-done | bytes 73760 | tf_op jit(solution)/shard_map/ppermute | solution.py:266
  28.0 1.1 %collective-permute-done.9.refs_1_ = bf16[32,1152]{1,0:T(8,128)(2,1)S(1)} collective-permute-done((bf16[32,1152]{1,0:T(8,128)(2,1)S(1)}, bf16[32,1152]{1,0:T(8,128)(2,1)S(1)}, u32[]{:S(2)}, u32[]{:S(2)}) %collective-permute-start.9) | collective-permute-done | bytes 73760 | tf_op jit(solution)/shard_map/ppermute | solution.py:266
  29.1 0.8 %collective-permute-done.10.refs_2_ = bf16[32,1152]{1,0:T(8,128)(2,1)S(1)} collective-permute-done((bf16[32,1152]{1,0:T(8,128)(2,1)S(1)}, bf16[32,1152]{1,0:T(8,128)(2,1)S(1)}, u32[]{:S(2)}, u32[]{:S(2)}) %collective-permute-start.10) | collective-permute-done | bytes 73760 | tf_op jit(solution)/shard_map/ppermute | solution.py:266
  29.9 0.0 copy-done
  29.9 0.8 %shard_map.56 = (f32[32,1024]{1,0:T(8,128)}, f32[1,32]{1,0:T(1,128)}) custom-call(f32[32,1024]{1,0:T(8,128)S(1)} %get-tuple-element.39.own_ref, f32[32,128]{1,0:T(8,128)S(1)} %get-tuple-element.40.own_mass_ref, f32[32,1024]{1,0:T(8,128)S(1)} %copy-done, bf16[32,1152]{1,0:T(8,128)(2,1)S(1)} %collective-permute-done.8.refs_0_, ...), custom_call_target="tpu_custom_call" | custom-call | bytes 499712 | tf_op jit(solution)/shard_map/pallas_call | solution.py:217
  (4 shorter events, 0.0 us)
Async XLA Ops:
  1.5 8.5 %collective-permute-start.2 = (bf16[32,1024]{1,0:T(8,128)(2,1)S(1)}, bf16[32,1024]{1,0:T(8,128)(2,1)S(1)}, u32[]{:S(2)}, u32[]{:S(2)}) collective-permute-start(bf16[32,1024]{1,0:T(8,128)(2,1)S(1)} %convert_element_type.3.follow_ref), channel_id=1, source_target_pairs={{0,7},{1,6},{2,5},{3,4},{4,3},{5,2},{6,1},{7,0},{8,15},{9,14},{10,... | collective-permute-start | bytes 196616 | tf_op jit(solution)/shard_map/ppermute | solution.py:234
  4.9 5.1 %collective-permute-start.1 = (bf16[32,1024]{1,0:T(8,128)(2,1)S(1)}, bf16[32,1024]{1,0:T(8,128)(2,1)S(1)}, u32[]{:S(2)}, u32[]{:S(2)}) collective-permute-start(bf16[32,1024]{1,0:T(8,128)(2,1)S(1)} %convert_element_type.3.follow_ref), channel_id=1, source_target_pairs={{0,5},{1,2},{2,7},{3,0},{4,1},{5,6},{6,3},{7,4},{8,13},{9,10},{10,... | collective-permute-start | bytes 196616 | tf_op jit(solution)/shard_map/ppermute | solution.py:234
  5.7 4.3 %collective-permute-start = (bf16[32,1024]{1,0:T(8,128)(2,1)S(1)}, bf16[32,1024]{1,0:T(8,128)(2,1)S(1)}, u32[]{:S(2)}, u32[]{:S(2)}) collective-permute-start(bf16[32,1024]{1,0:T(8,128)(2,1)S(1)} %convert_element_type.3.follow_ref), channel_id=1, source_target_pairs={{0,3},{1,4},{2,1},{3,6},{4,7},{5,0},{6,5},{7,2},{8,11},{9,12},{10,... | collective-permute-start | bytes 196616 | tf_op jit(solution)/shard_map/ppermute | solution.py:234
  10.1 1.6 %collective-permute-start.3 = (bf16[128,1024]{1,0:T(8,128)(2,1)S(1)}, bf16[128,1024]{1,0:T(8,128)(2,1)S(1)}, u32[]{:S(2)}, u32[]{:S(2)}) collective-permute-start(bf16[128,1024]{1,0:T(8,128)(2,1)S(1)} %constant_dynamic-update-slice_fusion.table_ref), channel_id=1, source_target_pairs={{0,1},{1,0},{2,3},{3,2},{4,5},{5,4},{6,7},{7,6},{8,9},{9,8},{10,11... | collective-permute-start | bytes 786440 | tf_op jit(solution)/shard_map/ppermute | solution.py:17
  12.6 6.4 %collective-permute-start.6 = (f32[16,128]{1,0:T(8,128)S(1)}, f32[16,128]{1,0:T(8,128)S(1)}, u32[]{:S(2)}, u32[]{:S(2)}) collective-permute-start(f32[16,128]{1,0:T(8,128)S(1)} %get-tuple-element.29.follow_ref), channel_id=1, source_target_pairs={{0,16},{8,24},{16,8},{24,0},{1,17},{9,25},{17,9},{25,1},{2,18},{10... | collective-permute-start | bytes 24584 | tf_op jit(solution)/shard_map/ppermute | solution.py:245
  15.2 4.5 %collective-permute-start.5 = (f32[16,128]{1,0:T(8,128)S(1)}, f32[16,128]{1,0:T(8,128)S(1)}, u32[]{:S(2)}, u32[]{:S(2)}) collective-permute-start(f32[16,128]{1,0:T(8,128)S(1)} %get-tuple-element.29.follow_ref), channel_id=1, source_target_pairs={{0,24},{8,16},{16,0},{24,8},{1,25},{9,17},{17,1},{25,9},{2,26},{10... | collective-permute-start | bytes 24584 | tf_op jit(solution)/shard_map/ppermute | solution.py:245
  16.5 3.7 %collective-permute-start.4 = (f32[16,128]{1,0:T(8,128)S(1)}, f32[16,128]{1,0:T(8,128)S(1)}, u32[]{:S(2)}, u32[]{:S(2)}) collective-permute-start(f32[16,128]{1,0:T(8,128)S(1)} %get-tuple-element.29.follow_ref), channel_id=1, source_target_pairs={{0,8},{8,0},{16,24},{24,16},{1,9},{9,1},{17,25},{25,17},{2,10},{10... | collective-permute-start | bytes 24584 | tf_op jit(solution)/shard_map/ppermute | solution.py:245
  21.0 8.9 %copy-start = (f32[32,1024]{1,0:T(8,128)S(1)}, f32[32,1024]{1,0:T(8,128)}, u32[]{:S(2)}) copy-start(f32[32,1024]{1,0:T(8,128)} %cent_ref.1) | copy-start | bytes 393220
  21.0 1.6 %collective-permute-start.7 = (bf16[128,1152]{1,0:T(8,128)(2,1)S(1)}, bf16[128,1152]{1,0:T(8,128)(2,1)S(1)}, u32[]{:S(2)}, u32[]{:S(2)}) collective-permute-start(bf16[128,1152]{1,0:T(8,128)(2,1)S(1)} %get-tuple-element.38), channel_id=1, source_target_pairs={{0,1},{1,0},{2,3},{3,2},{4,5},{5,4},{6,7},{7,6},{8,9},{9,8},{10,11... | collective-permute-start | bytes 884744 | tf_op jit(solution)/shard_map/ppermute | solution.py:17
  22.8 5.2 %collective-permute-start.8 = (bf16[32,1152]{1,0:T(8,128)(2,1)S(1)}, bf16[32,1152]{1,0:T(8,128)(2,1)S(1)}, u32[]{:S(2)}, u32[]{:S(2)}) collective-permute-start(bf16[32,1152]{1,0:T(8,128)(2,1)S(1)} %get-tuple-element.41), channel_id=1, source_target_pairs={{7,0},{6,1},{5,2},{4,3},{3,4},{2,5},{1,6},{0,7},{15,8},{14,9},{13,... | collective-permute-start | bytes 221192 | tf_op jit(solution)/shard_map/ppermute | solution.py:266
  24.5 4.6 %collective-permute-start.9 = (bf16[32,1152]{1,0:T(8,128)(2,1)S(1)}, bf16[32,1152]{1,0:T(8,128)(2,1)S(1)}, u32[]{:S(2)}, u32[]{:S(2)}) collective-permute-start(bf16[32,1152]{1,0:T(8,128)(2,1)S(1)} %get-tuple-element.42), channel_id=1, source_target_pairs={{3,0},{4,1},{1,2},{6,3},{7,4},{0,5},{5,6},{2,7},{11,8},{12,9},{9,1... | collective-permute-start | bytes 221192 | tf_op jit(solution)/shard_map/ppermute | solution.py:266
  25.2 4.7 %collective-permute-start.10 = (bf16[32,1152]{1,0:T(8,128)(2,1)S(1)}, bf16[32,1152]{1,0:T(8,128)(2,1)S(1)}, u32[]{:S(2)}, u32[]{:S(2)}) collective-permute-start(bf16[32,1152]{1,0:T(8,128)(2,1)S(1)} %get-tuple-element.43), channel_id=1, source_target_pairs={{5,0},{2,1},{7,2},{0,3},{1,4},{6,5},{3,6},{4,7},{13,8},{10,9},{15,... | collective-permute-start | bytes 221192 | tf_op jit(solution)/shard_map/ppermute | solution.py:266

commit v16 on v15

--- a/solution.py
+++ b/solution.py
@@ -20,16 +20,16 @@
 def chip_plan(n):
     near = list(range(2, n - 2, 2))
     turned = near[len(near) // 2:] + near[:len(near) // 2]
-    masks = list(zip(near, turned)) + [(n - 2, n - 2)]
+    masks = [(n - 2, n - 2)] + list(zip(near, turned))
     return [[(i, i ^ pair[i % 2] ^ 1) for i in range(n)] for pair in masks]
 
 
 def group_plan(g):
     if g == 4:
         return [
-            [(0, 1), (1, 0), (2, 3), (3, 2)],
-            [(0, 3), (1, 2), (2, 0), (3, 1)],
-            [(0, 2), (1, 3), (2, 1), (3, 0)],
+            [(0, 1), (1, 3), (2, 0), (3, 2)],
+            [(0, 3), (1, 2), (2, 1), (3, 0)],
+            [(0, 2), (1, 0), (2, 3), (3, 1)],
         ]
     return [[(i, i ^ m) for i in range(g)] for m in range(1, g)]
 
@@ -40,44 +40,34 @@
     return parts[0]
 
 
-def transpose_kernel(chunk, source_ref, follow_ref, docs_ref, own_ref, landing, sems):
+def load_kernel(chunk, source_ref, follow_ref, docs_t_ref, own_ref, *refs):
+    *docs_refs, sems = refs
+    size = docs_refs[0].shape[0]
     copies = []
-    for i, start in enumerate(range(0, source_ref.shape[0], chunk)):
-        here = pl.ds(start, chunk)
-        copies.append(pltpu.make_async_copy(source_ref.at[here], landing.at[here], sems.at[i]))
+    for start in range(0, source_ref.shape[0], chunk):
+        target = docs_refs[start // size].at[pl.ds(start % size, chunk)]
+        sem = sems.at[start // chunk]
+        copies.append(pltpu.make_async_copy(source_ref.at[pl.ds(start, chunk)], target, sem))
         copies[-1].start()
     own_ref[...] = follow_ref[...]
     for i, copy in enumerate(copies):
         copy.wait()
-        here = slice(i * chunk, (i + 1) * chunk)
-        docs_ref[:, here] = landing[here, :].T
-
-
-def load_kernel(source_ref, follow_ref, docs_ref, own_ref, sem):
-    copy = pltpu.make_async_copy(source_ref, docs_ref, sem)
-    copy.start()
-    own_ref[...] = follow_ref[...]
-    copy.wait()
-
-
-def load(source, follow, chunk=0):
+        start = i * chunk
+        landed = docs_refs[start // size][start % size:start % size + chunk, :]
+        docs_t_ref[:, start:start + chunk] = landed.T
+
+
+def load(source, follow, chunk, pieces):
     count, width = source.shape
-    kernel, dims, scratch = load_kernel, (count, width), [pltpu.SemaphoreType.DMA]
-    if chunk:
-        kernel, dims = functools.partial(transpose_kernel, chunk), (width, count)
-        scratch = [
-            pltpu.VMEM((count, width), source.dtype),
-            pltpu.SemaphoreType.DMA((count // chunk,)),
-        ]
+    piece = shape((count // pieces, width), source.dtype)
+    outs = [shape((width, count), source.dtype), shape(follow.shape, follow.dtype)]
     return pl.pallas_call(
-        kernel,
-        out_shape=[shape(dims, source.dtype), shape(follow.shape, follow.dtype)],
+        functools.partial(load_kernel, chunk),
+        out_shape=outs + [piece] * pieces,
         in_specs=[pl.BlockSpec(memory_space=pltpu.HBM), VMEM],
-        out_specs=[VMEM, VMEM],
-        scratch_shapes=scratch,
-        compiler_params=pltpu.CompilerParams(
-            vmem_limit_bytes=(4 << 20) + (2 * source.nbytes if chunk else 0)
-        ),
+        out_specs=[VMEM] * (2 + pieces),
+        scratch_shapes=[pltpu.SemaphoreType.DMA((count // chunk,))],
+        compiler_params=pltpu.CompilerParams(vmem_limit_bytes=(4 << 20) + 2 * source.nbytes),
         cost_estimate=pl.CostEstimate(
             flops=0, bytes_accessed=2 * source.nbytes, transcendentals=0
         ),
@@ -117,7 +107,7 @@
     lse_ref[...] = top + jnp.log(total)
 
 
-def weighted_sums(chunk, factor, docs_ref, part_ref, resp_ref, store):
+def weighted_sums(chunk, factor, docs_refs, part_ref, resp_ref, store):
     rows, count = part_ref.shape
     mass = jnp.zeros((rows, LANES), jnp.float32)
     for i in range(count // LANES):
@@ -125,9 +115,17 @@
         resp = part_ref[:, cols] * factor[i:i + 1]
         mass += resp
         resp_ref[:, cols] = resp.astype(jnp.bfloat16)
-    for start in range(0, docs_ref.shape[1], chunk):
+    size, width = docs_refs[0].shape
+    for start in range(0, width, chunk):
         cols = slice(start, start + chunk)
-        store(cols, jnp.dot(resp_ref[...], docs_ref[:, cols], preferred_element_type=jnp.float32))
+        terms = [
+            jnp.dot(
+                resp_ref[:, i * size:(i + 1) * size], ref[:, cols],
+                preferred_element_type=jnp.float32,
+            )
+            for i, ref in enumerate(docs_refs)
+        ]
+        store(cols, tree(terms, jnp.add))
     return jnp.sum(mass, axis=1, keepdims=True)
 
 
@@ -143,10 +141,9 @@
     return wide[:, :width], wide[:, width:width + 1] + wide[:, width + 1:width + 2]
 
 
-def send_kernel(groups, plan, chunk, me_ref, lse_ref, *refs):
-    got_refs = refs[:len(plan)]
-    docs_ref, part_ref, top_ref, keep_top_ref = refs[len(plan):len(plan) + 4]
-    doc_lse_ref, factor_ref, send_ref, resp_ref = refs[len(plan) + 4:]
+def send_kernel(groups, plan, chunk, me_ref, lse_ref, part_ref, top_ref, keep_top_ref, *refs):
+    got_refs, docs_refs = refs[:len(plan)], refs[len(plan):-4]
+    doc_lse_ref, factor_ref, send_ref, resp_ref = refs[-4:]
     me = me_ref[0]
     parts = [lse_ref[...]] * groups
     for got_ref, pairs in zip(got_refs, plan):
@@ -162,15 +159,17 @@
     def store(cols, term):
         send_ref[:, cols] = term.astype(jnp.bfloat16)
 
-    mass = weighted_sums(chunk, factor, docs_ref, part_ref, resp_ref, store)
-    send_ref[:, docs_ref.shape[1]:] = mass_lanes(mass)
-
-
-def keep_kernel(chunk, factor_ref, docs_ref, part_ref, keep_ref, keep_mass_ref, resp_ref):
+    mass = weighted_sums(chunk, factor, docs_refs, part_ref, resp_ref, store)
+    send_ref[:, docs_refs[0].shape[1]:] = mass_lanes(mass)
+
+
+def keep_kernel(chunk, factor_ref, part_ref, *refs):
+    *docs_refs, keep_ref, keep_mass_ref, resp_ref = refs
+
     def store(cols, term):
         keep_ref[:, cols] = term
 
-    mass = weighted_sums(chunk, factor_ref[...], docs_ref, part_ref, resp_ref, store)
+    mass = weighted_sums(chunk, factor_ref[...], docs_refs, part_ref, resp_ref, store)
     keep_mass_ref[...] = jnp.broadcast_to(mass, keep_mass_ref.shape)
 
 
@@ -232,7 +231,7 @@
         rounded = centroids.astype(jnp.bfloat16)
         routes = chip_plan(n)
         blocks = [lax.ppermute(rounded, "dev", pairs) for pairs in routes]
-        docs_t, own = load(docs, rounded, chunk)
+        docs_t, own, *docs = load(docs, rounded, chunk, 4)
         mine = jnp.concatenate([own] + blocks, axis=0)
         theirs = swap(mine, "dev", n, 1)
         part, top, total = call(
@@ -243,18 +242,17 @@
             docs_t, theirs, top, total, flops=flops,
         )
         others = [lax.ppermute(lse, "cgrp", pairs) for pairs in plan]
-        docs, lse = load(docs, lse)
         doc_lse, factor, send = call(
             functools.partial(send_kernel, g, plan, chunk),
             [shape((count // LANES, LANES)), shape((count // LANES, LANES)), shape((half, width + LANES), jnp.bfloat16)],
-            lax.axis_index("cgrp").reshape(1), lse, *others, docs, other_part, other_top, top,
+            lax.axis_index("cgrp").reshape(1), lse, other_part, other_top, top, *others, *docs,
             scratch=resp, flops=flops,
         )
         got = swap(send, "dev", n, 1)
         keep, keep_mass = call(
             functools.partial(keep_kernel, chunk),
             [shape((half, width)), shape((half, LANES))],
-            factor, docs, part, scratch=resp, flops=flops,
+            factor, part, *docs, scratch=resp, flops=flops,
         )
         own, own_mass, *sends = call(
             fold_kernel,
@@ -264,7 +262,7 @@
         )
         arrived = [
             lax.ppermute(x, "dev", [(target, source) for source, target in pairs])
-            for x, pairs in zip(sends[-1:] + sends[:-1], routes[-1:] + routes[:-1])
+            for x, pairs in zip(sends, routes)
         ]
         result, mass = call(
             final_kernel, [shape((rows, width)), shape((1, rows))],

time: 30.9 us -> 34.5 us (1.12)
  local copies, waits for them, and re-layouts: 0.03 us -> 4.79 us
  Pallas kernels: 9.31 us -> 7.05 us
  starting transfers between devices: 13 us -> 14 us
    unnamed x5 -> x17, local copies, waits for them, and re-layouts: 0.02 us -> 4.78 us
    pallas_call x2 -> x1, Pallas kernels: 4.93 us -> 2.74 us  [load(): pl.pallas_call(functools.partial(load_kernel, chunk), out_shape=outs + [p...]
    ppermute x3, starting transfers between devices: 4.22 us -> 5.62 us  [body(): others = [lax.ppermute(lse, 'cgrp', pairs) for pairs in plan]]
    ppermute x3, waiting for transfers between devices: 1.09 us -> 2.07 us  [body(): others = [lax.ppermute(lse, 'cgrp', pairs) for pairs in plan]]
    ppermute x2, waiting for transfers between devices: 1.33 us -> 0.5 us  [swap(): return lax.ppermute(x, axis, [(i, i ^ mask) for i in range(size)])]
    ppermute x3, starting transfers between devices: 3.41 us -> 3 us  [body(): lax.ppermute(x, 'dev', [(target, source) for source, target in pairs])]
  transfers between devices with their start and end apart: 11 -> 11, of which waited for: 8 -> 7; matrix products, arithmetic and copies ran while one was open for 0% -> 0% of each run, Pallas kernels for 22% -> 13%
where the time goes in v16:
time: 34.5 us; the launch traced here: 34.2 us
  starting transfers between devices  14 us (41%)
  Pallas kernels  7.05 us (20%)
  waiting for transfers between devices  6.69 us (19%)
  local copies, waits for them, and re-layouts  4.79 us (14%)
  other arithmetic  0.92 us (3%)
  between operations  0.76 us (2%)
    ppermute x3, starting transfers between devices, body(): others = [lax.ppermute(lse, 'cgrp', pairs) for pairs in plan]  5.62 us
    ppermute x3, starting transfers between devices, body(): blocks = [lax.ppermute(rounded, 'dev', pairs) for pairs in routes]  5.14 us
    unnamed x17, local copies, waits for them, and re-layouts  4.78 us
    pallas_call x6, Pallas kernels, call(): pl.pallas_call(kernel, out_shape=outs, in_specs=[SMEM if x.dtype == jnp.i...  4.31 us
    ppermute x3, waiting for transfers between devices, body(): lax.ppermute(x, 'dev', [(target, source) for source, target in pairs])  3.51 us
    ppermute x3, starting transfers between devices, body(): lax.ppermute(x, 'dev', [(target, source) for source, target in pairs])  3 us
    pallas_call x1, Pallas kernels, load(): pl.pallas_call(functools.partial(load_kernel, chunk), out_shape=outs + [p...  2.74 us
    ppermute x3, waiting for transfers between devices, body(): others = [lax.ppermute(lse, 'cgrp', pairs) for pairs in plan]  2.07 us
  transfers between devices with their start and end apart: 11, of which 7 were waited for; matrix products, arithmetic and copies ran while one was open for 0% of the time, Pallas kernels for 13%

profile of v16, /device:TPU:0, one launch (start us, length us, event | category | flops | bytes accessed | tf_op | source)
XLA Modules:
  0.0 34.2 jit_solution(17178077074012459393)
XLA Ops:
  0.6 0.9 %convert_element_type.3.follow_ref = bf16[32,1024]{1,0:T(8,128)(2,1)S(1)} convert(f32[32,1024]{1,0:T(8,128)} %cent_ref.1) | non-fusion elementwise | flops 32768 | bytes 196608 | tf_op jit(solution)/shard_map/convert_element_type | solution.py:231
  1.5 3.4 %collective-permute-start = (bf16[32,1024]{1,0:T(8,128)(2,1)S(1)}, bf16[32,1024]{1,0:T(8,128)(2,1)S(1)}, u32[]{:S(2)}, u32[]{:S(2)}) collective-permute-start(bf16[32,1024]{1,0:T(8,128)(2,1)S(1)} %convert_element_type.3.follow_ref), channel_id=1, source_target_pairs={{0,7},{1,6},{2,5},{3,4},{4,3},{5,2},{6,1},{7,0},{8,15},{9,14},{10,... | collective-permute-start | bytes 196616 | tf_op jit(solution)/shard_map/ppermute | solution.py:233
  4.9 0.8 %collective-permute-start.1 = (bf16[32,1024]{1,0:T(8,128)(2,1)S(1)}, bf16[32,1024]{1,0:T(8,128)(2,1)S(1)}, u32[]{:S(2)}, u32[]{:S(2)}) collective-permute-start(bf16[32,1024]{1,0:T(8,128)(2,1)S(1)} %convert_element_type.3.follow_ref), channel_id=1, source_target_pairs={{0,3},{1,4},{2,1},{3,6},{4,7},{5,0},{6,5},{7,2},{8,11},{9,12},{10,... | collective-permute-start | bytes 196616 | tf_op jit(solution)/shard_map/ppermute | solution.py:233
  5.8 0.9 %collective-permute-start.2 = (bf16[32,1024]{1,0:T(8,128)(2,1)S(1)}, bf16[32,1024]{1,0:T(8,128)(2,1)S(1)}, u32[]{:S(2)}, u32[]{:S(2)}) collective-permute-start(bf16[32,1024]{1,0:T(8,128)(2,1)S(1)} %convert_element_type.3.follow_ref), channel_id=1, source_target_pairs={{0,5},{1,2},{2,7},{3,0},{4,1},{5,6},{6,3},{7,4},{8,13},{9,10},{10,... | collective-permute-start | bytes 196616 | tf_op jit(solution)/shard_map/ppermute | solution.py:233
  6.7 2.7 %shard_map.49 = (bf16[1024,2048]{1,0:T(8,128)(2,1)S(1)}, bf16[32,1024]{1,0:T(8,128)(2,1)S(1)}, bf16[512,1024]{1,0:T(8,128)(2,1)S(1)}, bf16[512,1024]{1,0:T(8,128...) custom-call(bf16[2048,1024]{1,0:T(8,128)(2,1)} %source_ref.1, ...), custom_call_target="tpu_custom_call" | custom-call | bytes 8388608 | tf_op jit(solution)/shard_map/pallas_call | solution.py:64
  9.4 0.0 copy-start
  9.5 0.0 collective-permute-done
  9.5 0.0 collective-permute-done.1
  9.5 0.6 %collective-permute-done.2 = bf16[32,1024]{1,0:T(8,128)(2,1)S(1)} collective-permute-done((bf16[32,1024]{1,0:T(8,128)(2,1)S(1)}, bf16[32,1024]{1,0:T(8,128)(2,1)S(1)}, u32[]{:S(2)}, u32[]{:S(2)}) %collective-permute-start.2) | collective-permute-done | bytes 65568 | tf_op jit(solution)/shard_map/ppermute | solution.py:233
  10.1 0.2 collective-permute-start.3
  10.3 0.9 %shard_map.50 = (f32[128,2048]{1,0:T(8,128)S(1)}, f32[16,128]{1,0:T(8,128)S(1)}, f32[16,128]{1,0:T(8,128)S(1)}) custom-call(bf16[1024,2048]{1,0:T(8,128)(2,1)S(1)} %get-tuple-element.27.docs_ref, bf16[128,1024]{1,0:T(8,128)(2,1)S(1)} %constant_dynamic-update-slice_fusion.table_ref), custom_call_target="tpu_custom_call" | custom-call | flops 536870912 | bytes 4456448 | tf_op jit(solution)/shard_map/pallas_call | solution.py:216
  11.2 0.0 copy-start.2
  11.2 1.0 %copy-done.2 = f32[128,2048]{1,0:T(8,128)} copy-done((f32[128,2048]{1,0:T(8,128)}, f32[128,2048]{1,0:T(8,128)S(1)}, u32[]{:S(2)}) %copy-start.2) | copy-done | bytes 1048600
  12.2 0.0 collective-permute-done.3.table_ref
  12.2 0.9 %shard_map.51 = (f32[128,2048]{1,0:T(8,128)S(1)}, f32[16,128]{1,0:T(8,128)S(1)}, f32[16,128]{1,0:T(8,128)S(1)}) custom-call(bf16[1024,2048]{1,0:T(8,128)(2,1)S(1)} %get-tuple-element.27.docs_ref, bf16[128,1024]{1,0:T(8,128)(2,1)S(1)} %collective-permute-done.3.table_ref, f32[16,128]{1,0:T(8,128)S(1)} %get-tuple-element.29.first_top_ref.keep_top_ref, ...), custom_call_target="tpu_custom_call" | custom-call | flops 536870912 | bytes 4472832 | tf_op jit(solution)/shard_map/pallas_call | solution.py:216
  13.1 0.0 copy-done
  13.1 0.0 copy-start.4
  13.1 1.0 %copy-done.4 = f32[128,2048]{1,0:T(8,128)} copy-done((f32[128,2048]{1,0:T(8,128)}, f32[128,2048]{1,0:T(8,128)S(1)}, u32[]{:S(2)}) %copy-start.4) | copy-done | bytes 1048600
  14.1 1.6 %collective-permute-start.4 = (f32[16,128]{1,0:T(8,128)S(1)}, f32[16,128]{1,0:T(8,128)S(1)}, u32[]{:S(2)}, u32[]{:S(2)}) collective-permute-start(f32[16,128]{1,0:T(8,128)S(1)} %get-tuple-element.31.lse_ref), channel_id=1, source_target_pairs={{0,8},{8,24},{16,0},{24,16},{1,9},{9,25},{17,1},{25,17},{2,10},{10... | collective-permute-start | bytes 24584 | tf_op jit(solution)/shard_map/ppermute | solution.py:244
  15.7 2.5 %collective-permute-start.5 = (f32[16,128]{1,0:T(8,128)S(1)}, f32[16,128]{1,0:T(8,128)S(1)}, u32[]{:S(2)}, u32[]{:S(2)}) collective-permute-start(f32[16,128]{1,0:T(8,128)S(1)} %get-tuple-element.31.lse_ref), channel_id=1, source_target_pairs={{0,24},{8,16},{16,8},{24,0},{1,25},{9,17},{17,9},{25,1},{2,26},{10... | collective-permute-start | bytes 24584 | tf_op jit(solution)/shard_map/ppermute | solution.py:244
  18.2 1.6 %collective-permute-start.6 = (f32[16,128]{1,0:T(8,128)S(1)}, f32[16,128]{1,0:T(8,128)S(1)}, u32[]{:S(2)}, u32[]{:S(2)}) collective-permute-start(f32[16,128]{1,0:T(8,128)S(1)} %get-tuple-element.31.lse_ref), channel_id=1, source_target_pairs={{0,16},{8,0},{16,24},{24,8},{1,17},{9,1},{17,25},{25,9},{2,18},{10... | collective-permute-start | bytes 24584 | tf_op jit(solution)/shard_map/ppermute | solution.py:244
  19.7 0.0 collective-permute-done.4.refs_0_
  19.7 1.4 %collective-permute-done.5.refs_1_ = f32[16,128]{1,0:T(8,128)S(1)} collective-permute-done((f32[16,128]{1,0:T(8,128)S(1)}, f32[16,128]{1,0:T(8,128)S(1)}, u32[]{:S(2)}, u32[]{:S(2)}) %collective-permute-start.5) | collective-permute-done | bytes 8224 | tf_op jit(solution)/shard_map/ppermute | solution.py:244
  21.1 0.7 %collective-permute-done.6.refs_2_ = f32[16,128]{1,0:T(8,128)S(1)} collective-permute-done((f32[16,128]{1,0:T(8,128)S(1)}, f32[16,128]{1,0:T(8,128)S(1)}, u32[]{:S(2)}, u32[]{:S(2)}) %collective-permute-start.6) | collective-permute-done | bytes 8224 | tf_op jit(solution)/shard_map/ppermute | solution.py:244
  21.8 0.0 copy-start.1
  21.8 1.2 %copy-done.1 = bf16[512,1024]{1,0:T(8,128)(2,1)S(1)} copy-done((bf16[512,1024]{1,0:T(8,128)(2,1)S(1)}, bf16[512,1024]{1,0:T(8,128)(2,1)}, u32[]{:S(2)}) %copy-start.1) | copy-done | bytes 1048600
  23.0 0.0 copy-start.5
  23.0 1.2 %copy-done.5 = f32[128,2048]{1,0:T(8,128)S(1)} copy-done((f32[128,2048]{1,0:T(8,128)S(1)}, f32[128,2048]{1,0:T(8,128)}, u32[]{:S(2)}) %copy-start.5) | copy-done | bytes 1048600
  24.3 0.0 copy-start.3
  24.3 0.8 %shard_map.52 = (f32[16,128]{1,0:T(8,128)}, f32[16,128]{1,0:T(8,128)S(1)}, bf16[128,1152]{1,0:T(8,128)(2,1)S(1)}) custom-call(s32[1]{0:T(128)} %bitcast.me_ref, f32[16,128]{1,0:T(8,128)S(1)} %get-tuple-element.31.lse_ref, f32[128,2048]{1,0:T(8,128)S(1)} %copy-done.5, f32[16,128]{1,0:T(8,128)S(1)} %get-tuple-element.33.top_ref, ...), custom_call_target="tpu_custom_call" | custom-call | flops 536870912 | bytes 5292036 | tf_op jit(solution)/shard_map/pallas_call | solution.py:216
  25.1 0.0 copy-start.6
  25.1 0.1 collective-permute-start.7
  25.2 0.3 copy-done.3
  25.5 0.7 %shard_map.53 = (f32[128,1024]{1,0:T(8,128)S(1)}, f32[128,128]{1,0:T(8,128)S(1)}) custom-call(f32[16,128]{1,0:T(8,128)S(1)} %get-tuple-element.38.factor_ref, f32[128,2048]{1,0:T(8,128)S(1)} %copy-done.3, bf16[512,1024]{1,0:T(8,128)(2,1)S(1)} %get-tuple-element.34.refs_3_.refs_0_, bf16[512,1024]{1,0:T(8,128)(2,1)S(1)} %get-tuple-element.35.refs_4_.refs_1_, ...), custom_call_target="tpu_custom_call" | custom-call | flops 536870912 | bytes 5251072 | tf_op jit(solution)/shard_map/pallas_call | solution.py:216
  26.2 0.5 %collective-permute-done.7.got_ref = bf16[128,1152]{1,0:T(8,128)(2,1)S(1)} collective-permute-done((bf16[128,1152]{1,0:T(8,128)(2,1)S(1)}, bf16[128,1152]{1,0:T(8,128)(2,1)S(1)}, u32[]{:S(2)}, u32[]{:S(2)}) %collective-permute-start.7) | collective-permute-done | bytes 294944 | tf_op jit(solution)/shard_map/ppermute | solution.py:17
  26.7 0.2 shard_map.54
  26.9 0.8 %collective-permute-start.10 = (bf16[32,1152]{1,0:T(8,128)(2,1)S(1)}, bf16[32,1152]{1,0:T(8,128)(2,1)S(1)}, u32[]{:S(2)}, u32[]{:S(2)}) collective-permute-start(bf16[32,1152]{1,0:T(8,128)(2,1)S(1)} %get-tuple-element.47), channel_id=1, source_target_pairs={{5,0},{2,1},{7,2},{0,3},{1,4},{6,5},{3,6},{4,7},{13,8},{10,9},{15,... | collective-permute-start | bytes 221192 | tf_op jit(solution)/shard_map/ppermute | solution.py:264
  27.7 1.4 %collective-permute-start.8 = (bf16[32,1152]{1,0:T(8,128)(2,1)S(1)}, bf16[32,1152]{1,0:T(8,128)(2,1)S(1)}, u32[]{:S(2)}, u32[]{:S(2)}) collective-permute-start(bf16[32,1152]{1,0:T(8,128)(2,1)S(1)} %get-tuple-element.45), channel_id=1, source_target_pairs={{7,0},{6,1},{5,2},{4,3},{3,4},{2,5},{1,6},{0,7},{15,8},{14,9},{13,... | collective-permute-start | bytes 221192 | tf_op jit(solution)/shard_map/ppermute | solution.py:264
  29.2 0.7 %collective-permute-start.9 = (bf16[32,1152]{1,0:T(8,128)(2,1)S(1)}, bf16[32,1152]{1,0:T(8,128)(2,1)S(1)}, u32[]{:S(2)}, u32[]{:S(2)}) collective-permute-start(bf16[32,1152]{1,0:T(8,128)(2,1)S(1)} %get-tuple-element.46), channel_id=1, source_target_pairs={{3,0},{4,1},{1,2},{6,3},{7,4},{0,5},{5,6},{2,7},{11,8},{12,9},{9,1... | collective-permute-start | bytes 221192 | tf_op jit(solution)/shard_map/ppermute | solution.py:264
  29.9 0.8 %collective-permute-done.10.refs_2_ = bf16[32,1152]{1,0:T(8,128)(2,1)S(1)} collective-permute-done((bf16[32,1152]{1,0:T(8,128)(2,1)S(1)}, bf16[32,1152]{1,0:T(8,128)(2,1)S(1)}, u32[]{:S(2)}, u32[]{:S(2)}) %collective-permute-start.10) | collective-permute-done | bytes 73760 | tf_op jit(solution)/shard_map/ppermute | solution.py:264
  30.7 2.3 %collective-permute-done.8.refs_0_ = bf16[32,1152]{1,0:T(8,128)(2,1)S(1)} collective-permute-done((bf16[32,1152]{1,0:T(8,128)(2,1)S(1)}, bf16[32,1152]{1,0:T(8,128)(2,1)S(1)}, u32[]{:S(2)}, u32[]{:S(2)}) %collective-permute-start.8) | collective-permute-done | bytes 73760 | tf_op jit(solution)/shard_map/ppermute | solution.py:264
  33.0 0.4 %collective-permute-done.9.refs_1_ = bf16[32,1152]{1,0:T(8,128)(2,1)S(1)} collective-permute-done((bf16[32,1152]{1,0:T(8,128)(2,1)S(1)}, bf16[32,1152]{1,0:T(8,128)(2,1)S(1)}, u32[]{:S(2)}, u32[]{:S(2)}) %collective-permute-start.9) | collective-permute-done | bytes 73760 | tf_op jit(solution)/shard_map/ppermute | solution.py:264
  33.4 0.0 copy-done.6
  33.4 0.8 %shard_map.55 = (f32[32,1024]{1,0:T(8,128)}, f32[1,32]{1,0:T(1,128)}) custom-call(f32[32,1024]{1,0:T(8,128)S(1)} %get-tuple-element.43.own_ref, f32[32,128]{1,0:T(8,128)S(1)} %get-tuple-element.44.own_mass_ref, f32[32,1024]{1,0:T(8,128)S(1)} %copy-done.6, bf16[32,1152]{1,0:T(8,128)(2,1)S(1)} %collective-permute-done.8.refs_0_, ...), custom_call_target="tpu_custom_call" | custom-call | bytes 499712 | tf_op jit(solution)/shard_map/pallas_call | solution.py:216
  (4 shorter events, 0.0 us)
Async XLA Ops:
  1.5 7.9 %collective-permute-start = (bf16[32,1024]{1,0:T(8,128)(2,1)S(1)}, bf16[32,1024]{1,0:T(8,128)(2,1)S(1)}, u32[]{:S(2)}, u32[]{:S(2)}) collective-permute-start(bf16[32,1024]{1,0:T(8,128)(2,1)S(1)} %convert_element_type.3.follow_ref), channel_id=1, source_target_pairs={{0,7},{1,6},{2,5},{3,4},{4,3},{5,2},{6,1},{7,0},{8,15},{9,14},{10,... | collective-permute-start | bytes 196616 | tf_op jit(solution)/shard_map/ppermute | solution.py:233
  4.9 4.5 %collective-permute-start.1 = (bf16[32,1024]{1,0:T(8,128)(2,1)S(1)}, bf16[32,1024]{1,0:T(8,128)(2,1)S(1)}, u32[]{:S(2)}, u32[]{:S(2)}) collective-permute-start(bf16[32,1024]{1,0:T(8,128)(2,1)S(1)} %convert_element_type.3.follow_ref), channel_id=1, source_target_pairs={{0,3},{1,4},{2,1},{3,6},{4,7},{5,0},{6,5},{7,2},{8,11},{9,12},{10,... | collective-permute-start | bytes 196616 | tf_op jit(solution)/shard_map/ppermute | solution.py:233
  5.8 4.3 %collective-permute-start.2 = (bf16[32,1024]{1,0:T(8,128)(2,1)S(1)}, bf16[32,1024]{1,0:T(8,128)(2,1)S(1)}, u32[]{:S(2)}, u32[]{:S(2)}) collective-permute-start(bf16[32,1024]{1,0:T(8,128)(2,1)S(1)} %convert_element_type.3.follow_ref), channel_id=1, source_target_pairs={{0,5},{1,2},{2,7},{3,0},{4,1},{5,6},{6,3},{7,4},{8,13},{9,10},{10,... | collective-permute-start | bytes 196616 | tf_op jit(solution)/shard_map/ppermute | solution.py:233
  9.4 3.7 %copy-start = (bf16[512,1024]{1,0:T(8,128)(2,1)}, bf16[512,1024]{1,0:T(8,128)(2,1)S(1)}, u32[]{:S(2)}) copy-start(bf16[512,1024]{1,0:T(8,128)(2,1)S(1)} %get-tuple-element.37.refs_6_.refs_3_) | copy-start | bytes 3145732
  10.1 2.1 %collective-permute-start.3 = (bf16[128,1024]{1,0:T(8,128)(2,1)S(1)}, bf16[128,1024]{1,0:T(8,128)(2,1)S(1)}, u32[]{:S(2)}, u32[]{:S(2)}) collective-permute-start(bf16[128,1024]{1,0:T(8,128)(2,1)S(1)} %constant_dynamic-update-slice_fusion.table_ref), channel_id=1, source_target_pairs={{0,1},{1,0},{2,3},{3,2},{4,5},{5,4},{6,7},{7,6},{8,9},{9,8},{10,11... | collective-permute-start | bytes 786440 | tf_op jit(solution)/shard_map/ppermute | solution.py:17
  11.2 1.0 %copy-start.2 = (f32[128,2048]{1,0:T(8,128)}, f32[128,2048]{1,0:T(8,128)S(1)}, u32[]{:S(2)}) copy-start(f32[128,2048]{1,0:T(8,128)S(1)} %get-tuple-element.39.part_ref) | copy-start | bytes 3145732
  13.1 1.0 %copy-start.4 = (f32[128,2048]{1,0:T(8,128)}, f32[128,2048]{1,0:T(8,128)S(1)}, u32[]{:S(2)}) copy-start(f32[128,2048]{1,0:T(8,128)S(1)} %get-tuple-element.32.part_ref) | copy-start | bytes 3145732
  14.1 5.6 %collective-permute-start.4 = (f32[16,128]{1,0:T(8,128)S(1)}, f32[16,128]{1,0:T(8,128)S(1)}, u32[]{:S(2)}, u32[]{:S(2)}) collective-permute-start(f32[16,128]{1,0:T(8,128)S(1)} %get-tuple-element.31.lse_ref), channel_id=1, source_target_pairs={{0,8},{8,24},{16,0},{24,16},{1,9},{9,25},{17,1},{25,17},{2,10},{10... | collective-permute-start | bytes 24584 | tf_op jit(solution)/shard_map/ppermute | solution.py:244
  15.7 5.4 %collective-permute-start.5 = (f32[16,128]{1,0:T(8,128)S(1)}, f32[16,128]{1,0:T(8,128)S(1)}, u32[]{:S(2)}, u32[]{:S(2)}) collective-permute-start(f32[16,128]{1,0:T(8,128)S(1)} %get-tuple-element.31.lse_ref), channel_id=1, source_target_pairs={{0,24},{8,16},{16,8},{24,0},{1,25},{9,17},{17,9},{25,1},{2,26},{10... | collective-permute-start | bytes 24584 | tf_op jit(solution)/shard_map/ppermute | solution.py:244
  18.2 3.7 %collective-permute-start.6 = (f32[16,128]{1,0:T(8,128)S(1)}, f32[16,128]{1,0:T(8,128)S(1)}, u32[]{:S(2)}, u32[]{:S(2)}) collective-permute-start(f32[16,128]{1,0:T(8,128)S(1)} %get-tuple-element.31.lse_ref), channel_id=1, source_target_pairs={{0,16},{8,0},{16,24},{24,8},{1,17},{9,1},{17,25},{25,9},{2,18},{10... | collective-permute-start | bytes 24584 | tf_op jit(solution)/shard_map/ppermute | solution.py:244
  21.8 1.2 %copy-start.1 = (bf16[512,1024]{1,0:T(8,128)(2,1)S(1)}, bf16[512,1024]{1,0:T(8,128)(2,1)}, u32[]{:S(2)}) copy-start(bf16[512,1024]{1,0:T(8,128)(2,1)} %copy-done) | copy-start | bytes 3145732
  23.0 1.2 %copy-start.5 = (f32[128,2048]{1,0:T(8,128)S(1)}, f32[128,2048]{1,0:T(8,128)}, u32[]{:S(2)}) copy-start(f32[128,2048]{1,0:T(8,128)} %copy-done.4) | copy-start | bytes 3145732
  24.3 1.2 %copy-start.3 = (f32[128,2048]{1,0:T(8,128)S(1)}, f32[128,2048]{1,0:T(8,128)}, u32[]{:S(2)}) copy-start(f32[128,2048]{1,0:T(8,128)} %copy-done.2) | copy-start | bytes 3145732
  25.1 8.3 %copy-start.6 = (f32[32,1024]{1,0:T(8,128)S(1)}, f32[32,1024]{1,0:T(8,128)}, u32[]{:S(2)}) copy-start(f32[32,1024]{1,0:T(8,128)} %cent_ref.1) | copy-start | bytes 393220
  25.1 1.6 %collective-permute-start.7 = (bf16[128,1152]{1,0:T(8,128)(2,1)S(1)}, bf16[128,1152]{1,0:T(8,128)(2,1)S(1)}, u32[]{:S(2)}, u32[]{:S(2)}) collective-permute-start(bf16[128,1152]{1,0:T(8,128)(2,1)S(1)} %get-tuple-element.42), channel_id=1, source_target_pairs={{0,1},{1,0},{2,3},{3,2},{4,5},{5,4},{6,7},{7,6},{8,9},{9,8},{10,11... | collective-permute-start | bytes 884744 | tf_op jit(solution)/shard_map/ppermute | solution.py:17
  26.9 3.8 %collective-permute-start.10 = (bf16[32,1152]{1,0:T(8,128)(2,1)S(1)}, bf16[32,1152]{1,0:T(8,128)(2,1)S(1)}, u32[]{:S(2)}, u32[]{:S(2)}) collective-permute-start(bf16[32,1152]{1,0:T(8,128)(2,1)S(1)} %get-tuple-element.47), channel_id=1, source_target_pairs={{5,0},{2,1},{7,2},{0,3},{1,4},{6,5},{3,6},{4,7},{13,8},{10,9},{15,... | collective-permute-start | bytes 221192 | tf_op jit(solution)/shard_map/ppermute | solution.py:264
  27.7 5.2 %collective-permute-start.8 = (bf16[32,1152]{1,0:T(8,128)(2,1)S(1)}, bf16[32,1152]{1,0:T(8,128)(2,1)S(1)}, u32[]{:S(2)}, u32[]{:S(2)}) collective-permute-start(bf16[32,1152]{1,0:T(8,128)(2,1)S(1)} %get-tuple-element.45), channel_id=1, source_target_pairs={{7,0},{6,1},{5,2},{4,3},{3,4},{2,5},{1,6},{0,7},{15,8},{14,9},{13,... | collective-permute-start | bytes 221192 | tf_op jit(solution)/shard_map/ppermute | solution.py:264
  29.2 4.2 %collective-permute-start.9 = (bf16[32,1152]{1,0:T(8,128)(2,1)S(1)}, bf16[32,1152]{1,0:T(8,128)(2,1)S(1)}, u32[]{:S(2)}, u32[]{:S(2)}) collective-permute-start(bf16[32,1152]{1,0:T(8,128)(2,1)S(1)} %get-tuple-element.46), channel_id=1, source_target_pairs={{3,0},{4,1},{1,2},{6,3},{7,4},{0,5},{5,6},{2,7},{11,8},{12,9},{9,1... | collective-permute-start | bytes 221192 | tf_op jit(solution)/shard_map/ppermute | solution.py:264

commit v17 on v15

--- a/solution.py
+++ b/solution.py
@@ -17,11 +17,9 @@
     return lax.ppermute(x, axis, [(i, i ^ mask) for i in range(size)])
 
 
-def chip_plan(n):
-    near = list(range(2, n - 2, 2))
-    turned = near[len(near) // 2:] + near[:len(near) // 2]
-    masks = list(zip(near, turned)) + [(n - 2, n - 2)]
-    return [[(i, i ^ pair[i % 2] ^ 1) for i in range(n)] for pair in masks]
+def permute(x, n, even_mask, odd_mask):
+    masks = (even_mask ^ 1, odd_mask ^ 1)
+    return lax.ppermute(x, "dev", [(i, i ^ masks[i % 2]) for i in range(n)])
 
 
 def group_plan(g):
@@ -84,16 +82,25 @@
     )(pltpu.with_memory_space_constraint(source, pltpu.HBM), follow)
 
 
+def pair_kernel(own_ref, peer_ref, pair_ref, out_ref):
+    rows = own_ref.shape[0]
+    peer = peer_ref[...].astype(jnp.bfloat16)
+    pair_ref[:rows, :] = own_ref[...]
+    pair_ref[rows:, :] = peer
+    out_ref[...] = peer
+
+
 def put_row(ref, start, row):
     for i in range(row.shape[1] // LANES):
         at = start // LANES + i
         ref[at:at + 1, :] = row[:, i * LANES:(i + 1) * LANES]
 
 
-def scores_kernel(chunk, docs_ref, table_ref, part_ref, top_ref, sum_ref):
+def scores_kernel(chunk, docs_ref, *refs):
+    *table_refs, part_ref, top_ref, sum_ref = refs
     width, count = docs_ref.shape
     scale = 4.0 / math.sqrt(width)
-    table = table_ref[...]
+    table = jnp.concatenate([r[...] for r in table_refs], axis=0)
     wide = table.astype(jnp.float32)
     half_norms = 0.5 * jnp.sum(wide * wide, axis=1, keepdims=True)
     for start in range(0, count, chunk):
@@ -117,18 +124,29 @@
     lse_ref[...] = top + jnp.log(total)
 
 
-def weighted_sums(chunk, factor, docs_ref, part_ref, resp_ref, store):
-    rows, count = part_ref.shape
-    mass = jnp.zeros((rows, LANES), jnp.float32)
-    for i in range(count // LANES):
-        cols = slice(i * LANES, (i + 1) * LANES)
-        resp = part_ref[:, cols] * factor[i:i + 1]
-        mass += resp
-        resp_ref[:, cols] = resp.astype(jnp.bfloat16)
+def weighted_sums(chunk, blocks, docs_ref, resp_ref, store):
+    masses, at = [], 0
+    for part_ref, first, rows, factor in blocks:
+        mass = jnp.zeros((rows, LANES), jnp.float32)
+        for i in range(part_ref.shape[1] // LANES):
+            cols = slice(i * LANES, (i + 1) * LANES)
+            resp = part_ref[first:first + rows, cols] * factor[i:i + 1]
+            mass += resp
+            resp_ref[at:at + rows, cols] = resp.astype(jnp.bfloat16)
+        masses.append(jnp.sum(mass, axis=1, keepdims=True))
+        at += rows
     for start in range(0, docs_ref.shape[1], chunk):
         cols = slice(start, start + chunk)
         store(cols, jnp.dot(resp_ref[...], docs_ref[:, cols], preferred_element_type=jnp.float32))
-    return jnp.sum(mass, axis=1, keepdims=True)
+    return jnp.concatenate(masses, axis=0)
+
+
+def layout(rows, pairs):
+    send = [(0, 1)] + [(1, 2 * k) for k in range(pairs)]
+    send += [(0, 3 + 2 * k) for k in range(pairs)] + [(1, 2 * pairs)]
+    keep = [(0, 0)] + [(0, 2 + 2 * k) for k in range(pairs)]
+    keep += [(1, 1 + 2 * k) for k in range(pairs)] + [(0, 2 + 2 * pairs)]
+    return [[(which, i * rows) for which, i in blocks] for blocks in (send, keep)]
 
 
 def mass_lanes(mass):
@@ -143,10 +161,10 @@
     return wide[:, :width], wide[:, width:width + 1] + wide[:, width + 1:width + 2]
 
 
-def send_kernel(groups, plan, chunk, me_ref, lse_ref, *refs):
+def send_kernel(groups, plan, chunk, rows, blocks, me_ref, lse_ref, *refs):
     got_refs = refs[:len(plan)]
-    docs_ref, part_ref, top_ref, keep_top_ref = refs[len(plan):len(plan) + 4]
-    doc_lse_ref, factor_ref, send_ref, resp_ref = refs[len(plan) + 4:]
+    docs_ref, a_ref, b_ref, a_top_ref, b_top_ref = refs[len(plan):len(plan) + 5]
+    doc_lse_ref, a_factor_ref, b_factor_ref, send_ref, resp_ref = refs[len(plan) + 5:]
     me = me_ref[0]
     parts = [lse_ref[...]] * groups
     for got_ref, pairs in zip(got_refs, plan):
@@ -156,21 +174,28 @@
     best = tree(parts, jnp.maximum)
     doc_lse = best + jnp.log(tree([jnp.exp(x - best) for x in parts], jnp.add))
     doc_lse_ref[...] = doc_lse
-    factor_ref[...] = jnp.exp(keep_top_ref[...] - doc_lse)
-    factor = jnp.exp(top_ref[...] - doc_lse)
+    factors = [jnp.exp(r[...] - doc_lse) for r in (a_top_ref, b_top_ref)]
+    a_factor_ref[...], b_factor_ref[...] = factors
 
     def store(cols, term):
         send_ref[:, cols] = term.astype(jnp.bfloat16)
 
-    mass = weighted_sums(chunk, factor, docs_ref, part_ref, resp_ref, store)
+    blocks = [((a_ref, b_ref)[which], first, rows, factors[which]) for which, first in blocks]
+    mass = weighted_sums(chunk, blocks, docs_ref, resp_ref, store)
     send_ref[:, docs_ref.shape[1]:] = mass_lanes(mass)
 
 
-def keep_kernel(chunk, factor_ref, docs_ref, part_ref, keep_ref, keep_mass_ref, resp_ref):
+def keep_kernel(
+    chunk, rows, blocks, a_factor_ref, b_factor_ref, docs_ref, a_ref, b_ref,
+    keep_ref, keep_mass_ref, resp_ref,
+):
+    factors = (a_factor_ref[...], b_factor_ref[...])
+
     def store(cols, term):
         keep_ref[:, cols] = term
 
-    mass = weighted_sums(chunk, factor_ref[...], docs_ref, part_ref, resp_ref, store)
+    blocks = [((a_ref, b_ref)[which], first, rows, factors[which]) for which, first in blocks]
+    mass = weighted_sums(chunk, blocks, docs_ref, resp_ref, store)
     keep_mass_ref[...] = jnp.broadcast_to(mass, keep_mass_ref.shape)
 
 
@@ -227,34 +252,45 @@
             )(*args)
 
         flops = 2 * half * count * width
-        stats = [shape((half, count)), shape((count // LANES, LANES)), shape((count // LANES, LANES))]
+        stats = [shape((count // LANES, LANES))] * 2
         resp = [pltpu.VMEM((half, count), jnp.bfloat16)]
         rounded = centroids.astype(jnp.bfloat16)
-        routes = chip_plan(n)
-        blocks = [lax.ppermute(rounded, "dev", pairs) for pairs in routes]
+        near = list(range(2, n - 2, 2))
+        pairs = len(near) // 2
+        near_even, near_odd = near[:pairs], near[pairs:]
+        pair, peer = call(
+            pair_kernel, [shape((2 * rows, width), jnp.bfloat16), shape(rounded.shape, jnp.bfloat16)],
+            rounded, swap(centroids, "dev", n, 1),
+        )
+        far = permute(rounded, n, n - 2, n - 2)
+        came = [permute(pair, n, x, y) for x, y in zip(near_even, near_odd)]
         docs_t, own = load(docs, rounded, chunk)
-        mine = jnp.concatenate([own] + blocks, axis=0)
-        theirs = swap(mine, "dev", n, 1)
-        part, top, total = call(
-            functools.partial(scores_kernel, chunk), stats, docs_t, mine, flops=flops
-        )
-        other_part, other_top, lse = call(
-            functools.partial(last_scores_kernel, chunk), stats,
-            docs_t, theirs, top, total, flops=flops,
-        )
-        others = [lax.ppermute(lse, "cgrp", pairs) for pairs in plan]
+        came = jnp.concatenate(came + [far], axis=0)
+        came, own = lax.optimization_barrier((came, own))
+        theirs = swap(came, "dev", n, 1)
+        a_rows, b_rows = 2 * rows + came.shape[0], came.shape[0]
+        part_a, top_a, total = call(
+            functools.partial(scores_kernel, chunk), [shape((a_rows, count))] + stats,
+            docs_t, own, peer, came, flops=flops,
+        )
+        part_b, top_b, lse = call(
+            functools.partial(last_scores_kernel, chunk), [shape((b_rows, count))] + stats,
+            docs_t, theirs, top_a, total, flops=flops,
+        )
+        others = [lax.ppermute(lse, "cgrp", x) for x in plan]
         docs, lse = load(docs, lse)
-        doc_lse, factor, send = call(
-            functools.partial(send_kernel, g, plan, chunk),
-            [shape((count // LANES, LANES)), shape((count // LANES, LANES)), shape((half, width + LANES), jnp.bfloat16)],
-            lax.axis_index("cgrp").reshape(1), lse, *others, docs, other_part, other_top, top,
+        to_send, to_keep = layout(rows, pairs)
+        doc_lse, factor_a, factor_b, send = call(
+            functools.partial(send_kernel, g, plan, chunk, rows, to_send),
+            [shape((count // LANES, LANES))] * 3 + [shape((half, width + LANES), jnp.bfloat16)],
+            lax.axis_index("cgrp").reshape(1), lse, *others, docs, part_a, part_b, top_a, top_b,
             scratch=resp, flops=flops,
         )
         got = swap(send, "dev", n, 1)
         keep, keep_mass = call(
-            functools.partial(keep_kernel, chunk),
+            functools.partial(keep_kernel, chunk, rows, to_keep),
             [shape((half, width)), shape((half, LANES))],
-            factor, docs, part, scratch=resp, flops=flops,
+            factor_a, factor_b, docs, part_a, part_b, scratch=resp, flops=flops,
         )
         own, own_mass, *sends = call(
             fold_kernel,
@@ -262,10 +298,9 @@
             + [shape((rows, width + LANES), jnp.bfloat16)] * (n // 2 - 1),
             keep, keep_mass, got,
         )
-        arrived = [
-            lax.ppermute(x, "dev", [(target, source) for source, target in pairs])
-            for x, pairs in zip(sends[-1:] + sends[:-1], routes[-1:] + routes[:-1])
-        ]
+        masks = list(zip(near_odd + near_even, near_even + near_odd))
+        masks = [(n - 2, n - 2)] + masks
+        arrived = [permute(x, n, *m) for x, m in zip(sends[-1:] + sends[:-1], masks)]
         result, mass = call(
             final_kernel, [shape((rows, width)), shape((1, rows))],
             own, own_mass, centroids, *arrived,

time: 30.9 us -> 31 us (level)
  waiting for transfers between devices: 6.73 us -> 7.45 us
  starting transfers between devices: 13 us -> 12.3 us
    ppermute x9 -> x8, starting transfers between devices: 12.8 us -> 11.3 us  [the longest x5 7.09 us: permute(): return lax.ppermute(x, 'dev', [(i, i ^ masks[i % 2]) for i in range(n)])]
    ppermute x9 -> x8, waiting for transfers between devices: 5.4 us -> 6.32 us  [the longest x5 5.23 us: permute(): return lax.ppermute(x, 'dev', [(i, i ^ masks[i % 2]) for i in range(n)])]
    ppermute x2 -> x3, starting transfers between devices: 0.23 us -> 1 us  [swap(): return lax.ppermute(x, axis, [(i, i ^ mask) for i in range(size)])]
    ppermute x2 -> x3, waiting for transfers between devices: 1.33 us -> 1.13 us  [swap(): return lax.ppermute(x, axis, [(i, i ^ mask) for i in range(size)])]
    pallas_call x6 -> x7, Pallas kernels: 4.38 us -> 4.54 us  [call(): pl.pallas_call(kernel, out_shape=outs, in_specs=[SMEM if x.dtype == jnp.i...]
  transfers between devices with their start and end apart: 11 -> 11, of which waited for: 8 -> 8; matrix products, arithmetic and copies ran while one was open for 0% -> 3% of each run, Pallas kernels for 22% -> 22%
where the time goes in v17:
time: 31 us; the launch traced here: 30.9 us
  starting transfers between devices  12.3 us (40%)
  Pallas kernels  9.47 us (31%)
  waiting for transfers between devices  7.45 us (24%)
  other arithmetic  0.93 us (3%)
  between operations  0.7 us (2%)
    ppermute x5, starting transfers between devices, permute(): return lax.ppermute(x, 'dev', [(i, i ^ masks[i % 2]) for i in range(n)])  7.09 us
    ppermute x5, waiting for transfers between devices, permute(): return lax.ppermute(x, 'dev', [(i, i ^ masks[i % 2]) for i in range(n)])  5.23 us
    pallas_call x2, Pallas kernels, load(): pl.pallas_call(kernel, out_shape=[shape(dims, source.dtype), shape(follow...  4.93 us
    pallas_call x7, Pallas kernels, call(): pl.pallas_call(kernel, out_shape=outs, in_specs=[SMEM if x.dtype == jnp.i...  4.54 us
    ppermute x3, starting transfers between devices, body(): others = [lax.ppermute(lse, 'cgrp', x) for x in plan]  4.23 us
    ppermute x3, waiting for transfers between devices, swap(): return lax.ppermute(x, axis, [(i, i ^ mask) for i in range(size)])  1.13 us
    ppermute x3, waiting for transfers between devices, body(): others = [lax.ppermute(lse, 'cgrp', x) for x in plan]  1.09 us
    ppermute x3, starting transfers between devices, swap(): return lax.ppermute(x, axis, [(i, i ^ mask) for i in range(size)])  1 us
  transfers between devices with their start and end apart: 11, of which 8 were waited for; matrix products, arithmetic and copies ran while one was open for 3% of the time, Pallas kernels for 22%

profile of v17, /device:TPU:0, one launch (start us, length us, event | category | flops | bytes accessed | tf_op | source)
XLA Modules:
  0.0 30.9 jit_solution(17419173689159944532)
XLA Ops:
  0.6 0.5 %collective-permute-start = (f32[32,1024]{1,0:T(8,128)}, f32[32,1024]{1,0:T(8,128)S(1)}, u32[]{:S(2)}, u32[]{:S(2)}) collective-permute-start(f32[32,1024]{1,0:T(8,128)} %cent_ref.1), channel_id=1, source_target_pairs={{0,1},{1,0},{2,3},{3,2},{4,5},{5,4},{6,7},{7,6},{8,9},{9,8},{10,11... | collective-permute-start | bytes 393224 | tf_op jit(solution)/shard_map/ppermute | solution.py:17
  1.1 0.9 %convert_element_type.3.follow_ref.own_ref = bf16[32,1024]{1,0:T(8,128)(2,1)S(1)} convert(f32[32,1024]{1,0:T(8,128)} %cent_ref.1) | non-fusion elementwise | flops 32768 | bytes 196608 | tf_op jit(solution)/shard_map/convert_element_type | solution.py:257
  2.1 0.3 collective-permute-done.peer_ref
  2.4 2.7 %collective-permute-start.1 = (bf16[64,1024]{1,0:T(8,128)(2,1)S(1)}, bf16[64,1024]{1,0:T(8,128)(2,1)S(1)}, u32[]{:S(2)}, u32[]{:S(2)}) collective-permute-start(bf16[64,1024]{1,0:T(8,128)(2,1)S(1)} %get-tuple-element.31), channel_id=1, source_target_pairs={{0,3},{1,4},{2,1},{3,6},{4,7},{5,0},{6,5},{7,2},{8,11},{9,12},{10,... | collective-permute-start | bytes 393224 | tf_op jit(solution)/shard_map/ppermute | solution.py:22
  5.0 1.4 %collective-permute-start.2 = (bf16[32,1024]{1,0:T(8,128)(2,1)S(1)}, bf16[32,1024]{1,0:T(8,128)(2,1)S(1)}, u32[]{:S(2)}, u32[]{:S(2)}) collective-permute-start(bf16[32,1024]{1,0:T(8,128)(2,1)S(1)} %convert_element_type.3.follow_ref.own_ref), channel_id=1, source_target_pairs={{0,7},{1,6},{2,5},{3,4},{4,3},{5,2},{6,1},{7,0},{8,15},{9,14},{10,... | collective-permute-start | bytes 196616 | tf_op jit(solution)/shard_map/ppermute | solution.py:22
  6.4 2.7 %shard_map.49 = (bf16[1024,2048]{1,0:T(8,128)(2,1)S(1)}, bf16[32,1024]{1,0:T(8,128)(2,1)S(1)}) custom-call(bf16[2048,1024]{1,0:T(8,128)(2,1)} %source_ref.3, bf16[32,1024]{1,0:T(8,128)(2,1)S(1)} %convert_element_type.3.follow_ref.own_ref), custom_call_target="tpu_custom_call" | custom-call | bytes 8388608 | tf_op jit(solution)/shard_map/pallas_call | solution.py:70
  9.2 1.1 %collective-permute-done.2 = bf16[32,1024]{1,0:T(8,128)(2,1)S(1)} collective-permute-done((bf16[32,1024]{1,0:T(8,128)(2,1)S(1)}, bf16[32,1024]{1,0:T(8,128)(2,1)S(1)}, u32[]{:S(2)}, u32[]{:S(2)}) %collective-permute-start.2) | collective-permute-done | bytes 65568 | tf_op jit(solution)/shard_map/ppermute | solution.py:22
  10.3 0.0 collective-permute-done.1
  10.3 0.4 %collective-permute-start.3 = (bf16[96,1024]{1,0:T(8,128)(2,1)S(1)}, bf16[96,1024]{1,0:T(8,128)(2,1)S(1)}, u32[]{:S(2)}, u32[]{:S(2)}) collective-permute-start(bf16[96,1024]{1,0:T(8,128)(2,1)S(1)} %pad_maximum_fusion.refs_2_), channel_id=1, source_target_pairs={{0,1},{1,0},{2,3},{3,2},{4,5},{5,4},{6,7},{7,6},{8,9},{9,8},{10,11... | collective-permute-start | bytes 589832 | tf_op jit(solution)/shard_map/ppermute | solution.py:17
  10.8 1.1 %shard_map.51 = (f32[160,2048]{1,0:T(8,128)S(1)}, f32[16,128]{1,0:T(8,128)S(1)}, f32[16,128]{1,0:T(8,128)S(1)}) custom-call(bf16[1024,2048]{1,0:T(8,128)(2,1)S(1)} %get-tuple-element.30.docs_ref, bf16[32,1024]{1,0:T(8,128)(2,1)S(1)} %get-tuple-element.34.refs_0_, bf16[32,1024]{1,0:T(8,128)(2,1)S(1)} %get-tuple-element.35.refs_1_, ...), custom_call_target="tpu_custom_call" | custom-call | flops 536870912 | bytes 4521984 | tf_op jit(solution)/shard_map/pallas_call | solution.py:242
  11.8 0.0 collective-permute-done.3.table_ref
  11.9 1.0 %shard_map.52 = (f32[96,2048]{1,0:T(8,128)S(1)}, f32[16,128]{1,0:T(8,128)S(1)}, f32[16,128]{1,0:T(8,128)S(1)}) custom-call(bf16[1024,2048]{1,0:T(8,128)(2,1)S(1)} %get-tuple-element.30.docs_ref, bf16[96,1024]{1,0:T(8,128)(2,1)S(1)} %collective-permute-done.3.table_ref, f32[16,128]{1,0:T(8,128)S(1)} %get-tuple-element.36.first_top_ref.refs_6_, ...), custom_call_target="tpu_custom_call" | custom-call | flops 536870912 | bytes 4407296 | tf_op jit(solution)/shard_map/pallas_call | solution.py:242
  12.8 2.6 %collective-permute-start.6 = (f32[16,128]{1,0:T(8,128)S(1)}, f32[16,128]{1,0:T(8,128)S(1)}, u32[]{:S(2)}, u32[]{:S(2)}) collective-permute-start(f32[16,128]{1,0:T(8,128)S(1)} %get-tuple-element.38.follow_ref), channel_id=1, source_target_pairs={{0,16},{8,24},{16,8},{24,0},{1,17},{9,25},{17,9},{25,1},{2,18},{10... | collective-permute-start | bytes 24584 | tf_op jit(solution)/shard_map/ppermute | solution.py:280
  15.4 1.2 %collective-permute-start.5 = (f32[16,128]{1,0:T(8,128)S(1)}, f32[16,128]{1,0:T(8,128)S(1)}, u32[]{:S(2)}, u32[]{:S(2)}) collective-permute-start(f32[16,128]{1,0:T(8,128)S(1)} %get-tuple-element.38.follow_ref), channel_id=1, source_target_pairs={{0,24},{8,16},{16,0},{24,8},{1,25},{9,17},{17,1},{25,9},{2,26},{10... | collective-permute-start | bytes 24584 | tf_op jit(solution)/shard_map/ppermute | solution.py:280
  16.7 0.4 %collective-permute-start.4 = (f32[16,128]{1,0:T(8,128)S(1)}, f32[16,128]{1,0:T(8,128)S(1)}, u32[]{:S(2)}, u32[]{:S(2)}) collective-permute-start(f32[16,128]{1,0:T(8,128)S(1)} %get-tuple-element.38.follow_ref), channel_id=1, source_target_pairs={{0,8},{8,0},{16,24},{24,16},{1,9},{9,1},{17,25},{25,17},{2,10},{10... | collective-permute-start | bytes 24584 | tf_op jit(solution)/shard_map/ppermute | solution.py:280
  17.0 2.2 %shard_map.53 = (bf16[2048,1024]{1,0:T(8,128)(2,1)S(1)}, f32[16,128]{1,0:T(8,128)S(1)}) custom-call(bf16[2048,1024]{1,0:T(8,128)(2,1)} %source_ref.3, f32[16,128]{1,0:T(8,128)S(1)} %get-tuple-element.38.follow_ref), custom_call_target="tpu_custom_call" | custom-call | bytes 8388608 | tf_op jit(solution)/shard_map/pallas_call | solution.py:70
  19.2 0.0 collective-permute-done.6.refs_2_
  19.2 0.7 %collective-permute-done.5.refs_1_ = f32[16,128]{1,0:T(8,128)S(1)} collective-permute-done((f32[16,128]{1,0:T(8,128)S(1)}, f32[16,128]{1,0:T(8,128)S(1)}, u32[]{:S(2)}, u32[]{:S(2)}) %collective-permute-start.5) | collective-permute-done | bytes 8224 | tf_op jit(solution)/shard_map/ppermute | solution.py:280
  20.0 0.3 %collective-permute-done.4.refs_0_ = f32[16,128]{1,0:T(8,128)S(1)} collective-permute-done((f32[16,128]{1,0:T(8,128)S(1)}, f32[16,128]{1,0:T(8,128)S(1)}, u32[]{:S(2)}, u32[]{:S(2)}) %collective-permute-start.4) | collective-permute-done | bytes 8224 | tf_op jit(solution)/shard_map/ppermute | solution.py:280
  20.3 0.8 %shard_map.54 = (f32[16,128]{1,0:T(8,128)}, f32[16,128]{1,0:T(8,128)S(1)}, f32[16,128]{1,0:T(8,128)S(1)}, bf16[128,1152]{1,0:T(8,128)(2,1)S(1)}) custom-call(s32[1]{0:T(128)} %bitcast.me_ref, f32[16,128]{1,0:T(8,128)S(1)} %get-tuple-element.39.lse_ref, f32[16,128]{1,0:T(8,128)S(1)} %collective-permute-done.4.refs_0_, ...), custom_call_target="tpu_custom_call" | custom-call | flops 536870912 | bytes 6340612 | tf_op jit(solution)/shard_map/pallas_call | solution.py:242
  21.1 0.0 copy-start
  21.1 0.1 collective-permute-start.7
  21.2 0.7 %shard_map.55 = (f32[128,1024]{1,0:T(8,128)S(1)}, f32[128,128]{1,0:T(8,128)S(1)}) custom-call(f32[16,128]{1,0:T(8,128)S(1)} %get-tuple-element.44.a_factor_ref, f32[16,128]{1,0:T(8,128)S(1)} %get-tuple-element.45.b_factor_ref, bf16[2048,1024]{1,0:T(8,128)(2,1)S(1)} %get-tuple-element.40.refs_3_.docs_ref, f32[160,2048]{1,0:T(8,128)S(1)} %get-tuple-element.41.refs_4_.a_ref, ...), custom_call_target="tpu_custom_call" | custom-call | flops 536870912 | bytes 6307840 | tf_op jit(solution)/shard_map/pallas_call | solution.py:242
  21.9 0.8 %collective-permute-done.7.got_ref = bf16[128,1152]{1,0:T(8,128)(2,1)S(1)} collective-permute-done((bf16[128,1152]{1,0:T(8,128)(2,1)S(1)}, bf16[128,1152]{1,0:T(8,128)(2,1)S(1)}, u32[]{:S(2)}, u32[]{:S(2)}) %collective-permute-start.7) | collective-permute-done | bytes 294944 | tf_op jit(solution)/shard_map/ppermute | solution.py:17
  22.8 0.2 shard_map.56
  22.9 1.3 %collective-permute-start.8 = (bf16[32,1152]{1,0:T(8,128)(2,1)S(1)}, bf16[32,1152]{1,0:T(8,128)(2,1)S(1)}, u32[]{:S(2)}, u32[]{:S(2)}) collective-permute-start(bf16[32,1152]{1,0:T(8,128)(2,1)S(1)} %get-tuple-element.51), channel_id=1, source_target_pairs={{0,7},{1,6},{2,5},{3,4},{4,3},{5,2},{6,1},{7,0},{8,15},{9,14},{10,... | collective-permute-start | bytes 221192 | tf_op jit(solution)/shard_map/ppermute | solution.py:22
  24.2 1.2 %collective-permute-start.9 = (bf16[32,1152]{1,0:T(8,128)(2,1)S(1)}, bf16[32,1152]{1,0:T(8,128)(2,1)S(1)}, u32[]{:S(2)}, u32[]{:S(2)}) collective-permute-start(bf16[32,1152]{1,0:T(8,128)(2,1)S(1)} %get-tuple-element.52), channel_id=1, source_target_pairs={{0,5},{1,2},{2,7},{3,0},{4,1},{5,6},{6,3},{7,4},{8,13},{9,10},{10,... | collective-permute-start | bytes 221192 | tf_op jit(solution)/shard_map/ppermute | solution.py:22
  25.4 0.5 %collective-permute-start.10 = (bf16[32,1152]{1,0:T(8,128)(2,1)S(1)}, bf16[32,1152]{1,0:T(8,128)(2,1)S(1)}, u32[]{:S(2)}, u32[]{:S(2)}) collective-permute-start(bf16[32,1152]{1,0:T(8,128)(2,1)S(1)} %get-tuple-element.53), channel_id=1, source_target_pairs={{0,3},{1,4},{2,1},{3,6},{4,7},{5,0},{6,5},{7,2},{8,11},{9,12},{10,... | collective-permute-start | bytes 221192 | tf_op jit(solution)/shard_map/ppermute | solution.py:22
  25.9 2.2 %collective-permute-done.8.refs_0_ = bf16[32,1152]{1,0:T(8,128)(2,1)S(1)} collective-permute-done((bf16[32,1152]{1,0:T(8,128)(2,1)S(1)}, bf16[32,1152]{1,0:T(8,128)(2,1)S(1)}, u32[]{:S(2)}, u32[]{:S(2)}) %collective-permute-start.8) | collective-permute-done | bytes 73760 | tf_op jit(solution)/shard_map/ppermute | solution.py:22
  28.2 0.7 %collective-permute-done.9.refs_1_ = bf16[32,1152]{1,0:T(8,128)(2,1)S(1)} collective-permute-done((bf16[32,1152]{1,0:T(8,128)(2,1)S(1)}, bf16[32,1152]{1,0:T(8,128)(2,1)S(1)}, u32[]{:S(2)}, u32[]{:S(2)}) %collective-permute-start.9) | collective-permute-done | bytes 73760 | tf_op jit(solution)/shard_map/ppermute | solution.py:22
  28.9 1.1 %collective-permute-done.10.refs_2_ = bf16[32,1152]{1,0:T(8,128)(2,1)S(1)} collective-permute-done((bf16[32,1152]{1,0:T(8,128)(2,1)S(1)}, bf16[32,1152]{1,0:T(8,128)(2,1)S(1)}, u32[]{:S(2)}, u32[]{:S(2)}) %collective-permute-start.10) | collective-permute-done | bytes 73760 | tf_op jit(solution)/shard_map/ppermute | solution.py:22
  30.0 0.0 copy-done
  30.0 0.8 %shard_map.57 = (f32[32,1024]{1,0:T(8,128)}, f32[1,32]{1,0:T(1,128)}) custom-call(f32[32,1024]{1,0:T(8,128)S(1)} %get-tuple-element.49.own_ref, f32[32,128]{1,0:T(8,128)S(1)} %get-tuple-element.50.own_mass_ref, f32[32,1024]{1,0:T(8,128)S(1)} %copy-done, bf16[32,1152]{1,0:T(8,128)(2,1)S(1)} %collective-permute-done.8.refs_0_, ...), custom_call_target="tpu_custom_call" | custom-call | bytes 499712 | tf_op jit(solution)/shard_map/pallas_call | solution.py:242
  (2 shorter events, 0.0 us)
Async XLA Ops:
  0.6 1.7 %collective-permute-start = (f32[32,1024]{1,0:T(8,128)}, f32[32,1024]{1,0:T(8,128)S(1)}, u32[]{:S(2)}, u32[]{:S(2)}) collective-permute-start(f32[32,1024]{1,0:T(8,128)} %cent_ref.1), channel_id=1, source_target_pairs={{0,1},{1,0},{2,3},{3,2},{4,5},{5,4},{6,7},{7,6},{8,9},{9,8},{10,11... | collective-permute-start | bytes 393224 | tf_op jit(solution)/shard_map/ppermute | solution.py:17
  2.4 8.0 %collective-permute-start.1 = (bf16[64,1024]{1,0:T(8,128)(2,1)S(1)}, bf16[64,1024]{1,0:T(8,128)(2,1)S(1)}, u32[]{:S(2)}, u32[]{:S(2)}) collective-permute-start(bf16[64,1024]{1,0:T(8,128)(2,1)S(1)} %get-tuple-element.31), channel_id=1, source_target_pairs={{0,3},{1,4},{2,1},{3,6},{4,7},{5,0},{6,5},{7,2},{8,11},{9,12},{10,... | collective-permute-start | bytes 393224 | tf_op jit(solution)/shard_map/ppermute | solution.py:22
  5.0 5.3 %collective-permute-start.2 = (bf16[32,1024]{1,0:T(8,128)(2,1)S(1)}, bf16[32,1024]{1,0:T(8,128)(2,1)S(1)}, u32[]{:S(2)}, u32[]{:S(2)}) collective-permute-start(bf16[32,1024]{1,0:T(8,128)(2,1)S(1)} %convert_element_type.3.follow_ref.own_ref), channel_id=1, source_target_pairs={{0,7},{1,6},{2,5},{3,4},{4,3},{5,2},{6,1},{7,0},{8,15},{9,14},{10,... | collective-permute-start | bytes 196616 | tf_op jit(solution)/shard_map/ppermute | solution.py:22
  10.3 1.5 %collective-permute-start.3 = (bf16[96,1024]{1,0:T(8,128)(2,1)S(1)}, bf16[96,1024]{1,0:T(8,128)(2,1)S(1)}, u32[]{:S(2)}, u32[]{:S(2)}) collective-permute-start(bf16[96,1024]{1,0:T(8,128)(2,1)S(1)} %pad_maximum_fusion.refs_2_), channel_id=1, source_target_pairs={{0,1},{1,0},{2,3},{3,2},{4,5},{5,4},{6,7},{7,6},{8,9},{9,8},{10,11... | collective-permute-start | bytes 589832 | tf_op jit(solution)/shard_map/ppermute | solution.py:17
  12.8 6.4 %collective-permute-start.6 = (f32[16,128]{1,0:T(8,128)S(1)}, f32[16,128]{1,0:T(8,128)S(1)}, u32[]{:S(2)}, u32[]{:S(2)}) collective-permute-start(f32[16,128]{1,0:T(8,128)S(1)} %get-tuple-element.38.follow_ref), channel_id=1, source_target_pairs={{0,16},{8,24},{16,8},{24,0},{1,17},{9,25},{17,9},{25,1},{2,18},{10... | collective-permute-start | bytes 24584 | tf_op jit(solution)/shard_map/ppermute | solution.py:280
  15.4 4.5 %collective-permute-start.5 = (f32[16,128]{1,0:T(8,128)S(1)}, f32[16,128]{1,0:T(8,128)S(1)}, u32[]{:S(2)}, u32[]{:S(2)}) collective-permute-start(f32[16,128]{1,0:T(8,128)S(1)} %get-tuple-element.38.follow_ref), channel_id=1, source_target_pairs={{0,24},{8,16},{16,0},{24,8},{1,25},{9,17},{17,1},{25,9},{2,26},{10... | collective-permute-start | bytes 24584 | tf_op jit(solution)/shard_map/ppermute | solution.py:280
  16.7 3.7 %collective-permute-start.4 = (f32[16,128]{1,0:T(8,128)S(1)}, f32[16,128]{1,0:T(8,128)S(1)}, u32[]{:S(2)}, u32[]{:S(2)}) collective-permute-start(f32[16,128]{1,0:T(8,128)S(1)} %get-tuple-element.38.follow_ref), channel_id=1, source_target_pairs={{0,8},{8,0},{16,24},{24,16},{1,9},{9,1},{17,25},{25,17},{2,10},{10... | collective-permute-start | bytes 24584 | tf_op jit(solution)/shard_map/ppermute | solution.py:280
  21.1 8.9 %copy-start = (f32[32,1024]{1,0:T(8,128)S(1)}, f32[32,1024]{1,0:T(8,128)}, u32[]{:S(2)}) copy-start(f32[32,1024]{1,0:T(8,128)} %cent_ref.1) | copy-start | bytes 393220
  21.1 1.6 %collective-permute-start.7 = (bf16[128,1152]{1,0:T(8,128)(2,1)S(1)}, bf16[128,1152]{1,0:T(8,128)(2,1)S(1)}, u32[]{:S(2)}, u32[]{:S(2)}) collective-permute-start(bf16[128,1152]{1,0:T(8,128)(2,1)S(1)} %get-tuple-element.48), channel_id=1, source_target_pairs={{0,1},{1,0},{2,3},{3,2},{4,5},{5,4},{6,7},{7,6},{8,9},{9,8},{10,11... | collective-permute-start | bytes 884744 | tf_op jit(solution)/shard_map/ppermute | solution.py:17
  22.9 5.3 %collective-permute-start.8 = (bf16[32,1152]{1,0:T(8,128)(2,1)S(1)}, bf16[32,1152]{1,0:T(8,128)(2,1)S(1)}, u32[]{:S(2)}, u32[]{:S(2)}) collective-permute-start(bf16[32,1152]{1,0:T(8,128)(2,1)S(1)} %get-tuple-element.51), channel_id=1, source_target_pairs={{0,7},{1,6},{2,5},{3,4},{4,3},{5,2},{6,1},{7,0},{8,15},{9,14},{10,... | collective-permute-start | bytes 221192 | tf_op jit(solution)/shard_map/ppermute | solution.py:22
  24.2 4.7 %collective-permute-start.9 = (bf16[32,1152]{1,0:T(8,128)(2,1)S(1)}, bf16[32,1152]{1,0:T(8,128)(2,1)S(1)}, u32[]{:S(2)}, u32[]{:S(2)}) collective-permute-start(bf16[32,1152]{1,0:T(8,128)(2,1)S(1)} %get-tuple-element.52), channel_id=1, source_target_pairs={{0,5},{1,2},{2,7},{3,0},{4,1},{5,6},{6,3},{7,4},{8,13},{9,10},{10,... | collective-permute-start | bytes 221192 | tf_op jit(solution)/shard_map/ppermute | solution.py:22
  25.4 4.6 %collective-permute-start.10 = (bf16[32,1152]{1,0:T(8,128)(2,1)S(1)}, bf16[32,1152]{1,0:T(8,128)(2,1)S(1)}, u32[]{:S(2)}, u32[]{:S(2)}) collective-permute-start(bf16[32,1152]{1,0:T(8,128)(2,1)S(1)} %get-tuple-element.53), channel_id=1, source_target_pairs={{0,3},{1,4},{2,1},{3,6},{4,7},{5,0},{6,5},{7,2},{8,11},{9,12},{10,... | collective-permute-start | bytes 221192 | tf_op jit(solution)/shard_map/ppermute | solution.py:22

commit v18 on v15

--- a/solution.py
+++ b/solution.py
@@ -90,10 +90,11 @@
         ref[at:at + 1, :] = row[:, i * LANES:(i + 1) * LANES]
 
 
-def scores_kernel(chunk, docs_ref, table_ref, part_ref, top_ref, sum_ref):
+def scores_kernel(chunk, docs_ref, *refs):
+    *table_refs, part_ref, top_ref, sum_ref = refs
     width, count = docs_ref.shape
     scale = 4.0 / math.sqrt(width)
-    table = table_ref[...]
+    table = jnp.concatenate([r[...] for r in table_refs], axis=0)
     wide = table.astype(jnp.float32)
     half_norms = 0.5 * jnp.sum(wide * wide, axis=1, keepdims=True)
     for start in range(0, count, chunk):
@@ -108,9 +109,9 @@
 
 
 def last_scores_kernel(
-    chunk, docs_ref, table_ref, first_top_ref, first_sum_ref, part_ref, top_ref, lse_ref
+    chunk, docs_ref, one_ref, two_ref, first_top_ref, first_sum_ref, part_ref, top_ref, lse_ref
 ):
-    scores_kernel(chunk, docs_ref, table_ref, part_ref, top_ref, lse_ref)
+    scores_kernel(chunk, docs_ref, one_ref, two_ref, part_ref, top_ref, lse_ref)
     top = jnp.maximum(first_top_ref[...], top_ref[...])
     total = first_sum_ref[...] * jnp.exp(first_top_ref[...] - top)
     total += lse_ref[...] * jnp.exp(top_ref[...] - top)
@@ -146,7 +147,7 @@
 def send_kernel(groups, plan, chunk, me_ref, lse_ref, *refs):
     got_refs = refs[:len(plan)]
     docs_ref, part_ref, top_ref, keep_top_ref = refs[len(plan):len(plan) + 4]
-    doc_lse_ref, factor_ref, send_ref, resp_ref = refs[len(plan) + 4:]
+    doc_lse_ref, factor_ref, one_ref, two_ref, resp_ref = refs[len(plan) + 4:]
     me = me_ref[0]
     parts = [lse_ref[...]] * groups
     for got_ref, pairs in zip(got_refs, plan):
@@ -160,10 +161,13 @@
     factor = jnp.exp(top_ref[...] - doc_lse)
 
     def store(cols, term):
-        send_ref[:, cols] = term.astype(jnp.bfloat16)
+        term = term.astype(jnp.bfloat16)
+        one_ref[:, cols] = term[:one_ref.shape[0]]
+        two_ref[:, cols] = term[one_ref.shape[0]:]
 
     mass = weighted_sums(chunk, factor, docs_ref, part_ref, resp_ref, store)
-    send_ref[:, docs_ref.shape[1]:] = mass_lanes(mass)
+    width = docs_ref.shape[1]
+    store(slice(width, width + LANES), mass_lanes(mass))
 
 
 def keep_kernel(chunk, factor_ref, docs_ref, part_ref, keep_ref, keep_mass_ref, resp_ref):
@@ -174,11 +178,14 @@
     keep_mass_ref[...] = jnp.broadcast_to(mass, keep_mass_ref.shape)
 
 
-def fold_kernel(keep_ref, keep_mass_ref, got_ref, own_ref, own_mass_ref, *send_refs):
+def fold_kernel(keep_ref, keep_mass_ref, one_ref, two_ref, own_ref, own_mass_ref, *send_refs):
     rows, width = own_ref.shape
     for slot in range(keep_ref.shape[0] // rows):
         here = slice(slot * rows, (slot + 1) * rows)
-        got, got_mass = read_rows(got_ref[here], width)
+        first = one_ref.shape[0]
+        there = here if here.start < first else slice(here.start - first, here.stop - first)
+        got_ref = one_ref if here.start < first else two_ref
+        got, got_mass = read_rows(got_ref[there], width)
         term = keep_ref[here] + got
         mass = keep_mass_ref[here, :1] + got_mass
         if slot == 0:
@@ -233,24 +240,26 @@
         routes = chip_plan(n)
         blocks = [lax.ppermute(rounded, "dev", pairs) for pairs in routes]
         docs_t, own = load(docs, rounded, chunk)
-        mine = jnp.concatenate([own] + blocks, axis=0)
-        theirs = swap(mine, "dev", n, 1)
+        blocks = [own] + blocks
+        mine = [jnp.concatenate(x, axis=0) for x in (blocks[:n // 4], blocks[n // 4:])]
+        theirs = [swap(x, "dev", n, 1) for x in mine]
         part, top, total = call(
-            functools.partial(scores_kernel, chunk), stats, docs_t, mine, flops=flops
+            functools.partial(scores_kernel, chunk), stats, docs_t, *mine, flops=flops
         )
         other_part, other_top, lse = call(
             functools.partial(last_scores_kernel, chunk), stats,
-            docs_t, theirs, top, total, flops=flops,
+            docs_t, *theirs, top, total, flops=flops,
         )
         others = [lax.ppermute(lse, "cgrp", pairs) for pairs in plan]
         docs, lse = load(docs, lse)
-        doc_lse, factor, send = call(
+        doc_lse, factor, *send = call(
             functools.partial(send_kernel, g, plan, chunk),
-            [shape((count // LANES, LANES)), shape((count // LANES, LANES)), shape((half, width + LANES), jnp.bfloat16)],
+            [shape((count // LANES, LANES)), shape((count // LANES, LANES))]
+            + [shape((half // 2, width + LANES), jnp.bfloat16)] * 2,
             lax.axis_index("cgrp").reshape(1), lse, *others, docs, other_part, other_top, top,
             scratch=resp, flops=flops,
         )
-        got = swap(send, "dev", n, 1)
+        got = [swap(x, "dev", n, 1) for x in send]
         keep, keep_mass = call(
             functools.partial(keep_kernel, chunk),
             [shape((half, width)), shape((half, LANES))],
@@ -260,7 +269,7 @@
             fold_kernel,
             [shape((rows, width)), shape((rows, LANES))]
             + [shape((rows, width + LANES), jnp.bfloat16)] * (n // 2 - 1),
-            keep, keep_mass, got,
+            keep, keep_mass, *got,
         )
         arrived = [
             lax.ppermute(x, "dev", [(target, source) for source, target in pairs])

time: 30.9 us -> 30.9 us (level)
  waiting for transfers between devices: 6.73 us -> 5.57 us
  starting transfers between devices: 13 us -> 14.1 us
    ppermute x2 -> x4, starting transfers between devices: 0.23 us -> 1.42 us  [swap(): return lax.ppermute(x, axis, [(i, i ^ mask) for i in range(size)])]
    ppermute x2 -> x4, waiting for transfers between devices: 1.33 us -> 0.71 us  [swap(): return lax.ppermute(x, axis, [(i, i ^ mask) for i in range(size)])]
    ppermute x3, waiting for transfers between devices: 0.61 us -> 0.01 us  [body(): blocks = [lax.ppermute(rounded, 'dev', pairs) for pairs in routes]]
  transfers between devices with their start and end apart: 11 -> 13, of which waited for: 8 -> 8; matrix products, arithmetic and copies ran while one was open for 0% -> 0% of each run, Pallas kernels for 22% -> 21%
where the time goes in v18:
time: 30.9 us; the launch traced here: 30.7 us
  starting transfers between devices  14.1 us (46%)
  Pallas kernels  9.31 us (30%)
  waiting for transfers between devices  5.57 us (18%)
  other arithmetic  0.92 us (3%)
  between operations  0.75 us (2%)
    ppermute x3, starting transfers between devices, body(): blocks = [lax.ppermute(rounded, 'dev', pairs) for pairs in routes]  5.14 us
    pallas_call x2, Pallas kernels, load(): pl.pallas_call(kernel, out_shape=[shape(dims, source.dtype), shape(follow...  4.93 us
    pallas_call x6, Pallas kernels, call(): pl.pallas_call(kernel, out_shape=outs, in_specs=[SMEM if x.dtype == jnp.i...  4.38 us
    ppermute x3, starting transfers between devices, body(): others = [lax.ppermute(lse, 'cgrp', pairs) for pairs in plan]  4.22 us
    ppermute x3, waiting for transfers between devices, body(): lax.ppermute(x, 'dev', [(target, source) for source, target in pairs])  3.76 us
    ppermute x3, starting transfers between devices, body(): lax.ppermute(x, 'dev', [(target, source) for source, target in pairs])  3.35 us
    ppermute x4, starting transfers between devices, swap(): return lax.ppermute(x, axis, [(i, i ^ mask) for i in range(size)])  1.42 us
    ppermute x3, waiting for transfers between devices, body(): others = [lax.ppermute(lse, 'cgrp', pairs) for pairs in plan]  1.09 us
  transfers between devices with their start and end apart: 13, of which 8 were waited for; matrix products, arithmetic and copies ran while one was open for 0% of the time, Pallas kernels for 21%

profile of v18, /device:TPU:0, one launch (start us, length us, event | category | flops | bytes accessed | tf_op | source)
XLA Modules:
  0.0 30.7 jit_solution(7070388053621181682)
XLA Ops:
  0.6 0.9 %convert_element_type.3.follow_ref = bf16[32,1024]{1,0:T(8,128)(2,1)S(1)} convert(f32[32,1024]{1,0:T(8,128)} %cent_ref.1) | non-fusion elementwise | flops 32768 | bytes 196608 | tf_op jit(solution)/shard_map/convert_element_type | solution.py:239
  1.5 3.4 %collective-permute-start.3 = (bf16[32,1024]{1,0:T(8,128)(2,1)S(1)}, bf16[32,1024]{1,0:T(8,128)(2,1)S(1)}, u32[]{:S(2)}, u32[]{:S(2)}) collective-permute-start(bf16[32,1024]{1,0:T(8,128)(2,1)S(1)} %convert_element_type.3.follow_ref), channel_id=1, source_target_pairs={{0,7},{1,6},{2,5},{3,4},{4,3},{5,2},{6,1},{7,0},{8,15},{9,14},{10,... | collective-permute-start | bytes 196616 | tf_op jit(solution)/shard_map/ppermute | solution.py:241
  4.9 0.8 %collective-permute-start.2 = (bf16[32,1024]{1,0:T(8,128)(2,1)S(1)}, bf16[32,1024]{1,0:T(8,128)(2,1)S(1)}, u32[]{:S(2)}, u32[]{:S(2)}) collective-permute-start(bf16[32,1024]{1,0:T(8,128)(2,1)S(1)} %convert_element_type.3.follow_ref), channel_id=1, source_target_pairs={{0,5},{1,2},{2,7},{3,0},{4,1},{5,6},{6,3},{7,4},{8,13},{9,10},{10,... | collective-permute-start | bytes 196616 | tf_op jit(solution)/shard_map/ppermute | solution.py:241
  5.7 1.0 %collective-permute-start = (bf16[32,1024]{1,0:T(8,128)(2,1)S(1)}, bf16[32,1024]{1,0:T(8,128)(2,1)S(1)}, u32[]{:S(2)}, u32[]{:S(2)}) collective-permute-start(bf16[32,1024]{1,0:T(8,128)(2,1)S(1)} %convert_element_type.3.follow_ref), channel_id=1, source_target_pairs={{0,3},{1,4},{2,1},{3,6},{4,7},{5,0},{6,5},{7,2},{8,11},{9,12},{10,... | collective-permute-start | bytes 196616 | tf_op jit(solution)/shard_map/ppermute | solution.py:241
  6.7 2.7 %shard_map.49 = (bf16[1024,2048]{1,0:T(8,128)(2,1)S(1)}, bf16[32,1024]{1,0:T(8,128)(2,1)S(1)}) custom-call(bf16[2048,1024]{1,0:T(8,128)(2,1)} %source_ref.3, bf16[32,1024]{1,0:T(8,128)(2,1)S(1)} %convert_element_type.3.follow_ref), custom_call_target="tpu_custom_call" | custom-call | bytes 8388608 | tf_op jit(solution)/shard_map/pallas_call | solution.py:72
  9.4 0.0 collective-permute-done.2
  9.5 0.0 collective-permute-done.3
  9.5 0.8 %collective-permute-start.4 = (bf16[64,1024]{1,0:T(8,128)(2,1)S(1)}, bf16[64,1024]{1,0:T(8,128)(2,1)S(1)}, u32[]{:S(2)}, u32[]{:S(2)}) collective-permute-start(bf16[64,1024]{1,0:T(8,128)(2,1)S(1)} %constant_dynamic-update-slice_fusion.2.refs_1_), channel_id=1, source_target_pairs={{0,1},{1,0},{2,3},{3,2},{4,5},{5,4},{6,7},{7,6},{8,9},{9,8},{10,11... | collective-permute-start | bytes 393224 | tf_op jit(solution)/shard_map/ppermute | solution.py:17
  10.3 0.0 collective-permute-done
  10.3 0.1 collective-permute-start.1
  10.4 0.9 %shard_map.50 = (f32[128,2048]{1,0:T(8,128)S(1)}, f32[16,128]{1,0:T(8,128)S(1)}, f32[16,128]{1,0:T(8,128)S(1)}) custom-call(bf16[1024,2048]{1,0:T(8,128)(2,1)S(1)} %get-tuple-element.26.docs_ref, bf16[64,1024]{1,0:T(8,128)(2,1)S(1)} %constant_dynamic-update-slice_fusion.refs_0_, bf16[64,1024]{1,0:T(8,128)(2,1)S(1)} %constant_dynamic-update-slice_fusion.2.refs_1_), custom_call_target="tpu_custom_call" | custom-call | flops 536870912 | bytes 4456448 | tf_op jit(solution)/shard_map/pallas_call | solution.py:224
  11.2 0.0 collective-permute-done.4.two_ref
  11.3 0.4 %collective-permute-done.1.one_ref = bf16[64,1024]{1,0:T(8,128)(2,1)S(1)} collective-permute-done((bf16[64,1024]{1,0:T(8,128)(2,1)S(1)}, bf16[64,1024]{1,0:T(8,128)(2,1)S(1)}, u32[]{:S(2)}, u32[]{:S(2)}) %collective-permute-start.1) | collective-permute-done | bytes 131104 | tf_op jit(solution)/shard_map/ppermute | solution.py:17
  11.7 0.9 %shard_map.51 = (f32[128,2048]{1,0:T(8,128)S(1)}, f32[16,128]{1,0:T(8,128)S(1)}, f32[16,128]{1,0:T(8,128)S(1)}) custom-call(bf16[1024,2048]{1,0:T(8,128)(2,1)S(1)} %get-tuple-element.26.docs_ref, bf16[64,1024]{1,0:T(8,128)(2,1)S(1)} %collective-permute-done.1.one_ref, bf16[64,1024]{1,0:T(8,128)(2,1)S(1)} %collective-permute-done.4.two_ref, ...), custom_call_target="tpu_custom_call" | custom-call | flops 536870912 | bytes 4472832 | tf_op jit(solution)/shard_map/pallas_call | solution.py:224
  12.6 2.6 %collective-permute-start.7 = (f32[16,128]{1,0:T(8,128)S(1)}, f32[16,128]{1,0:T(8,128)S(1)}, u32[]{:S(2)}, u32[]{:S(2)}) collective-permute-start(f32[16,128]{1,0:T(8,128)S(1)} %get-tuple-element.30.follow_ref), channel_id=1, source_target_pairs={{0,16},{8,24},{16,8},{24,0},{1,17},{9,25},{17,9},{25,1},{2,18},{10... | collective-permute-start | bytes 24584 | tf_op jit(solution)/shard_map/ppermute | solution.py:253
  15.2 1.2 %collective-permute-start.6 = (f32[16,128]{1,0:T(8,128)S(1)}, f32[16,128]{1,0:T(8,128)S(1)}, u32[]{:S(2)}, u32[]{:S(2)}) collective-permute-start(f32[16,128]{1,0:T(8,128)S(1)} %get-tuple-element.30.follow_ref), channel_id=1, source_target_pairs={{0,24},{8,16},{16,0},{24,8},{1,25},{9,17},{17,1},{25,9},{2,26},{10... | collective-permute-start | bytes 24584 | tf_op jit(solution)/shard_map/ppermute | solution.py:253
  16.5 0.3 %collective-permute-start.5 = (f32[16,128]{1,0:T(8,128)S(1)}, f32[16,128]{1,0:T(8,128)S(1)}, u32[]{:S(2)}, u32[]{:S(2)}) collective-permute-start(f32[16,128]{1,0:T(8,128)S(1)} %get-tuple-element.30.follow_ref), channel_id=1, source_target_pairs={{0,8},{8,0},{16,24},{24,16},{1,9},{9,1},{17,25},{25,17},{2,10},{10... | collective-permute-start | bytes 24584 | tf_op jit(solution)/shard_map/ppermute | solution.py:253
  16.8 2.2 %shard_map.52 = (bf16[2048,1024]{1,0:T(8,128)(2,1)S(1)}, f32[16,128]{1,0:T(8,128)S(1)}) custom-call(bf16[2048,1024]{1,0:T(8,128)(2,1)} %source_ref.3, f32[16,128]{1,0:T(8,128)S(1)} %get-tuple-element.30.follow_ref), custom_call_target="tpu_custom_call" | custom-call | bytes 8388608 | tf_op jit(solution)/shard_map/pallas_call | solution.py:72
  19.0 0.0 collective-permute-done.7.refs_2_
  19.0 0.8 %collective-permute-done.6.refs_1_ = f32[16,128]{1,0:T(8,128)S(1)} collective-permute-done((f32[16,128]{1,0:T(8,128)S(1)}, f32[16,128]{1,0:T(8,128)S(1)}, u32[]{:S(2)}, u32[]{:S(2)}) %collective-permute-start.6) | collective-permute-done | bytes 8224 | tf_op jit(solution)/shard_map/ppermute | solution.py:253
  19.8 0.3 %collective-permute-done.5.refs_0_ = f32[16,128]{1,0:T(8,128)S(1)} collective-permute-done((f32[16,128]{1,0:T(8,128)S(1)}, f32[16,128]{1,0:T(8,128)S(1)}, u32[]{:S(2)}, u32[]{:S(2)}) %collective-permute-start.5) | collective-permute-done | bytes 8224 | tf_op jit(solution)/shard_map/ppermute | solution.py:253
  20.1 0.8 %shard_map.53 = (f32[16,128]{1,0:T(8,128)}, f32[16,128]{1,0:T(8,128)S(1)}, bf16[64,1152]{1,0:T(8,128)(2,1)S(1)}, bf16[64,1152]{1,0:T(8,128)(2,1)S(1)}) custom-call(s32[1]{0:T(128)} %bitcast.me_ref, f32[16,128]{1,0:T(8,128)S(1)} %get-tuple-element.31.lse_ref, f32[16,128]{1,0:T(8,128)S(1)} %collective-permute-done.5.refs_0_, ...), custom_call_target="tpu_custom_call" | custom-call | flops 536870912 | bytes 5292036 | tf_op jit(solution)/shard_map/pallas_call | solution.py:224
  20.9 0.0 copy-start
  20.9 0.1 collective-permute-start.8
  21.0 0.5 %collective-permute-start.9 = (bf16[64,1152]{1,0:T(8,128)(2,1)S(1)}, bf16[64,1152]{1,0:T(8,128)(2,1)S(1)}, u32[]{:S(2)}, u32[]{:S(2)}) collective-permute-start(bf16[64,1152]{1,0:T(8,128)(2,1)S(1)} %get-tuple-element.40), channel_id=1, source_target_pairs={{0,1},{1,0},{2,3},{3,2},{4,5},{5,4},{6,7},{7,6},{8,9},{9,8},{10,11... | collective-permute-start | bytes 442376 | tf_op jit(solution)/shard_map/ppermute | solution.py:17
  21.5 0.8 %shard_map.54 = (f32[128,1024]{1,0:T(8,128)S(1)}, f32[128,128]{1,0:T(8,128)S(1)}) custom-call(f32[16,128]{1,0:T(8,128)S(1)} %get-tuple-element.35.factor_ref, bf16[2048,1024]{1,0:T(8,128)(2,1)S(1)} %get-tuple-element.32.refs_3_.docs_ref, f32[128,2048]{1,0:T(8,128)S(1)} %get-tuple-element.36.part_ref), custom_call_target="tpu_custom_call" | custom-call | flops 536870912 | bytes 5251072 | tf_op jit(solution)/shard_map/pallas_call | solution.py:224
  22.3 0.1 collective-permute-done.8.one_ref
  22.4 0.2 collective-permute-done.9.two_ref
  22.6 0.2 shard_map.55
  22.8 1.6 %collective-permute-start.10 = (bf16[32,1152]{1,0:T(8,128)(2,1)S(1)}, bf16[32,1152]{1,0:T(8,128)(2,1)S(1)}, u32[]{:S(2)}, u32[]{:S(2)}) collective-permute-start(bf16[32,1152]{1,0:T(8,128)(2,1)S(1)} %get-tuple-element.43), channel_id=1, source_target_pairs={{7,0},{6,1},{5,2},{4,3},{3,4},{2,5},{1,6},{0,7},{15,8},{14,9},{13,... | collective-permute-start | bytes 221192 | tf_op jit(solution)/shard_map/ppermute | solution.py:275
  24.4 0.8 %collective-permute-start.11 = (bf16[32,1152]{1,0:T(8,128)(2,1)S(1)}, bf16[32,1152]{1,0:T(8,128)(2,1)S(1)}, u32[]{:S(2)}, u32[]{:S(2)}) collective-permute-start(bf16[32,1152]{1,0:T(8,128)(2,1)S(1)} %get-tuple-element.44), channel_id=1, source_target_pairs={{3,0},{4,1},{1,2},{6,3},{7,4},{0,5},{5,6},{2,7},{11,8},{12,9},{9,1... | collective-permute-start | bytes 221192 | tf_op jit(solution)/shard_map/ppermute | solution.py:275
  25.1 1.0 %collective-permute-start.12 = (bf16[32,1152]{1,0:T(8,128)(2,1)S(1)}, bf16[32,1152]{1,0:T(8,128)(2,1)S(1)}, u32[]{:S(2)}, u32[]{:S(2)}) collective-permute-start(bf16[32,1152]{1,0:T(8,128)(2,1)S(1)} %get-tuple-element.45), channel_id=1, source_target_pairs={{5,0},{2,1},{7,2},{0,3},{1,4},{6,5},{3,6},{4,7},{13,8},{10,9},{15,... | collective-permute-start | bytes 221192 | tf_op jit(solution)/shard_map/ppermute | solution.py:275
  26.1 1.8 %collective-permute-done.10.refs_0_ = bf16[32,1152]{1,0:T(8,128)(2,1)S(1)} collective-permute-done((bf16[32,1152]{1,0:T(8,128)(2,1)S(1)}, bf16[32,1152]{1,0:T(8,128)(2,1)S(1)}, u32[]{:S(2)}, u32[]{:S(2)}) %collective-permute-start.10) | collective-permute-done | bytes 73760 | tf_op jit(solution)/shard_map/ppermute | solution.py:275
  27.9 0.7 %collective-permute-done.11.refs_1_ = bf16[32,1152]{1,0:T(8,128)(2,1)S(1)} collective-permute-done((bf16[32,1152]{1,0:T(8,128)(2,1)S(1)}, bf16[32,1152]{1,0:T(8,128)(2,1)S(1)}, u32[]{:S(2)}, u32[]{:S(2)}) %collective-permute-start.11) | collective-permute-done | bytes 73760 | tf_op jit(solution)/shard_map/ppermute | solution.py:275
  28.6 1.2 %collective-permute-done.12.refs_2_ = bf16[32,1152]{1,0:T(8,128)(2,1)S(1)} collective-permute-done((bf16[32,1152]{1,0:T(8,128)(2,1)S(1)}, bf16[32,1152]{1,0:T(8,128)(2,1)S(1)}, u32[]{:S(2)}, u32[]{:S(2)}) %collective-permute-start.12) | collective-permute-done | bytes 73760 | tf_op jit(solution)/shard_map/ppermute | solution.py:275
  29.9 0.0 copy-done
  29.9 0.8 %shard_map.56 = (f32[32,1024]{1,0:T(8,128)}, f32[1,32]{1,0:T(1,128)}) custom-call(f32[32,1024]{1,0:T(8,128)S(1)} %get-tuple-element.41.own_ref, f32[32,128]{1,0:T(8,128)S(1)} %get-tuple-element.42.own_mass_ref, f32[32,1024]{1,0:T(8,128)S(1)} %copy-done, bf16[32,1152]{1,0:T(8,128)(2,1)S(1)} %collective-permute-done.10.refs_0_, ...), custom_call_target="tpu_custom_call" | custom-call | bytes 499712 | tf_op jit(solution)/shard_map/pallas_call | solution.py:224
  (4 shorter events, 0.0 us)
Async XLA Ops:
  1.5 7.9 %collective-permute-start.3 = (bf16[32,1024]{1,0:T(8,128)(2,1)S(1)}, bf16[32,1024]{1,0:T(8,128)(2,1)S(1)}, u32[]{:S(2)}, u32[]{:S(2)}) collective-permute-start(bf16[32,1024]{1,0:T(8,128)(2,1)S(1)} %convert_element_type.3.follow_ref), channel_id=1, source_target_pairs={{0,7},{1,6},{2,5},{3,4},{4,3},{5,2},{6,1},{7,0},{8,15},{9,14},{10,... | collective-permute-start | bytes 196616 | tf_op jit(solution)/shard_map/ppermute | solution.py:241
  4.9 4.5 %collective-permute-start.2 = (bf16[32,1024]{1,0:T(8,128)(2,1)S(1)}, bf16[32,1024]{1,0:T(8,128)(2,1)S(1)}, u32[]{:S(2)}, u32[]{:S(2)}) collective-permute-start(bf16[32,1024]{1,0:T(8,128)(2,1)S(1)} %convert_element_type.3.follow_ref), channel_id=1, source_target_pairs={{0,5},{1,2},{2,7},{3,0},{4,1},{5,6},{6,3},{7,4},{8,13},{9,10},{10,... | collective-permute-start | bytes 196616 | tf_op jit(solution)/shard_map/ppermute | solution.py:241
  5.7 4.5 %collective-permute-start = (bf16[32,1024]{1,0:T(8,128)(2,1)S(1)}, bf16[32,1024]{1,0:T(8,128)(2,1)S(1)}, u32[]{:S(2)}, u32[]{:S(2)}) collective-permute-start(bf16[32,1024]{1,0:T(8,128)(2,1)S(1)} %convert_element_type.3.follow_ref), channel_id=1, source_target_pairs={{0,3},{1,4},{2,1},{3,6},{4,7},{5,0},{6,5},{7,2},{8,11},{9,12},{10,... | collective-permute-start | bytes 196616 | tf_op jit(solution)/shard_map/ppermute | solution.py:241
  9.5 1.8 %collective-permute-start.4 = (bf16[64,1024]{1,0:T(8,128)(2,1)S(1)}, bf16[64,1024]{1,0:T(8,128)(2,1)S(1)}, u32[]{:S(2)}, u32[]{:S(2)}) collective-permute-start(bf16[64,1024]{1,0:T(8,128)(2,1)S(1)} %constant_dynamic-update-slice_fusion.2.refs_1_), channel_id=1, source_target_pairs={{0,1},{1,0},{2,3},{3,2},{4,5},{5,4},{6,7},{7,6},{8,9},{9,8},{10,11... | collective-permute-start | bytes 393224 | tf_op jit(solution)/shard_map/ppermute | solution.py:17
  10.3 1.4 %collective-permute-start.1 = (bf16[64,1024]{1,0:T(8,128)(2,1)S(1)}, bf16[64,1024]{1,0:T(8,128)(2,1)S(1)}, u32[]{:S(2)}, u32[]{:S(2)}) collective-permute-start(bf16[64,1024]{1,0:T(8,128)(2,1)S(1)} %constant_dynamic-update-slice_fusion.refs_0_), channel_id=1, source_target_pairs={{0,1},{1,0},{2,3},{3,2},{4,5},{5,4},{6,7},{7,6},{8,9},{9,8},{10,11... | collective-permute-start | bytes 393224 | tf_op jit(solution)/shard_map/ppermute | solution.py:17
  12.6 6.4 %collective-permute-start.7 = (f32[16,128]{1,0:T(8,128)S(1)}, f32[16,128]{1,0:T(8,128)S(1)}, u32[]{:S(2)}, u32[]{:S(2)}) collective-permute-start(f32[16,128]{1,0:T(8,128)S(1)} %get-tuple-element.30.follow_ref), channel_id=1, source_target_pairs={{0,16},{8,24},{16,8},{24,0},{1,17},{9,25},{17,9},{25,1},{2,18},{10... | collective-permute-start | bytes 24584 | tf_op jit(solution)/shard_map/ppermute | solution.py:253
  15.2 4.6 %collective-permute-start.6 = (f32[16,128]{1,0:T(8,128)S(1)}, f32[16,128]{1,0:T(8,128)S(1)}, u32[]{:S(2)}, u32[]{:S(2)}) collective-permute-start(f32[16,128]{1,0:T(8,128)S(1)} %get-tuple-element.30.follow_ref), channel_id=1, source_target_pairs={{0,24},{8,16},{16,0},{24,8},{1,25},{9,17},{17,1},{25,9},{2,26},{10... | collective-permute-start | bytes 24584 | tf_op jit(solution)/shard_map/ppermute | solution.py:253
  16.5 3.7 %collective-permute-start.5 = (f32[16,128]{1,0:T(8,128)S(1)}, f32[16,128]{1,0:T(8,128)S(1)}, u32[]{:S(2)}, u32[]{:S(2)}) collective-permute-start(f32[16,128]{1,0:T(8,128)S(1)} %get-tuple-element.30.follow_ref), channel_id=1, source_target_pairs={{0,8},{8,0},{16,24},{24,16},{1,9},{9,1},{17,25},{25,17},{2,10},{10... | collective-permute-start | bytes 24584 | tf_op jit(solution)/shard_map/ppermute | solution.py:253
  20.9 9.0 %copy-start = (f32[32,1024]{1,0:T(8,128)S(1)}, f32[32,1024]{1,0:T(8,128)}, u32[]{:S(2)}) copy-start(f32[32,1024]{1,0:T(8,128)} %cent_ref.1) | copy-start | bytes 393220
  20.9 1.4 %collective-permute-start.8 = (bf16[64,1152]{1,0:T(8,128)(2,1)S(1)}, bf16[64,1152]{1,0:T(8,128)(2,1)S(1)}, u32[]{:S(2)}, u32[]{:S(2)}) collective-permute-start(bf16[64,1152]{1,0:T(8,128)(2,1)S(1)} %get-tuple-element.39), channel_id=1, source_target_pairs={{0,1},{1,0},{2,3},{3,2},{4,5},{5,4},{6,7},{7,6},{8,9},{9,8},{10,11... | collective-permute-start | bytes 442376 | tf_op jit(solution)/shard_map/ppermute | solution.py:17
  21.0 1.6 %collective-permute-start.9 = (bf16[64,1152]{1,0:T(8,128)(2,1)S(1)}, bf16[64,1152]{1,0:T(8,128)(2,1)S(1)}, u32[]{:S(2)}, u32[]{:S(2)}) collective-permute-start(bf16[64,1152]{1,0:T(8,128)(2,1)S(1)} %get-tuple-element.40), channel_id=1, source_target_pairs={{0,1},{1,0},{2,3},{3,2},{4,5},{5,4},{6,7},{7,6},{8,9},{9,8},{10,11... | collective-permute-start | bytes 442376 | tf_op jit(solution)/shard_map/ppermute | solution.py:17
  22.8 5.1 %collective-permute-start.10 = (bf16[32,1152]{1,0:T(8,128)(2,1)S(1)}, bf16[32,1152]{1,0:T(8,128)(2,1)S(1)}, u32[]{:S(2)}, u32[]{:S(2)}) collective-permute-start(bf16[32,1152]{1,0:T(8,128)(2,1)S(1)} %get-tuple-element.43), channel_id=1, source_target_pairs={{7,0},{6,1},{5,2},{4,3},{3,4},{2,5},{1,6},{0,7},{15,8},{14,9},{13,... | collective-permute-start | bytes 221192 | tf_op jit(solution)/shard_map/ppermute | solution.py:275
  24.4 4.3 %collective-permute-start.11 = (bf16[32,1152]{1,0:T(8,128)(2,1)S(1)}, bf16[32,1152]{1,0:T(8,128)(2,1)S(1)}, u32[]{:S(2)}, u32[]{:S(2)}) collective-permute-start(bf16[32,1152]{1,0:T(8,128)(2,1)S(1)} %get-tuple-element.44), channel_id=1, source_target_pairs={{3,0},{4,1},{1,2},{6,3},{7,4},{0,5},{5,6},{2,7},{11,8},{12,9},{9,1... | collective-permute-start | bytes 221192 | tf_op jit(solution)/shard_map/ppermute | solution.py:275
  25.1 4.7 %collective-permute-start.12 = (bf16[32,1152]{1,0:T(8,128)(2,1)S(1)}, bf16[32,1152]{1,0:T(8,128)(2,1)S(1)}, u32[]{:S(2)}, u32[]{:S(2)}) collective-permute-start(bf16[32,1152]{1,0:T(8,128)(2,1)S(1)} %get-tuple-element.45), channel_id=1, source_target_pairs={{5,0},{2,1},{7,2},{0,3},{1,4},{6,5},{3,6},{4,7},{13,8},{10,9},{15,... | collective-permute-start | bytes 221192 | tf_op jit(solution)/shard_map/ppermute | solution.py:275

commit v19 on v14

--- a/solution.py
+++ b/solution.py
@@ -92,6 +92,12 @@
     )(*[pltpu.with_memory_space_constraint(x, pltpu.HBM) for x in sources], follow)
 
 
+def put_row(ref, start, row):
+    for i in range(row.shape[1] // LANES):
+        at = start // LANES + i
+        ref[at:at + 1, :] = row[:, i * LANES:(i + 1) * LANES]
+
+
 def scores_kernel(chunk, docs_ref, table_ref, part_ref, top_ref, sum_ref):
     width, count = docs_ref.shape
     scale = 4.0 / math.sqrt(width)
@@ -105,8 +111,8 @@
         top = jnp.max(scores, axis=0, keepdims=True)
         part = jnp.exp(scores - top)
         part_ref[:, cols] = part.astype(part_ref.dtype)
-        top_ref[:, cols] = top
-        sum_ref[:, cols] = jnp.sum(part, axis=0, keepdims=True)
+        put_row(top_ref, start, top)
+        put_row(sum_ref, start, jnp.sum(part, axis=0, keepdims=True))
 
 
 def last_scores_kernel(
@@ -121,16 +127,16 @@
 
 def weighted_sums(chunk, factor, docs_ref, part_ref, resp_ref, store):
     rows, count = part_ref.shape
-    mass = jnp.zeros((rows, 1), jnp.float32)
-    for start in range(0, count, chunk):
-        cols = slice(start, start + chunk)
-        resp = part_ref[:, cols].astype(jnp.float32) * factor[:, cols]
-        mass += jnp.sum(resp, axis=1, keepdims=True)
+    mass = jnp.zeros((rows, LANES), jnp.float32)
+    for i in range(count // LANES):
+        cols = slice(i * LANES, (i + 1) * LANES)
+        resp = part_ref[:, cols].astype(jnp.float32) * factor[i:i + 1]
+        mass += resp
         resp_ref[:, cols] = resp.astype(jnp.bfloat16)
     for start in range(0, docs_ref.shape[1], chunk):
         cols = slice(start, start + chunk)
         store(cols, jnp.dot(resp_ref[...], docs_ref[:, cols], preferred_element_type=jnp.float32))
-    return mass
+    return jnp.sum(mass, axis=1, keepdims=True)
 
 
 def mass_lanes(mass):
@@ -188,8 +194,9 @@
     store(slice(width, width + LANES), mass_lanes(mass))
 
 
-def final_kernel(own_ref, own_mass_ref, cent_ref, *refs):
-    *got_refs, next_ref, mass_ref = refs
+def final_kernel(own_ref, own_mass_ref, cent_ref, lse_ref, *refs):
+    *got_refs, next_ref, mass_ref, doc_lse_ref = refs
+    doc_lse_ref[...] = lse_ref[...]
     width = own_ref.shape[1]
     got = [read_rows(r[...], width) for r in got_refs]
     term = tree([own_ref[...]] + [a for a, _ in got], jnp.add)
@@ -226,7 +233,7 @@
             )(*args)
 
         flops = 2 * half * count * width
-        stats = [shape((1, count)), shape((1, count))]
+        stats = [shape((count // LANES, LANES)), shape((count // LANES, LANES))]
         resp = [pltpu.VMEM((half, count), jnp.bfloat16)]
         rounded = centroids.astype(jnp.bfloat16)
         routes = chip_plan(n)
@@ -246,9 +253,9 @@
         )
         others = [lax.ppermute(lse, "cgrp", pairs) for pairs in plan]
         their_part = swap(other_part, "dev", n, 1)
-        docs, lse = load([docs], lse)
+        docs, their_docs, lse = load([docs, their_docs], lse)
         doc_lse, factor, their_factor = call(
-            functools.partial(factors_kernel, g, plan), [shape((1, count))] * 3,
+            functools.partial(factors_kernel, g, plan), [shape((count // LANES, LANES))] * 3,
             lax.axis_index("cgrp").reshape(1), lse, *others, top, other_top,
         )
         their_factor = swap(their_factor, "dev", n, 1)
@@ -267,9 +274,9 @@
             lax.ppermute(x, "dev", [(target, source) for source, target in pairs])
             for x, pairs in zip(sends, routes)
         ]
-        result, mass = call(
-            final_kernel, [shape((rows, width)), shape((1, rows))],
-            own, own_mass, centroids, *arrived,
+        result, mass, doc_lse = call(
+            final_kernel, [shape((rows, width)), shape((1, rows)), shape(doc_lse.shape)],
+            own, own_mass, centroids, doc_lse, *arrived,
         )
         return (result, mass.reshape(rows), doc_lse.reshape(count))
 

time: 33.4 us -> 30.9 us (0.925)
  waiting for transfers between devices: 6.57 us -> 5.16 us
  Pallas kernels: 11.9 us -> 10.5 us
    pallas_call x6, Pallas kernels: 6.95 us -> 4.24 us  [call(): pl.pallas_call(kernel, out_shape=outs, in_specs=[SMEM if x.dtype == jnp.i...]
    pallas_call x2, Pallas kernels: 4.93 us -> 6.22 us  [load(): pl.pallas_call(kernel, out_shape=[shape(dims, x.dtype) for x in sources]...]
    ppermute x3, waiting for transfers between devices: 1.1 us -> 0.01 us  [body(): others = [lax.ppermute(lse, 'cgrp', pairs) for pairs in plan]]
  transfers between devices with their start and end apart: 13 -> 13, of which waited for: 7 -> 5; matrix products, arithmetic and copies ran while one was open for 3% -> 3% of each run, Pallas kernels for 25% -> 29%
where the time goes in v19:
time: 30.9 us; the launch traced here: 30.7 us
  starting transfers between devices  13.4 us (43%)
  Pallas kernels  10.5 us (34%)
  waiting for transfers between devices  5.16 us (17%)
  other arithmetic  0.91 us (3%)
  between operations  0.78 us (3%)
    pallas_call x2, Pallas kernels, load(): pl.pallas_call(kernel, out_shape=[shape(dims, x.dtype) for x in sources]...  6.22 us
    ppermute x3, starting transfers between devices, body(): blocks = [lax.ppermute(rounded, 'dev', pairs) for pairs in routes]  5.36 us
    pallas_call x6, Pallas kernels, call(): pl.pallas_call(kernel, out_shape=outs, in_specs=[SMEM if x.dtype == jnp.i...  4.24 us
    ppermute x3, waiting for transfers between devices, body(): lax.ppermute(x, 'dev', [(target, source) for source, target in pairs])  4.23 us
    ppermute x3, starting transfers between devices, body(): others = [lax.ppermute(lse, 'cgrp', pairs) for pairs in plan]  4.18 us
    ppermute x3, starting transfers between devices, body(): lax.ppermute(x, 'dev', [(target, source) for source, target in pairs])  2.88 us
    ppermute x4, starting transfers between devices, swap(): return lax.ppermute(x, axis, [(i, i ^ mask) for i in range(size)])  0.92 us
    ppermute x4, waiting for transfers between devices, swap(): return lax.ppermute(x, axis, [(i, i ^ mask) for i in range(size)])  0.92 us
  transfers between devices with their start and end apart: 13, of which 5 were waited for; matrix products, arithmetic and copies ran while one was open for 3% of the time, Pallas kernels for 29%

profile of v19, /device:TPU:0, one launch (start us, length us, event | category | flops | bytes accessed | tf_op | source)
XLA Modules:
  0.0 30.7 jit_solution(507039493445541111)
XLA Ops:
  0.6 0.5 %collective-permute-start = (bf16[2048,1024]{1,0:T(8,128)(2,1)}, bf16[2048,1024]{1,0:T(8,128)(2,1)}, u32[]{:S(2)}, u32[]{:S(2)}) collective-permute-start(bf16[2048,1024]{1,0:T(8,128)(2,1)} %refs_0_.1), channel_id=1, source_target_pairs={{0,1},{1,0},{2,3},{3,2},{4,5},{5,4},{6,7},{7,6},{8,9},{9,8},{10,11... | collective-permute-start | bytes 12582920 | tf_op jit(solution)/shard_map/ppermute | solution.py:17
  1.1 0.9 %convert_element_type.3.follow_ref = bf16[32,1024]{1,0:T(8,128)(2,1)S(1)} convert(f32[32,1024]{1,0:T(8,128)} %cent_ref.1) | non-fusion elementwise | flops 32768 | bytes 196608 | tf_op jit(solution)/shard_map/convert_element_type | solution.py:238
  2.1 3.6 %collective-permute-start.1 = (bf16[32,1024]{1,0:T(8,128)(2,1)S(1)}, bf16[32,1024]{1,0:T(8,128)(2,1)S(1)}, u32[]{:S(2)}, u32[]{:S(2)}) collective-permute-start(bf16[32,1024]{1,0:T(8,128)(2,1)S(1)} %convert_element_type.3.follow_ref), channel_id=1, source_target_pairs={{0,7},{1,6},{2,5},{3,4},{4,3},{5,2},{6,1},{7,0},{8,15},{9,14},{10,... | collective-permute-start | bytes 196616 | tf_op jit(solution)/shard_map/ppermute | solution.py:240
  5.7 0.2 collective-permute-start.2
  5.8 1.6 %collective-permute-start.3 = (bf16[32,1024]{1,0:T(8,128)(2,1)S(1)}, bf16[32,1024]{1,0:T(8,128)(2,1)S(1)}, u32[]{:S(2)}, u32[]{:S(2)}) collective-permute-start(bf16[32,1024]{1,0:T(8,128)(2,1)S(1)} %convert_element_type.3.follow_ref), channel_id=1, source_target_pairs={{0,5},{1,2},{2,7},{3,0},{4,1},{5,6},{6,3},{7,4},{8,13},{9,10},{10,... | collective-permute-start | bytes 196616 | tf_op jit(solution)/shard_map/ppermute | solution.py:240
  7.4 2.7 %shard_map.49 = (bf16[1024,2048]{1,0:T(8,128)(2,1)S(1)}, bf16[32,1024]{1,0:T(8,128)(2,1)S(1)}) custom-call(bf16[2048,1024]{1,0:T(8,128)(2,1)} %refs_0_.1, bf16[32,1024]{1,0:T(8,128)(2,1)S(1)} %convert_element_type.3.follow_ref), custom_call_target="tpu_custom_call" | custom-call | bytes 8388608 | tf_op jit(solution)/shard_map/pallas_call | solution.py:82
  10.2 0.0 collective-permute-done.1
  10.2 0.0 collective-permute-done.2
  10.2 0.0 collective-permute-done.3
  10.3 0.1 collective-permute-start.4
  10.4 0.9 %shard_map.50 = (f32[128,2048]{1,0:T(8,128)S(1)}, f32[16,128]{1,0:T(8,128)S(1)}, f32[16,128]{1,0:T(8,128)S(1)}) custom-call(bf16[1024,2048]{1,0:T(8,128)(2,1)S(1)} %get-tuple-element.27.docs_ref, bf16[128,1024]{1,0:T(8,128)(2,1)S(1)} %constant_dynamic-update-slice_fusion.table_ref), custom_call_target="tpu_custom_call" | custom-call | flops 536870912 | bytes 4456448 | tf_op jit(solution)/shard_map/pallas_call | solution.py:223
  11.3 0.6 %collective-permute-done.4.table_ref = bf16[128,1024]{1,0:T(8,128)(2,1)S(1)} collective-permute-done((bf16[128,1024]{1,0:T(8,128)(2,1)S(1)}, bf16[128,1024]{1,0:T(8,128)(2,1)S(1)}, u32[]{:S(2)}, u32[]{:S(2)}) %collective-permute-start.4) | collective-permute-done | bytes 262176 | tf_op jit(solution)/shard_map/ppermute | solution.py:17
  11.9 0.9 %shard_map.51 = (bf16[128,2048]{1,0:T(8,128)(2,1)S(1)}, f32[16,128]{1,0:T(8,128)S(1)}, f32[16,128]{1,0:T(8,128)S(1)}) custom-call(bf16[1024,2048]{1,0:T(8,128)(2,1)S(1)} %get-tuple-element.27.docs_ref, bf16[128,1024]{1,0:T(8,128)(2,1)S(1)} %collective-permute-done.4.table_ref, f32[16,128]{1,0:T(8,128)S(1)} %get-tuple-element.29.first_top_ref.refs_3_, ...), custom_call_target="tpu_custom_call" | custom-call | flops 536870912 | bytes 4472832 | tf_op jit(solution)/shard_map/pallas_call | solution.py:223
  12.8 0.2 collective-permute-start.9
  13.0 2.6 %collective-permute-start.5 = (f32[16,128]{1,0:T(8,128)S(1)}, f32[16,128]{1,0:T(8,128)S(1)}, u32[]{:S(2)}, u32[]{:S(2)}) collective-permute-start(f32[16,128]{1,0:T(8,128)S(1)} %get-tuple-element.31.refs_2_), channel_id=1, source_target_pairs={{0,16},{8,24},{16,8},{24,0},{1,17},{9,25},{17,9},{25,1},{2,18},{10... | collective-permute-start | bytes 24584 | tf_op jit(solution)/shard_map/ppermute | solution.py:254
  15.6 1.2 %collective-permute-start.6 = (f32[16,128]{1,0:T(8,128)S(1)}, f32[16,128]{1,0:T(8,128)S(1)}, u32[]{:S(2)}, u32[]{:S(2)}) collective-permute-start(f32[16,128]{1,0:T(8,128)S(1)} %get-tuple-element.31.refs_2_), channel_id=1, source_target_pairs={{0,24},{8,16},{16,0},{24,8},{1,25},{9,17},{17,1},{25,9},{2,26},{10... | collective-permute-start | bytes 24584 | tf_op jit(solution)/shard_map/ppermute | solution.py:254
  16.8 0.3 %collective-permute-start.7 = (f32[16,128]{1,0:T(8,128)S(1)}, f32[16,128]{1,0:T(8,128)S(1)}, u32[]{:S(2)}, u32[]{:S(2)}) collective-permute-start(f32[16,128]{1,0:T(8,128)S(1)} %get-tuple-element.31.refs_2_), channel_id=1, source_target_pairs={{0,8},{8,0},{16,24},{24,16},{1,9},{9,1},{17,25},{25,17},{2,10},{10... | collective-permute-start | bytes 24584 | tf_op jit(solution)/shard_map/ppermute | solution.py:254
  17.1 0.0 collective-permute-done.refs_1_
  17.2 3.5 %shard_map.52 = (bf16[2048,1024]{1,0:T(8,128)(2,1)S(1)}, bf16[2048,1024]{1,0:T(8,128)(2,1)S(1)}, f32[16,128]{1,0:T(8,128)S(1)}) custom-call(bf16[2048,1024]{1,0:T(8,128)(2,1)} %refs_0_.1, bf16[2048,1024]{1,0:T(8,128)(2,1)} %collective-permute-done.refs_1_, f32[16,128]{1,0:T(8,128)S(1)} %get-tuple-element.31.refs_2_), custom_call_target="tpu_custom_call" | custom-call | bytes 16777216 | tf_op jit(solution)/shard_map/pallas_call | solution.py:82
  20.6 0.0 collective-permute-done.5.refs_0_
  20.7 0.0 collective-permute-done.6.refs_1_
  20.7 0.0 collective-permute-done.7.refs_2_
  20.7 0.1 collective-permute-start.8
  20.8 0.0 copy-start
  20.8 0.8 %shard_map.54 = (f32[128,1024]{1,0:T(8,128)S(1)}, f32[128,128]{1,0:T(8,128)S(1)}) custom-call(f32[16,128]{1,0:T(8,128)S(1)} %get-tuple-element.37.factor_ref, bf16[2048,1024]{1,0:T(8,128)(2,1)S(1)} %get-tuple-element.38.docs_ref, f32[128,2048]{1,0:T(8,128)S(1)} %get-tuple-element.39.part_ref), custom_call_target="tpu_custom_call" | custom-call | flops 536870912 | bytes 5251072 | tf_op jit(solution)/shard_map/pallas_call | solution.py:223
  21.6 0.0 collective-permute-done.9.part_ref
  21.6 0.3 %collective-permute-done.8.factor_ref = f32[16,128]{1,0:T(8,128)S(1)} collective-permute-done((f32[16,128]{1,0:T(8,128)S(1)}, f32[16,128]{1,0:T(8,128)S(1)}, u32[]{:S(2)}, u32[]{:S(2)}) %collective-permute-start.8) | collective-permute-done | bytes 8224 | tf_op jit(solution)/shard_map/ppermute | solution.py:17
  22.0 0.8 %shard_map.55 = (f32[32,1024]{1,0:T(8,128)S(1)}, f32[32,128]{1,0:T(8,128)S(1)}, bf16[32,1152]{1,0:T(8,128)(2,1)S(1)}, bf16[32,1152]{1,0:T(8,128)(2,1)S(1)}, bf16[32,1152]{1,0:T(8,128)(2,1)S(1)}) custom-call(f32[16,128]{1,0:T(8,128)S(1)} %collective-permute-done.8.factor_ref, bf16[2048,1024]{1,0:T(8,128)(2,1)S(1)} %get-tuple-element.35.docs_ref, ...), custom_call_target="tpu_custom_call" | custom-call | flops 536870912 | bytes 5316608 | tf_op jit(solution)/shard_map/pallas_call | solution.py:223
  22.8 1.1 %collective-permute-start.10 = (bf16[32,1152]{1,0:T(8,128)(2,1)S(1)}, bf16[32,1152]{1,0:T(8,128)(2,1)S(1)}, u32[]{:S(2)}, u32[]{:S(2)}) collective-permute-start(bf16[32,1152]{1,0:T(8,128)(2,1)S(1)} %get-tuple-element.45), channel_id=1, source_target_pairs={{7,0},{6,1},{5,2},{4,3},{3,4},{2,5},{1,6},{0,7},{15,8},{14,9},{13,... | collective-permute-start | bytes 221192 | tf_op jit(solution)/shard_map/ppermute | solution.py:274
  23.9 1.2 %collective-permute-start.11 = (bf16[32,1152]{1,0:T(8,128)(2,1)S(1)}, bf16[32,1152]{1,0:T(8,128)(2,1)S(1)}, u32[]{:S(2)}, u32[]{:S(2)}) collective-permute-start(bf16[32,1152]{1,0:T(8,128)(2,1)S(1)} %get-tuple-element.46), channel_id=1, source_target_pairs={{3,0},{4,1},{1,2},{6,3},{7,4},{0,5},{5,6},{2,7},{11,8},{12,9},{9,1... | collective-permute-start | bytes 221192 | tf_op jit(solution)/shard_map/ppermute | solution.py:274
  25.1 0.5 %collective-permute-start.12 = (bf16[32,1152]{1,0:T(8,128)(2,1)S(1)}, bf16[32,1152]{1,0:T(8,128)(2,1)S(1)}, u32[]{:S(2)}, u32[]{:S(2)}) collective-permute-start(bf16[32,1152]{1,0:T(8,128)(2,1)S(1)} %get-tuple-element.47), channel_id=1, source_target_pairs={{5,0},{2,1},{7,2},{0,3},{1,4},{6,5},{3,6},{4,7},{13,8},{10,9},{15,... | collective-permute-start | bytes 221192 | tf_op jit(solution)/shard_map/ppermute | solution.py:274
  25.6 2.5 %collective-permute-done.10.refs_0_ = bf16[32,1152]{1,0:T(8,128)(2,1)S(1)} collective-permute-done((bf16[32,1152]{1,0:T(8,128)(2,1)S(1)}, bf16[32,1152]{1,0:T(8,128)(2,1)S(1)}, u32[]{:S(2)}, u32[]{:S(2)}) %collective-permute-start.10) | collective-permute-done | bytes 73760 | tf_op jit(solution)/shard_map/ppermute | solution.py:274
  28.1 0.8 %collective-permute-done.11.refs_1_ = bf16[32,1152]{1,0:T(8,128)(2,1)S(1)} collective-permute-done((bf16[32,1152]{1,0:T(8,128)(2,1)S(1)}, bf16[32,1152]{1,0:T(8,128)(2,1)S(1)}, u32[]{:S(2)}, u32[]{:S(2)}) %collective-permute-start.11) | collective-permute-done | bytes 73760 | tf_op jit(solution)/shard_map/ppermute | solution.py:274
  28.9 1.0 %collective-permute-done.12.refs_2_ = bf16[32,1152]{1,0:T(8,128)(2,1)S(1)} collective-permute-done((bf16[32,1152]{1,0:T(8,128)(2,1)S(1)}, bf16[32,1152]{1,0:T(8,128)(2,1)S(1)}, u32[]{:S(2)}, u32[]{:S(2)}) %collective-permute-start.12) | collective-permute-done | bytes 73760 | tf_op jit(solution)/shard_map/ppermute | solution.py:274
  29.9 0.0 copy-done
  29.9 0.8 %shard_map.56 = (f32[32,1024]{1,0:T(8,128)}, f32[1,32]{1,0:T(1,128)}, f32[16,128]{1,0:T(8,128)}) custom-call(f32[32,1024]{1,0:T(8,128)S(1)} %get-tuple-element.42.own_ref, f32[32,128]{1,0:T(8,128)S(1)} %get-tuple-element.43.own_mass_ref, f32[32,1024]{1,0:T(8,128)S(1)} %copy-done, f32[16,128]{1,0:T(8,128)S(1)} %get-tuple-element.44.lse_ref, ...), custom_call_target="tpu_custom_call" | custom-call | bytes 507904 | tf_op jit(solution)/shard_map/pallas_call | solution.py:223
  (5 shorter events, 0.1 us)
Async XLA Ops:
  0.6 16.5 %collective-permute-start = (bf16[2048,1024]{1,0:T(8,128)(2,1)}, bf16[2048,1024]{1,0:T(8,128)(2,1)}, u32[]{:S(2)}, u32[]{:S(2)}) collective-permute-start(bf16[2048,1024]{1,0:T(8,128)(2,1)} %refs_0_.1), channel_id=1, source_target_pairs={{0,1},{1,0},{2,3},{3,2},{4,5},{5,4},{6,7},{7,6},{8,9},{9,8},{10,11... | collective-permute-start | bytes 12582920 | tf_op jit(solution)/shard_map/ppermute | solution.py:17
  2.1 8.1 %collective-permute-start.1 = (bf16[32,1024]{1,0:T(8,128)(2,1)S(1)}, bf16[32,1024]{1,0:T(8,128)(2,1)S(1)}, u32[]{:S(2)}, u32[]{:S(2)}) collective-permute-start(bf16[32,1024]{1,0:T(8,128)(2,1)S(1)} %convert_element_type.3.follow_ref), channel_id=1, source_target_pairs={{0,7},{1,6},{2,5},{3,4},{4,3},{5,2},{6,1},{7,0},{8,15},{9,14},{10,... | collective-permute-start | bytes 196616 | tf_op jit(solution)/shard_map/ppermute | solution.py:240
  5.7 4.5 %collective-permute-start.2 = (bf16[32,1024]{1,0:T(8,128)(2,1)S(1)}, bf16[32,1024]{1,0:T(8,128)(2,1)S(1)}, u32[]{:S(2)}, u32[]{:S(2)}) collective-permute-start(bf16[32,1024]{1,0:T(8,128)(2,1)S(1)} %convert_element_type.3.follow_ref), channel_id=1, source_target_pairs={{0,3},{1,4},{2,1},{3,6},{4,7},{5,0},{6,5},{7,2},{8,11},{9,12},{10,... | collective-permute-start | bytes 196616 | tf_op jit(solution)/shard_map/ppermute | solution.py:240
  5.8 4.4 %collective-permute-start.3 = (bf16[32,1024]{1,0:T(8,128)(2,1)S(1)}, bf16[32,1024]{1,0:T(8,128)(2,1)S(1)}, u32[]{:S(2)}, u32[]{:S(2)}) collective-permute-start(bf16[32,1024]{1,0:T(8,128)(2,1)S(1)} %convert_element_type.3.follow_ref), channel_id=1, source_target_pairs={{0,5},{1,2},{2,7},{3,0},{4,1},{5,6},{6,3},{7,4},{8,13},{9,10},{10,... | collective-permute-start | bytes 196616 | tf_op jit(solution)/shard_map/ppermute | solution.py:240
  10.3 1.6 %collective-permute-start.4 = (bf16[128,1024]{1,0:T(8,128)(2,1)S(1)}, bf16[128,1024]{1,0:T(8,128)(2,1)S(1)}, u32[]{:S(2)}, u32[]{:S(2)}) collective-permute-start(bf16[128,1024]{1,0:T(8,128)(2,1)S(1)} %constant_dynamic-update-slice_fusion.table_ref), channel_id=1, source_target_pairs={{0,1},{1,0},{2,3},{3,2},{4,5},{5,4},{6,7},{7,6},{8,9},{9,8},{10,11... | collective-permute-start | bytes 786440 | tf_op jit(solution)/shard_map/ppermute | solution.py:17
  12.8 8.8 %collective-permute-start.9 = (bf16[128,2048]{1,0:T(8,128)(2,1)S(1)}, bf16[128,2048]{1,0:T(8,128)(2,1)S(1)}, u32[]{:S(2)}, u32[]{:S(2)}) collective-permute-start(bf16[128,2048]{1,0:T(8,128)(2,1)S(1)} %get-tuple-element.36), channel_id=1, source_target_pairs={{0,1},{1,0},{2,3},{3,2},{4,5},{5,4},{6,7},{7,6},{8,9},{9,8},{10,11... | collective-permute-start | bytes 1572872 | tf_op jit(solution)/shard_map/ppermute | solution.py:17
  13.0 7.7 %collective-permute-start.5 = (f32[16,128]{1,0:T(8,128)S(1)}, f32[16,128]{1,0:T(8,128)S(1)}, u32[]{:S(2)}, u32[]{:S(2)}) collective-permute-start(f32[16,128]{1,0:T(8,128)S(1)} %get-tuple-element.31.refs_2_), channel_id=1, source_target_pairs={{0,16},{8,24},{16,8},{24,0},{1,17},{9,25},{17,9},{25,1},{2,18},{10... | collective-permute-start | bytes 24584 | tf_op jit(solution)/shard_map/ppermute | solution.py:254
  15.6 5.1 %collective-permute-start.6 = (f32[16,128]{1,0:T(8,128)S(1)}, f32[16,128]{1,0:T(8,128)S(1)}, u32[]{:S(2)}, u32[]{:S(2)}) collective-permute-start(f32[16,128]{1,0:T(8,128)S(1)} %get-tuple-element.31.refs_2_), channel_id=1, source_target_pairs={{0,24},{8,16},{16,0},{24,8},{1,25},{9,17},{17,1},{25,9},{2,26},{10... | collective-permute-start | bytes 24584 | tf_op jit(solution)/shard_map/ppermute | solution.py:254
  16.8 3.9 %collective-permute-start.7 = (f32[16,128]{1,0:T(8,128)S(1)}, f32[16,128]{1,0:T(8,128)S(1)}, u32[]{:S(2)}, u32[]{:S(2)}) collective-permute-start(f32[16,128]{1,0:T(8,128)S(1)} %get-tuple-element.31.refs_2_), channel_id=1, source_target_pairs={{0,8},{8,0},{16,24},{24,16},{1,9},{9,1},{17,25},{25,17},{2,10},{10... | collective-permute-start | bytes 24584 | tf_op jit(solution)/shard_map/ppermute | solution.py:254
  20.7 1.2 %collective-permute-start.8 = (f32[16,128]{1,0:T(8,128)S(1)}, f32[16,128]{1,0:T(8,128)S(1)}, u32[]{:S(2)}, u32[]{:S(2)}) collective-permute-start(f32[16,128]{1,0:T(8,128)S(1)} %get-tuple-element.34), channel_id=1, source_target_pairs={{0,1},{1,0},{2,3},{3,2},{4,5},{5,4},{6,7},{7,6},{8,9},{9,8},{10,11... | collective-permute-start | bytes 24584 | tf_op jit(solution)/shard_map/ppermute | solution.py:17
  20.8 9.1 %copy-start = (f32[32,1024]{1,0:T(8,128)S(1)}, f32[32,1024]{1,0:T(8,128)}, u32[]{:S(2)}) copy-start(f32[32,1024]{1,0:T(8,128)} %cent_ref.1) | copy-start | bytes 393220
  22.8 5.3 %collective-permute-start.10 = (bf16[32,1152]{1,0:T(8,128)(2,1)S(1)}, bf16[32,1152]{1,0:T(8,128)(2,1)S(1)}, u32[]{:S(2)}, u32[]{:S(2)}) collective-permute-start(bf16[32,1152]{1,0:T(8,128)(2,1)S(1)} %get-tuple-element.45), channel_id=1, source_target_pairs={{7,0},{6,1},{5,2},{4,3},{3,4},{2,5},{1,6},{0,7},{15,8},{14,9},{13,... | collective-permute-start | bytes 221192 | tf_op jit(solution)/shard_map/ppermute | solution.py:274
  23.9 5.0 %collective-permute-start.11 = (bf16[32,1152]{1,0:T(8,128)(2,1)S(1)}, bf16[32,1152]{1,0:T(8,128)(2,1)S(1)}, u32[]{:S(2)}, u32[]{:S(2)}) collective-permute-start(bf16[32,1152]{1,0:T(8,128)(2,1)S(1)} %get-tuple-element.46), channel_id=1, source_target_pairs={{3,0},{4,1},{1,2},{6,3},{7,4},{0,5},{5,6},{2,7},{11,8},{12,9},{9,1... | collective-permute-start | bytes 221192 | tf_op jit(solution)/shard_map/ppermute | solution.py:274
  25.1 4.8 %collective-permute-start.12 = (bf16[32,1152]{1,0:T(8,128)(2,1)S(1)}, bf16[32,1152]{1,0:T(8,128)(2,1)S(1)}, u32[]{:S(2)}, u32[]{:S(2)}) collective-permute-start(bf16[32,1152]{1,0:T(8,128)(2,1)S(1)} %get-tuple-element.47), channel_id=1, source_target_pairs={{5,0},{2,1},{7,2},{0,3},{1,4},{6,5},{3,6},{4,7},{13,8},{10,9},{15,... | collective-permute-start | bytes 221192 | tf_op jit(solution)/shard_map/ppermute | solution.py:274

commit v20 on v19

--- a/solution.py
+++ b/solution.py
@@ -20,16 +20,16 @@
 def chip_plan(n):
     near = list(range(2, n - 2, 2))
     turned = near[len(near) // 2:] + near[:len(near) // 2]
-    masks = [(n - 2, n - 2)] + list(zip(near, turned))
+    masks = list(zip(near, turned)) + [(n - 2, n - 2)]
     return [[(i, i ^ pair[i % 2] ^ 1) for i in range(n)] for pair in masks]
 
 
 def group_plan(g):
     if g == 4:
         return [
+            [(0, 1), (1, 0), (2, 3), (3, 2)],
+            [(0, 3), (1, 2), (2, 0), (3, 1)],
             [(0, 2), (1, 3), (2, 1), (3, 0)],
-            [(0, 3), (1, 2), (2, 0), (3, 1)],
-            [(0, 1), (1, 0), (2, 3), (3, 2)],
         ]
     return [[(i, i ^ m) for i in range(g)] for m in range(1, g)]
 
@@ -58,7 +58,7 @@
     sources, follow_ref = refs[:half - 1], refs[half - 1]
     targets, own_ref, sems = refs[half:-2], refs[-2], refs[-1]
     copies = [
-        pltpu.make_async_copy(source, target, sems.at[i])
+        pltpu.make_async_copy(source.at[pl.ds(0, target.shape[0])], target, sems.at[i])
         for i, (source, target) in enumerate(zip(sources, targets))
     ]
     for copy in copies:
@@ -68,7 +68,7 @@
         copy.wait()
 
 
-def load(sources, follow, chunk=0):
+def load(sources, follow, chunk=0, last_rows=0):
     kernel, dims = load_kernel, sources[0].shape
     scratch = [pltpu.SemaphoreType.DMA((len(sources),))]
     if chunk:
@@ -78,10 +78,13 @@
             pltpu.VMEM((count, width), follow.dtype),
             pltpu.SemaphoreType.DMA((count // chunk,)),
         ]
+    outs = [shape(dims, x.dtype) for x in sources]
+    if last_rows:
+        outs[-1] = shape((last_rows, dims[1]), sources[-1].dtype)
     size = sum(x.nbytes for x in sources)
     return pl.pallas_call(
         kernel,
-        out_shape=[shape(dims, x.dtype) for x in sources] + [shape(follow.shape, follow.dtype)],
+        out_shape=outs + [shape(follow.shape, follow.dtype)],
         in_specs=[pl.BlockSpec(memory_space=pltpu.HBM)] * len(sources) + [VMEM],
         out_specs=[VMEM] * (len(sources) + 1),
         scratch_shapes=scratch,
@@ -125,7 +128,7 @@
     lse_ref[...] = top + jnp.log(total)
 
 
-def weighted_sums(chunk, factor, docs_ref, part_ref, resp_ref, store):
+def weighted_sums(chunk, factor, docs_refs, part_ref, resp_ref, store):
     rows, count = part_ref.shape
     mass = jnp.zeros((rows, LANES), jnp.float32)
     for i in range(count // LANES):
@@ -133,9 +136,14 @@
         resp = part_ref[:, cols].astype(jnp.float32) * factor[i:i + 1]
         mass += resp
         resp_ref[:, cols] = resp.astype(jnp.bfloat16)
-    for start in range(0, docs_ref.shape[1], chunk):
+    for start in range(0, docs_refs[0].shape[1], chunk):
         cols = slice(start, start + chunk)
-        store(cols, jnp.dot(resp_ref[...], docs_ref[:, cols], preferred_element_type=jnp.float32))
+        term, first = 0.0, 0
+        for ref in docs_refs:
+            here = slice(first, first + ref.shape[0])
+            term += jnp.dot(resp_ref[:, here], ref[:, cols], preferred_element_type=jnp.float32)
+            first = here.stop
+        store(cols, term)
     return jnp.sum(mass, axis=1, keepdims=True)
 
 
@@ -167,16 +175,24 @@
     send_ref[...] = jnp.exp(their_top_ref[...] - doc_lse)
 
 
-def first_sums_kernel(chunk, factor_ref, docs_ref, part_ref, sum_ref, mass_ref, resp_ref):
+def first_sums_kernel(
+    chunk, factor_ref, docs_ref, part_ref, source_ref, sum_ref, mass_ref, rest_ref, resp_ref, sem
+):
+    rest = rest_ref.shape[0]
+    rest_rows = pl.ds(source_ref.shape[0] - rest, rest)
+    copy = pltpu.make_async_copy(source_ref.at[rest_rows], rest_ref, sem)
+    copy.start()
+
     def store(cols, term):
         sum_ref[:, cols] = term
 
-    mass = weighted_sums(chunk, factor_ref[...], docs_ref, part_ref, resp_ref, store)
+    mass = weighted_sums(chunk, factor_ref[...], [docs_ref], part_ref, resp_ref, store)
     mass_ref[...] = jnp.broadcast_to(mass, mass_ref.shape)
+    copy.wait()
 
 
 def second_sums_kernel(
-    chunk, factor_ref, docs_ref, part_ref, sum_ref, mass_ref, own_ref, own_mass_ref, *refs
+    chunk, factor_ref, docs_ref, rest_ref, part_ref, sum_ref, mass_ref, own_ref, own_mass_ref, *refs
 ):
     *send_refs, resp_ref = refs
     rows, width = own_ref.shape
@@ -188,7 +204,7 @@
         for slot, ref in enumerate(send_refs, 1):
             ref[:, cols] = term[slot * rows:(slot + 1) * rows].astype(jnp.bfloat16)
 
-    mass = weighted_sums(chunk, factor_ref[...], docs_ref, part_ref, resp_ref, store)
+    mass = weighted_sums(chunk, factor_ref[...], [docs_ref, rest_ref], part_ref, resp_ref, store)
     mass += mass_ref[:, :1]
     own_mass_ref[...] = jnp.broadcast_to(mass[:rows], own_mass_ref.shape)
     store(slice(width, width + LANES), mass_lanes(mass))
@@ -218,12 +234,12 @@
         plan = group_plan(g)
         limit = (4 << 20) + half * (48 << 10)
 
-        def call(kernel, outs, *args, scratch=(), flops=0):
+        def call(kernel, outs, *args, scratch=(), flops=0, specs=None):
             nbytes = sum(x.nbytes for x in args)
             return pl.pallas_call(
                 kernel,
                 out_shape=outs,
-                in_specs=[SMEM if x.dtype == jnp.int32 else VMEM for x in args],
+                in_specs=specs or [SMEM if x.dtype == jnp.int32 else VMEM for x in args],
                 out_specs=[VMEM] * len(outs),
                 scratch_shapes=scratch,
                 compiler_params=pltpu.CompilerParams(vmem_limit_bytes=limit),
@@ -253,26 +269,29 @@
         )
         others = [lax.ppermute(lse, "cgrp", pairs) for pairs in plan]
         their_part = swap(other_part, "dev", n, 1)
-        docs, their_docs, lse = load([docs, their_docs], lse)
+        rest = count // 4
+        docs, their_first, lse = load([docs, their_docs], lse, last_rows=count - rest)
         doc_lse, factor, their_factor = call(
             functools.partial(factors_kernel, g, plan), [shape((count // LANES, LANES))] * 3,
             lax.axis_index("cgrp").reshape(1), lse, *others, top, other_top,
         )
         their_factor = swap(their_factor, "dev", n, 1)
-        sums, mass = call(
+        sums, mass, their_rest = call(
             functools.partial(first_sums_kernel, chunk),
-            [shape((half, width)), shape((half, LANES))],
-            factor, docs, part, scratch=resp, flops=flops,
+            [shape((half, width)), shape((half, LANES)), shape((rest, width), docs.dtype)],
+            factor, docs, part, pltpu.with_memory_space_constraint(their_docs, pltpu.HBM),
+            scratch=resp + [pltpu.SemaphoreType.DMA], flops=flops,
+            specs=[VMEM] * 3 + [pl.BlockSpec(memory_space=pltpu.HBM)],
         )
         own, own_mass, *sends = call(
             functools.partial(second_sums_kernel, chunk),
             [shape((rows, width)), shape((rows, LANES))]
             + [shape((rows, width + LANES), jnp.bfloat16)] * (n // 2 - 1),
-            their_factor, their_docs, their_part, sums, mass, scratch=resp, flops=flops,
+            their_factor, their_first, their_rest, their_part, sums, mass, scratch=resp, flops=flops,
         )
         arrived = [
             lax.ppermute(x, "dev", [(target, source) for source, target in pairs])
-            for x, pairs in zip(sends, routes)
+            for x, pairs in zip(sends[-1:] + sends[:-1], routes[-1:] + routes[:-1])
         ]
         result, mass, doc_lse = call(
             final_kernel, [shape((rows, width)), shape((1, rows)), shape(doc_lse.shape)],

time: 30.9 us -> 30.8 us (level)
  waiting for transfers between devices: 5.16 us -> 4.06 us
  starting transfers between devices: 13.4 us -> 14.3 us
    ppermute x3, starting transfers between devices: 2.88 us -> 3.82 us  [body(): lax.ppermute(x, 'dev', [(target, source) for source, target in pairs])]
    ppermute x3, waiting for transfers between devices: 4.23 us -> 3.34 us  [body(): lax.ppermute(x, 'dev', [(target, source) for source, target in pairs])]
where the time goes in v20:
time: 30.8 us; the launch traced here: 30.6 us
  starting transfers between devices  14.3 us (46%)
  Pallas kernels  10.6 us (34%)
  waiting for transfers between devices  4.06 us (13%)
  other arithmetic  0.91 us (3%)
  between operations  0.78 us (3%)
    pallas_call x2, Pallas kernels, load(): pl.pallas_call(kernel, out_shape=outs + [shape(follow.shape, follow.dtype...  5.92 us
    ppermute x3, starting transfers between devices, body(): blocks = [lax.ppermute(rounded, 'dev', pairs) for pairs in routes]  5.36 us
    pallas_call x6, Pallas kernels, call(): pl.pallas_call(kernel, out_shape=outs, in_specs=specs or [SMEM if x.dtype...  4.67 us
    ppermute x3, starting transfers between devices, body(): others = [lax.ppermute(lse, 'cgrp', pairs) for pairs in plan]  4.18 us
    ppermute x3, starting transfers between devices, body(): lax.ppermute(x, 'dev', [(target, source) for source, target in pairs])  3.82 us
    ppermute x3, waiting for transfers between devices, body(): lax.ppermute(x, 'dev', [(target, source) for source, target in pairs])  3.34 us
    convert_element_type x1, other arithmetic, body(): rounded = centroids.astype(jnp.bfloat16)  0.91 us
    ppermute x4, starting transfers between devices, swap(): return lax.ppermute(x, axis, [(i, i ^ mask) for i in range(size)])  0.89 us
  transfers between devices with their start and end apart: 13, of which 5 were waited for; matrix products, arithmetic and copies ran while one was open for 3% of the time, Pallas kernels for 29%

profile of v20, /device:TPU:0, one launch (start us, length us, event | category | flops | bytes accessed | tf_op | source)
XLA Modules:
  0.0 30.6 jit_solution(15188276913345208762)
XLA Ops:
  0.6 0.5 %collective-permute-start = (bf16[2048,1024]{1,0:T(8,128)(2,1)}, bf16[2048,1024]{1,0:T(8,128)(2,1)}, u32[]{:S(2)}, u32[]{:S(2)}) collective-permute-start(bf16[2048,1024]{1,0:T(8,128)(2,1)} %refs_0_.1), channel_id=1, source_target_pairs={{0,1},{1,0},{2,3},{3,2},{4,5},{5,4},{6,7},{7,6},{8,9},{9,8},{10,11... | collective-permute-start | bytes 12582920 | tf_op jit(solution)/shard_map/ppermute | solution.py:17
  1.1 0.9 %convert_element_type.3.follow_ref = bf16[32,1024]{1,0:T(8,128)(2,1)S(1)} convert(f32[32,1024]{1,0:T(8,128)} %cent_ref.1) | non-fusion elementwise | flops 32768 | bytes 196608 | tf_op jit(solution)/shard_map/convert_element_type | solution.py:254
  2.1 3.6 %collective-permute-start.3 = (bf16[32,1024]{1,0:T(8,128)(2,1)S(1)}, bf16[32,1024]{1,0:T(8,128)(2,1)S(1)}, u32[]{:S(2)}, u32[]{:S(2)}) collective-permute-start(bf16[32,1024]{1,0:T(8,128)(2,1)S(1)} %convert_element_type.3.follow_ref), channel_id=1, source_target_pairs={{0,7},{1,6},{2,5},{3,4},{4,3},{5,2},{6,1},{7,0},{8,15},{9,14},{10,... | collective-permute-start | bytes 196616 | tf_op jit(solution)/shard_map/ppermute | solution.py:256
  5.7 0.1 collective-permute-start.2
  5.8 1.6 %collective-permute-start.1 = (bf16[32,1024]{1,0:T(8,128)(2,1)S(1)}, bf16[32,1024]{1,0:T(8,128)(2,1)S(1)}, u32[]{:S(2)}, u32[]{:S(2)}) collective-permute-start(bf16[32,1024]{1,0:T(8,128)(2,1)S(1)} %convert_element_type.3.follow_ref), channel_id=1, source_target_pairs={{0,3},{1,4},{2,1},{3,6},{4,7},{5,0},{6,5},{7,2},{8,11},{9,12},{10,... | collective-permute-start | bytes 196616 | tf_op jit(solution)/shard_map/ppermute | solution.py:256
  7.4 2.7 %shard_map.49 = (bf16[1024,2048]{1,0:T(8,128)(2,1)S(1)}, bf16[32,1024]{1,0:T(8,128)(2,1)S(1)}) custom-call(bf16[2048,1024]{1,0:T(8,128)(2,1)} %refs_0_.1, bf16[32,1024]{1,0:T(8,128)(2,1)S(1)} %convert_element_type.3.follow_ref), custom_call_target="tpu_custom_call" | custom-call | bytes 8388608 | tf_op jit(solution)/shard_map/pallas_call | solution.py:85
  10.2 0.0 collective-permute-done.1
  10.2 0.0 collective-permute-done.2
  10.2 0.0 collective-permute-done.3
  10.3 0.1 collective-permute-start.4
  10.4 0.9 %shard_map.50 = (f32[128,2048]{1,0:T(8,128)S(1)}, f32[16,128]{1,0:T(8,128)S(1)}, f32[16,128]{1,0:T(8,128)S(1)}) custom-call(bf16[1024,2048]{1,0:T(8,128)(2,1)S(1)} %get-tuple-element.28.docs_ref, bf16[128,1024]{1,0:T(8,128)(2,1)S(1)} %constant_dynamic-update-slice_fusion.table_ref), custom_call_target="tpu_custom_call" | custom-call | flops 536870912 | bytes 4456448 | tf_op jit(solution)/shard_map/pallas_call | solution.py:239
  11.3 0.6 %collective-permute-done.4.table_ref = bf16[128,1024]{1,0:T(8,128)(2,1)S(1)} collective-permute-done((bf16[128,1024]{1,0:T(8,128)(2,1)S(1)}, bf16[128,1024]{1,0:T(8,128)(2,1)S(1)}, u32[]{:S(2)}, u32[]{:S(2)}) %collective-permute-start.4) | collective-permute-done | bytes 262176 | tf_op jit(solution)/shard_map/ppermute | solution.py:17
  11.9 0.9 %shard_map.51 = (bf16[128,2048]{1,0:T(8,128)(2,1)S(1)}, f32[16,128]{1,0:T(8,128)S(1)}, f32[16,128]{1,0:T(8,128)S(1)}) custom-call(bf16[1024,2048]{1,0:T(8,128)(2,1)S(1)} %get-tuple-element.28.docs_ref, bf16[128,1024]{1,0:T(8,128)(2,1)S(1)} %collective-permute-done.4.table_ref, f32[16,128]{1,0:T(8,128)S(1)} %get-tuple-element.30.first_top_ref.refs_3_, ...), custom_call_target="tpu_custom_call" | custom-call | flops 536870912 | bytes 4472832 | tf_op jit(solution)/shard_map/pallas_call | solution.py:239
  12.8 0.2 collective-permute-start.9
  13.0 2.6 %collective-permute-start.7 = (f32[16,128]{1,0:T(8,128)S(1)}, f32[16,128]{1,0:T(8,128)S(1)}, u32[]{:S(2)}, u32[]{:S(2)}) collective-permute-start(f32[16,128]{1,0:T(8,128)S(1)} %get-tuple-element.32.refs_2_), channel_id=1, source_target_pairs={{0,16},{8,24},{16,8},{24,0},{1,17},{9,25},{17,9},{25,1},{2,18},{10... | collective-permute-start | bytes 24584 | tf_op jit(solution)/shard_map/ppermute | solution.py:270
  15.6 1.2 %collective-permute-start.6 = (f32[16,128]{1,0:T(8,128)S(1)}, f32[16,128]{1,0:T(8,128)S(1)}, u32[]{:S(2)}, u32[]{:S(2)}) collective-permute-start(f32[16,128]{1,0:T(8,128)S(1)} %get-tuple-element.32.refs_2_), channel_id=1, source_target_pairs={{0,24},{8,16},{16,0},{24,8},{1,25},{9,17},{17,1},{25,9},{2,26},{10... | collective-permute-start | bytes 24584 | tf_op jit(solution)/shard_map/ppermute | solution.py:270
  16.8 0.3 %collective-permute-start.5 = (f32[16,128]{1,0:T(8,128)S(1)}, f32[16,128]{1,0:T(8,128)S(1)}, u32[]{:S(2)}, u32[]{:S(2)}) collective-permute-start(f32[16,128]{1,0:T(8,128)S(1)} %get-tuple-element.32.refs_2_), channel_id=1, source_target_pairs={{0,8},{8,0},{16,24},{24,16},{1,9},{9,1},{17,25},{25,17},{2,10},{10... | collective-permute-start | bytes 24584 | tf_op jit(solution)/shard_map/ppermute | solution.py:270
  17.1 0.0 collective-permute-done.refs_1_.source_ref
  17.2 3.2 %shard_map.52 = (bf16[2048,1024]{1,0:T(8,128)(2,1)S(1)}, bf16[1536,1024]{1,0:T(8,128)(2,1)S(1)}, f32[16,128]{1,0:T(8,128)S(1)}) custom-call(bf16[2048,1024]{1,0:T(8,128)(2,1)} %refs_0_.1, bf16[2048,1024]{1,0:T(8,128)(2,1)} %collective-permute-done.refs_1_.source_ref, f32[16,128]{1,0:T(8,128)S(1)} %get-tuple-element.32.refs_2_), custom_call_target="tpu_custom_call" | custom-call | bytes 16777216 | tf_op jit(solution)/shard_map/pallas_call | solution.py:85
  20.3 0.0 collective-permute-done.7.refs_2_
  20.4 0.0 collective-permute-done.6.refs_1_
  20.4 0.1 collective-permute-done.5.refs_0_
  20.5 0.1 collective-permute-start.8
  20.6 1.2 %shard_map.54 = (f32[128,1024]{1,0:T(8,128)S(1)}, f32[128,128]{1,0:T(8,128)S(1)}, bf16[512,1024]{1,0:T(8,128)(2,1)S(1)}) custom-call(f32[16,128]{1,0:T(8,128)S(1)} %get-tuple-element.37.factor_ref, bf16[2048,1024]{1,0:T(8,128)(2,1)S(1)} %get-tuple-element.38.docs_ref, f32[128,2048]{1,0:T(8,128)S(1)} %get-tuple-element.39.part_ref, ...), custom_call_target="tpu_custom_call" | custom-call | flops 536870912 | bytes 9445376 | tf_op jit(solution)/shard_map/pallas_call | solution.py:239
  21.8 0.0 copy-start
  21.8 0.0 collective-permute-done.9.part_ref
  21.8 0.0 collective-permute-done.8.factor_ref
  21.8 0.8 %shard_map.55 = (f32[32,1024]{1,0:T(8,128)S(1)}, f32[32,128]{1,0:T(8,128)S(1)}, bf16[32,1152]{1,0:T(8,128)(2,1)S(1)}, bf16[32,1152]{1,0:T(8,128)(2,1)S(1)}, bf16[32,1152]{1,0:T(8,128)(2,1)S(1)}) custom-call(f32[16,128]{1,0:T(8,128)S(1)} %collective-permute-done.8.factor_ref, bf16[1536,1024]{1,0:T(8,128)(2,1)S(1)} %get-tuple-element.36.docs_ref, ...), custom_call_target="tpu_custom_call" | custom-call | flops 536870912 | bytes 5316608 | tf_op jit(solution)/shard_map/pallas_call | solution.py:239
  22.6 2.1 %collective-permute-start.10 = (bf16[32,1152]{1,0:T(8,128)(2,1)S(1)}, bf16[32,1152]{1,0:T(8,128)(2,1)S(1)}, u32[]{:S(2)}, u32[]{:S(2)}) collective-permute-start(bf16[32,1152]{1,0:T(8,128)(2,1)S(1)} %get-tuple-element.47), channel_id=1, source_target_pairs={{7,0},{6,1},{5,2},{4,3},{3,4},{2,5},{1,6},{0,7},{15,8},{14,9},{13,... | collective-permute-start | bytes 221192 | tf_op jit(solution)/shard_map/ppermute | solution.py:293
  24.7 0.3 %collective-permute-start.11 = (bf16[32,1152]{1,0:T(8,128)(2,1)S(1)}, bf16[32,1152]{1,0:T(8,128)(2,1)S(1)}, u32[]{:S(2)}, u32[]{:S(2)}) collective-permute-start(bf16[32,1152]{1,0:T(8,128)(2,1)S(1)} %get-tuple-element.48), channel_id=1, source_target_pairs={{3,0},{4,1},{1,2},{6,3},{7,4},{0,5},{5,6},{2,7},{11,8},{12,9},{9,1... | collective-permute-start | bytes 221192 | tf_op jit(solution)/shard_map/ppermute | solution.py:293
  25.0 1.4 %collective-permute-start.12 = (bf16[32,1152]{1,0:T(8,128)(2,1)S(1)}, bf16[32,1152]{1,0:T(8,128)(2,1)S(1)}, u32[]{:S(2)}, u32[]{:S(2)}) collective-permute-start(bf16[32,1152]{1,0:T(8,128)(2,1)S(1)} %get-tuple-element.49), channel_id=1, source_target_pairs={{5,0},{2,1},{7,2},{0,3},{1,4},{6,5},{3,6},{4,7},{13,8},{10,9},{15,... | collective-permute-start | bytes 221192 | tf_op jit(solution)/shard_map/ppermute | solution.py:293
  26.5 1.1 %collective-permute-done.10.refs_0_ = bf16[32,1152]{1,0:T(8,128)(2,1)S(1)} collective-permute-done((bf16[32,1152]{1,0:T(8,128)(2,1)S(1)}, bf16[32,1152]{1,0:T(8,128)(2,1)S(1)}, u32[]{:S(2)}, u32[]{:S(2)}) %collective-permute-start.10) | collective-permute-done | bytes 73760 | tf_op jit(solution)/shard_map/ppermute | solution.py:293
  27.5 1.1 %collective-permute-done.11.refs_1_ = bf16[32,1152]{1,0:T(8,128)(2,1)S(1)} collective-permute-done((bf16[32,1152]{1,0:T(8,128)(2,1)S(1)}, bf16[32,1152]{1,0:T(8,128)(2,1)S(1)}, u32[]{:S(2)}, u32[]{:S(2)}) %collective-permute-start.11) | collective-permute-done | bytes 73760 | tf_op jit(solution)/shard_map/ppermute | solution.py:293
  28.6 1.2 %collective-permute-done.12.refs_2_ = bf16[32,1152]{1,0:T(8,128)(2,1)S(1)} collective-permute-done((bf16[32,1152]{1,0:T(8,128)(2,1)S(1)}, bf16[32,1152]{1,0:T(8,128)(2,1)S(1)}, u32[]{:S(2)}, u32[]{:S(2)}) %collective-permute-start.12) | collective-permute-done | bytes 73760 | tf_op jit(solution)/shard_map/ppermute | solution.py:293
  29.8 0.0 copy-done
  29.8 0.8 %shard_map.56 = (f32[32,1024]{1,0:T(8,128)}, f32[1,32]{1,0:T(1,128)}, f32[16,128]{1,0:T(8,128)}) custom-call(f32[32,1024]{1,0:T(8,128)S(1)} %get-tuple-element.44.own_ref, f32[32,128]{1,0:T(8,128)S(1)} %get-tuple-element.45.own_mass_ref, f32[32,1024]{1,0:T(8,128)S(1)} %copy-done, f32[16,128]{1,0:T(8,128)S(1)} %get-tuple-element.46.lse_ref, ...), custom_call_target="tpu_custom_call" | custom-call | bytes 507904 | tf_op jit(solution)/shard_map/pallas_call | solution.py:239
  (5 shorter events, 0.1 us)
Async XLA Ops:
  0.6 16.5 %collective-permute-start = (bf16[2048,1024]{1,0:T(8,128)(2,1)}, bf16[2048,1024]{1,0:T(8,128)(2,1)}, u32[]{:S(2)}, u32[]{:S(2)}) collective-permute-start(bf16[2048,1024]{1,0:T(8,128)(2,1)} %refs_0_.1), channel_id=1, source_target_pairs={{0,1},{1,0},{2,3},{3,2},{4,5},{5,4},{6,7},{7,6},{8,9},{9,8},{10,11... | collective-permute-start | bytes 12582920 | tf_op jit(solution)/shard_map/ppermute | solution.py:17
  2.1 8.2 %collective-permute-start.3 = (bf16[32,1024]{1,0:T(8,128)(2,1)S(1)}, bf16[32,1024]{1,0:T(8,128)(2,1)S(1)}, u32[]{:S(2)}, u32[]{:S(2)}) collective-permute-start(bf16[32,1024]{1,0:T(8,128)(2,1)S(1)} %convert_element_type.3.follow_ref), channel_id=1, source_target_pairs={{0,7},{1,6},{2,5},{3,4},{4,3},{5,2},{6,1},{7,0},{8,15},{9,14},{10,... | collective-permute-start | bytes 196616 | tf_op jit(solution)/shard_map/ppermute | solution.py:256
  5.7 4.5 %collective-permute-start.2 = (bf16[32,1024]{1,0:T(8,128)(2,1)S(1)}, bf16[32,1024]{1,0:T(8,128)(2,1)S(1)}, u32[]{:S(2)}, u32[]{:S(2)}) collective-permute-start(bf16[32,1024]{1,0:T(8,128)(2,1)S(1)} %convert_element_type.3.follow_ref), channel_id=1, source_target_pairs={{0,5},{1,2},{2,7},{3,0},{4,1},{5,6},{6,3},{7,4},{8,13},{9,10},{10,... | collective-permute-start | bytes 196616 | tf_op jit(solution)/shard_map/ppermute | solution.py:256
  5.8 4.4 %collective-permute-start.1 = (bf16[32,1024]{1,0:T(8,128)(2,1)S(1)}, bf16[32,1024]{1,0:T(8,128)(2,1)S(1)}, u32[]{:S(2)}, u32[]{:S(2)}) collective-permute-start(bf16[32,1024]{1,0:T(8,128)(2,1)S(1)} %convert_element_type.3.follow_ref), channel_id=1, source_target_pairs={{0,3},{1,4},{2,1},{3,6},{4,7},{5,0},{6,5},{7,2},{8,11},{9,12},{10,... | collective-permute-start | bytes 196616 | tf_op jit(solution)/shard_map/ppermute | solution.py:256
  10.3 1.6 %collective-permute-start.4 = (bf16[128,1024]{1,0:T(8,128)(2,1)S(1)}, bf16[128,1024]{1,0:T(8,128)(2,1)S(1)}, u32[]{:S(2)}, u32[]{:S(2)}) collective-permute-start(bf16[128,1024]{1,0:T(8,128)(2,1)S(1)} %constant_dynamic-update-slice_fusion.table_ref), channel_id=1, source_target_pairs={{0,1},{1,0},{2,3},{3,2},{4,5},{5,4},{6,7},{7,6},{8,9},{9,8},{10,11... | collective-permute-start | bytes 786440 | tf_op jit(solution)/shard_map/ppermute | solution.py:17
  12.8 9.1 %collective-permute-start.9 = (bf16[128,2048]{1,0:T(8,128)(2,1)S(1)}, bf16[128,2048]{1,0:T(8,128)(2,1)S(1)}, u32[]{:S(2)}, u32[]{:S(2)}) collective-permute-start(bf16[128,2048]{1,0:T(8,128)(2,1)S(1)} %get-tuple-element.41), channel_id=1, source_target_pairs={{0,1},{1,0},{2,3},{3,2},{4,5},{5,4},{6,7},{7,6},{8,9},{9,8},{10,11... | collective-permute-start | bytes 1572872 | tf_op jit(solution)/shard_map/ppermute | solution.py:17
  13.0 7.4 %collective-permute-start.7 = (f32[16,128]{1,0:T(8,128)S(1)}, f32[16,128]{1,0:T(8,128)S(1)}, u32[]{:S(2)}, u32[]{:S(2)}) collective-permute-start(f32[16,128]{1,0:T(8,128)S(1)} %get-tuple-element.32.refs_2_), channel_id=1, source_target_pairs={{0,16},{8,24},{16,8},{24,0},{1,17},{9,25},{17,9},{25,1},{2,18},{10... | collective-permute-start | bytes 24584 | tf_op jit(solution)/shard_map/ppermute | solution.py:270
  15.6 4.8 %collective-permute-start.6 = (f32[16,128]{1,0:T(8,128)S(1)}, f32[16,128]{1,0:T(8,128)S(1)}, u32[]{:S(2)}, u32[]{:S(2)}) collective-permute-start(f32[16,128]{1,0:T(8,128)S(1)} %get-tuple-element.32.refs_2_), channel_id=1, source_target_pairs={{0,24},{8,16},{16,0},{24,8},{1,25},{9,17},{17,1},{25,9},{2,26},{10... | collective-permute-start | bytes 24584 | tf_op jit(solution)/shard_map/ppermute | solution.py:270
  16.8 3.7 %collective-permute-start.5 = (f32[16,128]{1,0:T(8,128)S(1)}, f32[16,128]{1,0:T(8,128)S(1)}, u32[]{:S(2)}, u32[]{:S(2)}) collective-permute-start(f32[16,128]{1,0:T(8,128)S(1)} %get-tuple-element.32.refs_2_), channel_id=1, source_target_pairs={{0,8},{8,0},{16,24},{24,16},{1,9},{9,1},{17,25},{25,17},{2,10},{10... | collective-permute-start | bytes 24584 | tf_op jit(solution)/shard_map/ppermute | solution.py:270
  20.5 1.3 %collective-permute-start.8 = (f32[16,128]{1,0:T(8,128)S(1)}, f32[16,128]{1,0:T(8,128)S(1)}, u32[]{:S(2)}, u32[]{:S(2)}) collective-permute-start(f32[16,128]{1,0:T(8,128)S(1)} %get-tuple-element.35), channel_id=1, source_target_pairs={{0,1},{1,0},{2,3},{3,2},{4,5},{5,4},{6,7},{7,6},{8,9},{9,8},{10,11... | collective-permute-start | bytes 24584 | tf_op jit(solution)/shard_map/ppermute | solution.py:17
  21.8 8.0 %copy-start = (f32[32,1024]{1,0:T(8,128)S(1)}, f32[32,1024]{1,0:T(8,128)}, u32[]{:S(2)}) copy-start(f32[32,1024]{1,0:T(8,128)} %cent_ref.1) | copy-start | bytes 393220
  22.6 4.9 %collective-permute-start.10 = (bf16[32,1152]{1,0:T(8,128)(2,1)S(1)}, bf16[32,1152]{1,0:T(8,128)(2,1)S(1)}, u32[]{:S(2)}, u32[]{:S(2)}) collective-permute-start(bf16[32,1152]{1,0:T(8,128)(2,1)S(1)} %get-tuple-element.47), channel_id=1, source_target_pairs={{7,0},{6,1},{5,2},{4,3},{3,4},{2,5},{1,6},{0,7},{15,8},{14,9},{13,... | collective-permute-start | bytes 221192 | tf_op jit(solution)/shard_map/ppermute | solution.py:293
  24.7 3.9 %collective-permute-start.11 = (bf16[32,1152]{1,0:T(8,128)(2,1)S(1)}, bf16[32,1152]{1,0:T(8,128)(2,1)S(1)}, u32[]{:S(2)}, u32[]{:S(2)}) collective-permute-start(bf16[32,1152]{1,0:T(8,128)(2,1)S(1)} %get-tuple-element.48), channel_id=1, source_target_pairs={{3,0},{4,1},{1,2},{6,3},{7,4},{0,5},{5,6},{2,7},{11,8},{12,9},{9,1... | collective-permute-start | bytes 221192 | tf_op jit(solution)/shard_map/ppermute | solution.py:293
  25.0 4.8 %collective-permute-start.12 = (bf16[32,1152]{1,0:T(8,128)(2,1)S(1)}, bf16[32,1152]{1,0:T(8,128)(2,1)S(1)}, u32[]{:S(2)}, u32[]{:S(2)}) collective-permute-start(bf16[32,1152]{1,0:T(8,128)(2,1)S(1)} %get-tuple-element.49), channel_id=1, source_target_pairs={{5,0},{2,1},{7,2},{0,3},{1,4},{6,5},{3,6},{4,7},{13,8},{10,9},{15,... | collective-permute-start | bytes 221192 | tf_op jit(solution)/shard_map/ppermute | solution.py:293

commit v21 on v15

--- a/solution.py
+++ b/solution.py
@@ -264,7 +264,7 @@
         )
         arrived = [
             lax.ppermute(x, "dev", [(target, source) for source, target in pairs])
-            for x, pairs in zip(sends[-1:] + sends[:-1], routes[-1:] + routes[:-1])
+            for x, pairs in zip(sends[1:] + sends[:1], routes[1:] + routes[:1])
         ]
         result, mass = call(
             final_kernel, [shape((rows, width)), shape((1, rows))],

time: 30.9 us -> 30.8 us (level)
  starting transfers between devices: 13 us -> 12.6 us
  waiting for transfers between devices: 6.73 us -> 7.04 us
    ppermute x3, starting transfers between devices: 3.41 us -> 3 us  [body(): lax.ppermute(x, 'dev', [(target, source) for source, target in pairs])]
    ppermute x3, waiting for transfers between devices: 3.7 us -> 4.01 us  [body(): lax.ppermute(x, 'dev', [(target, source) for source, target in pairs])]
where the time goes in v21:
time: 30.8 us; the launch traced here: 30.6 us
  starting transfers between devices  12.6 us (41%)
  Pallas kernels  9.31 us (30%)
  waiting for transfers between devices  7.04 us (23%)
  other arithmetic  0.92 us (3%)
  between operations  0.74 us (2%)
    ppermute x3, starting transfers between devices, body(): blocks = [lax.ppermute(rounded, 'dev', pairs) for pairs in routes]  5.14 us
    pallas_call x2, Pallas kernels, load(): pl.pallas_call(kernel, out_shape=[shape(dims, source.dtype), shape(follow...  4.93 us
    pallas_call x6, Pallas kernels, call(): pl.pallas_call(kernel, out_shape=outs, in_specs=[SMEM if x.dtype == jnp.i...  4.38 us
    ppermute x3, starting transfers between devices, body(): others = [lax.ppermute(lse, 'cgrp', pairs) for pairs in plan]  4.22 us
    ppermute x3, waiting for transfers between devices, body(): lax.ppermute(x, 'dev', [(target, source) for source, target in pairs])  4.01 us
    ppermute x3, starting transfers between devices, body(): lax.ppermute(x, 'dev', [(target, source) for source, target in pairs])  3 us
    ppermute x2, waiting for transfers between devices, swap(): return lax.ppermute(x, axis, [(i, i ^ mask) for i in range(size)])  1.33 us
    ppermute x3, waiting for transfers between devices, body(): others = [lax.ppermute(lse, 'cgrp', pairs) for pairs in plan]  1.09 us
  transfers between devices with their start and end apart: 11, of which 8 were waited for; matrix products, arithmetic and copies ran while one was open for 0% of the time, Pallas kernels for 22%

profile of v21, /device:TPU:0, one launch (start us, length us, event | category | flops | bytes accessed | tf_op | source)
XLA Modules:
  0.0 30.6 jit_solution(7284453040557302334)
XLA Ops:
  0.6 0.9 %convert_element_type.3.follow_ref = bf16[32,1024]{1,0:T(8,128)(2,1)S(1)} convert(f32[32,1024]{1,0:T(8,128)} %cent_ref.1) | non-fusion elementwise | flops 32768 | bytes 196608 | tf_op jit(solution)/shard_map/convert_element_type | solution.py:232
  1.5 3.4 %collective-permute-start.2 = (bf16[32,1024]{1,0:T(8,128)(2,1)S(1)}, bf16[32,1024]{1,0:T(8,128)(2,1)S(1)}, u32[]{:S(2)}, u32[]{:S(2)}) collective-permute-start(bf16[32,1024]{1,0:T(8,128)(2,1)S(1)} %convert_element_type.3.follow_ref), channel_id=1, source_target_pairs={{0,7},{1,6},{2,5},{3,4},{4,3},{5,2},{6,1},{7,0},{8,15},{9,14},{10,... | collective-permute-start | bytes 196616 | tf_op jit(solution)/shard_map/ppermute | solution.py:234
  4.9 0.8 %collective-permute-start.1 = (bf16[32,1024]{1,0:T(8,128)(2,1)S(1)}, bf16[32,1024]{1,0:T(8,128)(2,1)S(1)}, u32[]{:S(2)}, u32[]{:S(2)}) collective-permute-start(bf16[32,1024]{1,0:T(8,128)(2,1)S(1)} %convert_element_type.3.follow_ref), channel_id=1, source_target_pairs={{0,5},{1,2},{2,7},{3,0},{4,1},{5,6},{6,3},{7,4},{8,13},{9,10},{10,... | collective-permute-start | bytes 196616 | tf_op jit(solution)/shard_map/ppermute | solution.py:234
  5.7 1.0 %collective-permute-start = (bf16[32,1024]{1,0:T(8,128)(2,1)S(1)}, bf16[32,1024]{1,0:T(8,128)(2,1)S(1)}, u32[]{:S(2)}, u32[]{:S(2)}) collective-permute-start(bf16[32,1024]{1,0:T(8,128)(2,1)S(1)} %convert_element_type.3.follow_ref), channel_id=1, source_target_pairs={{0,3},{1,4},{2,1},{3,6},{4,7},{5,0},{6,5},{7,2},{8,11},{9,12},{10,... | collective-permute-start | bytes 196616 | tf_op jit(solution)/shard_map/ppermute | solution.py:234
  6.7 2.7 %shard_map.49 = (bf16[1024,2048]{1,0:T(8,128)(2,1)S(1)}, bf16[32,1024]{1,0:T(8,128)(2,1)S(1)}) custom-call(bf16[2048,1024]{1,0:T(8,128)(2,1)} %source_ref.3, bf16[32,1024]{1,0:T(8,128)(2,1)S(1)} %convert_element_type.3.follow_ref), custom_call_target="tpu_custom_call" | custom-call | bytes 8388608 | tf_op jit(solution)/shard_map/pallas_call | solution.py:72
  9.4 0.6 %collective-permute-done = bf16[32,1024]{1,0:T(8,128)(2,1)S(1)} collective-permute-done((bf16[32,1024]{1,0:T(8,128)(2,1)S(1)}, bf16[32,1024]{1,0:T(8,128)(2,1)S(1)}, u32[]{:S(2)}, u32[]{:S(2)}) %collective-permute-start) | collective-permute-done | bytes 65568 | tf_op jit(solution)/shard_map/ppermute | solution.py:234
  10.1 0.0 collective-permute-done.1
  10.1 0.0 collective-permute-done.2
  10.1 0.2 collective-permute-start.3
  10.3 0.9 %shard_map.50 = (f32[128,2048]{1,0:T(8,128)S(1)}, f32[16,128]{1,0:T(8,128)S(1)}, f32[16,128]{1,0:T(8,128)S(1)}) custom-call(bf16[1024,2048]{1,0:T(8,128)(2,1)S(1)} %get-tuple-element.25.docs_ref, bf16[128,1024]{1,0:T(8,128)(2,1)S(1)} %constant_dynamic-update-slice_fusion.table_ref), custom_call_target="tpu_custom_call" | custom-call | flops 536870912 | bytes 4456448 | tf_op jit(solution)/shard_map/pallas_call | solution.py:217
  11.2 0.6 %collective-permute-done.3.table_ref = bf16[128,1024]{1,0:T(8,128)(2,1)S(1)} collective-permute-done((bf16[128,1024]{1,0:T(8,128)(2,1)S(1)}, bf16[128,1024]{1,0:T(8,128)(2,1)S(1)}, u32[]{:S(2)}, u32[]{:S(2)}) %collective-permute-start.3) | collective-permute-done | bytes 262176 | tf_op jit(solution)/shard_map/ppermute | solution.py:17
  11.7 0.9 %shard_map.51 = (f32[128,2048]{1,0:T(8,128)S(1)}, f32[16,128]{1,0:T(8,128)S(1)}, f32[16,128]{1,0:T(8,128)S(1)}) custom-call(bf16[1024,2048]{1,0:T(8,128)(2,1)S(1)} %get-tuple-element.25.docs_ref, bf16[128,1024]{1,0:T(8,128)(2,1)S(1)} %collective-permute-done.3.table_ref, f32[16,128]{1,0:T(8,128)S(1)} %get-tuple-element.27.first_top_ref.refs_6_, ...), custom_call_target="tpu_custom_call" | custom-call | flops 536870912 | bytes 4472832 | tf_op jit(solution)/shard_map/pallas_call | solution.py:217
  12.6 2.6 %collective-permute-start.6 = (f32[16,128]{1,0:T(8,128)S(1)}, f32[16,128]{1,0:T(8,128)S(1)}, u32[]{:S(2)}, u32[]{:S(2)}) collective-permute-start(f32[16,128]{1,0:T(8,128)S(1)} %get-tuple-element.29.follow_ref), channel_id=1, source_target_pairs={{0,16},{8,24},{16,8},{24,0},{1,17},{9,25},{17,9},{25,1},{2,18},{10... | collective-permute-start | bytes 24584 | tf_op jit(solution)/shard_map/ppermute | solution.py:245
  15.2 1.2 %collective-permute-start.5 = (f32[16,128]{1,0:T(8,128)S(1)}, f32[16,128]{1,0:T(8,128)S(1)}, u32[]{:S(2)}, u32[]{:S(2)}) collective-permute-start(f32[16,128]{1,0:T(8,128)S(1)} %get-tuple-element.29.follow_ref), channel_id=1, source_target_pairs={{0,24},{8,16},{16,0},{24,8},{1,25},{9,17},{17,1},{25,9},{2,26},{10... | collective-permute-start | bytes 24584 | tf_op jit(solution)/shard_map/ppermute | solution.py:245
  16.5 0.3 %collective-permute-start.4 = (f32[16,128]{1,0:T(8,128)S(1)}, f32[16,128]{1,0:T(8,128)S(1)}, u32[]{:S(2)}, u32[]{:S(2)}) collective-permute-start(f32[16,128]{1,0:T(8,128)S(1)} %get-tuple-element.29.follow_ref), channel_id=1, source_target_pairs={{0,8},{8,0},{16,24},{24,16},{1,9},{9,1},{17,25},{25,17},{2,10},{10... | collective-permute-start | bytes 24584 | tf_op jit(solution)/shard_map/ppermute | solution.py:245
  16.8 2.2 %shard_map.52 = (bf16[2048,1024]{1,0:T(8,128)(2,1)S(1)}, f32[16,128]{1,0:T(8,128)S(1)}) custom-call(bf16[2048,1024]{1,0:T(8,128)(2,1)} %source_ref.3, f32[16,128]{1,0:T(8,128)S(1)} %get-tuple-element.29.follow_ref), custom_call_target="tpu_custom_call" | custom-call | bytes 8388608 | tf_op jit(solution)/shard_map/pallas_call | solution.py:72
  19.0 0.0 collective-permute-done.6.refs_2_
  19.0 0.8 %collective-permute-done.5.refs_1_ = f32[16,128]{1,0:T(8,128)S(1)} collective-permute-done((f32[16,128]{1,0:T(8,128)S(1)}, f32[16,128]{1,0:T(8,128)S(1)}, u32[]{:S(2)}, u32[]{:S(2)}) %collective-permute-start.5) | collective-permute-done | bytes 8224 | tf_op jit(solution)/shard_map/ppermute | solution.py:245
  19.8 0.3 %collective-permute-done.4.refs_0_ = f32[16,128]{1,0:T(8,128)S(1)} collective-permute-done((f32[16,128]{1,0:T(8,128)S(1)}, f32[16,128]{1,0:T(8,128)S(1)}, u32[]{:S(2)}, u32[]{:S(2)}) %collective-permute-start.4) | collective-permute-done | bytes 8224 | tf_op jit(solution)/shard_map/ppermute | solution.py:245
  20.1 0.8 %shard_map.53 = (f32[16,128]{1,0:T(8,128)}, f32[16,128]{1,0:T(8,128)S(1)}, bf16[128,1152]{1,0:T(8,128)(2,1)S(1)}) custom-call(s32[1]{0:T(128)} %bitcast.me_ref, f32[16,128]{1,0:T(8,128)S(1)} %get-tuple-element.30.lse_ref, f32[16,128]{1,0:T(8,128)S(1)} %collective-permute-done.4.refs_0_, f32[16,128]{1,0:T(8,128)S(1)} %collective-permute-done.5.refs_1_, ...), custom_call_target="tpu_custom_call" | custom-call | flops 536870912 | bytes 5292036 | tf_op jit(solution)/shard_map/pallas_call | solution.py:217
  21.0 0.0 copy-start
  21.0 0.1 collective-permute-start.7
  21.0 0.8 %shard_map.54 = (f32[128,1024]{1,0:T(8,128)S(1)}, f32[128,128]{1,0:T(8,128)S(1)}) custom-call(f32[16,128]{1,0:T(8,128)S(1)} %get-tuple-element.34.factor_ref, bf16[2048,1024]{1,0:T(8,128)(2,1)S(1)} %get-tuple-element.31.refs_3_.docs_ref, f32[128,2048]{1,0:T(8,128)S(1)} %get-tuple-element.35.part_ref), custom_call_target="tpu_custom_call" | custom-call | flops 536870912 | bytes 5251072 | tf_op jit(solution)/shard_map/pallas_call | solution.py:217
  21.8 0.8 %collective-permute-done.7.got_ref = bf16[128,1152]{1,0:T(8,128)(2,1)S(1)} collective-permute-done((bf16[128,1152]{1,0:T(8,128)(2,1)S(1)}, bf16[128,1152]{1,0:T(8,128)(2,1)S(1)}, u32[]{:S(2)}, u32[]{:S(2)}) %collective-permute-start.7) | collective-permute-done | bytes 294944 | tf_op jit(solution)/shard_map/ppermute | solution.py:17
  22.6 0.2 shard_map.55
  22.8 0.9 %collective-permute-start.8 = (bf16[32,1152]{1,0:T(8,128)(2,1)S(1)}, bf16[32,1152]{1,0:T(8,128)(2,1)S(1)}, u32[]{:S(2)}, u32[]{:S(2)}) collective-permute-start(bf16[32,1152]{1,0:T(8,128)(2,1)S(1)} %get-tuple-element.41), channel_id=1, source_target_pairs={{5,0},{2,1},{7,2},{0,3},{1,4},{6,5},{3,6},{4,7},{13,8},{10,9},{15,... | collective-permute-start | bytes 221192 | tf_op jit(solution)/shard_map/ppermute | solution.py:266
  23.7 1.4 %collective-permute-start.9 = (bf16[32,1152]{1,0:T(8,128)(2,1)S(1)}, bf16[32,1152]{1,0:T(8,128)(2,1)S(1)}, u32[]{:S(2)}, u32[]{:S(2)}) collective-permute-start(bf16[32,1152]{1,0:T(8,128)(2,1)S(1)} %get-tuple-element.42), channel_id=1, source_target_pairs={{7,0},{6,1},{5,2},{4,3},{3,4},{2,5},{1,6},{0,7},{15,8},{14,9},{13,... | collective-permute-start | bytes 221192 | tf_op jit(solution)/shard_map/ppermute | solution.py:266
  25.1 0.6 %collective-permute-start.10 = (bf16[32,1152]{1,0:T(8,128)(2,1)S(1)}, bf16[32,1152]{1,0:T(8,128)(2,1)S(1)}, u32[]{:S(2)}, u32[]{:S(2)}) collective-permute-start(bf16[32,1152]{1,0:T(8,128)(2,1)S(1)} %get-tuple-element.43), channel_id=1, source_target_pairs={{3,0},{4,1},{1,2},{6,3},{7,4},{0,5},{5,6},{2,7},{11,8},{12,9},{9,1... | collective-permute-start | bytes 221192 | tf_op jit(solution)/shard_map/ppermute | solution.py:266
  25.8 0.8 %collective-permute-done.8.refs_0_ = bf16[32,1152]{1,0:T(8,128)(2,1)S(1)} collective-permute-done((bf16[32,1152]{1,0:T(8,128)(2,1)S(1)}, bf16[32,1152]{1,0:T(8,128)(2,1)S(1)}, u32[]{:S(2)}, u32[]{:S(2)}) %collective-permute-start.8) | collective-permute-done | bytes 73760 | tf_op jit(solution)/shard_map/ppermute | solution.py:266
  26.6 1.9 %collective-permute-done.9.refs_1_ = bf16[32,1152]{1,0:T(8,128)(2,1)S(1)} collective-permute-done((bf16[32,1152]{1,0:T(8,128)(2,1)S(1)}, bf16[32,1152]{1,0:T(8,128)(2,1)S(1)}, u32[]{:S(2)}, u32[]{:S(2)}) %collective-permute-start.9) | collective-permute-done | bytes 73760 | tf_op jit(solution)/shard_map/ppermute | solution.py:266
  28.6 1.2 %collective-permute-done.10.refs_2_ = bf16[32,1152]{1,0:T(8,128)(2,1)S(1)} collective-permute-done((bf16[32,1152]{1,0:T(8,128)(2,1)S(1)}, bf16[32,1152]{1,0:T(8,128)(2,1)S(1)}, u32[]{:S(2)}, u32[]{:S(2)}) %collective-permute-start.10) | collective-permute-done | bytes 73760 | tf_op jit(solution)/shard_map/ppermute | solution.py:266
  29.8 0.0 copy-done
  29.8 0.8 %shard_map.56 = (f32[32,1024]{1,0:T(8,128)}, f32[1,32]{1,0:T(1,128)}) custom-call(f32[32,1024]{1,0:T(8,128)S(1)} %get-tuple-element.39.own_ref, f32[32,128]{1,0:T(8,128)S(1)} %get-tuple-element.40.own_mass_ref, f32[32,1024]{1,0:T(8,128)S(1)} %copy-done, bf16[32,1152]{1,0:T(8,128)(2,1)S(1)} %collective-permute-done.8.refs_0_, ...), custom_call_target="tpu_custom_call" | custom-call | bytes 499712 | tf_op jit(solution)/shard_map/pallas_call | solution.py:217
  (4 shorter events, 0.0 us)
Async XLA Ops:
  1.5 8.5 %collective-permute-start.2 = (bf16[32,1024]{1,0:T(8,128)(2,1)S(1)}, bf16[32,1024]{1,0:T(8,128)(2,1)S(1)}, u32[]{:S(2)}, u32[]{:S(2)}) collective-permute-start(bf16[32,1024]{1,0:T(8,128)(2,1)S(1)} %convert_element_type.3.follow_ref), channel_id=1, source_target_pairs={{0,7},{1,6},{2,5},{3,4},{4,3},{5,2},{6,1},{7,0},{8,15},{9,14},{10,... | collective-permute-start | bytes 196616 | tf_op jit(solution)/shard_map/ppermute | solution.py:234
  4.9 5.1 %collective-permute-start.1 = (bf16[32,1024]{1,0:T(8,128)(2,1)S(1)}, bf16[32,1024]{1,0:T(8,128)(2,1)S(1)}, u32[]{:S(2)}, u32[]{:S(2)}) collective-permute-start(bf16[32,1024]{1,0:T(8,128)(2,1)S(1)} %convert_element_type.3.follow_ref), channel_id=1, source_target_pairs={{0,5},{1,2},{2,7},{3,0},{4,1},{5,6},{6,3},{7,4},{8,13},{9,10},{10,... | collective-permute-start | bytes 196616 | tf_op jit(solution)/shard_map/ppermute | solution.py:234
  5.7 4.3 %collective-permute-start = (bf16[32,1024]{1,0:T(8,128)(2,1)S(1)}, bf16[32,1024]{1,0:T(8,128)(2,1)S(1)}, u32[]{:S(2)}, u32[]{:S(2)}) collective-permute-start(bf16[32,1024]{1,0:T(8,128)(2,1)S(1)} %convert_element_type.3.follow_ref), channel_id=1, source_target_pairs={{0,3},{1,4},{2,1},{3,6},{4,7},{5,0},{6,5},{7,2},{8,11},{9,12},{10,... | collective-permute-start | bytes 196616 | tf_op jit(solution)/shard_map/ppermute | solution.py:234
  10.1 1.6 %collective-permute-start.3 = (bf16[128,1024]{1,0:T(8,128)(2,1)S(1)}, bf16[128,1024]{1,0:T(8,128)(2,1)S(1)}, u32[]{:S(2)}, u32[]{:S(2)}) collective-permute-start(bf16[128,1024]{1,0:T(8,128)(2,1)S(1)} %constant_dynamic-update-slice_fusion.table_ref), channel_id=1, source_target_pairs={{0,1},{1,0},{2,3},{3,2},{4,5},{5,4},{6,7},{7,6},{8,9},{9,8},{10,11... | collective-permute-start | bytes 786440 | tf_op jit(solution)/shard_map/ppermute | solution.py:17
  12.6 6.4 %collective-permute-start.6 = (f32[16,128]{1,0:T(8,128)S(1)}, f32[16,128]{1,0:T(8,128)S(1)}, u32[]{:S(2)}, u32[]{:S(2)}) collective-permute-start(f32[16,128]{1,0:T(8,128)S(1)} %get-tuple-element.29.follow_ref), channel_id=1, source_target_pairs={{0,16},{8,24},{16,8},{24,0},{1,17},{9,25},{17,9},{25,1},{2,18},{10... | collective-permute-start | bytes 24584 | tf_op jit(solution)/shard_map/ppermute | solution.py:245
  15.2 4.5 %collective-permute-start.5 = (f32[16,128]{1,0:T(8,128)S(1)}, f32[16,128]{1,0:T(8,128)S(1)}, u32[]{:S(2)}, u32[]{:S(2)}) collective-permute-start(f32[16,128]{1,0:T(8,128)S(1)} %get-tuple-element.29.follow_ref), channel_id=1, source_target_pairs={{0,24},{8,16},{16,0},{24,8},{1,25},{9,17},{17,1},{25,9},{2,26},{10... | collective-permute-start | bytes 24584 | tf_op jit(solution)/shard_map/ppermute | solution.py:245
  16.5 3.7 %collective-permute-start.4 = (f32[16,128]{1,0:T(8,128)S(1)}, f32[16,128]{1,0:T(8,128)S(1)}, u32[]{:S(2)}, u32[]{:S(2)}) collective-permute-start(f32[16,128]{1,0:T(8,128)S(1)} %get-tuple-element.29.follow_ref), channel_id=1, source_target_pairs={{0,8},{8,0},{16,24},{24,16},{1,9},{9,1},{17,25},{25,17},{2,10},{10... | collective-permute-start | bytes 24584 | tf_op jit(solution)/shard_map/ppermute | solution.py:245
  21.0 8.8 %copy-start = (f32[32,1024]{1,0:T(8,128)S(1)}, f32[32,1024]{1,0:T(8,128)}, u32[]{:S(2)}) copy-start(f32[32,1024]{1,0:T(8,128)} %cent_ref.1) | copy-start | bytes 393220
  21.0 1.6 %collective-permute-start.7 = (bf16[128,1152]{1,0:T(8,128)(2,1)S(1)}, bf16[128,1152]{1,0:T(8,128)(2,1)S(1)}, u32[]{:S(2)}, u32[]{:S(2)}) collective-permute-start(bf16[128,1152]{1,0:T(8,128)(2,1)S(1)} %get-tuple-element.38), channel_id=1, source_target_pairs={{0,1},{1,0},{2,3},{3,2},{4,5},{5,4},{6,7},{7,6},{8,9},{9,8},{10,11... | collective-permute-start | bytes 884744 | tf_op jit(solution)/shard_map/ppermute | solution.py:17
  22.8 3.8 %collective-permute-start.8 = (bf16[32,1152]{1,0:T(8,128)(2,1)S(1)}, bf16[32,1152]{1,0:T(8,128)(2,1)S(1)}, u32[]{:S(2)}, u32[]{:S(2)}) collective-permute-start(bf16[32,1152]{1,0:T(8,128)(2,1)S(1)} %get-tuple-element.41), channel_id=1, source_target_pairs={{5,0},{2,1},{7,2},{0,3},{1,4},{6,5},{3,6},{4,7},{13,8},{10,9},{15,... | collective-permute-start | bytes 221192 | tf_op jit(solution)/shard_map/ppermute | solution.py:266
  23.7 4.9 %collective-permute-start.9 = (bf16[32,1152]{1,0:T(8,128)(2,1)S(1)}, bf16[32,1152]{1,0:T(8,128)(2,1)S(1)}, u32[]{:S(2)}, u32[]{:S(2)}) collective-permute-start(bf16[32,1152]{1,0:T(8,128)(2,1)S(1)} %get-tuple-element.42), channel_id=1, source_target_pairs={{7,0},{6,1},{5,2},{4,3},{3,4},{2,5},{1,6},{0,7},{15,8},{14,9},{13,... | collective-permute-start | bytes 221192 | tf_op jit(solution)/shard_map/ppermute | solution.py:266
  25.1 4.7 %collective-permute-start.10 = (bf16[32,1152]{1,0:T(8,128)(2,1)S(1)}, bf16[32,1152]{1,0:T(8,128)(2,1)S(1)}, u32[]{:S(2)}, u32[]{:S(2)}) collective-permute-start(bf16[32,1152]{1,0:T(8,128)(2,1)S(1)} %get-tuple-element.43), channel_id=1, source_target_pairs={{3,0},{4,1},{1,2},{6,3},{7,4},{0,5},{5,6},{2,7},{11,8},{12,9},{9,1... | collective-permute-start | bytes 221192 | tf_op jit(solution)/shard_map/ppermute | solution.py:266

commit v22 on v20

--- a/solution.py
+++ b/solution.py
@@ -291,7 +291,7 @@
         )
         arrived = [
             lax.ppermute(x, "dev", [(target, source) for source, target in pairs])
-            for x, pairs in zip(sends[-1:] + sends[:-1], routes[-1:] + routes[:-1])
+            for x, pairs in zip(sends[1:] + sends[:1], routes[1:] + routes[:1])
         ]
         result, mass, doc_lse = call(
             final_kernel, [shape((rows, width)), shape((1, rows)), shape(doc_lse.shape)],

time: 30.8 us -> 30.8 us (level)
  starting transfers between devices: 14.3 us -> 13.8 us
  waiting for transfers between devices: 4.06 us -> 4.52 us
    ppermute x3, waiting for transfers between devices: 3.34 us -> 3.81 us  [body(): lax.ppermute(x, 'dev', [(target, source) for source, target in pairs])]
    ppermute x3, starting transfers between devices: 3.82 us -> 3.36 us  [body(): lax.ppermute(x, 'dev', [(target, source) for source, target in pairs])]
where the time goes in v22:
time: 30.8 us; the launch traced here: 30.6 us
  starting transfers between devices  13.8 us (45%)
  Pallas kernels  10.6 us (34%)
  waiting for transfers between devices  4.52 us (15%)
  other arithmetic  0.91 us (3%)
  between operations  0.78 us (3%)
    pallas_call x2, Pallas kernels, load(): pl.pallas_call(kernel, out_shape=outs + [shape(follow.shape, follow.dtype...  5.92 us
    ppermute x3, starting transfers between devices, body(): blocks = [lax.ppermute(rounded, 'dev', pairs) for pairs in routes]  5.36 us
    pallas_call x6, Pallas kernels, call(): pl.pallas_call(kernel, out_shape=outs, in_specs=specs or [SMEM if x.dtype...  4.67 us
    ppermute x3, starting transfers between devices, body(): others = [lax.ppermute(lse, 'cgrp', pairs) for pairs in plan]  4.18 us
    ppermute x3, waiting for transfers between devices, body(): lax.ppermute(x, 'dev', [(target, source) for source, target in pairs])  3.81 us
    ppermute x3, starting transfers between devices, body(): lax.ppermute(x, 'dev', [(target, source) for source, target in pairs])  3.36 us
    convert_element_type x1, other arithmetic, body(): rounded = centroids.astype(jnp.bfloat16)  0.91 us
    ppermute x4, starting transfers between devices, swap(): return lax.ppermute(x, axis, [(i, i ^ mask) for i in range(size)])  0.89 us
  transfers between devices with their start and end apart: 13, of which 5 were waited for; matrix products, arithmetic and copies ran while one was open for 3% of the time, Pallas kernels for 29%

profile of v22, /device:TPU:0, one launch (start us, length us, event | category | flops | bytes accessed | tf_op | source)
XLA Modules:
  0.0 30.6 jit_solution(15273771222305110556)
XLA Ops:
  0.6 0.5 %collective-permute-start = (bf16[2048,1024]{1,0:T(8,128)(2,1)}, bf16[2048,1024]{1,0:T(8,128)(2,1)}, u32[]{:S(2)}, u32[]{:S(2)}) collective-permute-start(bf16[2048,1024]{1,0:T(8,128)(2,1)} %refs_0_.1), channel_id=1, source_target_pairs={{0,1},{1,0},{2,3},{3,2},{4,5},{5,4},{6,7},{7,6},{8,9},{9,8},{10,11... | collective-permute-start | bytes 12582920 | tf_op jit(solution)/shard_map/ppermute | solution.py:17
  1.1 0.9 %convert_element_type.3.follow_ref = bf16[32,1024]{1,0:T(8,128)(2,1)S(1)} convert(f32[32,1024]{1,0:T(8,128)} %cent_ref.1) | non-fusion elementwise | flops 32768 | bytes 196608 | tf_op jit(solution)/shard_map/convert_element_type | solution.py:254
  2.1 3.6 %collective-permute-start.3 = (bf16[32,1024]{1,0:T(8,128)(2,1)S(1)}, bf16[32,1024]{1,0:T(8,128)(2,1)S(1)}, u32[]{:S(2)}, u32[]{:S(2)}) collective-permute-start(bf16[32,1024]{1,0:T(8,128)(2,1)S(1)} %convert_element_type.3.follow_ref), channel_id=1, source_target_pairs={{0,7},{1,6},{2,5},{3,4},{4,3},{5,2},{6,1},{7,0},{8,15},{9,14},{10,... | collective-permute-start | bytes 196616 | tf_op jit(solution)/shard_map/ppermute | solution.py:256
  5.7 0.1 collective-permute-start.2
  5.8 1.6 %collective-permute-start.1 = (bf16[32,1024]{1,0:T(8,128)(2,1)S(1)}, bf16[32,1024]{1,0:T(8,128)(2,1)S(1)}, u32[]{:S(2)}, u32[]{:S(2)}) collective-permute-start(bf16[32,1024]{1,0:T(8,128)(2,1)S(1)} %convert_element_type.3.follow_ref), channel_id=1, source_target_pairs={{0,3},{1,4},{2,1},{3,6},{4,7},{5,0},{6,5},{7,2},{8,11},{9,12},{10,... | collective-permute-start | bytes 196616 | tf_op jit(solution)/shard_map/ppermute | solution.py:256
  7.4 2.7 %shard_map.49 = (bf16[1024,2048]{1,0:T(8,128)(2,1)S(1)}, bf16[32,1024]{1,0:T(8,128)(2,1)S(1)}) custom-call(bf16[2048,1024]{1,0:T(8,128)(2,1)} %refs_0_.1, bf16[32,1024]{1,0:T(8,128)(2,1)S(1)} %convert_element_type.3.follow_ref), custom_call_target="tpu_custom_call" | custom-call | bytes 8388608 | tf_op jit(solution)/shard_map/pallas_call | solution.py:85
  10.2 0.0 collective-permute-done.1
  10.2 0.0 collective-permute-done.2
  10.2 0.0 collective-permute-done.3
  10.3 0.1 collective-permute-start.4
  10.4 0.9 %shard_map.50 = (f32[128,2048]{1,0:T(8,128)S(1)}, f32[16,128]{1,0:T(8,128)S(1)}, f32[16,128]{1,0:T(8,128)S(1)}) custom-call(bf16[1024,2048]{1,0:T(8,128)(2,1)S(1)} %get-tuple-element.28.docs_ref, bf16[128,1024]{1,0:T(8,128)(2,1)S(1)} %constant_dynamic-update-slice_fusion.table_ref), custom_call_target="tpu_custom_call" | custom-call | flops 536870912 | bytes 4456448 | tf_op jit(solution)/shard_map/pallas_call | solution.py:239
  11.3 0.6 %collective-permute-done.4.table_ref = bf16[128,1024]{1,0:T(8,128)(2,1)S(1)} collective-permute-done((bf16[128,1024]{1,0:T(8,128)(2,1)S(1)}, bf16[128,1024]{1,0:T(8,128)(2,1)S(1)}, u32[]{:S(2)}, u32[]{:S(2)}) %collective-permute-start.4) | collective-permute-done | bytes 262176 | tf_op jit(solution)/shard_map/ppermute | solution.py:17
  11.9 0.9 %shard_map.51 = (bf16[128,2048]{1,0:T(8,128)(2,1)S(1)}, f32[16,128]{1,0:T(8,128)S(1)}, f32[16,128]{1,0:T(8,128)S(1)}) custom-call(bf16[1024,2048]{1,0:T(8,128)(2,1)S(1)} %get-tuple-element.28.docs_ref, bf16[128,1024]{1,0:T(8,128)(2,1)S(1)} %collective-permute-done.4.table_ref, f32[16,128]{1,0:T(8,128)S(1)} %get-tuple-element.30.first_top_ref.refs_3_, ...), custom_call_target="tpu_custom_call" | custom-call | flops 536870912 | bytes 4472832 | tf_op jit(solution)/shard_map/pallas_call | solution.py:239
  12.8 0.2 collective-permute-start.9
  13.0 2.6 %collective-permute-start.7 = (f32[16,128]{1,0:T(8,128)S(1)}, f32[16,128]{1,0:T(8,128)S(1)}, u32[]{:S(2)}, u32[]{:S(2)}) collective-permute-start(f32[16,128]{1,0:T(8,128)S(1)} %get-tuple-element.32.refs_2_), channel_id=1, source_target_pairs={{0,16},{8,24},{16,8},{24,0},{1,17},{9,25},{17,9},{25,1},{2,18},{10... | collective-permute-start | bytes 24584 | tf_op jit(solution)/shard_map/ppermute | solution.py:270
  15.6 1.2 %collective-permute-start.6 = (f32[16,128]{1,0:T(8,128)S(1)}, f32[16,128]{1,0:T(8,128)S(1)}, u32[]{:S(2)}, u32[]{:S(2)}) collective-permute-start(f32[16,128]{1,0:T(8,128)S(1)} %get-tuple-element.32.refs_2_), channel_id=1, source_target_pairs={{0,24},{8,16},{16,0},{24,8},{1,25},{9,17},{17,1},{25,9},{2,26},{10... | collective-permute-start | bytes 24584 | tf_op jit(solution)/shard_map/ppermute | solution.py:270
  16.8 0.3 %collective-permute-start.5 = (f32[16,128]{1,0:T(8,128)S(1)}, f32[16,128]{1,0:T(8,128)S(1)}, u32[]{:S(2)}, u32[]{:S(2)}) collective-permute-start(f32[16,128]{1,0:T(8,128)S(1)} %get-tuple-element.32.refs_2_), channel_id=1, source_target_pairs={{0,8},{8,0},{16,24},{24,16},{1,9},{9,1},{17,25},{25,17},{2,10},{10... | collective-permute-start | bytes 24584 | tf_op jit(solution)/shard_map/ppermute | solution.py:270
  17.1 0.0 collective-permute-done.refs_1_.source_ref
  17.2 3.2 %shard_map.52 = (bf16[2048,1024]{1,0:T(8,128)(2,1)S(1)}, bf16[1536,1024]{1,0:T(8,128)(2,1)S(1)}, f32[16,128]{1,0:T(8,128)S(1)}) custom-call(bf16[2048,1024]{1,0:T(8,128)(2,1)} %refs_0_.1, bf16[2048,1024]{1,0:T(8,128)(2,1)} %collective-permute-done.refs_1_.source_ref, f32[16,128]{1,0:T(8,128)S(1)} %get-tuple-element.32.refs_2_), custom_call_target="tpu_custom_call" | custom-call | bytes 16777216 | tf_op jit(solution)/shard_map/pallas_call | solution.py:85
  20.3 0.0 collective-permute-done.7.refs_2_
  20.4 0.0 collective-permute-done.6.refs_1_
  20.4 0.1 collective-permute-done.5.refs_0_
  20.5 0.1 collective-permute-start.8
  20.6 1.2 %shard_map.54 = (f32[128,1024]{1,0:T(8,128)S(1)}, f32[128,128]{1,0:T(8,128)S(1)}, bf16[512,1024]{1,0:T(8,128)(2,1)S(1)}) custom-call(f32[16,128]{1,0:T(8,128)S(1)} %get-tuple-element.37.factor_ref, bf16[2048,1024]{1,0:T(8,128)(2,1)S(1)} %get-tuple-element.38.docs_ref, f32[128,2048]{1,0:T(8,128)S(1)} %get-tuple-element.39.part_ref, ...), custom_call_target="tpu_custom_call" | custom-call | flops 536870912 | bytes 9445376 | tf_op jit(solution)/shard_map/pallas_call | solution.py:239
  21.8 0.0 copy-start
  21.8 0.0 collective-permute-done.9.part_ref
  21.8 0.0 collective-permute-done.8.factor_ref
  21.8 0.8 %shard_map.55 = (f32[32,1024]{1,0:T(8,128)S(1)}, f32[32,128]{1,0:T(8,128)S(1)}, bf16[32,1152]{1,0:T(8,128)(2,1)S(1)}, bf16[32,1152]{1,0:T(8,128)(2,1)S(1)}, bf16[32,1152]{1,0:T(8,128)(2,1)S(1)}) custom-call(f32[16,128]{1,0:T(8,128)S(1)} %collective-permute-done.8.factor_ref, bf16[1536,1024]{1,0:T(8,128)(2,1)S(1)} %get-tuple-element.36.docs_ref, ...), custom_call_target="tpu_custom_call" | custom-call | flops 536870912 | bytes 5316608 | tf_op jit(solution)/shard_map/pallas_call | solution.py:239
  22.6 1.3 %collective-permute-start.10 = (bf16[32,1152]{1,0:T(8,128)(2,1)S(1)}, bf16[32,1152]{1,0:T(8,128)(2,1)S(1)}, u32[]{:S(2)}, u32[]{:S(2)}) collective-permute-start(bf16[32,1152]{1,0:T(8,128)(2,1)S(1)} %get-tuple-element.47), channel_id=1, source_target_pairs={{5,0},{2,1},{7,2},{0,3},{1,4},{6,5},{3,6},{4,7},{13,8},{10,9},{15,... | collective-permute-start | bytes 221192 | tf_op jit(solution)/shard_map/ppermute | solution.py:293
  23.9 1.1 %collective-permute-start.11 = (bf16[32,1152]{1,0:T(8,128)(2,1)S(1)}, bf16[32,1152]{1,0:T(8,128)(2,1)S(1)}, u32[]{:S(2)}, u32[]{:S(2)}) collective-permute-start(bf16[32,1152]{1,0:T(8,128)(2,1)S(1)} %get-tuple-element.48), channel_id=1, source_target_pairs={{7,0},{6,1},{5,2},{4,3},{3,4},{2,5},{1,6},{0,7},{15,8},{14,9},{13,... | collective-permute-start | bytes 221192 | tf_op jit(solution)/shard_map/ppermute | solution.py:293
  25.0 1.0 %collective-permute-start.12 = (bf16[32,1152]{1,0:T(8,128)(2,1)S(1)}, bf16[32,1152]{1,0:T(8,128)(2,1)S(1)}, u32[]{:S(2)}, u32[]{:S(2)}) collective-permute-start(bf16[32,1152]{1,0:T(8,128)(2,1)S(1)} %get-tuple-element.49), channel_id=1, source_target_pairs={{3,0},{4,1},{1,2},{6,3},{7,4},{0,5},{5,6},{2,7},{11,8},{12,9},{9,1... | collective-permute-start | bytes 221192 | tf_op jit(solution)/shard_map/ppermute | solution.py:293
  26.0 0.5 %collective-permute-done.10.refs_0_ = bf16[32,1152]{1,0:T(8,128)(2,1)S(1)} collective-permute-done((bf16[32,1152]{1,0:T(8,128)(2,1)S(1)}, bf16[32,1152]{1,0:T(8,128)(2,1)S(1)}, u32[]{:S(2)}, u32[]{:S(2)}) %collective-permute-start.10) | collective-permute-done | bytes 73760 | tf_op jit(solution)/shard_map/ppermute | solution.py:293
  26.5 2.8 %collective-permute-done.11.refs_1_ = bf16[32,1152]{1,0:T(8,128)(2,1)S(1)} collective-permute-done((bf16[32,1152]{1,0:T(8,128)(2,1)S(1)}, bf16[32,1152]{1,0:T(8,128)(2,1)S(1)}, u32[]{:S(2)}, u32[]{:S(2)}) %collective-permute-start.11) | collective-permute-done | bytes 73760 | tf_op jit(solution)/shard_map/ppermute | solution.py:293
  29.3 0.5 %collective-permute-done.12.refs_2_ = bf16[32,1152]{1,0:T(8,128)(2,1)S(1)} collective-permute-done((bf16[32,1152]{1,0:T(8,128)(2,1)S(1)}, bf16[32,1152]{1,0:T(8,128)(2,1)S(1)}, u32[]{:S(2)}, u32[]{:S(2)}) %collective-permute-start.12) | collective-permute-done | bytes 73760 | tf_op jit(solution)/shard_map/ppermute | solution.py:293
  29.8 0.0 copy-done
  29.8 0.8 %shard_map.56 = (f32[32,1024]{1,0:T(8,128)}, f32[1,32]{1,0:T(1,128)}, f32[16,128]{1,0:T(8,128)}) custom-call(f32[32,1024]{1,0:T(8,128)S(1)} %get-tuple-element.44.own_ref, f32[32,128]{1,0:T(8,128)S(1)} %get-tuple-element.45.own_mass_ref, f32[32,1024]{1,0:T(8,128)S(1)} %copy-done, f32[16,128]{1,0:T(8,128)S(1)} %get-tuple-element.46.lse_ref, ...), custom_call_target="tpu_custom_call" | custom-call | bytes 507904 | tf_op jit(solution)/shard_map/pallas_call | solution.py:239
  (5 shorter events, 0.1 us)
Async XLA Ops:
  0.6 16.5 %collective-permute-start = (bf16[2048,1024]{1,0:T(8,128)(2,1)}, bf16[2048,1024]{1,0:T(8,128)(2,1)}, u32[]{:S(2)}, u32[]{:S(2)}) collective-permute-start(bf16[2048,1024]{1,0:T(8,128)(2,1)} %refs_0_.1), channel_id=1, source_target_pairs={{0,1},{1,0},{2,3},{3,2},{4,5},{5,4},{6,7},{7,6},{8,9},{9,8},{10,11... | collective-permute-start | bytes 12582920 | tf_op jit(solution)/shard_map/ppermute | solution.py:17
  2.1 8.2 %collective-permute-start.3 = (bf16[32,1024]{1,0:T(8,128)(2,1)S(1)}, bf16[32,1024]{1,0:T(8,128)(2,1)S(1)}, u32[]{:S(2)}, u32[]{:S(2)}) collective-permute-start(bf16[32,1024]{1,0:T(8,128)(2,1)S(1)} %convert_element_type.3.follow_ref), channel_id=1, source_target_pairs={{0,7},{1,6},{2,5},{3,4},{4,3},{5,2},{6,1},{7,0},{8,15},{9,14},{10,... | collective-permute-start | bytes 196616 | tf_op jit(solution)/shard_map/ppermute | solution.py:256
  5.7 4.5 %collective-permute-start.2 = (bf16[32,1024]{1,0:T(8,128)(2,1)S(1)}, bf16[32,1024]{1,0:T(8,128)(2,1)S(1)}, u32[]{:S(2)}, u32[]{:S(2)}) collective-permute-start(bf16[32,1024]{1,0:T(8,128)(2,1)S(1)} %convert_element_type.3.follow_ref), channel_id=1, source_target_pairs={{0,5},{1,2},{2,7},{3,0},{4,1},{5,6},{6,3},{7,4},{8,13},{9,10},{10,... | collective-permute-start | bytes 196616 | tf_op jit(solution)/shard_map/ppermute | solution.py:256
  5.8 4.4 %collective-permute-start.1 = (bf16[32,1024]{1,0:T(8,128)(2,1)S(1)}, bf16[32,1024]{1,0:T(8,128)(2,1)S(1)}, u32[]{:S(2)}, u32[]{:S(2)}) collective-permute-start(bf16[32,1024]{1,0:T(8,128)(2,1)S(1)} %convert_element_type.3.follow_ref), channel_id=1, source_target_pairs={{0,3},{1,4},{2,1},{3,6},{4,7},{5,0},{6,5},{7,2},{8,11},{9,12},{10,... | collective-permute-start | bytes 196616 | tf_op jit(solution)/shard_map/ppermute | solution.py:256
  10.3 1.6 %collective-permute-start.4 = (bf16[128,1024]{1,0:T(8,128)(2,1)S(1)}, bf16[128,1024]{1,0:T(8,128)(2,1)S(1)}, u32[]{:S(2)}, u32[]{:S(2)}) collective-permute-start(bf16[128,1024]{1,0:T(8,128)(2,1)S(1)} %constant_dynamic-update-slice_fusion.table_ref), channel_id=1, source_target_pairs={{0,1},{1,0},{2,3},{3,2},{4,5},{5,4},{6,7},{7,6},{8,9},{9,8},{10,11... | collective-permute-start | bytes 786440 | tf_op jit(solution)/shard_map/ppermute | solution.py:17
  12.8 9.1 %collective-permute-start.9 = (bf16[128,2048]{1,0:T(8,128)(2,1)S(1)}, bf16[128,2048]{1,0:T(8,128)(2,1)S(1)}, u32[]{:S(2)}, u32[]{:S(2)}) collective-permute-start(bf16[128,2048]{1,0:T(8,128)(2,1)S(1)} %get-tuple-element.41), channel_id=1, source_target_pairs={{0,1},{1,0},{2,3},{3,2},{4,5},{5,4},{6,7},{7,6},{8,9},{9,8},{10,11... | collective-permute-start | bytes 1572872 | tf_op jit(solution)/shard_map/ppermute | solution.py:17
  13.0 7.4 %collective-permute-start.7 = (f32[16,128]{1,0:T(8,128)S(1)}, f32[16,128]{1,0:T(8,128)S(1)}, u32[]{:S(2)}, u32[]{:S(2)}) collective-permute-start(f32[16,128]{1,0:T(8,128)S(1)} %get-tuple-element.32.refs_2_), channel_id=1, source_target_pairs={{0,16},{8,24},{16,8},{24,0},{1,17},{9,25},{17,9},{25,1},{2,18},{10... | collective-permute-start | bytes 24584 | tf_op jit(solution)/shard_map/ppermute | solution.py:270
  15.6 4.8 %collective-permute-start.6 = (f32[16,128]{1,0:T(8,128)S(1)}, f32[16,128]{1,0:T(8,128)S(1)}, u32[]{:S(2)}, u32[]{:S(2)}) collective-permute-start(f32[16,128]{1,0:T(8,128)S(1)} %get-tuple-element.32.refs_2_), channel_id=1, source_target_pairs={{0,24},{8,16},{16,0},{24,8},{1,25},{9,17},{17,1},{25,9},{2,26},{10... | collective-permute-start | bytes 24584 | tf_op jit(solution)/shard_map/ppermute | solution.py:270
  16.8 3.7 %collective-permute-start.5 = (f32[16,128]{1,0:T(8,128)S(1)}, f32[16,128]{1,0:T(8,128)S(1)}, u32[]{:S(2)}, u32[]{:S(2)}) collective-permute-start(f32[16,128]{1,0:T(8,128)S(1)} %get-tuple-element.32.refs_2_), channel_id=1, source_target_pairs={{0,8},{8,0},{16,24},{24,16},{1,9},{9,1},{17,25},{25,17},{2,10},{10... | collective-permute-start | bytes 24584 | tf_op jit(solution)/shard_map/ppermute | solution.py:270
  20.5 1.3 %collective-permute-start.8 = (f32[16,128]{1,0:T(8,128)S(1)}, f32[16,128]{1,0:T(8,128)S(1)}, u32[]{:S(2)}, u32[]{:S(2)}) collective-permute-start(f32[16,128]{1,0:T(8,128)S(1)} %get-tuple-element.35), channel_id=1, source_target_pairs={{0,1},{1,0},{2,3},{3,2},{4,5},{5,4},{6,7},{7,6},{8,9},{9,8},{10,11... | collective-permute-start | bytes 24584 | tf_op jit(solution)/shard_map/ppermute | solution.py:17
  21.8 8.0 %copy-start = (f32[32,1024]{1,0:T(8,128)S(1)}, f32[32,1024]{1,0:T(8,128)}, u32[]{:S(2)}) copy-start(f32[32,1024]{1,0:T(8,128)} %cent_ref.1) | copy-start | bytes 393220
  22.6 3.8 %collective-permute-start.10 = (bf16[32,1152]{1,0:T(8,128)(2,1)S(1)}, bf16[32,1152]{1,0:T(8,128)(2,1)S(1)}, u32[]{:S(2)}, u32[]{:S(2)}) collective-permute-start(bf16[32,1152]{1,0:T(8,128)(2,1)S(1)} %get-tuple-element.47), channel_id=1, source_target_pairs={{5,0},{2,1},{7,2},{0,3},{1,4},{6,5},{3,6},{4,7},{13,8},{10,9},{15,... | collective-permute-start | bytes 221192 | tf_op jit(solution)/shard_map/ppermute | solution.py:293
  23.9 5.3 %collective-permute-start.11 = (bf16[32,1152]{1,0:T(8,128)(2,1)S(1)}, bf16[32,1152]{1,0:T(8,128)(2,1)S(1)}, u32[]{:S(2)}, u32[]{:S(2)}) collective-permute-start(bf16[32,1152]{1,0:T(8,128)(2,1)S(1)} %get-tuple-element.48), channel_id=1, source_target_pairs={{7,0},{6,1},{5,2},{4,3},{3,4},{2,5},{1,6},{0,7},{15,8},{14,9},{13,... | collective-permute-start | bytes 221192 | tf_op jit(solution)/shard_map/ppermute | solution.py:293
  25.0 4.8 %collective-permute-start.12 = (bf16[32,1152]{1,0:T(8,128)(2,1)S(1)}, bf16[32,1152]{1,0:T(8,128)(2,1)S(1)}, u32[]{:S(2)}, u32[]{:S(2)}) collective-permute-start(bf16[32,1152]{1,0:T(8,128)(2,1)S(1)} %get-tuple-element.49), channel_id=1, source_target_pairs={{3,0},{4,1},{1,2},{6,3},{7,4},{0,5},{5,6},{2,7},{11,8},{12,9},{9,1... | collective-permute-start | bytes 221192 | tf_op jit(solution)/shard_map/ppermute | solution.py:293

commit v23 on v21

--- a/solution.py
+++ b/solution.py
@@ -20,7 +20,8 @@
 def chip_plan(n):
     near = list(range(2, n - 2, 2))
     turned = near[len(near) // 2:] + near[:len(near) // 2]
-    masks = list(zip(near, turned)) + [(n - 2, n - 2)]
+    masks = list(zip(near, turned))
+    masks = masks[:1] + [(n - 2, n - 2)] + masks[1:]
     return [[(i, i ^ pair[i % 2] ^ 1) for i in range(n)] for pair in masks]
 
 
@@ -264,7 +265,7 @@
         )
         arrived = [
             lax.ppermute(x, "dev", [(target, source) for source, target in pairs])
-            for x, pairs in zip(sends[1:] + sends[:1], routes[1:] + routes[:1])
+            for x, pairs in zip(sends[::-1], routes[::-1])
         ]
         result, mass = call(
             final_kernel, [shape((rows, width)), shape((1, rows))],

time: 30.8 us -> 30.5 us (level)
  starting transfers between devices: 12.6 us -> 11.8 us
  waiting for transfers between devices: 7.04 us -> 7.56 us
    ppermute x3, waiting for transfers between devices: 0.61 us -> 1.54 us  [body(): blocks = [lax.ppermute(rounded, 'dev', pairs) for pairs in routes]]
    ppermute x3, starting transfers between devices: 5.14 us -> 4.28 us  [body(): blocks = [lax.ppermute(rounded, 'dev', pairs) for pairs in routes]]
    ppermute x3, waiting for transfers between devices: 4.01 us -> 3.61 us  [body(): lax.ppermute(x, 'dev', [(target, source) for source, target in pairs])]
where the time goes in v23:
time: 30.5 us; the launch traced here: 30.3 us
  starting transfers between devices  11.8 us (39%)
  Pallas kernels  9.31 us (31%)
  waiting for transfers between devices  7.56 us (25%)
  other arithmetic  0.92 us (3%)
  between operations  0.74 us (2%)
    pallas_call x2, Pallas kernels, load(): pl.pallas_call(kernel, out_shape=[shape(dims, source.dtype), shape(follow...  4.93 us
    pallas_call x6, Pallas kernels, call(): pl.pallas_call(kernel, out_shape=outs, in_specs=[SMEM if x.dtype == jnp.i...  4.38 us
    ppermute x3, starting transfers between devices, body(): blocks = [lax.ppermute(rounded, 'dev', pairs) for pairs in routes]  4.28 us
    ppermute x3, starting transfers between devices, body(): others = [lax.ppermute(lse, 'cgrp', pairs) for pairs in plan]  4.22 us
    ppermute x3, waiting for transfers between devices, body(): lax.ppermute(x, 'dev', [(target, source) for source, target in pairs])  3.61 us
    ppermute x3, starting transfers between devices, body(): lax.ppermute(x, 'dev', [(target, source) for source, target in pairs])  3.02 us
    ppermute x3, waiting for transfers between devices, body(): blocks = [lax.ppermute(rounded, 'dev', pairs) for pairs in routes]  1.54 us
    ppermute x2, waiting for transfers between devices, swap(): return lax.ppermute(x, axis, [(i, i ^ mask) for i in range(size)])  1.31 us
  transfers between devices with their start and end apart: 11, of which 8 were waited for; matrix products, arithmetic and copies ran while one was open for 0% of the time, Pallas kernels for 22%

profile of v23, /device:TPU:0, one launch (start us, length us, event | category | flops | bytes accessed | tf_op | source)
XLA Modules:
  0.0 30.3 jit_solution(6350577466548038414)
XLA Ops:
  0.6 0.9 %convert_element_type.3.follow_ref = bf16[32,1024]{1,0:T(8,128)(2,1)S(1)} convert(f32[32,1024]{1,0:T(8,128)} %cent_ref.1) | non-fusion elementwise | flops 32768 | bytes 196608 | tf_op jit(solution)/shard_map/convert_element_type | solution.py:233
  1.5 2.5 %collective-permute-start.2 = (bf16[32,1024]{1,0:T(8,128)(2,1)S(1)}, bf16[32,1024]{1,0:T(8,128)(2,1)S(1)}, u32[]{:S(2)}, u32[]{:S(2)}) collective-permute-start(bf16[32,1024]{1,0:T(8,128)(2,1)S(1)} %convert_element_type.3.follow_ref), channel_id=1, source_target_pairs={{0,5},{1,2},{2,7},{3,0},{4,1},{5,6},{6,3},{7,4},{8,13},{9,10},{10,... | collective-permute-start | bytes 196616 | tf_op jit(solution)/shard_map/ppermute | solution.py:235
  4.0 1.7 %collective-permute-start.1 = (bf16[32,1024]{1,0:T(8,128)(2,1)S(1)}, bf16[32,1024]{1,0:T(8,128)(2,1)S(1)}, u32[]{:S(2)}, u32[]{:S(2)}) collective-permute-start(bf16[32,1024]{1,0:T(8,128)(2,1)S(1)} %convert_element_type.3.follow_ref), channel_id=1, source_target_pairs={{0,7},{1,6},{2,5},{3,4},{4,3},{5,2},{6,1},{7,0},{8,15},{9,14},{10,... | collective-permute-start | bytes 196616 | tf_op jit(solution)/shard_map/ppermute | solution.py:235
  5.7 0.1 collective-permute-start
  5.8 2.7 %shard_map.49 = (bf16[1024,2048]{1,0:T(8,128)(2,1)S(1)}, bf16[32,1024]{1,0:T(8,128)(2,1)S(1)}) custom-call(bf16[2048,1024]{1,0:T(8,128)(2,1)} %source_ref.3, bf16[32,1024]{1,0:T(8,128)(2,1)S(1)} %convert_element_type.3.follow_ref), custom_call_target="tpu_custom_call" | custom-call | bytes 8388608 | tf_op jit(solution)/shard_map/pallas_call | solution.py:73
  8.6 1.5 %collective-permute-done = bf16[32,1024]{1,0:T(8,128)(2,1)S(1)} collective-permute-done((bf16[32,1024]{1,0:T(8,128)(2,1)S(1)}, bf16[32,1024]{1,0:T(8,128)(2,1)S(1)}, u32[]{:S(2)}, u32[]{:S(2)}) %collective-permute-start) | collective-permute-done | bytes 65568 | tf_op jit(solution)/shard_map/ppermute | solution.py:235
  10.1 0.0 collective-permute-done.1
  10.1 0.0 collective-permute-done.2
  10.2 0.2 collective-permute-start.3
  10.4 0.9 %shard_map.50 = (f32[128,2048]{1,0:T(8,128)S(1)}, f32[16,128]{1,0:T(8,128)S(1)}, f32[16,128]{1,0:T(8,128)S(1)}) custom-call(bf16[1024,2048]{1,0:T(8,128)(2,1)S(1)} %get-tuple-element.25.docs_ref, bf16[128,1024]{1,0:T(8,128)(2,1)S(1)} %constant_dynamic-update-slice_fusion.table_ref), custom_call_target="tpu_custom_call" | custom-call | flops 536870912 | bytes 4456448 | tf_op jit(solution)/shard_map/pallas_call | solution.py:218
  11.2 0.5 %collective-permute-done.3.table_ref = bf16[128,1024]{1,0:T(8,128)(2,1)S(1)} collective-permute-done((bf16[128,1024]{1,0:T(8,128)(2,1)S(1)}, bf16[128,1024]{1,0:T(8,128)(2,1)S(1)}, u32[]{:S(2)}, u32[]{:S(2)}) %collective-permute-start.3) | collective-permute-done | bytes 262176 | tf_op jit(solution)/shard_map/ppermute | solution.py:17
  11.8 0.9 %shard_map.51 = (f32[128,2048]{1,0:T(8,128)S(1)}, f32[16,128]{1,0:T(8,128)S(1)}, f32[16,128]{1,0:T(8,128)S(1)}) custom-call(bf16[1024,2048]{1,0:T(8,128)(2,1)S(1)} %get-tuple-element.25.docs_ref, bf16[128,1024]{1,0:T(8,128)(2,1)S(1)} %collective-permute-done.3.table_ref, f32[16,128]{1,0:T(8,128)S(1)} %get-tuple-element.27.first_top_ref.refs_6_, ...), custom_call_target="tpu_custom_call" | custom-call | flops 536870912 | bytes 4472832 | tf_op jit(solution)/shard_map/pallas_call | solution.py:218
  12.7 2.6 %collective-permute-start.6 = (f32[16,128]{1,0:T(8,128)S(1)}, f32[16,128]{1,0:T(8,128)S(1)}, u32[]{:S(2)}, u32[]{:S(2)}) collective-permute-start(f32[16,128]{1,0:T(8,128)S(1)} %get-tuple-element.29.follow_ref), channel_id=1, source_target_pairs={{0,16},{8,24},{16,8},{24,0},{1,17},{9,25},{17,9},{25,1},{2,18},{10... | collective-permute-start | bytes 24584 | tf_op jit(solution)/shard_map/ppermute | solution.py:246
  15.3 1.2 %collective-permute-start.5 = (f32[16,128]{1,0:T(8,128)S(1)}, f32[16,128]{1,0:T(8,128)S(1)}, u32[]{:S(2)}, u32[]{:S(2)}) collective-permute-start(f32[16,128]{1,0:T(8,128)S(1)} %get-tuple-element.29.follow_ref), channel_id=1, source_target_pairs={{0,24},{8,16},{16,0},{24,8},{1,25},{9,17},{17,1},{25,9},{2,26},{10... | collective-permute-start | bytes 24584 | tf_op jit(solution)/shard_map/ppermute | solution.py:246
  16.5 0.3 %collective-permute-start.4 = (f32[16,128]{1,0:T(8,128)S(1)}, f32[16,128]{1,0:T(8,128)S(1)}, u32[]{:S(2)}, u32[]{:S(2)}) collective-permute-start(f32[16,128]{1,0:T(8,128)S(1)} %get-tuple-element.29.follow_ref), channel_id=1, source_target_pairs={{0,8},{8,0},{16,24},{24,16},{1,9},{9,1},{17,25},{25,17},{2,10},{10... | collective-permute-start | bytes 24584 | tf_op jit(solution)/shard_map/ppermute | solution.py:246
  16.9 2.2 %shard_map.52 = (bf16[2048,1024]{1,0:T(8,128)(2,1)S(1)}, f32[16,128]{1,0:T(8,128)S(1)}) custom-call(bf16[2048,1024]{1,0:T(8,128)(2,1)} %source_ref.3, f32[16,128]{1,0:T(8,128)S(1)} %get-tuple-element.29.follow_ref), custom_call_target="tpu_custom_call" | custom-call | bytes 8388608 | tf_op jit(solution)/shard_map/pallas_call | solution.py:73
  19.1 0.0 collective-permute-done.6.refs_2_
  19.1 0.8 %collective-permute-done.5.refs_1_ = f32[16,128]{1,0:T(8,128)S(1)} collective-permute-done((f32[16,128]{1,0:T(8,128)S(1)}, f32[16,128]{1,0:T(8,128)S(1)}, u32[]{:S(2)}, u32[]{:S(2)}) %collective-permute-start.5) | collective-permute-done | bytes 8224 | tf_op jit(solution)/shard_map/ppermute | solution.py:246
  19.9 0.3 %collective-permute-done.4.refs_0_ = f32[16,128]{1,0:T(8,128)S(1)} collective-permute-done((f32[16,128]{1,0:T(8,128)S(1)}, f32[16,128]{1,0:T(8,128)S(1)}, u32[]{:S(2)}, u32[]{:S(2)}) %collective-permute-start.4) | collective-permute-done | bytes 8224 | tf_op jit(solution)/shard_map/ppermute | solution.py:246
  20.2 0.8 %shard_map.53 = (f32[16,128]{1,0:T(8,128)}, f32[16,128]{1,0:T(8,128)S(1)}, bf16[128,1152]{1,0:T(8,128)(2,1)S(1)}) custom-call(s32[1]{0:T(128)} %bitcast.me_ref, f32[16,128]{1,0:T(8,128)S(1)} %get-tuple-element.30.lse_ref, f32[16,128]{1,0:T(8,128)S(1)} %collective-permute-done.4.refs_0_, f32[16,128]{1,0:T(8,128)S(1)} %collective-permute-done.5.refs_1_, ...), custom_call_target="tpu_custom_call" | custom-call | flops 536870912 | bytes 5292036 | tf_op jit(solution)/shard_map/pallas_call | solution.py:218
  21.0 0.0 copy-start
  21.0 0.1 collective-permute-start.7
  21.1 0.8 %shard_map.54 = (f32[128,1024]{1,0:T(8,128)S(1)}, f32[128,128]{1,0:T(8,128)S(1)}) custom-call(f32[16,128]{1,0:T(8,128)S(1)} %get-tuple-element.34.factor_ref, bf16[2048,1024]{1,0:T(8,128)(2,1)S(1)} %get-tuple-element.31.refs_3_.docs_ref, f32[128,2048]{1,0:T(8,128)S(1)} %get-tuple-element.35.part_ref), custom_call_target="tpu_custom_call" | custom-call | flops 536870912 | bytes 5251072 | tf_op jit(solution)/shard_map/pallas_call | solution.py:218
  21.9 0.8 %collective-permute-done.7.got_ref = bf16[128,1152]{1,0:T(8,128)(2,1)S(1)} collective-permute-done((bf16[128,1152]{1,0:T(8,128)(2,1)S(1)}, bf16[128,1152]{1,0:T(8,128)(2,1)S(1)}, u32[]{:S(2)}, u32[]{:S(2)}) %collective-permute-start.7) | collective-permute-done | bytes 294944 | tf_op jit(solution)/shard_map/ppermute | solution.py:17
  22.7 0.2 shard_map.55
  22.9 1.0 %collective-permute-start.8 = (bf16[32,1152]{1,0:T(8,128)(2,1)S(1)}, bf16[32,1152]{1,0:T(8,128)(2,1)S(1)}, u32[]{:S(2)}, u32[]{:S(2)}) collective-permute-start(bf16[32,1152]{1,0:T(8,128)(2,1)S(1)} %get-tuple-element.41), channel_id=1, source_target_pairs={{5,0},{2,1},{7,2},{0,3},{1,4},{6,5},{3,6},{4,7},{13,8},{10,9},{15,... | collective-permute-start | bytes 221192 | tf_op jit(solution)/shard_map/ppermute | solution.py:267
  23.8 1.4 %collective-permute-start.9 = (bf16[32,1152]{1,0:T(8,128)(2,1)S(1)}, bf16[32,1152]{1,0:T(8,128)(2,1)S(1)}, u32[]{:S(2)}, u32[]{:S(2)}) collective-permute-start(bf16[32,1152]{1,0:T(8,128)(2,1)S(1)} %get-tuple-element.42), channel_id=1, source_target_pairs={{7,0},{6,1},{5,2},{4,3},{3,4},{2,5},{1,6},{0,7},{15,8},{14,9},{13,... | collective-permute-start | bytes 221192 | tf_op jit(solution)/shard_map/ppermute | solution.py:267
  25.3 0.6 %collective-permute-start.10 = (bf16[32,1152]{1,0:T(8,128)(2,1)S(1)}, bf16[32,1152]{1,0:T(8,128)(2,1)S(1)}, u32[]{:S(2)}, u32[]{:S(2)}) collective-permute-start(bf16[32,1152]{1,0:T(8,128)(2,1)S(1)} %get-tuple-element.43), channel_id=1, source_target_pairs={{3,0},{4,1},{1,2},{6,3},{7,4},{0,5},{5,6},{2,7},{11,8},{12,9},{9,1... | collective-permute-start | bytes 221192 | tf_op jit(solution)/shard_map/ppermute | solution.py:267
  25.9 0.8 %collective-permute-done.8.refs_0_ = bf16[32,1152]{1,0:T(8,128)(2,1)S(1)} collective-permute-done((bf16[32,1152]{1,0:T(8,128)(2,1)S(1)}, bf16[32,1152]{1,0:T(8,128)(2,1)S(1)}, u32[]{:S(2)}, u32[]{:S(2)}) %collective-permute-start.8) | collective-permute-done | bytes 73760 | tf_op jit(solution)/shard_map/ppermute | solution.py:267
  26.7 2.4 %collective-permute-done.9.refs_1_ = bf16[32,1152]{1,0:T(8,128)(2,1)S(1)} collective-permute-done((bf16[32,1152]{1,0:T(8,128)(2,1)S(1)}, bf16[32,1152]{1,0:T(8,128)(2,1)S(1)}, u32[]{:S(2)}, u32[]{:S(2)}) %collective-permute-start.9) | collective-permute-done | bytes 73760 | tf_op jit(solution)/shard_map/ppermute | solution.py:267
  29.1 0.4 %collective-permute-done.10.refs_2_ = bf16[32,1152]{1,0:T(8,128)(2,1)S(1)} collective-permute-done((bf16[32,1152]{1,0:T(8,128)(2,1)S(1)}, bf16[32,1152]{1,0:T(8,128)(2,1)S(1)}, u32[]{:S(2)}, u32[]{:S(2)}) %collective-permute-start.10) | collective-permute-done | bytes 73760 | tf_op jit(solution)/shard_map/ppermute | solution.py:267
  29.5 0.0 copy-done
  29.5 0.8 %shard_map.56 = (f32[32,1024]{1,0:T(8,128)}, f32[1,32]{1,0:T(1,128)}) custom-call(f32[32,1024]{1,0:T(8,128)S(1)} %get-tuple-element.39.own_ref, f32[32,128]{1,0:T(8,128)S(1)} %get-tuple-element.40.own_mass_ref, f32[32,1024]{1,0:T(8,128)S(1)} %copy-done, bf16[32,1152]{1,0:T(8,128)(2,1)S(1)} %collective-permute-done.8.refs_0_, ...), custom_call_target="tpu_custom_call" | custom-call | bytes 499712 | tf_op jit(solution)/shard_map/pallas_call | solution.py:218
  (4 shorter events, 0.0 us)
Async XLA Ops:
  1.5 8.6 %collective-permute-start.2 = (bf16[32,1024]{1,0:T(8,128)(2,1)S(1)}, bf16[32,1024]{1,0:T(8,128)(2,1)S(1)}, u32[]{:S(2)}, u32[]{:S(2)}) collective-permute-start(bf16[32,1024]{1,0:T(8,128)(2,1)S(1)} %convert_element_type.3.follow_ref), channel_id=1, source_target_pairs={{0,5},{1,2},{2,7},{3,0},{4,1},{5,6},{6,3},{7,4},{8,13},{9,10},{10,... | collective-permute-start | bytes 196616 | tf_op jit(solution)/shard_map/ppermute | solution.py:235
  4.0 6.1 %collective-permute-start.1 = (bf16[32,1024]{1,0:T(8,128)(2,1)S(1)}, bf16[32,1024]{1,0:T(8,128)(2,1)S(1)}, u32[]{:S(2)}, u32[]{:S(2)}) collective-permute-start(bf16[32,1024]{1,0:T(8,128)(2,1)S(1)} %convert_element_type.3.follow_ref), channel_id=1, source_target_pairs={{0,7},{1,6},{2,5},{3,4},{4,3},{5,2},{6,1},{7,0},{8,15},{9,14},{10,... | collective-permute-start | bytes 196616 | tf_op jit(solution)/shard_map/ppermute | solution.py:235
  5.7 4.4 %collective-permute-start = (bf16[32,1024]{1,0:T(8,128)(2,1)S(1)}, bf16[32,1024]{1,0:T(8,128)(2,1)S(1)}, u32[]{:S(2)}, u32[]{:S(2)}) collective-permute-start(bf16[32,1024]{1,0:T(8,128)(2,1)S(1)} %convert_element_type.3.follow_ref), channel_id=1, source_target_pairs={{0,3},{1,4},{2,1},{3,6},{4,7},{5,0},{6,5},{7,2},{8,11},{9,12},{10,... | collective-permute-start | bytes 196616 | tf_op jit(solution)/shard_map/ppermute | solution.py:235
  10.2 1.6 %collective-permute-start.3 = (bf16[128,1024]{1,0:T(8,128)(2,1)S(1)}, bf16[128,1024]{1,0:T(8,128)(2,1)S(1)}, u32[]{:S(2)}, u32[]{:S(2)}) collective-permute-start(bf16[128,1024]{1,0:T(8,128)(2,1)S(1)} %constant_dynamic-update-slice_fusion.table_ref), channel_id=1, source_target_pairs={{0,1},{1,0},{2,3},{3,2},{4,5},{5,4},{6,7},{7,6},{8,9},{9,8},{10,11... | collective-permute-start | bytes 786440 | tf_op jit(solution)/shard_map/ppermute | solution.py:17
  12.7 6.4 %collective-permute-start.6 = (f32[16,128]{1,0:T(8,128)S(1)}, f32[16,128]{1,0:T(8,128)S(1)}, u32[]{:S(2)}, u32[]{:S(2)}) collective-permute-start(f32[16,128]{1,0:T(8,128)S(1)} %get-tuple-element.29.follow_ref), channel_id=1, source_target_pairs={{0,16},{8,24},{16,8},{24,0},{1,17},{9,25},{17,9},{25,1},{2,18},{10... | collective-permute-start | bytes 24584 | tf_op jit(solution)/shard_map/ppermute | solution.py:246
  15.3 4.5 %collective-permute-start.5 = (f32[16,128]{1,0:T(8,128)S(1)}, f32[16,128]{1,0:T(8,128)S(1)}, u32[]{:S(2)}, u32[]{:S(2)}) collective-permute-start(f32[16,128]{1,0:T(8,128)S(1)} %get-tuple-element.29.follow_ref), channel_id=1, source_target_pairs={{0,24},{8,16},{16,0},{24,8},{1,25},{9,17},{17,1},{25,9},{2,26},{10... | collective-permute-start | bytes 24584 | tf_op jit(solution)/shard_map/ppermute | solution.py:246
  16.5 3.7 %collective-permute-start.4 = (f32[16,128]{1,0:T(8,128)S(1)}, f32[16,128]{1,0:T(8,128)S(1)}, u32[]{:S(2)}, u32[]{:S(2)}) collective-permute-start(f32[16,128]{1,0:T(8,128)S(1)} %get-tuple-element.29.follow_ref), channel_id=1, source_target_pairs={{0,8},{8,0},{16,24},{24,16},{1,9},{9,1},{17,25},{25,17},{2,10},{10... | collective-permute-start | bytes 24584 | tf_op jit(solution)/shard_map/ppermute | solution.py:246
  21.0 8.5 %copy-start = (f32[32,1024]{1,0:T(8,128)S(1)}, f32[32,1024]{1,0:T(8,128)}, u32[]{:S(2)}) copy-start(f32[32,1024]{1,0:T(8,128)} %cent_ref.1) | copy-start | bytes 393220
  21.0 1.6 %collective-permute-start.7 = (bf16[128,1152]{1,0:T(8,128)(2,1)S(1)}, bf16[128,1152]{1,0:T(8,128)(2,1)S(1)}, u32[]{:S(2)}, u32[]{:S(2)}) collective-permute-start(bf16[128,1152]{1,0:T(8,128)(2,1)S(1)} %get-tuple-element.38), channel_id=1, source_target_pairs={{0,1},{1,0},{2,3},{3,2},{4,5},{5,4},{6,7},{7,6},{8,9},{9,8},{10,11... | collective-permute-start | bytes 884744 | tf_op jit(solution)/shard_map/ppermute | solution.py:17
  22.9 3.8 %collective-permute-start.8 = (bf16[32,1152]{1,0:T(8,128)(2,1)S(1)}, bf16[32,1152]{1,0:T(8,128)(2,1)S(1)}, u32[]{:S(2)}, u32[]{:S(2)}) collective-permute-start(bf16[32,1152]{1,0:T(8,128)(2,1)S(1)} %get-tuple-element.41), channel_id=1, source_target_pairs={{5,0},{2,1},{7,2},{0,3},{1,4},{6,5},{3,6},{4,7},{13,8},{10,9},{15,... | collective-permute-start | bytes 221192 | tf_op jit(solution)/shard_map/ppermute | solution.py:267
  23.8 5.2 %collective-permute-start.9 = (bf16[32,1152]{1,0:T(8,128)(2,1)S(1)}, bf16[32,1152]{1,0:T(8,128)(2,1)S(1)}, u32[]{:S(2)}, u32[]{:S(2)}) collective-permute-start(bf16[32,1152]{1,0:T(8,128)(2,1)S(1)} %get-tuple-element.42), channel_id=1, source_target_pairs={{7,0},{6,1},{5,2},{4,3},{3,4},{2,5},{1,6},{0,7},{15,8},{14,9},{13,... | collective-permute-start | bytes 221192 | tf_op jit(solution)/shard_map/ppermute | solution.py:267
  25.3 4.2 %collective-permute-start.10 = (bf16[32,1152]{1,0:T(8,128)(2,1)S(1)}, bf16[32,1152]{1,0:T(8,128)(2,1)S(1)}, u32[]{:S(2)}, u32[]{:S(2)}) collective-permute-start(bf16[32,1152]{1,0:T(8,128)(2,1)S(1)} %get-tuple-element.43), channel_id=1, source_target_pairs={{3,0},{4,1},{1,2},{6,3},{7,4},{0,5},{5,6},{2,7},{11,8},{12,9},{9,1... | collective-permute-start | bytes 221192 | tf_op jit(solution)/shard_map/ppermute | solution.py:267

commit v24 on v22

--- a/solution.py
+++ b/solution.py
@@ -20,7 +20,8 @@
 def chip_plan(n):
     near = list(range(2, n - 2, 2))
     turned = near[len(near) // 2:] + near[:len(near) // 2]
-    masks = list(zip(near, turned)) + [(n - 2, n - 2)]
+    masks = list(zip(near, turned))
+    masks = masks[:1] + [(n - 2, n - 2)] + masks[1:]
     return [[(i, i ^ pair[i % 2] ^ 1) for i in range(n)] for pair in masks]
 
 
@@ -291,7 +292,7 @@
         )
         arrived = [
             lax.ppermute(x, "dev", [(target, source) for source, target in pairs])
-            for x, pairs in zip(sends[1:] + sends[:1], routes[1:] + routes[:1])
+            for x, pairs in zip(sends[::-1], routes[::-1])
         ]
         result, mass, doc_lse = call(
             final_kernel, [shape((rows, width)), shape((1, rows)), shape(doc_lse.shape)],

time: 30.8 us -> 31.1 us (level)
  waiting for transfers between devices: 4.52 us -> 6.39 us
  starting transfers between devices: 13.8 us -> 12.2 us
    ppermute x3, waiting for transfers between devices: 0.01 us -> 2.07 us  [body(): blocks = [lax.ppermute(rounded, 'dev', pairs) for pairs in routes]]
    ppermute x3, starting transfers between devices: 5.36 us -> 3.84 us  [body(): blocks = [lax.ppermute(rounded, 'dev', pairs) for pairs in routes]]
  transfers between devices with their start and end apart: 13 -> 13, of which waited for: 5 -> 6; matrix products, arithmetic and copies ran while one was open for 3% -> 3% of each run, Pallas kernels for 29% -> 29%
where the time goes in v24:
time: 31.1 us; the launch traced here: 30.9 us
  starting transfers between devices  12.2 us (39%)
  Pallas kernels  10.6 us (34%)
  waiting for transfers between devices  6.39 us (21%)
  other arithmetic  0.91 us (3%)
  between operations  0.77 us (2%)
    pallas_call x2, Pallas kernels, load(): pl.pallas_call(kernel, out_shape=outs + [shape(follow.shape, follow.dtype...  5.92 us
    pallas_call x6, Pallas kernels, call(): pl.pallas_call(kernel, out_shape=outs, in_specs=specs or [SMEM if x.dtype...  4.66 us
    ppermute x3, starting transfers between devices, body(): others = [lax.ppermute(lse, 'cgrp', pairs) for pairs in plan]  4.18 us
    ppermute x3, starting transfers between devices, body(): blocks = [lax.ppermute(rounded, 'dev', pairs) for pairs in routes]  3.84 us
    ppermute x3, waiting for transfers between devices, body(): lax.ppermute(x, 'dev', [(target, source) for source, target in pairs])  3.58 us
    ppermute x3, starting transfers between devices, body(): lax.ppermute(x, 'dev', [(target, source) for source, target in pairs])  3.36 us
    ppermute x3, waiting for transfers between devices, body(): blocks = [lax.ppermute(rounded, 'dev', pairs) for pairs in routes]  2.07 us
    convert_element_type x1, other arithmetic, body(): rounded = centroids.astype(jnp.bfloat16)  0.91 us
  transfers between devices with their start and end apart: 13, of which 6 were waited for; matrix products, arithmetic and copies ran while one was open for 3% of the time, Pallas kernels for 29%

profile of v24, /device:TPU:0, one launch (start us, length us, event | category | flops | bytes accessed | tf_op | source)
XLA Modules:
  0.0 30.9 jit_solution(6790926670708088623)
XLA Ops:
  0.6 0.5 %collective-permute-start = (bf16[2048,1024]{1,0:T(8,128)(2,1)}, bf16[2048,1024]{1,0:T(8,128)(2,1)}, u32[]{:S(2)}, u32[]{:S(2)}) collective-permute-start(bf16[2048,1024]{1,0:T(8,128)(2,1)} %refs_0_.1), channel_id=1, source_target_pairs={{0,1},{1,0},{2,3},{3,2},{4,5},{5,4},{6,7},{7,6},{8,9},{9,8},{10,11... | collective-permute-start | bytes 12582920 | tf_op jit(solution)/shard_map/ppermute | solution.py:17
  1.1 0.9 %convert_element_type.3.follow_ref = bf16[32,1024]{1,0:T(8,128)(2,1)S(1)} convert(f32[32,1024]{1,0:T(8,128)} %cent_ref.1) | non-fusion elementwise | flops 32768 | bytes 196608 | tf_op jit(solution)/shard_map/convert_element_type | solution.py:255
  2.1 2.7 %collective-permute-start.3 = (bf16[32,1024]{1,0:T(8,128)(2,1)S(1)}, bf16[32,1024]{1,0:T(8,128)(2,1)S(1)}, u32[]{:S(2)}, u32[]{:S(2)}) collective-permute-start(bf16[32,1024]{1,0:T(8,128)(2,1)S(1)} %convert_element_type.3.follow_ref), channel_id=1, source_target_pairs={{0,5},{1,2},{2,7},{3,0},{4,1},{5,6},{6,3},{7,4},{8,13},{9,10},{10,... | collective-permute-start | bytes 196616 | tf_op jit(solution)/shard_map/ppermute | solution.py:257
  4.7 1.1 %collective-permute-start.2 = (bf16[32,1024]{1,0:T(8,128)(2,1)S(1)}, bf16[32,1024]{1,0:T(8,128)(2,1)S(1)}, u32[]{:S(2)}, u32[]{:S(2)}) collective-permute-start(bf16[32,1024]{1,0:T(8,128)(2,1)S(1)} %convert_element_type.3.follow_ref), channel_id=1, source_target_pairs={{0,7},{1,6},{2,5},{3,4},{4,3},{5,2},{6,1},{7,0},{8,15},{9,14},{10,... | collective-permute-start | bytes 196616 | tf_op jit(solution)/shard_map/ppermute | solution.py:257
  5.8 0.1 collective-permute-start.1
  5.9 2.7 %shard_map.49 = (bf16[1024,2048]{1,0:T(8,128)(2,1)S(1)}, bf16[32,1024]{1,0:T(8,128)(2,1)S(1)}) custom-call(bf16[2048,1024]{1,0:T(8,128)(2,1)} %refs_0_.1, bf16[32,1024]{1,0:T(8,128)(2,1)S(1)} %convert_element_type.3.follow_ref), custom_call_target="tpu_custom_call" | custom-call | bytes 8388608 | tf_op jit(solution)/shard_map/pallas_call | solution.py:86
  8.7 2.1 %collective-permute-done.1 = bf16[32,1024]{1,0:T(8,128)(2,1)S(1)} collective-permute-done((bf16[32,1024]{1,0:T(8,128)(2,1)S(1)}, bf16[32,1024]{1,0:T(8,128)(2,1)S(1)}, u32[]{:S(2)}, u32[]{:S(2)}) %collective-permute-start.1) | collective-permute-done | bytes 65568 | tf_op jit(solution)/shard_map/ppermute | solution.py:257
  10.7 0.0 collective-permute-done.2
  10.8 0.0 collective-permute-done.3
  10.8 0.1 collective-permute-start.4
  10.9 0.9 %shard_map.50 = (f32[128,2048]{1,0:T(8,128)S(1)}, f32[16,128]{1,0:T(8,128)S(1)}, f32[16,128]{1,0:T(8,128)S(1)}) custom-call(bf16[1024,2048]{1,0:T(8,128)(2,1)S(1)} %get-tuple-element.28.docs_ref, bf16[128,1024]{1,0:T(8,128)(2,1)S(1)} %constant_dynamic-update-slice_fusion.table_ref), custom_call_target="tpu_custom_call" | custom-call | flops 536870912 | bytes 4456448 | tf_op jit(solution)/shard_map/pallas_call | solution.py:240
  11.8 0.6 %collective-permute-done.4.table_ref = bf16[128,1024]{1,0:T(8,128)(2,1)S(1)} collective-permute-done((bf16[128,1024]{1,0:T(8,128)(2,1)S(1)}, bf16[128,1024]{1,0:T(8,128)(2,1)S(1)}, u32[]{:S(2)}, u32[]{:S(2)}) %collective-permute-start.4) | collective-permute-done | bytes 262176 | tf_op jit(solution)/shard_map/ppermute | solution.py:17
  12.4 0.9 %shard_map.51 = (bf16[128,2048]{1,0:T(8,128)(2,1)S(1)}, f32[16,128]{1,0:T(8,128)S(1)}, f32[16,128]{1,0:T(8,128)S(1)}) custom-call(bf16[1024,2048]{1,0:T(8,128)(2,1)S(1)} %get-tuple-element.28.docs_ref, bf16[128,1024]{1,0:T(8,128)(2,1)S(1)} %collective-permute-done.4.table_ref, f32[16,128]{1,0:T(8,128)S(1)} %get-tuple-element.30.first_top_ref.refs_3_, ...), custom_call_target="tpu_custom_call" | custom-call | flops 536870912 | bytes 4472832 | tf_op jit(solution)/shard_map/pallas_call | solution.py:240
  13.3 0.2 collective-permute-start.9
  13.5 2.6 %collective-permute-start.7 = (f32[16,128]{1,0:T(8,128)S(1)}, f32[16,128]{1,0:T(8,128)S(1)}, u32[]{:S(2)}, u32[]{:S(2)}) collective-permute-start(f32[16,128]{1,0:T(8,128)S(1)} %get-tuple-element.32.refs_2_), channel_id=1, source_target_pairs={{0,16},{8,24},{16,8},{24,0},{1,17},{9,25},{17,9},{25,1},{2,18},{10... | collective-permute-start | bytes 24584 | tf_op jit(solution)/shard_map/ppermute | solution.py:271
  16.1 1.2 %collective-permute-start.6 = (f32[16,128]{1,0:T(8,128)S(1)}, f32[16,128]{1,0:T(8,128)S(1)}, u32[]{:S(2)}, u32[]{:S(2)}) collective-permute-start(f32[16,128]{1,0:T(8,128)S(1)} %get-tuple-element.32.refs_2_), channel_id=1, source_target_pairs={{0,24},{8,16},{16,0},{24,8},{1,25},{9,17},{17,1},{25,9},{2,26},{10... | collective-permute-start | bytes 24584 | tf_op jit(solution)/shard_map/ppermute | solution.py:271
  17.3 0.3 %collective-permute-start.5 = (f32[16,128]{1,0:T(8,128)S(1)}, f32[16,128]{1,0:T(8,128)S(1)}, u32[]{:S(2)}, u32[]{:S(2)}) collective-permute-start(f32[16,128]{1,0:T(8,128)S(1)} %get-tuple-element.32.refs_2_), channel_id=1, source_target_pairs={{0,8},{8,0},{16,24},{24,16},{1,9},{9,1},{17,25},{25,17},{2,10},{10... | collective-permute-start | bytes 24584 | tf_op jit(solution)/shard_map/ppermute | solution.py:271
  17.7 0.0 collective-permute-done.refs_1_.source_ref
  17.7 3.2 %shard_map.52 = (bf16[2048,1024]{1,0:T(8,128)(2,1)S(1)}, bf16[1536,1024]{1,0:T(8,128)(2,1)S(1)}, f32[16,128]{1,0:T(8,128)S(1)}) custom-call(bf16[2048,1024]{1,0:T(8,128)(2,1)} %refs_0_.1, bf16[2048,1024]{1,0:T(8,128)(2,1)} %collective-permute-done.refs_1_.source_ref, f32[16,128]{1,0:T(8,128)S(1)} %get-tuple-element.32.refs_2_), custom_call_target="tpu_custom_call" | custom-call | bytes 16777216 | tf_op jit(solution)/shard_map/pallas_call | solution.py:86
  20.9 0.0 collective-permute-done.7.refs_2_
  20.9 0.0 collective-permute-done.6.refs_1_
  20.9 0.1 collective-permute-done.5.refs_0_
  21.0 0.1 collective-permute-start.8
  21.1 1.2 %shard_map.54 = (f32[128,1024]{1,0:T(8,128)S(1)}, f32[128,128]{1,0:T(8,128)S(1)}, bf16[512,1024]{1,0:T(8,128)(2,1)S(1)}) custom-call(f32[16,128]{1,0:T(8,128)S(1)} %get-tuple-element.37.factor_ref, bf16[2048,1024]{1,0:T(8,128)(2,1)S(1)} %get-tuple-element.38.docs_ref, f32[128,2048]{1,0:T(8,128)S(1)} %get-tuple-element.39.part_ref, ...), custom_call_target="tpu_custom_call" | custom-call | flops 536870912 | bytes 9445376 | tf_op jit(solution)/shard_map/pallas_call | solution.py:240
  22.3 0.0 copy-start
  22.4 0.0 collective-permute-done.9.part_ref
  22.4 0.0 collective-permute-done.8.factor_ref
  22.4 0.8 %shard_map.55 = (f32[32,1024]{1,0:T(8,128)S(1)}, f32[32,128]{1,0:T(8,128)S(1)}, bf16[32,1152]{1,0:T(8,128)(2,1)S(1)}, bf16[32,1152]{1,0:T(8,128)(2,1)S(1)}, bf16[32,1152]{1,0:T(8,128)(2,1)S(1)}) custom-call(f32[16,128]{1,0:T(8,128)S(1)} %collective-permute-done.8.factor_ref, bf16[1536,1024]{1,0:T(8,128)(2,1)S(1)} %get-tuple-element.36.docs_ref, ...), custom_call_target="tpu_custom_call" | custom-call | flops 536870912 | bytes 5316608 | tf_op jit(solution)/shard_map/pallas_call | solution.py:240
  23.2 0.9 %collective-permute-start.10 = (bf16[32,1152]{1,0:T(8,128)(2,1)S(1)}, bf16[32,1152]{1,0:T(8,128)(2,1)S(1)}, u32[]{:S(2)}, u32[]{:S(2)}) collective-permute-start(bf16[32,1152]{1,0:T(8,128)(2,1)S(1)} %get-tuple-element.47), channel_id=1, source_target_pairs={{5,0},{2,1},{7,2},{0,3},{1,4},{6,5},{3,6},{4,7},{13,8},{10,9},{15,... | collective-permute-start | bytes 221192 | tf_op jit(solution)/shard_map/ppermute | solution.py:294
  24.1 1.1 %collective-permute-start.11 = (bf16[32,1152]{1,0:T(8,128)(2,1)S(1)}, bf16[32,1152]{1,0:T(8,128)(2,1)S(1)}, u32[]{:S(2)}, u32[]{:S(2)}) collective-permute-start(bf16[32,1152]{1,0:T(8,128)(2,1)S(1)} %get-tuple-element.48), channel_id=1, source_target_pairs={{7,0},{6,1},{5,2},{4,3},{3,4},{2,5},{1,6},{0,7},{15,8},{14,9},{13,... | collective-permute-start | bytes 221192 | tf_op jit(solution)/shard_map/ppermute | solution.py:294
  25.2 1.3 %collective-permute-start.12 = (bf16[32,1152]{1,0:T(8,128)(2,1)S(1)}, bf16[32,1152]{1,0:T(8,128)(2,1)S(1)}, u32[]{:S(2)}, u32[]{:S(2)}) collective-permute-start(bf16[32,1152]{1,0:T(8,128)(2,1)S(1)} %get-tuple-element.49), channel_id=1, source_target_pairs={{3,0},{4,1},{1,2},{6,3},{7,4},{0,5},{5,6},{2,7},{11,8},{12,9},{9,1... | collective-permute-start | bytes 221192 | tf_op jit(solution)/shard_map/ppermute | solution.py:294
  26.5 0.5 %collective-permute-done.10.refs_0_ = bf16[32,1152]{1,0:T(8,128)(2,1)S(1)} collective-permute-done((bf16[32,1152]{1,0:T(8,128)(2,1)S(1)}, bf16[32,1152]{1,0:T(8,128)(2,1)S(1)}, u32[]{:S(2)}, u32[]{:S(2)}) %collective-permute-start.10) | collective-permute-done | bytes 73760 | tf_op jit(solution)/shard_map/ppermute | solution.py:294
  27.0 2.6 %collective-permute-done.11.refs_1_ = bf16[32,1152]{1,0:T(8,128)(2,1)S(1)} collective-permute-done((bf16[32,1152]{1,0:T(8,128)(2,1)S(1)}, bf16[32,1152]{1,0:T(8,128)(2,1)S(1)}, u32[]{:S(2)}, u32[]{:S(2)}) %collective-permute-start.11) | collective-permute-done | bytes 73760 | tf_op jit(solution)/shard_map/ppermute | solution.py:294
  29.6 0.5 %collective-permute-done.12.refs_2_ = bf16[32,1152]{1,0:T(8,128)(2,1)S(1)} collective-permute-done((bf16[32,1152]{1,0:T(8,128)(2,1)S(1)}, bf16[32,1152]{1,0:T(8,128)(2,1)S(1)}, u32[]{:S(2)}, u32[]{:S(2)}) %collective-permute-start.12) | collective-permute-done | bytes 73760 | tf_op jit(solution)/shard_map/ppermute | solution.py:294
  30.1 0.0 copy-done
  30.1 0.8 %shard_map.56 = (f32[32,1024]{1,0:T(8,128)}, f32[1,32]{1,0:T(1,128)}, f32[16,128]{1,0:T(8,128)}) custom-call(f32[32,1024]{1,0:T(8,128)S(1)} %get-tuple-element.44.own_ref, f32[32,128]{1,0:T(8,128)S(1)} %get-tuple-element.45.own_mass_ref, f32[32,1024]{1,0:T(8,128)S(1)} %copy-done, f32[16,128]{1,0:T(8,128)S(1)} %get-tuple-element.46.lse_ref, ...), custom_call_target="tpu_custom_call" | custom-call | bytes 507904 | tf_op jit(solution)/shard_map/pallas_call | solution.py:240
  (5 shorter events, 0.1 us)
Async XLA Ops:
  0.6 17.0 %collective-permute-start = (bf16[2048,1024]{1,0:T(8,128)(2,1)}, bf16[2048,1024]{1,0:T(8,128)(2,1)}, u32[]{:S(2)}, u32[]{:S(2)}) collective-permute-start(bf16[2048,1024]{1,0:T(8,128)(2,1)} %refs_0_.1), channel_id=1, source_target_pairs={{0,1},{1,0},{2,3},{3,2},{4,5},{5,4},{6,7},{7,6},{8,9},{9,8},{10,11... | collective-permute-start | bytes 12582920 | tf_op jit(solution)/shard_map/ppermute | solution.py:17
  2.1 8.7 %collective-permute-start.3 = (bf16[32,1024]{1,0:T(8,128)(2,1)S(1)}, bf16[32,1024]{1,0:T(8,128)(2,1)S(1)}, u32[]{:S(2)}, u32[]{:S(2)}) collective-permute-start(bf16[32,1024]{1,0:T(8,128)(2,1)S(1)} %convert_element_type.3.follow_ref), channel_id=1, source_target_pairs={{0,5},{1,2},{2,7},{3,0},{4,1},{5,6},{6,3},{7,4},{8,13},{9,10},{10,... | collective-permute-start | bytes 196616 | tf_op jit(solution)/shard_map/ppermute | solution.py:257
  4.7 6.0 %collective-permute-start.2 = (bf16[32,1024]{1,0:T(8,128)(2,1)S(1)}, bf16[32,1024]{1,0:T(8,128)(2,1)S(1)}, u32[]{:S(2)}, u32[]{:S(2)}) collective-permute-start(bf16[32,1024]{1,0:T(8,128)(2,1)S(1)} %convert_element_type.3.follow_ref), channel_id=1, source_target_pairs={{0,7},{1,6},{2,5},{3,4},{4,3},{5,2},{6,1},{7,0},{8,15},{9,14},{10,... | collective-permute-start | bytes 196616 | tf_op jit(solution)/shard_map/ppermute | solution.py:257
  5.8 4.9 %collective-permute-start.1 = (bf16[32,1024]{1,0:T(8,128)(2,1)S(1)}, bf16[32,1024]{1,0:T(8,128)(2,1)S(1)}, u32[]{:S(2)}, u32[]{:S(2)}) collective-permute-start(bf16[32,1024]{1,0:T(8,128)(2,1)S(1)} %convert_element_type.3.follow_ref), channel_id=1, source_target_pairs={{0,3},{1,4},{2,1},{3,6},{4,7},{5,0},{6,5},{7,2},{8,11},{9,12},{10,... | collective-permute-start | bytes 196616 | tf_op jit(solution)/shard_map/ppermute | solution.py:257
  10.8 1.6 %collective-permute-start.4 = (bf16[128,1024]{1,0:T(8,128)(2,1)S(1)}, bf16[128,1024]{1,0:T(8,128)(2,1)S(1)}, u32[]{:S(2)}, u32[]{:S(2)}) collective-permute-start(bf16[128,1024]{1,0:T(8,128)(2,1)S(1)} %constant_dynamic-update-slice_fusion.table_ref), channel_id=1, source_target_pairs={{0,1},{1,0},{2,3},{3,2},{4,5},{5,4},{6,7},{7,6},{8,9},{9,8},{10,11... | collective-permute-start | bytes 786440 | tf_op jit(solution)/shard_map/ppermute | solution.py:17
  13.3 9.1 %collective-permute-start.9 = (bf16[128,2048]{1,0:T(8,128)(2,1)S(1)}, bf16[128,2048]{1,0:T(8,128)(2,1)S(1)}, u32[]{:S(2)}, u32[]{:S(2)}) collective-permute-start(bf16[128,2048]{1,0:T(8,128)(2,1)S(1)} %get-tuple-element.41), channel_id=1, source_target_pairs={{0,1},{1,0},{2,3},{3,2},{4,5},{5,4},{6,7},{7,6},{8,9},{9,8},{10,11... | collective-permute-start | bytes 1572872 | tf_op jit(solution)/shard_map/ppermute | solution.py:17
  13.5 7.4 %collective-permute-start.7 = (f32[16,128]{1,0:T(8,128)S(1)}, f32[16,128]{1,0:T(8,128)S(1)}, u32[]{:S(2)}, u32[]{:S(2)}) collective-permute-start(f32[16,128]{1,0:T(8,128)S(1)} %get-tuple-element.32.refs_2_), channel_id=1, source_target_pairs={{0,16},{8,24},{16,8},{24,0},{1,17},{9,25},{17,9},{25,1},{2,18},{10... | collective-permute-start | bytes 24584 | tf_op jit(solution)/shard_map/ppermute | solution.py:271
  16.1 4.8 %collective-permute-start.6 = (f32[16,128]{1,0:T(8,128)S(1)}, f32[16,128]{1,0:T(8,128)S(1)}, u32[]{:S(2)}, u32[]{:S(2)}) collective-permute-start(f32[16,128]{1,0:T(8,128)S(1)} %get-tuple-element.32.refs_2_), channel_id=1, source_target_pairs={{0,24},{8,16},{16,0},{24,8},{1,25},{9,17},{17,1},{25,9},{2,26},{10... | collective-permute-start | bytes 24584 | tf_op jit(solution)/shard_map/ppermute | solution.py:271
  17.3 3.7 %collective-permute-start.5 = (f32[16,128]{1,0:T(8,128)S(1)}, f32[16,128]{1,0:T(8,128)S(1)}, u32[]{:S(2)}, u32[]{:S(2)}) collective-permute-start(f32[16,128]{1,0:T(8,128)S(1)} %get-tuple-element.32.refs_2_), channel_id=1, source_target_pairs={{0,8},{8,0},{16,24},{24,16},{1,9},{9,1},{17,25},{25,17},{2,10},{10... | collective-permute-start | bytes 24584 | tf_op jit(solution)/shard_map/ppermute | solution.py:271
  21.0 1.3 %collective-permute-start.8 = (f32[16,128]{1,0:T(8,128)S(1)}, f32[16,128]{1,0:T(8,128)S(1)}, u32[]{:S(2)}, u32[]{:S(2)}) collective-permute-start(f32[16,128]{1,0:T(8,128)S(1)} %get-tuple-element.35), channel_id=1, source_target_pairs={{0,1},{1,0},{2,3},{3,2},{4,5},{5,4},{6,7},{7,6},{8,9},{9,8},{10,11... | collective-permute-start | bytes 24584 | tf_op jit(solution)/shard_map/ppermute | solution.py:17
  22.3 7.8 %copy-start = (f32[32,1024]{1,0:T(8,128)S(1)}, f32[32,1024]{1,0:T(8,128)}, u32[]{:S(2)}) copy-start(f32[32,1024]{1,0:T(8,128)} %cent_ref.1) | copy-start | bytes 393220
  23.2 3.8 %collective-permute-start.10 = (bf16[32,1152]{1,0:T(8,128)(2,1)S(1)}, bf16[32,1152]{1,0:T(8,128)(2,1)S(1)}, u32[]{:S(2)}, u32[]{:S(2)}) collective-permute-start(bf16[32,1152]{1,0:T(8,128)(2,1)S(1)} %get-tuple-element.47), channel_id=1, source_target_pairs={{5,0},{2,1},{7,2},{0,3},{1,4},{6,5},{3,6},{4,7},{13,8},{10,9},{15,... | collective-permute-start | bytes 221192 | tf_op jit(solution)/shard_map/ppermute | solution.py:294
  24.1 5.5 %collective-permute-start.11 = (bf16[32,1152]{1,0:T(8,128)(2,1)S(1)}, bf16[32,1152]{1,0:T(8,128)(2,1)S(1)}, u32[]{:S(2)}, u32[]{:S(2)}) collective-permute-start(bf16[32,1152]{1,0:T(8,128)(2,1)S(1)} %get-tuple-element.48), channel_id=1, source_target_pairs={{7,0},{6,1},{5,2},{4,3},{3,4},{2,5},{1,6},{0,7},{15,8},{14,9},{13,... | collective-permute-start | bytes 221192 | tf_op jit(solution)/shard_map/ppermute | solution.py:294
  25.2 4.9 %collective-permute-start.12 = (bf16[32,1152]{1,0:T(8,128)(2,1)S(1)}, bf16[32,1152]{1,0:T(8,128)(2,1)S(1)}, u32[]{:S(2)}, u32[]{:S(2)}) collective-permute-start(bf16[32,1152]{1,0:T(8,128)(2,1)S(1)} %get-tuple-element.49), channel_id=1, source_target_pairs={{3,0},{4,1},{1,2},{6,3},{7,4},{0,5},{5,6},{2,7},{11,8},{12,9},{9,1... | collective-permute-start | bytes 221192 | tf_op jit(solution)/shard_map/ppermute | solution.py:294

commit v25 on v23

--- a/solution.py
+++ b/solution.py
@@ -190,8 +190,9 @@
             send_refs[slot - 1][:, width:] = mass_lanes(mass)
 
 
-def final_kernel(own_ref, own_mass_ref, cent_ref, *refs):
-    *got_refs, next_ref, mass_ref = refs
+def final_kernel(own_ref, own_mass_ref, cent_ref, lse_ref, *refs):
+    *got_refs, next_ref, mass_ref, doc_lse_ref = refs
+    doc_lse_ref[...] = lse_ref[...]
     width = own_ref.shape[1]
     got = [read_rows(r[...], width) for r in got_refs]
     term = tree([own_ref[...]] + [a for a, _ in got], jnp.add)
@@ -267,9 +268,9 @@
             lax.ppermute(x, "dev", [(target, source) for source, target in pairs])
             for x, pairs in zip(sends[::-1], routes[::-1])
         ]
-        result, mass = call(
-            final_kernel, [shape((rows, width)), shape((1, rows))],
-            own, own_mass, centroids, *arrived,
+        result, mass, doc_lse = call(
+            final_kernel, [shape((rows, width)), shape((1, rows)), shape(doc_lse.shape)],
+            own, own_mass, centroids, doc_lse, *arrived,
         )
         return (result, mass.reshape(rows), doc_lse.reshape(count))
 

time: 30.5 us -> 30.5 us (level)
  no operation moved by 1% of the time
where the time goes in v25:
time: 30.5 us; the launch traced here: 30.3 us
  starting transfers between devices  11.8 us (39%)
  Pallas kernels  9.3 us (30%)
  waiting for transfers between devices  7.56 us (25%)
  other arithmetic  0.92 us (3%)
  between operations  0.74 us (2%)
    pallas_call x2, Pallas kernels, load(): pl.pallas_call(kernel, out_shape=[shape(dims, source.dtype), shape(follow...  4.93 us
    pallas_call x6, Pallas kernels, call(): pl.pallas_call(kernel, out_shape=outs, in_specs=[SMEM if x.dtype == jnp.i...  4.37 us
    ppermute x3, starting transfers between devices, body(): blocks = [lax.ppermute(rounded, 'dev', pairs) for pairs in routes]  4.28 us
    ppermute x3, starting transfers between devices, body(): others = [lax.ppermute(lse, 'cgrp', pairs) for pairs in plan]  4.22 us
    ppermute x3, waiting for transfers between devices, body(): lax.ppermute(x, 'dev', [(target, source) for source, target in pairs])  3.61 us
    ppermute x3, starting transfers between devices, body(): lax.ppermute(x, 'dev', [(target, source) for source, target in pairs])  3.02 us
    ppermute x3, waiting for transfers between devices, body(): blocks = [lax.ppermute(rounded, 'dev', pairs) for pairs in routes]  1.54 us
    ppermute x2, waiting for transfers between devices, swap(): return lax.ppermute(x, axis, [(i, i ^ mask) for i in range(size)])  1.31 us
  transfers between devices with their start and end apart: 11, of which 8 were waited for; matrix products, arithmetic and copies ran while one was open for 0% of the time, Pallas kernels for 22%

profile of v25, /device:TPU:0, one launch (start us, length us, event | category | flops | bytes accessed | tf_op | source)
XLA Modules:
  0.0 30.3 jit_solution(3874423644261131979)
XLA Ops:
  0.6 0.9 %convert_element_type.3.follow_ref = bf16[32,1024]{1,0:T(8,128)(2,1)S(1)} convert(f32[32,1024]{1,0:T(8,128)} %cent_ref.1) | non-fusion elementwise | flops 32768 | bytes 196608 | tf_op jit(solution)/shard_map/convert_element_type | solution.py:234
  1.5 2.5 %collective-permute-start.2 = (bf16[32,1024]{1,0:T(8,128)(2,1)S(1)}, bf16[32,1024]{1,0:T(8,128)(2,1)S(1)}, u32[]{:S(2)}, u32[]{:S(2)}) collective-permute-start(bf16[32,1024]{1,0:T(8,128)(2,1)S(1)} %convert_element_type.3.follow_ref), channel_id=1, source_target_pairs={{0,5},{1,2},{2,7},{3,0},{4,1},{5,6},{6,3},{7,4},{8,13},{9,10},{10,... | collective-permute-start | bytes 196616 | tf_op jit(solution)/shard_map/ppermute | solution.py:236
  4.0 1.7 %collective-permute-start.1 = (bf16[32,1024]{1,0:T(8,128)(2,1)S(1)}, bf16[32,1024]{1,0:T(8,128)(2,1)S(1)}, u32[]{:S(2)}, u32[]{:S(2)}) collective-permute-start(bf16[32,1024]{1,0:T(8,128)(2,1)S(1)} %convert_element_type.3.follow_ref), channel_id=1, source_target_pairs={{0,7},{1,6},{2,5},{3,4},{4,3},{5,2},{6,1},{7,0},{8,15},{9,14},{10,... | collective-permute-start | bytes 196616 | tf_op jit(solution)/shard_map/ppermute | solution.py:236
  5.7 0.1 collective-permute-start
  5.8 2.7 %shard_map.49 = (bf16[1024,2048]{1,0:T(8,128)(2,1)S(1)}, bf16[32,1024]{1,0:T(8,128)(2,1)S(1)}) custom-call(bf16[2048,1024]{1,0:T(8,128)(2,1)} %source_ref.3, bf16[32,1024]{1,0:T(8,128)(2,1)S(1)} %convert_element_type.3.follow_ref), custom_call_target="tpu_custom_call" | custom-call | bytes 8388608 | tf_op jit(solution)/shard_map/pallas_call | solution.py:73
  8.6 1.5 %collective-permute-done = bf16[32,1024]{1,0:T(8,128)(2,1)S(1)} collective-permute-done((bf16[32,1024]{1,0:T(8,128)(2,1)S(1)}, bf16[32,1024]{1,0:T(8,128)(2,1)S(1)}, u32[]{:S(2)}, u32[]{:S(2)}) %collective-permute-start) | collective-permute-done | bytes 65568 | tf_op jit(solution)/shard_map/ppermute | solution.py:236
  10.1 0.0 collective-permute-done.1
  10.1 0.0 collective-permute-done.2
  10.2 0.2 collective-permute-start.3
  10.4 0.9 %shard_map.50 = (f32[128,2048]{1,0:T(8,128)S(1)}, f32[16,128]{1,0:T(8,128)S(1)}, f32[16,128]{1,0:T(8,128)S(1)}) custom-call(bf16[1024,2048]{1,0:T(8,128)(2,1)S(1)} %get-tuple-element.26.docs_ref, bf16[128,1024]{1,0:T(8,128)(2,1)S(1)} %constant_dynamic-update-slice_fusion.table_ref), custom_call_target="tpu_custom_call" | custom-call | flops 536870912 | bytes 4456448 | tf_op jit(solution)/shard_map/pallas_call | solution.py:219
  11.2 0.5 %collective-permute-done.3.table_ref = bf16[128,1024]{1,0:T(8,128)(2,1)S(1)} collective-permute-done((bf16[128,1024]{1,0:T(8,128)(2,1)S(1)}, bf16[128,1024]{1,0:T(8,128)(2,1)S(1)}, u32[]{:S(2)}, u32[]{:S(2)}) %collective-permute-start.3) | collective-permute-done | bytes 262176 | tf_op jit(solution)/shard_map/ppermute | solution.py:17
  11.8 0.9 %shard_map.51 = (f32[128,2048]{1,0:T(8,128)S(1)}, f32[16,128]{1,0:T(8,128)S(1)}, f32[16,128]{1,0:T(8,128)S(1)}) custom-call(bf16[1024,2048]{1,0:T(8,128)(2,1)S(1)} %get-tuple-element.26.docs_ref, bf16[128,1024]{1,0:T(8,128)(2,1)S(1)} %collective-permute-done.3.table_ref, f32[16,128]{1,0:T(8,128)S(1)} %get-tuple-element.28.first_top_ref.refs_6_, ...), custom_call_target="tpu_custom_call" | custom-call | flops 536870912 | bytes 4472832 | tf_op jit(solution)/shard_map/pallas_call | solution.py:219
  12.7 2.6 %collective-permute-start.6 = (f32[16,128]{1,0:T(8,128)S(1)}, f32[16,128]{1,0:T(8,128)S(1)}, u32[]{:S(2)}, u32[]{:S(2)}) collective-permute-start(f32[16,128]{1,0:T(8,128)S(1)} %get-tuple-element.30.follow_ref), channel_id=1, source_target_pairs={{0,16},{8,24},{16,8},{24,0},{1,17},{9,25},{17,9},{25,1},{2,18},{10... | collective-permute-start | bytes 24584 | tf_op jit(solution)/shard_map/ppermute | solution.py:247
  15.3 1.2 %collective-permute-start.5 = (f32[16,128]{1,0:T(8,128)S(1)}, f32[16,128]{1,0:T(8,128)S(1)}, u32[]{:S(2)}, u32[]{:S(2)}) collective-permute-start(f32[16,128]{1,0:T(8,128)S(1)} %get-tuple-element.30.follow_ref), channel_id=1, source_target_pairs={{0,24},{8,16},{16,0},{24,8},{1,25},{9,17},{17,1},{25,9},{2,26},{10... | collective-permute-start | bytes 24584 | tf_op jit(solution)/shard_map/ppermute | solution.py:247
  16.5 0.3 %collective-permute-start.4 = (f32[16,128]{1,0:T(8,128)S(1)}, f32[16,128]{1,0:T(8,128)S(1)}, u32[]{:S(2)}, u32[]{:S(2)}) collective-permute-start(f32[16,128]{1,0:T(8,128)S(1)} %get-tuple-element.30.follow_ref), channel_id=1, source_target_pairs={{0,8},{8,0},{16,24},{24,16},{1,9},{9,1},{17,25},{25,17},{2,10},{10... | collective-permute-start | bytes 24584 | tf_op jit(solution)/shard_map/ppermute | solution.py:247
  16.9 2.2 %shard_map.52 = (bf16[2048,1024]{1,0:T(8,128)(2,1)S(1)}, f32[16,128]{1,0:T(8,128)S(1)}) custom-call(bf16[2048,1024]{1,0:T(8,128)(2,1)} %source_ref.3, f32[16,128]{1,0:T(8,128)S(1)} %get-tuple-element.30.follow_ref), custom_call_target="tpu_custom_call" | custom-call | bytes 8388608 | tf_op jit(solution)/shard_map/pallas_call | solution.py:73
  19.1 0.0 collective-permute-done.6.refs_2_
  19.1 0.8 %collective-permute-done.5.refs_1_ = f32[16,128]{1,0:T(8,128)S(1)} collective-permute-done((f32[16,128]{1,0:T(8,128)S(1)}, f32[16,128]{1,0:T(8,128)S(1)}, u32[]{:S(2)}, u32[]{:S(2)}) %collective-permute-start.5) | collective-permute-done | bytes 8224 | tf_op jit(solution)/shard_map/ppermute | solution.py:247
  19.9 0.3 %collective-permute-done.4.refs_0_ = f32[16,128]{1,0:T(8,128)S(1)} collective-permute-done((f32[16,128]{1,0:T(8,128)S(1)}, f32[16,128]{1,0:T(8,128)S(1)}, u32[]{:S(2)}, u32[]{:S(2)}) %collective-permute-start.4) | collective-permute-done | bytes 8224 | tf_op jit(solution)/shard_map/ppermute | solution.py:247
  20.2 0.8 %shard_map.53 = (f32[16,128]{1,0:T(8,128)S(1)}, f32[16,128]{1,0:T(8,128)S(1)}, bf16[128,1152]{1,0:T(8,128)(2,1)S(1)}) custom-call(s32[1]{0:T(128)} %bitcast.me_ref, f32[16,128]{1,0:T(8,128)S(1)} %get-tuple-element.31.lse_ref, f32[16,128]{1,0:T(8,128)S(1)} %collective-permute-done.4.refs_0_, f32[16,128]{1,0:T(8,128)S(1)} %collective-permute-done.5.refs_1_, ...), custom_call_target="tpu_custom_call" | custom-call | flops 536870912 | bytes 5292036 | tf_op jit(solution)/shard_map/pallas_call | solution.py:219
  21.0 0.0 copy-start
  21.0 0.1 collective-permute-start.7
  21.1 0.8 %shard_map.54 = (f32[128,1024]{1,0:T(8,128)S(1)}, f32[128,128]{1,0:T(8,128)S(1)}) custom-call(f32[16,128]{1,0:T(8,128)S(1)} %get-tuple-element.35.factor_ref, bf16[2048,1024]{1,0:T(8,128)(2,1)S(1)} %get-tuple-element.32.refs_3_.docs_ref, f32[128,2048]{1,0:T(8,128)S(1)} %get-tuple-element.36.part_ref), custom_call_target="tpu_custom_call" | custom-call | flops 536870912 | bytes 5251072 | tf_op jit(solution)/shard_map/pallas_call | solution.py:219
  21.9 0.8 %collective-permute-done.7.got_ref = bf16[128,1152]{1,0:T(8,128)(2,1)S(1)} collective-permute-done((bf16[128,1152]{1,0:T(8,128)(2,1)S(1)}, bf16[128,1152]{1,0:T(8,128)(2,1)S(1)}, u32[]{:S(2)}, u32[]{:S(2)}) %collective-permute-start.7) | collective-permute-done | bytes 294944 | tf_op jit(solution)/shard_map/ppermute | solution.py:17
  22.7 0.2 shard_map.55
  22.8 1.0 %collective-permute-start.8 = (bf16[32,1152]{1,0:T(8,128)(2,1)S(1)}, bf16[32,1152]{1,0:T(8,128)(2,1)S(1)}, u32[]{:S(2)}, u32[]{:S(2)}) collective-permute-start(bf16[32,1152]{1,0:T(8,128)(2,1)S(1)} %get-tuple-element.43), channel_id=1, source_target_pairs={{5,0},{2,1},{7,2},{0,3},{1,4},{6,5},{3,6},{4,7},{13,8},{10,9},{15,... | collective-permute-start | bytes 221192 | tf_op jit(solution)/shard_map/ppermute | solution.py:268
  23.8 1.4 %collective-permute-start.9 = (bf16[32,1152]{1,0:T(8,128)(2,1)S(1)}, bf16[32,1152]{1,0:T(8,128)(2,1)S(1)}, u32[]{:S(2)}, u32[]{:S(2)}) collective-permute-start(bf16[32,1152]{1,0:T(8,128)(2,1)S(1)} %get-tuple-element.44), channel_id=1, source_target_pairs={{7,0},{6,1},{5,2},{4,3},{3,4},{2,5},{1,6},{0,7},{15,8},{14,9},{13,... | collective-permute-start | bytes 221192 | tf_op jit(solution)/shard_map/ppermute | solution.py:268
  25.2 0.6 %collective-permute-start.10 = (bf16[32,1152]{1,0:T(8,128)(2,1)S(1)}, bf16[32,1152]{1,0:T(8,128)(2,1)S(1)}, u32[]{:S(2)}, u32[]{:S(2)}) collective-permute-start(bf16[32,1152]{1,0:T(8,128)(2,1)S(1)} %get-tuple-element.45), channel_id=1, source_target_pairs={{3,0},{4,1},{1,2},{6,3},{7,4},{0,5},{5,6},{2,7},{11,8},{12,9},{9,1... | collective-permute-start | bytes 221192 | tf_op jit(solution)/shard_map/ppermute | solution.py:268
  25.9 0.8 %collective-permute-done.8.refs_0_ = bf16[32,1152]{1,0:T(8,128)(2,1)S(1)} collective-permute-done((bf16[32,1152]{1,0:T(8,128)(2,1)S(1)}, bf16[32,1152]{1,0:T(8,128)(2,1)S(1)}, u32[]{:S(2)}, u32[]{:S(2)}) %collective-permute-start.8) | collective-permute-done | bytes 73760 | tf_op jit(solution)/shard_map/ppermute | solution.py:268
  26.7 2.4 %collective-permute-done.9.refs_1_ = bf16[32,1152]{1,0:T(8,128)(2,1)S(1)} collective-permute-done((bf16[32,1152]{1,0:T(8,128)(2,1)S(1)}, bf16[32,1152]{1,0:T(8,128)(2,1)S(1)}, u32[]{:S(2)}, u32[]{:S(2)}) %collective-permute-start.9) | collective-permute-done | bytes 73760 | tf_op jit(solution)/shard_map/ppermute | solution.py:268
  29.0 0.4 %collective-permute-done.10.refs_2_ = bf16[32,1152]{1,0:T(8,128)(2,1)S(1)} collective-permute-done((bf16[32,1152]{1,0:T(8,128)(2,1)S(1)}, bf16[32,1152]{1,0:T(8,128)(2,1)S(1)}, u32[]{:S(2)}, u32[]{:S(2)}) %collective-permute-start.10) | collective-permute-done | bytes 73760 | tf_op jit(solution)/shard_map/ppermute | solution.py:268
  29.5 0.0 copy-done
  29.5 0.8 %shard_map.56 = (f32[32,1024]{1,0:T(8,128)}, f32[1,32]{1,0:T(1,128)}, f32[16,128]{1,0:T(8,128)}) custom-call(f32[32,1024]{1,0:T(8,128)S(1)} %get-tuple-element.40.own_ref, f32[32,128]{1,0:T(8,128)S(1)} %get-tuple-element.41.own_mass_ref, f32[32,1024]{1,0:T(8,128)S(1)} %copy-done, f32[16,128]{1,0:T(8,128)S(1)} %get-tuple-element.42.lse_ref, ...), custom_call_target="tpu_custom_call" | custom-call | bytes 507904 | tf_op jit(solution)/shard_map/pallas_call | solution.py:219
  (4 shorter events, 0.0 us)
Async XLA Ops:
  1.5 8.6 %collective-permute-start.2 = (bf16[32,1024]{1,0:T(8,128)(2,1)S(1)}, bf16[32,1024]{1,0:T(8,128)(2,1)S(1)}, u32[]{:S(2)}, u32[]{:S(2)}) collective-permute-start(bf16[32,1024]{1,0:T(8,128)(2,1)S(1)} %convert_element_type.3.follow_ref), channel_id=1, source_target_pairs={{0,5},{1,2},{2,7},{3,0},{4,1},{5,6},{6,3},{7,4},{8,13},{9,10},{10,... | collective-permute-start | bytes 196616 | tf_op jit(solution)/shard_map/ppermute | solution.py:236
  4.0 6.1 %collective-permute-start.1 = (bf16[32,1024]{1,0:T(8,128)(2,1)S(1)}, bf16[32,1024]{1,0:T(8,128)(2,1)S(1)}, u32[]{:S(2)}, u32[]{:S(2)}) collective-permute-start(bf16[32,1024]{1,0:T(8,128)(2,1)S(1)} %convert_element_type.3.follow_ref), channel_id=1, source_target_pairs={{0,7},{1,6},{2,5},{3,4},{4,3},{5,2},{6,1},{7,0},{8,15},{9,14},{10,... | collective-permute-start | bytes 196616 | tf_op jit(solution)/shard_map/ppermute | solution.py:236
  5.7 4.4 %collective-permute-start = (bf16[32,1024]{1,0:T(8,128)(2,1)S(1)}, bf16[32,1024]{1,0:T(8,128)(2,1)S(1)}, u32[]{:S(2)}, u32[]{:S(2)}) collective-permute-start(bf16[32,1024]{1,0:T(8,128)(2,1)S(1)} %convert_element_type.3.follow_ref), channel_id=1, source_target_pairs={{0,3},{1,4},{2,1},{3,6},{4,7},{5,0},{6,5},{7,2},{8,11},{9,12},{10,... | collective-permute-start | bytes 196616 | tf_op jit(solution)/shard_map/ppermute | solution.py:236
  10.2 1.6 %collective-permute-start.3 = (bf16[128,1024]{1,0:T(8,128)(2,1)S(1)}, bf16[128,1024]{1,0:T(8,128)(2,1)S(1)}, u32[]{:S(2)}, u32[]{:S(2)}) collective-permute-start(bf16[128,1024]{1,0:T(8,128)(2,1)S(1)} %constant_dynamic-update-slice_fusion.table_ref), channel_id=1, source_target_pairs={{0,1},{1,0},{2,3},{3,2},{4,5},{5,4},{6,7},{7,6},{8,9},{9,8},{10,11... | collective-permute-start | bytes 786440 | tf_op jit(solution)/shard_map/ppermute | solution.py:17
  12.7 6.4 %collective-permute-start.6 = (f32[16,128]{1,0:T(8,128)S(1)}, f32[16,128]{1,0:T(8,128)S(1)}, u32[]{:S(2)}, u32[]{:S(2)}) collective-permute-start(f32[16,128]{1,0:T(8,128)S(1)} %get-tuple-element.30.follow_ref), channel_id=1, source_target_pairs={{0,16},{8,24},{16,8},{24,0},{1,17},{9,25},{17,9},{25,1},{2,18},{10... | collective-permute-start | bytes 24584 | tf_op jit(solution)/shard_map/ppermute | solution.py:247
  15.3 4.5 %collective-permute-start.5 = (f32[16,128]{1,0:T(8,128)S(1)}, f32[16,128]{1,0:T(8,128)S(1)}, u32[]{:S(2)}, u32[]{:S(2)}) collective-permute-start(f32[16,128]{1,0:T(8,128)S(1)} %get-tuple-element.30.follow_ref), channel_id=1, source_target_pairs={{0,24},{8,16},{16,0},{24,8},{1,25},{9,17},{17,1},{25,9},{2,26},{10... | collective-permute-start | bytes 24584 | tf_op jit(solution)/shard_map/ppermute | solution.py:247
  16.5 3.7 %collective-permute-start.4 = (f32[16,128]{1,0:T(8,128)S(1)}, f32[16,128]{1,0:T(8,128)S(1)}, u32[]{:S(2)}, u32[]{:S(2)}) collective-permute-start(f32[16,128]{1,0:T(8,128)S(1)} %get-tuple-element.30.follow_ref), channel_id=1, source_target_pairs={{0,8},{8,0},{16,24},{24,16},{1,9},{9,1},{17,25},{25,17},{2,10},{10... | collective-permute-start | bytes 24584 | tf_op jit(solution)/shard_map/ppermute | solution.py:247
  21.0 8.5 %copy-start = (f32[32,1024]{1,0:T(8,128)S(1)}, f32[32,1024]{1,0:T(8,128)}, u32[]{:S(2)}) copy-start(f32[32,1024]{1,0:T(8,128)} %cent_ref.1) | copy-start | bytes 393220
  21.0 1.6 %collective-permute-start.7 = (bf16[128,1152]{1,0:T(8,128)(2,1)S(1)}, bf16[128,1152]{1,0:T(8,128)(2,1)S(1)}, u32[]{:S(2)}, u32[]{:S(2)}) collective-permute-start(bf16[128,1152]{1,0:T(8,128)(2,1)S(1)} %get-tuple-element.39), channel_id=1, source_target_pairs={{0,1},{1,0},{2,3},{3,2},{4,5},{5,4},{6,7},{7,6},{8,9},{9,8},{10,11... | collective-permute-start | bytes 884744 | tf_op jit(solution)/shard_map/ppermute | solution.py:17
  22.8 3.8 %collective-permute-start.8 = (bf16[32,1152]{1,0:T(8,128)(2,1)S(1)}, bf16[32,1152]{1,0:T(8,128)(2,1)S(1)}, u32[]{:S(2)}, u32[]{:S(2)}) collective-permute-start(bf16[32,1152]{1,0:T(8,128)(2,1)S(1)} %get-tuple-element.43), channel_id=1, source_target_pairs={{5,0},{2,1},{7,2},{0,3},{1,4},{6,5},{3,6},{4,7},{13,8},{10,9},{15,... | collective-permute-start | bytes 221192 | tf_op jit(solution)/shard_map/ppermute | solution.py:268
  23.8 5.2 %collective-permute-start.9 = (bf16[32,1152]{1,0:T(8,128)(2,1)S(1)}, bf16[32,1152]{1,0:T(8,128)(2,1)S(1)}, u32[]{:S(2)}, u32[]{:S(2)}) collective-permute-start(bf16[32,1152]{1,0:T(8,128)(2,1)S(1)} %get-tuple-element.44), channel_id=1, source_target_pairs={{7,0},{6,1},{5,2},{4,3},{3,4},{2,5},{1,6},{0,7},{15,8},{14,9},{13,... | collective-permute-start | bytes 221192 | tf_op jit(solution)/shard_map/ppermute | solution.py:268
  25.2 4.2 %collective-permute-start.10 = (bf16[32,1152]{1,0:T(8,128)(2,1)S(1)}, bf16[32,1152]{1,0:T(8,128)(2,1)S(1)}, u32[]{:S(2)}, u32[]{:S(2)}) collective-permute-start(bf16[32,1152]{1,0:T(8,128)(2,1)S(1)} %get-tuple-element.45), channel_id=1, source_target_pairs={{3,0},{4,1},{1,2},{6,3},{7,4},{0,5},{5,6},{2,7},{11,8},{12,9},{9,1... | collective-permute-start | bytes 221192 | tf_op jit(solution)/shard_map/ppermute | solution.py:268

commit v26 on v25

--- a/solution.py
+++ b/solution.py
@@ -20,7 +20,7 @@
 def chip_plan(n):
     near = list(range(2, n - 2, 2))
     turned = near[len(near) // 2:] + near[:len(near) // 2]
-    masks = list(zip(near, turned))
+    masks = list(zip(turned, near))
     masks = masks[:1] + [(n - 2, n - 2)] + masks[1:]
     return [[(i, i ^ pair[i % 2] ^ 1) for i in range(n)] for pair in masks]
 

time: 30.5 us -> 30.7 us (level)
  starting transfers between devices: 11.8 us -> 12.5 us
  waiting for transfers between devices: 7.56 us -> 7.08 us
    ppermute x3, waiting for transfers between devices: 1.54 us -> 0.86 us  [body(): blocks = [lax.ppermute(rounded, 'dev', pairs) for pairs in routes]]
    ppermute x3, waiting for transfers between devices: 3.61 us -> 4.24 us  [body(): lax.ppermute(x, 'dev', [(target, source) for source, target in pairs])]
    ppermute x2, starting transfers between devices: 0.25 us -> 0.7 us  [swap(): return lax.ppermute(x, axis, [(i, i ^ mask) for i in range(size)])]
where the time goes in v26:
time: 30.7 us; the launch traced here: 30.5 us
  starting transfers between devices  12.5 us (41%)
  Pallas kernels  9.3 us (30%)
  waiting for transfers between devices  7.08 us (23%)
  other arithmetic  0.92 us (3%)
  between operations  0.74 us (2%)
    pallas_call x2, Pallas kernels, load(): pl.pallas_call(kernel, out_shape=[shape(dims, source.dtype), shape(follow...  4.93 us
    ppermute x3, starting transfers between devices, body(): others = [lax.ppermute(lse, 'cgrp', pairs) for pairs in plan]  4.52 us
    pallas_call x6, Pallas kernels, call(): pl.pallas_call(kernel, out_shape=outs, in_specs=[SMEM if x.dtype == jnp.i...  4.37 us
    ppermute x3, starting transfers between devices, body(): blocks = [lax.ppermute(rounded, 'dev', pairs) for pairs in routes]  4.25 us
    ppermute x3, waiting for transfers between devices, body(): lax.ppermute(x, 'dev', [(target, source) for source, target in pairs])  4.24 us
    ppermute x3, starting transfers between devices, body(): lax.ppermute(x, 'dev', [(target, source) for source, target in pairs])  3 us
    ppermute x2, waiting for transfers between devices, swap(): return lax.ppermute(x, axis, [(i, i ^ mask) for i in range(size)])  1.05 us
    ppermute x3, waiting for transfers between devices, body(): others = [lax.ppermute(lse, 'cgrp', pairs) for pairs in plan]  0.94 us
  transfers between devices with their start and end apart: 11, of which 8 were waited for; matrix products, arithmetic and copies ran while one was open for 0% of the time, Pallas kernels for 22%

profile of v26, /device:TPU:0, one launch (start us, length us, event | category | flops | bytes accessed | tf_op | source)
XLA Modules:
  0.0 30.5 jit_solution(5391585696618000085)
XLA Ops:
  0.6 0.9 %convert_element_type.3.follow_ref = bf16[32,1024]{1,0:T(8,128)(2,1)S(1)} convert(f32[32,1024]{1,0:T(8,128)} %cent_ref.1) | non-fusion elementwise | flops 32768 | bytes 196608 | tf_op jit(solution)/shard_map/convert_element_type | solution.py:234
  1.5 2.4 %collective-permute-start.2 = (bf16[32,1024]{1,0:T(8,128)(2,1)S(1)}, bf16[32,1024]{1,0:T(8,128)(2,1)S(1)}, u32[]{:S(2)}, u32[]{:S(2)}) collective-permute-start(bf16[32,1024]{1,0:T(8,128)(2,1)S(1)} %convert_element_type.3.follow_ref), channel_id=1, source_target_pairs={{0,3},{1,4},{2,1},{3,6},{4,7},{5,0},{6,5},{7,2},{8,11},{9,12},{10,... | collective-permute-start | bytes 196616 | tf_op jit(solution)/shard_map/ppermute | solution.py:236
  4.0 1.7 %collective-permute-start.1 = (bf16[32,1024]{1,0:T(8,128)(2,1)S(1)}, bf16[32,1024]{1,0:T(8,128)(2,1)S(1)}, u32[]{:S(2)}, u32[]{:S(2)}) collective-permute-start(bf16[32,1024]{1,0:T(8,128)(2,1)S(1)} %convert_element_type.3.follow_ref), channel_id=1, source_target_pairs={{0,7},{1,6},{2,5},{3,4},{4,3},{5,2},{6,1},{7,0},{8,15},{9,14},{10,... | collective-permute-start | bytes 196616 | tf_op jit(solution)/shard_map/ppermute | solution.py:236
  5.7 0.1 collective-permute-start
  5.8 2.7 %shard_map.49 = (bf16[1024,2048]{1,0:T(8,128)(2,1)S(1)}, bf16[32,1024]{1,0:T(8,128)(2,1)S(1)}) custom-call(bf16[2048,1024]{1,0:T(8,128)(2,1)} %source_ref.3, bf16[32,1024]{1,0:T(8,128)(2,1)S(1)} %convert_element_type.3.follow_ref), custom_call_target="tpu_custom_call" | custom-call | bytes 8388608 | tf_op jit(solution)/shard_map/pallas_call | solution.py:73
  8.6 0.9 %collective-permute-done = bf16[32,1024]{1,0:T(8,128)(2,1)S(1)} collective-permute-done((bf16[32,1024]{1,0:T(8,128)(2,1)S(1)}, bf16[32,1024]{1,0:T(8,128)(2,1)S(1)}, u32[]{:S(2)}, u32[]{:S(2)}) %collective-permute-start) | collective-permute-done | bytes 65568 | tf_op jit(solution)/shard_map/ppermute | solution.py:236
  9.4 0.0 collective-permute-done.1
  9.4 0.0 collective-permute-done.2
  9.5 0.6 %collective-permute-start.3 = (bf16[128,1024]{1,0:T(8,128)(2,1)S(1)}, bf16[128,1024]{1,0:T(8,128)(2,1)S(1)}, u32[]{:S(2)}, u32[]{:S(2)}) collective-permute-start(bf16[128,1024]{1,0:T(8,128)(2,1)S(1)} %constant_dynamic-update-slice_fusion.table_ref), channel_id=1, source_target_pairs={{0,1},{1,0},{2,3},{3,2},{4,5},{5,4},{6,7},{7,6},{8,9},{9,8},{10,11... | collective-permute-start | bytes 786440 | tf_op jit(solution)/shard_map/ppermute | solution.py:17
  10.1 0.9 %shard_map.50 = (f32[128,2048]{1,0:T(8,128)S(1)}, f32[16,128]{1,0:T(8,128)S(1)}, f32[16,128]{1,0:T(8,128)S(1)}) custom-call(bf16[1024,2048]{1,0:T(8,128)(2,1)S(1)} %get-tuple-element.26.docs_ref, bf16[128,1024]{1,0:T(8,128)(2,1)S(1)} %constant_dynamic-update-slice_fusion.table_ref), custom_call_target="tpu_custom_call" | custom-call | flops 536870912 | bytes 4456448 | tf_op jit(solution)/shard_map/pallas_call | solution.py:219
  11.0 0.3 collective-permute-done.3.table_ref
  11.2 0.9 %shard_map.51 = (f32[128,2048]{1,0:T(8,128)S(1)}, f32[16,128]{1,0:T(8,128)S(1)}, f32[16,128]{1,0:T(8,128)S(1)}) custom-call(bf16[1024,2048]{1,0:T(8,128)(2,1)S(1)} %get-tuple-element.26.docs_ref, bf16[128,1024]{1,0:T(8,128)(2,1)S(1)} %collective-permute-done.3.table_ref, f32[16,128]{1,0:T(8,128)S(1)} %get-tuple-element.28.first_top_ref.refs_6_, ...), custom_call_target="tpu_custom_call" | custom-call | flops 536870912 | bytes 4472832 | tf_op jit(solution)/shard_map/pallas_call | solution.py:219
  12.1 2.9 %collective-permute-start.6 = (f32[16,128]{1,0:T(8,128)S(1)}, f32[16,128]{1,0:T(8,128)S(1)}, u32[]{:S(2)}, u32[]{:S(2)}) collective-permute-start(f32[16,128]{1,0:T(8,128)S(1)} %get-tuple-element.30.follow_ref), channel_id=1, source_target_pairs={{0,16},{8,24},{16,8},{24,0},{1,17},{9,25},{17,9},{25,1},{2,18},{10... | collective-permute-start | bytes 24584 | tf_op jit(solution)/shard_map/ppermute | solution.py:247
  15.1 1.1 %collective-permute-start.5 = (f32[16,128]{1,0:T(8,128)S(1)}, f32[16,128]{1,0:T(8,128)S(1)}, u32[]{:S(2)}, u32[]{:S(2)}) collective-permute-start(f32[16,128]{1,0:T(8,128)S(1)} %get-tuple-element.30.follow_ref), channel_id=1, source_target_pairs={{0,24},{8,16},{16,0},{24,8},{1,25},{9,17},{17,1},{25,9},{2,26},{10... | collective-permute-start | bytes 24584 | tf_op jit(solution)/shard_map/ppermute | solution.py:247
  16.2 0.5 %collective-permute-start.4 = (f32[16,128]{1,0:T(8,128)S(1)}, f32[16,128]{1,0:T(8,128)S(1)}, u32[]{:S(2)}, u32[]{:S(2)}) collective-permute-start(f32[16,128]{1,0:T(8,128)S(1)} %get-tuple-element.30.follow_ref), channel_id=1, source_target_pairs={{0,8},{8,0},{16,24},{24,16},{1,9},{9,1},{17,25},{25,17},{2,10},{10... | collective-permute-start | bytes 24584 | tf_op jit(solution)/shard_map/ppermute | solution.py:247
  16.7 2.2 %shard_map.52 = (bf16[2048,1024]{1,0:T(8,128)(2,1)S(1)}, f32[16,128]{1,0:T(8,128)S(1)}) custom-call(bf16[2048,1024]{1,0:T(8,128)(2,1)} %source_ref.3, f32[16,128]{1,0:T(8,128)S(1)} %get-tuple-element.30.follow_ref), custom_call_target="tpu_custom_call" | custom-call | bytes 8388608 | tf_op jit(solution)/shard_map/pallas_call | solution.py:73
  18.9 0.0 collective-permute-done.6.refs_2_
  18.9 0.8 %collective-permute-done.5.refs_1_ = f32[16,128]{1,0:T(8,128)S(1)} collective-permute-done((f32[16,128]{1,0:T(8,128)S(1)}, f32[16,128]{1,0:T(8,128)S(1)}, u32[]{:S(2)}, u32[]{:S(2)}) %collective-permute-start.5) | collective-permute-done | bytes 8224 | tf_op jit(solution)/shard_map/ppermute | solution.py:247
  19.6 0.2 collective-permute-done.4.refs_0_
  19.8 0.8 %shard_map.53 = (f32[16,128]{1,0:T(8,128)S(1)}, f32[16,128]{1,0:T(8,128)S(1)}, bf16[128,1152]{1,0:T(8,128)(2,1)S(1)}) custom-call(s32[1]{0:T(128)} %bitcast.me_ref, f32[16,128]{1,0:T(8,128)S(1)} %get-tuple-element.31.lse_ref, f32[16,128]{1,0:T(8,128)S(1)} %collective-permute-done.4.refs_0_, f32[16,128]{1,0:T(8,128)S(1)} %collective-permute-done.5.refs_1_, ...), custom_call_target="tpu_custom_call" | custom-call | flops 536870912 | bytes 5292036 | tf_op jit(solution)/shard_map/pallas_call | solution.py:219
  20.6 0.0 copy-start
  20.6 0.1 collective-permute-start.7
  20.7 0.8 %shard_map.54 = (f32[128,1024]{1,0:T(8,128)S(1)}, f32[128,128]{1,0:T(8,128)S(1)}) custom-call(f32[16,128]{1,0:T(8,128)S(1)} %get-tuple-element.35.factor_ref, bf16[2048,1024]{1,0:T(8,128)(2,1)S(1)} %get-tuple-element.32.refs_3_.docs_ref, f32[128,2048]{1,0:T(8,128)S(1)} %get-tuple-element.36.part_ref), custom_call_target="tpu_custom_call" | custom-call | flops 536870912 | bytes 5251072 | tf_op jit(solution)/shard_map/pallas_call | solution.py:219
  21.5 0.8 %collective-permute-done.7.got_ref = bf16[128,1152]{1,0:T(8,128)(2,1)S(1)} collective-permute-done((bf16[128,1152]{1,0:T(8,128)(2,1)S(1)}, bf16[128,1152]{1,0:T(8,128)(2,1)S(1)}, u32[]{:S(2)}, u32[]{:S(2)}) %collective-permute-start.7) | collective-permute-done | bytes 294944 | tf_op jit(solution)/shard_map/ppermute | solution.py:17
  22.3 0.2 shard_map.55
  22.5 1.0 %collective-permute-start.8 = (bf16[32,1152]{1,0:T(8,128)(2,1)S(1)}, bf16[32,1152]{1,0:T(8,128)(2,1)S(1)}, u32[]{:S(2)}, u32[]{:S(2)}) collective-permute-start(bf16[32,1152]{1,0:T(8,128)(2,1)S(1)} %get-tuple-element.43), channel_id=1, source_target_pairs={{3,0},{4,1},{1,2},{6,3},{7,4},{0,5},{5,6},{2,7},{11,8},{12,9},{9,1... | collective-permute-start | bytes 221192 | tf_op jit(solution)/shard_map/ppermute | solution.py:268
  23.4 1.4 %collective-permute-start.9 = (bf16[32,1152]{1,0:T(8,128)(2,1)S(1)}, bf16[32,1152]{1,0:T(8,128)(2,1)S(1)}, u32[]{:S(2)}, u32[]{:S(2)}) collective-permute-start(bf16[32,1152]{1,0:T(8,128)(2,1)S(1)} %get-tuple-element.44), channel_id=1, source_target_pairs={{7,0},{6,1},{5,2},{4,3},{3,4},{2,5},{1,6},{0,7},{15,8},{14,9},{13,... | collective-permute-start | bytes 221192 | tf_op jit(solution)/shard_map/ppermute | solution.py:268
  24.9 0.6 %collective-permute-start.10 = (bf16[32,1152]{1,0:T(8,128)(2,1)S(1)}, bf16[32,1152]{1,0:T(8,128)(2,1)S(1)}, u32[]{:S(2)}, u32[]{:S(2)}) collective-permute-start(bf16[32,1152]{1,0:T(8,128)(2,1)S(1)} %get-tuple-element.45), channel_id=1, source_target_pairs={{5,0},{2,1},{7,2},{0,3},{1,4},{6,5},{3,6},{4,7},{13,8},{10,9},{15,... | collective-permute-start | bytes 221192 | tf_op jit(solution)/shard_map/ppermute | solution.py:268
  25.5 0.8 %collective-permute-done.8.refs_0_ = bf16[32,1152]{1,0:T(8,128)(2,1)S(1)} collective-permute-done((bf16[32,1152]{1,0:T(8,128)(2,1)S(1)}, bf16[32,1152]{1,0:T(8,128)(2,1)S(1)}, u32[]{:S(2)}, u32[]{:S(2)}) %collective-permute-start.8) | collective-permute-done | bytes 73760 | tf_op jit(solution)/shard_map/ppermute | solution.py:268
  26.3 2.0 %collective-permute-done.9.refs_1_ = bf16[32,1152]{1,0:T(8,128)(2,1)S(1)} collective-permute-done((bf16[32,1152]{1,0:T(8,128)(2,1)S(1)}, bf16[32,1152]{1,0:T(8,128)(2,1)S(1)}, u32[]{:S(2)}, u32[]{:S(2)}) %collective-permute-start.9) | collective-permute-done | bytes 73760 | tf_op jit(solution)/shard_map/ppermute | solution.py:268
  28.3 1.4 %collective-permute-done.10.refs_2_ = bf16[32,1152]{1,0:T(8,128)(2,1)S(1)} collective-permute-done((bf16[32,1152]{1,0:T(8,128)(2,1)S(1)}, bf16[32,1152]{1,0:T(8,128)(2,1)S(1)}, u32[]{:S(2)}, u32[]{:S(2)}) %collective-permute-start.10) | collective-permute-done | bytes 73760 | tf_op jit(solution)/shard_map/ppermute | solution.py:268
  29.7 0.0 copy-done
  29.7 0.8 %shard_map.56 = (f32[32,1024]{1,0:T(8,128)}, f32[1,32]{1,0:T(1,128)}, f32[16,128]{1,0:T(8,128)}) custom-call(f32[32,1024]{1,0:T(8,128)S(1)} %get-tuple-element.40.own_ref, f32[32,128]{1,0:T(8,128)S(1)} %get-tuple-element.41.own_mass_ref, f32[32,1024]{1,0:T(8,128)S(1)} %copy-done, f32[16,128]{1,0:T(8,128)S(1)} %get-tuple-element.42.lse_ref, ...), custom_call_target="tpu_custom_call" | custom-call | bytes 507904 | tf_op jit(solution)/shard_map/pallas_call | solution.py:219
  (4 shorter events, 0.0 us)
Async XLA Ops:
  1.5 7.9 %collective-permute-start.2 = (bf16[32,1024]{1,0:T(8,128)(2,1)S(1)}, bf16[32,1024]{1,0:T(8,128)(2,1)S(1)}, u32[]{:S(2)}, u32[]{:S(2)}) collective-permute-start(bf16[32,1024]{1,0:T(8,128)(2,1)S(1)} %convert_element_type.3.follow_ref), channel_id=1, source_target_pairs={{0,3},{1,4},{2,1},{3,6},{4,7},{5,0},{6,5},{7,2},{8,11},{9,12},{10,... | collective-permute-start | bytes 196616 | tf_op jit(solution)/shard_map/ppermute | solution.py:236
  4.0 5.4 %collective-permute-start.1 = (bf16[32,1024]{1,0:T(8,128)(2,1)S(1)}, bf16[32,1024]{1,0:T(8,128)(2,1)S(1)}, u32[]{:S(2)}, u32[]{:S(2)}) collective-permute-start(bf16[32,1024]{1,0:T(8,128)(2,1)S(1)} %convert_element_type.3.follow_ref), channel_id=1, source_target_pairs={{0,7},{1,6},{2,5},{3,4},{4,3},{5,2},{6,1},{7,0},{8,15},{9,14},{10,... | collective-permute-start | bytes 196616 | tf_op jit(solution)/shard_map/ppermute | solution.py:236
  5.7 3.7 %collective-permute-start = (bf16[32,1024]{1,0:T(8,128)(2,1)S(1)}, bf16[32,1024]{1,0:T(8,128)(2,1)S(1)}, u32[]{:S(2)}, u32[]{:S(2)}) collective-permute-start(bf16[32,1024]{1,0:T(8,128)(2,1)S(1)} %convert_element_type.3.follow_ref), channel_id=1, source_target_pairs={{0,5},{1,2},{2,7},{3,0},{4,1},{5,6},{6,3},{7,4},{8,13},{9,10},{10,... | collective-permute-start | bytes 196616 | tf_op jit(solution)/shard_map/ppermute | solution.py:236
  9.5 1.8 %collective-permute-start.3 = (bf16[128,1024]{1,0:T(8,128)(2,1)S(1)}, bf16[128,1024]{1,0:T(8,128)(2,1)S(1)}, u32[]{:S(2)}, u32[]{:S(2)}) collective-permute-start(bf16[128,1024]{1,0:T(8,128)(2,1)S(1)} %constant_dynamic-update-slice_fusion.table_ref), channel_id=1, source_target_pairs={{0,1},{1,0},{2,3},{3,2},{4,5},{5,4},{6,7},{7,6},{8,9},{9,8},{10,11... | collective-permute-start | bytes 786440 | tf_op jit(solution)/shard_map/ppermute | solution.py:17
  12.1 6.7 %collective-permute-start.6 = (f32[16,128]{1,0:T(8,128)S(1)}, f32[16,128]{1,0:T(8,128)S(1)}, u32[]{:S(2)}, u32[]{:S(2)}) collective-permute-start(f32[16,128]{1,0:T(8,128)S(1)} %get-tuple-element.30.follow_ref), channel_id=1, source_target_pairs={{0,16},{8,24},{16,8},{24,0},{1,17},{9,25},{17,9},{25,1},{2,18},{10... | collective-permute-start | bytes 24584 | tf_op jit(solution)/shard_map/ppermute | solution.py:247
  15.1 4.5 %collective-permute-start.5 = (f32[16,128]{1,0:T(8,128)S(1)}, f32[16,128]{1,0:T(8,128)S(1)}, u32[]{:S(2)}, u32[]{:S(2)}) collective-permute-start(f32[16,128]{1,0:T(8,128)S(1)} %get-tuple-element.30.follow_ref), channel_id=1, source_target_pairs={{0,24},{8,16},{16,0},{24,8},{1,25},{9,17},{17,1},{25,9},{2,26},{10... | collective-permute-start | bytes 24584 | tf_op jit(solution)/shard_map/ppermute | solution.py:247
  16.2 3.7 %collective-permute-start.4 = (f32[16,128]{1,0:T(8,128)S(1)}, f32[16,128]{1,0:T(8,128)S(1)}, u32[]{:S(2)}, u32[]{:S(2)}) collective-permute-start(f32[16,128]{1,0:T(8,128)S(1)} %get-tuple-element.30.follow_ref), channel_id=1, source_target_pairs={{0,8},{8,0},{16,24},{24,16},{1,9},{9,1},{17,25},{25,17},{2,10},{10... | collective-permute-start | bytes 24584 | tf_op jit(solution)/shard_map/ppermute | solution.py:247
  20.6 9.1 %copy-start = (f32[32,1024]{1,0:T(8,128)S(1)}, f32[32,1024]{1,0:T(8,128)}, u32[]{:S(2)}) copy-start(f32[32,1024]{1,0:T(8,128)} %cent_ref.1) | copy-start | bytes 393220
  20.6 1.6 %collective-permute-start.7 = (bf16[128,1152]{1,0:T(8,128)(2,1)S(1)}, bf16[128,1152]{1,0:T(8,128)(2,1)S(1)}, u32[]{:S(2)}, u32[]{:S(2)}) collective-permute-start(bf16[128,1152]{1,0:T(8,128)(2,1)S(1)} %get-tuple-element.39), channel_id=1, source_target_pairs={{0,1},{1,0},{2,3},{3,2},{4,5},{5,4},{6,7},{7,6},{8,9},{9,8},{10,11... | collective-permute-start | bytes 884744 | tf_op jit(solution)/shard_map/ppermute | solution.py:17
  22.5 3.8 %collective-permute-start.8 = (bf16[32,1152]{1,0:T(8,128)(2,1)S(1)}, bf16[32,1152]{1,0:T(8,128)(2,1)S(1)}, u32[]{:S(2)}, u32[]{:S(2)}) collective-permute-start(bf16[32,1152]{1,0:T(8,128)(2,1)S(1)} %get-tuple-element.43), channel_id=1, source_target_pairs={{3,0},{4,1},{1,2},{6,3},{7,4},{0,5},{5,6},{2,7},{11,8},{12,9},{9,1... | collective-permute-start | bytes 221192 | tf_op jit(solution)/shard_map/ppermute | solution.py:268
  23.4 4.8 %collective-permute-start.9 = (bf16[32,1152]{1,0:T(8,128)(2,1)S(1)}, bf16[32,1152]{1,0:T(8,128)(2,1)S(1)}, u32[]{:S(2)}, u32[]{:S(2)}) collective-permute-start(bf16[32,1152]{1,0:T(8,128)(2,1)S(1)} %get-tuple-element.44), channel_id=1, source_target_pairs={{7,0},{6,1},{5,2},{4,3},{3,4},{2,5},{1,6},{0,7},{15,8},{14,9},{13,... | collective-permute-start | bytes 221192 | tf_op jit(solution)/shard_map/ppermute | solution.py:268
  24.9 4.8 %collective-permute-start.10 = (bf16[32,1152]{1,0:T(8,128)(2,1)S(1)}, bf16[32,1152]{1,0:T(8,128)(2,1)S(1)}, u32[]{:S(2)}, u32[]{:S(2)}) collective-permute-start(bf16[32,1152]{1,0:T(8,128)(2,1)S(1)} %get-tuple-element.45), channel_id=1, source_target_pairs={{5,0},{2,1},{7,2},{0,3},{1,4},{6,5},{3,6},{4,7},{13,8},{10,9},{15,... | collective-permute-start | bytes 221192 | tf_op jit(solution)/shard_map/ppermute | solution.py:268
